TPU v7x, 32 devices: a whole 2x2x4 slice. The times are simulated.
32 devices in a mesh: seg: 8 (over z, core), dp: 4 (over y, x).
Axes of the slice: x: 2, y: 2, z: 4, core: 2. Of those that a mesh axis runs over, the one named last changes fastest.
Arguments:
- frames: bfloat16 [8, 4096, 80], P('dp', 'seg'), may hold values from -6 to 6
- speech_mask: int32 [8, 4096], P('dp', 'seg'), may hold values from 0 to 1
- targets: int32 [8, 4096], P('dp', 'seg'), may hold values from 0 to 1023
- in_proj: float32 [80, 512], replicated, may hold values from -0.625 to 0.625
- in_moment: float32 [80, 512], replicated, may hold values from -0.00061035156 to 0.00061035156
- in_second: float32 [80, 512], replicated, may hold values from 9.187344e-11 to 3.6749376e-10
- out_proj: float32 [512, 1024], replicated, may hold values from -0.25 to 0.25
- out_moment: float32 [512, 1024], replicated, may hold values from -0.00061035156 to 0.00061035156
- out_second: float32 [512, 1024], replicated, may hold values from 9.187344e-11 to 3.6749376e-10
- layer_vectors: float32 [2, 12, 512], replicated, may hold values from -0.5 to 2.07
- vectors_moment: float32 [2, 12, 512], replicated, may hold values from -0.0029296875 to 0.0029296875
- vectors_second: float32 [2, 12, 512], replicated, may hold values from 2.296836e-09 to 9.187344e-09
- outer_vectors: float32 [5, 512], replicated, may hold values from -0.5 to 2.07
- outer_moment: float32 [5, 512], replicated, may hold values from -0.0029296875 to 0.0029296875
- outer_second: float32 [5, 512], replicated, may hold values from 2.296836e-09 to 9.187344e-09
- attn_proj: float32 [2, 4, 512, 512], P(None, None, 'seg'), may hold values from -0.25 to 0.25
- attn_momentum: float32 [2, 4, 512, 512], P(None, None, 'seg'), may hold values from -0.00061035156 to 0.00061035156
- ff_up: float32 [2, 512, 2048], P(None, 'seg'), may hold values from -0.25 to 0.25
- up_momentum: float32 [2, 512, 2048], P(None, 'seg'), may hold values from -0.00061035156 to 0.00061035156
- ff_down: float32 [2, 2048, 512], P(None, 'seg'), may hold values from -0.125 to 0.125
- down_momentum: float32 [2, 2048, 512], P(None, 'seg'), may hold values from -0.00061035156 to 0.00061035156
- in_copy: bfloat16 [80, 512], replicated, may hold values from -0.625 to 0.625
- out_copy: bfloat16 [512, 1024], replicated, may hold values from -0.25 to 0.25
- attn_copy: bfloat16 [2, 4, 512, 512], replicated, may hold values from -0.25 to 0.25
- up_copy: bfloat16 [2, 512, 2048], replicated, may hold values from -0.25 to 0.25
- down_copy: bfloat16 [2, 2048, 512], replicated, may hold values from -0.125 to 0.125
Outputs:
- loss_sum: float32 [], replicated
- grad_norm: float32 [], replicated
- in_new: float32 [80, 512], replicated
- in_moment_new: float32 [80, 512], replicated
- in_second_new: float32 [80, 512], replicated
- out_new: float32 [512, 1024], replicated
- out_moment_new: float32 [512, 1024], replicated
- out_second_new: float32 [512, 1024], replicated
- vectors_new: float32 [2, 12, 512], replicated
- vectors_moment_new: float32 [2, 12, 512], replicated
- vectors_second_new: float32 [2, 12, 512], replicated
- outer_new: float32 [5, 512], replicated
- outer_moment_new: float32 [5, 512], replicated
- outer_second_new: float32 [5, 512], replicated
- attn_new: float32 [2, 4, 512, 512], P(None, None, 'seg')
- attn_momentum_new: float32 [2, 4, 512, 512], P(None, None, 'seg')
- up_new: float32 [2, 512, 2048], P(None, 'seg')
- up_momentum_new: float32 [2, 512, 2048], P(None, 'seg')
- down_new: float32 [2, 2048, 512], P(None, 'seg')
- down_momentum_new: float32 [2, 2048, 512], P(None, 'seg')
- in_copy_new: bfloat16 [80, 512], replicated
- out_copy_new: bfloat16 [512, 1024], replicated
- attn_copy_new: bfloat16 [2, 4, 512, 512], P(None, None, 'seg')
- up_copy_new: bfloat16 [2, 512, 2048], P(None, 'seg')
- down_copy_new: bfloat16 [2, 2048, 512], P(None, 'seg')
All inputs are finite; a program needn't handle non-finite values.
Results may differ from a plain program's by a relative error of at most 0.008.
Values may be sent and summed in bfloat16 or wider, within the bound.
A program may use at most 448 MiB of HBM per device.

v0:
```python
import jax
import jax.numpy as jnp
from jax import lax
from jax.sharding import PartitionSpec as P

D = 512
HEAD_DIM = 64
FF = 2048
LAYERS = 2
STEP = 10


HIGHEST = lax.Precision.HIGHEST


def from_behind(value, axis, steps):
    count = lax.axis_size(axis)
    leading, last = (max(0, -steps), min(count, count - steps))
    return lax.ppermute(value, axis, [(source, source + steps) for source in range(leading, last)])


def shortened(value):

    def short(part):
        return part.astype(jnp.bfloat16) if part.dtype == jnp.float32 else part

    return jax.tree.map(short, value)


def rounders():

    def round_value(value):
        return lax.optimization_barrier(value.astype(jnp.bfloat16)).astype(jnp.float32)

    def plain_value(value):
        return value

    rounded = jax.custom_vjp(round_value)
    passed = jax.custom_vjp(plain_value)

    def keep_round(value):
        return (round_value(value), None)

    def pass_grad(kept, grad):
        return (grad,)

    def keep_plain(value):
        return (value, None)

    def round_grad(kept, grad):
        return (round_value(grad),)

    rounded.defvjp(keep_round, pass_grad)
    passed.defvjp(keep_plain, round_grad)
    return (rounded, passed)


def half_product(form, left_form, right_form):

    def forward(left, right):
        return jnp.einsum(
            form,
            left.astype(jnp.bfloat16),
            right.astype(jnp.bfloat16),
            preferred_element_type=jnp.float32,
        )

    product = jax.custom_vjp(forward)

    def keep_both(left, right):
        return (forward(left, right), (left, right))

    def back_both(kept, grad):
        left, right = kept
        grad_half = grad.astype(jnp.bfloat16)
        grad_left = jnp.einsum(
            left_form, grad_half, right.astype(jnp.bfloat16), preferred_element_type=jnp.float32
        )
        grad_right = jnp.einsum(
            right_form, left.astype(jnp.bfloat16), grad_half, preferred_element_type=jnp.float32
        )
        return (grad_left, grad_right)

    product.defvjp(keep_both, back_both)
    return product


def layer_norm(values, gain, shift):
    centred = values - jnp.mean(values, -1, keepdims=True)
    spread = jnp.mean(centred * centred, -1, keepdims=True)
    return centred * lax.rsqrt(spread + 1e-05) * gain + shift


def attention_layer(hidden, memory, has_memory, attn, upper, lower, vectors):
    low, low_back = rounders()
    matmul = half_product("qd,de->qe", "qe,de->qd", "qd,qe->de")
    score_product = half_product("qhd,khd->hqk", "hqk,khd->qhd", "qhd,hqk->khd")
    mix_product = half_product("hqk,khd->qhd", "qhd,khd->hqk", "hqk,qhd->khd")
    length, width = hidden.shape
    heads = width // HEAD_DIM
    normed = low(layer_norm(hidden, vectors[0], vectors[1]))
    memory_normed = low(layer_norm(memory, vectors[0], vectors[1]))
    keyin = jnp.concatenate([memory_normed, normed], 0)
    queries = low(low_back(matmul(normed, attn[0]) + vectors[4])).reshape(length, heads, HEAD_DIM)
    keys_all = low(low_back(matmul(keyin, attn[1]))).reshape(2 * length, heads, HEAD_DIM)
    values = low(low_back(matmul(keyin, attn[2]) + vectors[5])).reshape(2 * length, heads, HEAD_DIM)
    scores = low_back(score_product(queries, keys_all) * HEAD_DIM ** (-0.5))
    query_pos = jnp.arange(length)[:, None]
    key_pos = jnp.arange(2 * length)[None, :]
    allowed = jnp.where(key_pos < length, has_memory, key_pos - length <= query_pos)
    scores = jnp.where(allowed[None], scores, -1e30)
    weights = low(jax.nn.softmax(scores, -1))
    mixed = mix_product(weights, values).reshape(length, width)
    mixed = low(low_back(mixed))
    after_attn = hidden + low_back(matmul(mixed, attn[3]) + vectors[6])
    normed_two = low(layer_norm(after_attn, vectors[2], vectors[3]))
    inner = low_back(matmul(normed_two, upper) + vectors[8:].reshape(-1))
    active = low(jax.nn.gelu(inner))
    return after_attn + low_back(matmul(active, lower) + vectors[7])


def head_loss(hidden, out_weight, outer_vectors, targets, weighting):
    low, low_back = rounders()
    matmul = half_product("sqd,de->sqe", "sqe,de->sqd", "sqd,sqe->de")
    normed = low(layer_norm(hidden, outer_vectors[1], outer_vectors[2]))
    logits = low_back(matmul(normed, out_weight) + outer_vectors[3:].reshape(-1))
    log_probs = jax.nn.log_softmax(logits, -1)
    picked = jnp.take_along_axis(log_probs, targets[..., None], -1)[..., 0]
    return -jnp.sum(picked * weighting)


def adamw(weight, moment, second, grad, rate, decay):
    moment = 0.5 * moment + 0.5 * grad
    second = 0.99 * second + 0.01 * grad * grad
    fixed_moment = moment / (1.0 - 0.5**STEP)
    fixed_second = second / (1.0 - 0.99**STEP)
    weight = weight * (1.0 - rate * decay) - rate * fixed_moment / (jnp.sqrt(fixed_second) + 1e-08)
    return (weight, moment, second)


def orthogonal(matrix):
    flipped = matrix.shape[0] > matrix.shape[1]
    if flipped:
        matrix = matrix.T
    matrix = matrix / (jnp.sqrt(jnp.sum(matrix * matrix)) + 1e-07)
    for sweep in range(5):
        gram_matrix = jnp.matmul(matrix, matrix.T, precision=HIGHEST)
        poly_term = -4.775 * gram_matrix + 2.0315 * jnp.matmul(
            gram_matrix, gram_matrix, precision=HIGHEST
        )
        matrix = 3.4445 * matrix + jnp.matmul(poly_term, matrix, precision=HIGHEST)
    return matrix.T if flipped else matrix


def owner_layout(stack, offset, owner_count):
    total_count = stack.shape[0]
    slot_count = -(-total_count // owner_count)
    filler = jnp.zeros((slot_count * owner_count - total_count,) + stack.shape[1:], stack.dtype)
    rolled = jnp.roll(jnp.concatenate([stack, filler], 0), offset, 0)
    return rolled.reshape((slot_count, owner_count) + stack.shape[1:])


def to_owner(stack, offset, owner_count, owner):
    return lax.dynamic_index_in_dim(
        owner_layout(stack, offset, owner_count), owner, 1, keepdims=False
    )


def from_owner(gathered, offset, total_count):
    owner_count, slot_count = (gathered.shape[0], gathered.shape[1])
    flat = jnp.swapaxes(gathered, 0, 1).reshape((slot_count * owner_count,) + gathered.shape[2:])
    return jnp.roll(flat, -offset, 0)[:total_count]


def own_rows(whole, row_count):
    return lax.dynamic_slice_in_dim(whole, lax.axis_index("seg") * row_count, row_count, 1)


def local(
    frames,
    speech_mask,
    targets,
    in_proj,
    in_moment,
    in_second,
    out_proj,
    out_moment,
    out_second,
    layer_vectors,
    vectors_moment,
    vectors_second,
    outer_vectors,
    outer_moment,
    outer_second,
    attn_proj,
    attn_momentum,
    ff_up,
    up_momentum,
    ff_down,
    down_momentum,
    in_copy,
    out_copy,
    attn_copy,
    up_copy,
    down_copy,
):
    has_memory = lax.axis_index("seg") > 0
    stream_total = frames.shape[0] * lax.axis_size("dp")
    local_counts = jnp.sum(speech_mask, 1)
    every_count = lax.all_gather(local_counts[None], "seg", axis=0, tiled=True)
    inverse = 1.0 / jnp.sum(every_count, 0).astype(jnp.float32)
    weighting = speech_mask.astype(jnp.float32) * inverse[:, None]
    frames_float = frames.astype(jnp.float32)
    attn_weight = attn_copy.astype(jnp.float32)
    up_weight = up_copy.astype(jnp.float32)
    down_weight = down_copy.astype(jnp.float32)
    out_weight = out_copy.astype(jnp.float32)
    hidden, embed_back = jax.vjp(
        lambda weight, outer: jnp.matmul(frames_float, weight, precision=HIGHEST) + outer[0],
        in_copy.astype(jnp.float32),
        outer_vectors,
    )
    mapped = jax.vmap(attention_layer, (0, 0, None, None, None, None, None))
    pullbacks = []
    for depth in range(LAYERS):
        memory = from_behind(hidden.astype(jnp.bfloat16), "seg", 1).astype(jnp.float32)
        hidden, pullback = jax.vjp(
            lambda rows, attn, upper, lower, vectors, held=memory: mapped(
                rows, held, has_memory, attn, upper, lower, vectors
            ),
            hidden,
            attn_weight[depth],
            up_weight[depth],
            down_weight[depth],
            layer_vectors[depth],
        )
        pullbacks.append(pullback)
    loss_here, head_back = jax.vjp(
        lambda rows, weight, outer: head_loss(rows, weight, outer, targets, weighting),
        hidden,
        out_weight,
        outer_vectors,
    )
    grad_hidden, grad_out, grad_outer = head_back(jnp.ones_like(loss_here) / stream_total)
    attn_grads, up_grads, down_grads, vector_grads = ([], [], [], [])
    for depth in reversed(range(LAYERS)):
        grad_hidden, grad_attn, grad_up, grad_down, grad_vector = pullbacks[depth](grad_hidden)
        attn_grads.insert(0, grad_attn)
        up_grads.insert(0, grad_up)
        down_grads.insert(0, grad_down)
        vector_grads.insert(0, grad_vector)
    grad_in, grad_outer_low = embed_back(grad_hidden)
    grad_outer = grad_outer + grad_outer_low
    grad_vectors = jnp.stack(vector_grads)
    grad_in, grad_out, grad_vectors, grad_outer, loss_sum = lax.psum(
        (grad_in, grad_out, grad_vectors, grad_outer, loss_here), ("seg", "dp")
    )
    attn_local = jnp.stack(attn_grads).reshape(4 * LAYERS, D, D)
    up_local = jnp.stack(up_grads)
    down_local = jnp.stack(down_grads)
    offsets = (0, 4 * LAYERS, 5 * LAYERS)
    owner = lax.axis_index("dp")
    owner_count = lax.axis_size("dp")
    attn_sum, up_sum, down_sum = (
        lax.psum_scatter(
            attn_local.astype(jnp.bfloat16), "seg", scatter_dimension=1, tiled=True
        ).astype(jnp.float32),
        lax.psum_scatter(
            up_local.astype(jnp.bfloat16), "seg", scatter_dimension=1, tiled=True
        ).astype(jnp.float32),
        lax.psum_scatter(
            down_local.astype(jnp.bfloat16), "seg", scatter_dimension=1, tiled=True
        ).astype(jnp.float32),
    )
    attn_sum, up_sum, down_sum = lax.psum((attn_sum, up_sum, down_sum), "dp")
    shard_squares = (
        jnp.sum(attn_sum * attn_sum) + jnp.sum(up_sum * up_sum) + jnp.sum(down_sum * down_sum)
    )
    matrix_squares = lax.psum(shard_squares, "seg")
    small_squares = (
        jnp.sum(grad_in * grad_in)
        + jnp.sum(grad_out * grad_out)
        + jnp.sum(grad_vectors * grad_vectors)
        + jnp.sum(grad_outer * grad_outer)
    )
    grad_norm = jnp.sqrt(matrix_squares + small_squares)
    clip = jnp.minimum(1.0, 0.25 / (grad_norm + 1e-06))
    in_new, in_moment_new, in_second_new = adamw(
        in_proj, in_moment, in_second, grad_in * clip, 0.05, 0.01
    )
    out_new, out_moment_new, out_second_new = adamw(
        out_proj, out_moment, out_second, grad_out * clip, 0.05, 0.01
    )
    vectors_new, vectors_moment_new, vectors_second_new = adamw(
        layer_vectors, vectors_moment, vectors_second, grad_vectors * clip, 0.25, 0.0
    )
    outer_new, outer_moment_new, outer_second_new = adamw(
        outer_vectors, outer_moment, outer_second, grad_outer * clip, 0.25, 0.0
    )
    block_rows = attn_momentum.shape[2]
    attn_old = attn_momentum.reshape(4 * LAYERS, block_rows, D)
    row_counts = (block_rows, up_momentum.shape[1], down_momentum.shape[1])
    attn_mom = 0.5 * attn_old + clip * attn_sum
    up_mom = 0.5 * up_momentum + clip * up_sum
    down_mom = 0.5 * down_momentum + clip * down_sum
    owned_attn = to_owner(attn_mom, offsets[0], owner_count, owner)
    owned_up = to_owner(up_mom, offsets[1], owner_count, owner)
    owned_down = to_owner(down_mom, offsets[2], owner_count, owner)
    whole_attn, whole_up, whole_down = (
        lax.all_gather(owned_attn, "seg", axis=1, tiled=True),
        lax.all_gather(owned_up, "seg", axis=1, tiled=True),
        lax.all_gather(owned_down, "seg", axis=1, tiled=True),
    )
    part_attn = own_rows(jax.vmap(orthogonal)(whole_attn), row_counts[0])
    part_up = own_rows(jax.vmap(orthogonal)(whole_up), row_counts[1])
    part_down = own_rows(jax.vmap(orthogonal)(whole_down), row_counts[2])
    back_attn, back_up, back_down = (
        lax.all_gather(shortened(part_attn[None]), "dp", axis=0, tiled=True),
        lax.all_gather(shortened(part_up[None]), "dp", axis=0, tiled=True),
        lax.all_gather(shortened(part_down[None]), "dp", axis=0, tiled=True),
    )
    attn_update = from_owner(back_attn, offsets[0], 4 * LAYERS)
    up_update = from_owner(back_up, offsets[1], LAYERS)
    down_update = from_owner(back_down, offsets[2], LAYERS)
    attn_new = attn_proj * (1.0 - 0.3 * 0.01) - 0.3 * attn_update.reshape(attn_proj.shape)
    up_new = ff_up * (1.0 - 0.3 * 0.01) - 0.3 * max(1.0, FF / D) ** 0.5 * up_update
    down_new = ff_down * (1.0 - 0.3 * 0.01) - 0.3 * max(1.0, D / FF) ** 0.5 * down_update
    return (
        loss_sum,
        grad_norm,
        in_new,
        in_moment_new,
        in_second_new,
        out_new,
        out_moment_new,
        out_second_new,
        vectors_new,
        vectors_moment_new,
        vectors_second_new,
        outer_new,
        outer_moment_new,
        outer_second_new,
        attn_new,
        attn_mom.reshape(attn_proj.shape),
        up_new,
        up_mom,
        down_new,
        down_mom,
        in_new.astype(jnp.bfloat16),
        out_new.astype(jnp.bfloat16),
        attn_new.astype(jnp.bfloat16),
        up_new.astype(jnp.bfloat16),
        down_new.astype(jnp.bfloat16),
    )


def solution(mesh):
    return jax.shard_map(
        local,
        mesh=mesh,
        in_specs=(
            P("dp", "seg", None),
            P("dp", "seg"),
            P("dp", "seg"),
            P(),
            P(),
            P(),
            P(),
            P(),
            P(),
            P(),
            P(),
            P(),
            P(),
            P(),
            P(),
            P(None, None, "seg", None),
            P(None, None, "seg", None),
            P(None, "seg", None),
            P(None, "seg", None),
            P(None, "seg", None),
            P(None, "seg", None),
            P(),
            P(),
            P(),
            P(),
            P(),
        ),
        out_specs=(
            P(),
            P(),
            P(),
            P(),
            P(),
            P(),
            P(),
            P(),
            P(),
            P(),
            P(),
            P(),
            P(),
            P(),
            P(None, None, "seg", None),
            P(None, None, "seg", None),
            P(None, "seg", None),
            P(None, "seg", None),
            P(None, "seg", None),
            P(None, "seg", None),
            P(),
            P(),
            P(None, None, "seg", None),
            P(None, "seg", None),
            P(None, "seg", None),
        ),
        check_vma=False,
    )
```

profile of v0, /device:TPU:0, one launch (start us, length us, event | category | flops | bytes accessed | tf_op | source)
XLA Modules:
  0.0 1155.4 jit_solution(11050327393279594569)
XLA Ops:
  21.1 9.4 all-reduce.36
  56.4 19.0 %fusion.311 = (f32[2,8,512]{2,1,0:T(8,128)S(1)}, f32[2,8,512,1024]{3,2,1,0:T(8,128)}) fusion(pred[512,1024]{1,0:T(8,128)(4,1)} %fusion.164, bf16[2,512,8,64]{1,3,2,0:T(8,128)(2,1)} %bitcast.558, bf16[2,1024,8,64]{1,3,2,0:T(8,128)(2,1)} %bitcast.545), kind=kOutput, calls=%fused_computation.501 | convolution fusion | flops 1107297280 | bytes 37257216 | tf_op jit(solution)/shard_map/jvp(vmap())/sub | solution.py:112
  75.4 18.5 %divide_convert_fusion.1 = bf16[2,8,512,1024]{3,2,1,0:T(8,128)(2,1)} fusion(f32[2,8,512,1024]{3,2,1,0:T(8,128)} %get-tuple-element.188, f32[2,8,512]{2,1,0:T(8,128)S(1)} %get-tuple-element.187), kind=kLoop, calls=%fused_computation.13 | loop fusion | flops 16777216 | bytes 50364416 | tf_op jit(solution)/shard_map/jvp(vmap())/convert_element_type | solution.py:33
  93.9 12.6 %convolution_convert_fusion.5 = bf16[2,8,64,512]{3,2,1,0:T(8,128)(2,1)} fusion(bf16[2,1024,8,64]{1,3,2,0:T(8,128)(2,1)} %bitcast.525, bf16[2,8,512,1024]{3,2,1,0:T(8,128)(2,1)} %divide_convert_fusion.1), kind=kOutput, calls=%fused_computation.280 | convolution fusion | flops 1074266112 | bytes 19922944 | tf_op jit(solution)/shard_map/jvp(vmap(hqk,khd->qhd))/dot_general | solution.py:61
  148.5 19.0 %fusion.314 = (f32[2,8,512]{2,1,0:T(8,128)S(1)}, f32[2,8,512,1024]{3,2,1,0:T(8,128)}) fusion(pred[512,1024]{1,0:T(8,128)(4,1)} %fusion.164, bf16[2,512,8,64]{1,3,2,0:T(8,128)(2,1)} %bitcast.563, bf16[2,1024,8,64]{1,3,2,0:T(8,128)(2,1)} %bitcast.547), kind=kOutput, calls=%fused_computation.504 | convolution fusion | flops 1107297280 | bytes 37257216 | tf_op jit(solution)/shard_map/jvp(vmap())/sub | solution.py:112
  167.5 18.4 %divide_convert_fusion = bf16[2,8,512,1024]{3,2,1,0:T(8,128)(2,1)} fusion(f32[2,8,512,1024]{3,2,1,0:T(8,128)} %get-tuple-element.196, f32[2,8,512]{2,1,0:T(8,128)S(1)} %get-tuple-element.195), kind=kLoop, calls=%fused_computation.10 | loop fusion | flops 16777216 | bytes 50364416 | tf_op jit(solution)/shard_map/jvp(vmap())/convert_element_type | solution.py:33
  185.9 11.9 %convolution_convert_fusion.4 = bf16[2,8,64,512]{3,2,1,0:T(8,128)(2,1)} fusion(bf16[2,1024,8,64]{1,3,2,0:T(8,128)(2,1)S(1)} %bitcast.527, bf16[2,8,512,1024]{3,2,1,0:T(8,128)(2,1)} %divide_convert_fusion), kind=kOutput, calls=%fused_computation.279 | convolution fusion | flops 1074266112 | bytes 19922944 | tf_op jit(solution)/shard_map/jvp(vmap(hqk,khd->qhd))/dot_general | solution.py:61
  234.3 10.5 fusion.32
  261.5 8.9 convolution_convert_fusion.1
  270.5 22.2 %multiply_reduce_fusion.1 = (f32[2,8,512]{2,1,0:T(8,128)S(1)}, f32[2,8,512,1024]{3,2,1,0:T(8,128)}) fusion(f32[2,8,512,1024]{3,2,1,0:T(8,128)} %get-tuple-element.196, f32[2,8,512]{2,1,0:T(8,128)S(1)} %multiply_divide_fusion.1, bf16[2,512,8,64]{1,3,2,0:T(8,128)(2,1)S(1)} %bitcast.537, bf16[2,1024,8,64]{1,3,2,0:T(8,128)(2,1)S(1)} %bitcast.528), kind=kOutput, calls=%fused_computation.9 | convolution fusion | flops 1098899456 | bytes 70320128 | tf_op jit(solution)/shard_map/transpose(jvp(vmap(qhd,khd->hqk)))/dot_general | solution.py:113
  292.7 27.9 %select_convert_fusion.1 = bf16[2,8,512,1024]{3,2,1,0:T(8,128)(2,1)} fusion(f32[2,8,512,1024]{3,2,1,0:T(8,128)} %get-tuple-element.196, f32[2,8,512,1024]{3,2,1,0:T(8,128)} %get-tuple-element.206, f32[2,8,512]{2,1,0:T(8,128)S(1)} %neg.38, f32[2,8,512]{2,1,0:T(8,128)S(1)} %get-tuple-element.195, pred[512,1024]{1,0:T(8,128)(4,1)} %fusion.164), kind=kLoop, calls=%fused_computation.8 | loop fusion | flops 41943040 | bytes 84475904 | tf_op jit(solution)/shard_map/transpose(jvp(vmap()))/convert_element_type | solution.py:107
  320.6 11.6 %fusion.184 = bf16[2,8,64,512]{3,2,1,0:T(8,128)(2,1)S(1)} fusion(bf16[2,1024,8,64]{1,3,2,0:T(8,128)(2,1)} %bitcast.548, bf16[2,8,512,1024]{3,2,1,0:T(8,128)(2,1)} %select_convert_fusion.1), kind=kOutput, calls=%fused_computation.278 | convolution fusion | flops 1099431936 | bytes 19922944 | tf_op jit(solution)/shard_map/transpose(jvp(vmap(hqk,khd->qhd)))/dot_general | solution.py:107
  332.3 10.1 fusion.166
  355.5 8.2 fusion.25
  381.4 8.9 convolution_convert_fusion
  390.4 22.1 %multiply_reduce_fusion = (f32[2,8,512]{2,1,0:T(8,128)S(1)}, f32[2,8,512,1024]{3,2,1,0:T(8,128)}) fusion(f32[2,8,512,1024]{3,2,1,0:T(8,128)} %get-tuple-element.188, f32[2,8,512]{2,1,0:T(8,128)S(1)} %copy-done.89, bf16[2,512,8,64]{1,3,2,0:T(8,128)(2,1)S(1)} %bitcast.539, bf16[2,1024,8,64]{1,3,2,0:T(8,128)(2,1)S(1)} %bitcast.526), kind=kOutput, calls=%fused_computation.6 | convolution fusion | flops 1098899456 | bytes 70320128 | tf_op jit(solution)/shard_map/transpose(jvp(vmap(qhd,khd->hqk)))/dot_general | solution.py:113
  412.5 28.3 %select_convert_fusion = bf16[2,8,512,1024]{3,2,1,0:T(8,128)(2,1)} fusion(f32[2,8,512,1024]{3,2,1,0:T(8,128)} %get-tuple-element.188, f32[2,8,512,1024]{3,2,1,0:T(8,128)} %get-tuple-element.211, f32[2,8,512]{2,1,0:T(8,128)S(1)} %neg.41, f32[2,8,512]{2,1,0:T(8,128)S(1)} %copy-done.93, pred[512,1024]{1,0:T(8,128)(4,1)} %fusion.164), kind=kLoop, calls=%fused_computation.5 | loop fusion | flops 41943040 | bytes 84475904 | tf_op jit(solution)/shard_map/transpose(jvp(vmap()))/convert_element_type | solution.py:107
  440.8 12.7 %fusion.183 = bf16[2,8,64,512]{3,2,1,0:T(8,128)(2,1)} fusion(bf16[2,1024,8,64]{1,3,2,0:T(8,128)(2,1)} %bitcast.546, bf16[2,8,512,1024]{3,2,1,0:T(8,128)(2,1)} %select_convert_fusion), kind=kOutput, calls=%fused_computation.277 | convolution fusion | flops 1099431936 | bytes 19922944 | tf_op jit(solution)/shard_map/transpose(jvp(vmap(hqk,khd->qhd)))/dot_general | solution.py:107
  453.5 9.4 fusion.165
  517.1 14.7 %gather_fusion = f32[1024]{0:T(1024)S(1)} fusion(f32[2,512,1024]{2,1,0:T(8,128)} %get-tuple-element.150, s32[1024]{0:T(1024)S(1)} %bitcast.524), kind=kCustom, calls=%fused_computation | custom fusion | bytes 20480 | tf_op jit(solution)/shard_map/jvp(jit(take_along_axis))/gather | solution.py:128
  553.0 52.8 %all-reduce.37 = (f32[]{:T(128)}, f32[2,12,512]{2,1,0:T(8,128)S(1)}, f32[5,512]{1,0:T(8,128)S(1)}) all-reduce(f32[]{:T(128)S(6)} %neg.34, f32[2,12,512]{2,1,0:T(8,128)S(1)} %pad_maximum_fusion.5, f32[5,512]{1,0:T(8,128)S(1)} %pad_add_fusion), channel_id=1, replica_groups=mesh['seg'=8,'dp'=4] {'seg','dp'}, use_global_device_ids=true, to_apply=%region_23.24 | all-reduce | flops 14849 | bytes 118792 | tf_op jit(solution)/shard_map/psum | solution.py:255
  607.1 70.8 %all-reduce.43.cloned.1.call-done = (f32[80,512]{1,0:T(8,128)}, f32[512,1024]{1,0:T(8,128)}) async-done(((f32[80,512]{1,0:T(8,128)}, f32[512,1024]{1,0:T(8,128)}), (f32[80,512]{1,0:T(8,128)}, f32[512,1024]{1,0:T(8,128)})) %all-reduce.43.cloned.1.call-update) | async-done | bytes 2261008 | tf_op jit(solution)/shard_map/psum | solution.py:255
  684.2 109.6 %all-reduce.44 = (f32[8,64,512]{2,1,0:T(8,128)}, f32[2,64,2048]{2,1,0:T(8,128)S(1)}, f32[2,256,512]{1,2,0:T(8,128)S(1)}) all-reduce(bf16[8,64,512]{2,1,0:T(8,128)(2,1)} %reduce-scatter.4.cloned.1.call-done, bf16[2,64,2048]{2,1,0:T(8,128)(2,1)} %reduce-scatter.6.cloned.1.call-done, ...), channel_id=1, replica_groups=mesh['seg'=8,'dp'=4] {'dp'}, use_global_device_ids=true, to_apply=%region_36.37 | all-reduce | flops 786432 | bytes 4718592 | tf_op jit(solution)/shard_map/psum | solution.py:275
  799.0 14.4 %psum.67 = f32[]{:T(128)} all-reduce(f32[]{:T(128)S(6)} %add.673), channel_id=1, replica_groups=mesh['seg'=8,'dp'=4] {'seg'}, use_global_device_ids=true, to_apply=%region_44.45 | all-reduce | flops 1 | bytes 8 | tf_op jit(solution)/shard_map/psum | solution.py:279
  830.4 7.8 fusion.297
  906.3 34.7 %all-gather.13.cloned.1.call-done = f32[1,2048,512]{1,2,0:T(8,128)} async-done(((f32[1,256,512]{1,2,0:T(8,128)}), f32[1,2048,512]{1,2,0:T(8,128)}) %all-gather.13.cloned.1.call-update) | async-done | bytes 4194320 | tf_op jit(solution)/shard_map/all_gather | solution.py:312
  945.6 9.6 fusion.36
  957.1 6.9 bitcast_add_fusion.3
  964.0 7.1 fusion.52
  973.0 6.9 bitcast_add_fusion.2
  980.0 7.1 fusion.48
  989.0 7.4 bitcast_add_fusion.1
  996.4 6.9 fusion.44
  1006.1 7.2 fusion.72
  1015.2 7.1 bitcast_add_fusion.7
  1022.4 6.9 fusion.68
  1031.2 7.3 bitcast_add_fusion.6
  1038.5 6.9 fusion.64
  1047.5 6.9 bitcast_add_fusion.5
  1054.5 7.1 fusion.60
  1063.5 6.9 bitcast_add_fusion.4
  1070.4 7.4 fusion.56
  1079.7 7.3 fusion.75
  1088.3 9.4 bitcast_add_fusion
  1097.7 6.9 fusion.40
  1106.5 7.3 fusion.78
  1120.4 12.2 %all-gather.2 = bf16[8,64,512]{2,1,0:T(8,128)(2,1)S(1)} all-gather(bf16[2,64,512]{2,1,0:T(8,128)(2,1)S(1)} %fusion.253), channel_id=4, replica_groups=mesh['seg'=8,'dp'=4] {'dp'}, dimensions={0}, use_global_device_ids=true | all-gather | bytes 655360 | tf_op jit(solution)/shard_map/all_gather | solution.py:318
  1136.5 8.0 all-gather.19.cloned.1.call-done
  (569 shorter events, 367.1 us)
Async XLA Ops:
  8.0 205.8 %copy-start = (bf16[512,1024]{1,0:T(8,128)(2,1)S(1)}, bf16[512,1024]{1,0:T(8,128)(2,1)}, u32[]{:S(2)}) copy-start(bf16[512,1024]{1,0:T(8,128)(2,1)} %param.48) | copy-start | bytes 3145732
  8.1 669.8 %all-reduce.43.cloned.1.call-start = ((), (), s32[]{:S(2)}) async-start(), calls=%async_computation.11 | async-start | bytes 4521984 | tf_op jit(solution)/shard_map/psum | solution.py:255
  8.9 97.5 %copy-start.115 = (f32[1,512]{1,0:T(1,128)}, f32[1,512]{1,0:T(1,128)S(1)}, u32[]{:S(2)}) copy-start(f32[1,512]{1,0:T(1,128)S(1)} %get-tuple-element.180) | copy-start | bytes 6148
  9.8 29.4 %copy-start.131 = (f32[1,1,512]{2,0,1:T(1,128)}, f32[1,1,512]{2,0,1:T(1,128)S(1)}, u32[]{:S(2)}) copy-start(f32[1,1,512]{2,0,1:T(1,128)S(1)} %get-tuple-element.174) | copy-start | bytes 6148
  9.8 99.1 %copy-start.111 = (f32[1,1,512]{2,0,1:T(1,128)}, f32[1,1,512]{2,0,1:T(1,128)S(1)}, u32[]{:S(2)}) copy-start(f32[1,1,512]{2,0,1:T(1,128)S(1)} %get-tuple-element.169) | copy-start | bytes 6148
  9.8 122.4 %copy-start.113 = (f32[1,1,512]{2,0,1:T(1,128)}, f32[1,1,512]{2,0,1:T(1,128)S(1)}, u32[]{:S(2)}) copy-start(f32[1,1,512]{2,0,1:T(1,128)S(1)} %get-tuple-element.166) | copy-start | bytes 6148
  11.3 95.1 %copy-start.6 = (f32[2,512,512]{1,2,0:T(8,128)}, f32[2,512,512]{1,2,0:T(8,128)S(1)}, u32[]{:S(2)}) copy-start(f32[2,512,512]{1,2,0:T(8,128)S(1)} %get-tuple-element.186) | copy-start | bytes 6291460
  13.2 23.0 %collective-permute-start = (bf16[2,512,512]{1,2,0:T(8,128)(2,1)}, bf16[2,512,512]{1,2,0:T(8,128)(2,1)}, u32[]{:S(2)}, u32[]{:S(2)}) collective-permute-start(bf16[2,512,512]{1,2,0:T(8,128)(2,1)} %get-tuple-element.151), channel_id=1, source_target_pairs={{0,4},{4,8},{8,12},{12,16},{16,20},{20,24},{24,28},{1,5},{5,9},{9,... | collective-permute-start | bytes 3145736 | tf_op jit(solution)/shard_map/ppermute | solution.py:19
  16.7 16.1 %copy-start.133 = (s32[2,512]{1,0:T(2,128)S(1)}, s32[2,512]{1,0:T(2,128)}, u32[]{:S(2)}) copy-start(s32[2,512]{1,0:T(2,128)} %param.28) | copy-start | bytes 12292
  35.0 74.9 %copy-start.140 = (f32[1,4,512]{2,0,1:T(1,128)}, f32[1,4,512]{2,0,1:T(1,128)S(1)}, u32[]{:S(2)}) copy-start(f32[1,4,512]{2,0,1:T(1,128)S(1)} %get-tuple-element.176) | copy-start | bytes 24580
  75.4 55.7 %copy-start.92 = (f32[2,8,512]{2,1,0:T(8,128)}, f32[2,8,512]{2,1,0:T(8,128)S(1)}, u32[]{:S(2)}) copy-start(f32[2,8,512]{2,1,0:T(8,128)S(1)} %get-tuple-element.187) | copy-start | bytes 98308
  108.6 9.9 copy-start.4
  108.9 9.6 copy-start.123
  108.9 9.5 copy-start.104
  122.8 14.5 %copy-start.76 = (bf16[2,512,512]{1,2,0:T(8,128)(2,1)}, bf16[2,512,512]{1,2,0:T(8,128)(2,1)S(1)}, u32[]{:S(2)}) copy-start(bf16[2,512,512]{1,2,0:T(8,128)(2,1)S(1)} %get-tuple-element.154) | copy-start | bytes 3145732
  122.8 9.0 collective-permute-start.1
  143.9 42.0 %copy-start.14 = (bf16[2,1024,512]{1,2,0:T(8,128)(2,1)}, bf16[2,1024,512]{1,2,0:T(8,128)(2,1)S(1)}, u32[]{:S(2)}) copy-start(bf16[2,1024,512]{1,2,0:T(8,128)(2,1)S(1)} %copy.218) | copy-start | bytes 6291460
  201.3 8.6 copy-start.85
  233.6 11.3 copy-start.53
  234.3 10.6 copy-start.153
  261.5 9.0 copy-start.15
  270.5 71.9 %copy-start.16 = (bf16[2,8,64,1024]{3,2,1,0:T(8,128)(2,1)}, bf16[2,8,64,1024]{3,2,1,0:T(8,128)(2,1)S(1)}, u32[]{:S(2)}) copy-start(bf16[2,8,64,1024]{3,2,1,0:T(8,128)(2,1)S(1)} %convolution_convert_fusion.1) | copy-start | bytes 6291460
  332.2 15.4 %copy-start.43 = (bf16[2,8,64,512]{3,2,1,0:T(8,128)(2,1)}, bf16[2,8,64,512]{3,2,1,0:T(8,128)(2,1)S(1)}, u32[]{:S(2)}) copy-start(bf16[2,8,64,512]{3,2,1,0:T(8,128)(2,1)S(1)} %fusion.184) | copy-start | bytes 3145732
  353.5 10.2 copy-start.60
  381.4 9.0 copy-start.13
  381.4 9.0 copy-start.89
  390.4 72.5 %copy-start.18 = (bf16[2,8,64,1024]{3,2,1,0:T(8,128)(2,1)}, bf16[2,8,64,1024]{3,2,1,0:T(8,128)(2,1)S(1)}, u32[]{:S(2)}) copy-start(bf16[2,8,64,1024]{3,2,1,0:T(8,128)(2,1)S(1)} %convolution_convert_fusion) | copy-start | bytes 6291460
  390.4 22.1 %copy-start.93 = (f32[2,8,512]{2,1,0:T(8,128)S(1)}, f32[2,8,512]{2,1,0:T(8,128)}, u32[]{:S(2)}) copy-start(f32[2,8,512]{2,1,0:T(8,128)} %copy-done.92) | copy-start | bytes 98308
  440.8 12.7 %copy-start.82 = (bf16[2,512,512]{1,2,0:T(8,128)(2,1)S(1)}, bf16[2,512,512]{1,2,0:T(8,128)(2,1)}, u32[]{:S(2)}) copy-start(bf16[2,512,512]{1,2,0:T(8,128)(2,1)} %copy.210) | copy-start | bytes 3145732
  475.3 208.8 %reduce-scatter.8.cloned.1.call-start = ((), (), s32[]{:S(2)}) async-start(), calls=%async_computation.5 | async-start | bytes 4718592 | tf_op jit(solution)/shard_map/reduce_scatter | solution.py:271
  486.0 198.2 %reduce-scatter.6.cloned.1.call-start = ((), (), s32[]{:S(2)}) async-start(), calls=%async_computation.4 | async-start | bytes 4718592 | tf_op jit(solution)/shard_map/reduce_scatter | solution.py:268
  496.7 187.5 %reduce-scatter.4.cloned.1.call-start = ((), (), s32[]{:S(2)}) async-start(), calls=%async_computation.3 | async-start | bytes 4718592 | tf_op jit(solution)/shard_map/reduce_scatter | solution.py:265
  514.1 330.6 %all-gather.15.cloned.1.call-start = ((), (), s32[]{:S(2)}) async-start(), calls=%async_computation.8 | async-start | bytes 2359296 | tf_op jit(solution)/shard_map/all_gather | solution.py:310
  517.1 14.7 %copy-start.128 = (s32[2,512]{1,0:T(2,128)S(1)}, s32[2,512]{1,0:T(2,128)}, u32[]{:S(2)}) copy-start(s32[2,512]{1,0:T(2,128)} %param.27) | copy-start | bytes 12292
  517.1 14.7 %copy-start.134 = (s32[2,512]{1,0:T(2,128)S(1)}, s32[2,512]{1,0:T(2,128)}, u32[]{:S(2)}) copy-start(s32[2,512]{1,0:T(2,128)} %param.28) | copy-start | bytes 12292
  517.1 14.7 %copy-start.146 = (f32[2]{0:T(128)S(1)}, f32[2]{0:T(128)}, u32[]{:S(2)}) copy-start(f32[2]{0:T(128)} %copy-done.145) | copy-start | bytes 28
  605.9 77.6 %copy-start.94 = (f32[2,12,512]{2,1,0:T(8,128)}, f32[2,12,512]{2,1,0:T(8,128)S(1)}, u32[]{:S(2)}) copy-start(f32[2,12,512]{2,1,0:T(8,128)S(1)} %get-tuple-element.117) | copy-start | bytes 147460
  605.9 77.6 %copy-start.106 = (f32[5,512]{1,0:T(8,128)}, f32[5,512]{1,0:T(8,128)S(1)}, u32[]{:S(2)}) copy-start(f32[5,512]{1,0:T(8,128)S(1)} %get-tuple-element.118) | copy-start | bytes 30724
  684.1 130.1 %copy-start.58 = (f32[2,4,64,512]{3,2,1,0:T(8,128)S(1)}, f32[2,4,64,512]{3,2,1,0:T(8,128)}, u32[]{:S(2)}) copy-start(f32[2,4,64,512]{3,2,1,0:T(8,128)} %broadcast_multiply_fusion.1) | copy-start | bytes 3145732
  817.4 83.9 %all-gather.11.cloned.1.call-start = ((), (), s32[]{:S(2)}) async-start(), calls=%async_computation.6 | async-start | bytes 4718592 | tf_op jit(solution)/shard_map/all_gather | solution.py:311
  819.8 121.2 %all-gather.13.cloned.1.call-start = ((), (), s32[]{:S(2)}) async-start(), calls=%async_computation.7 | async-start | bytes 4718592 | tf_op jit(solution)/shard_map/all_gather | solution.py:312
  823.4 310.6 %all-gather.17.cloned.1.call-start = ((), (), s32[]{:S(2)}) async-start(), calls=%async_computation.9 | async-start | bytes 1310720 | tf_op jit(solution)/shard_map/all_gather | solution.py:319
  945.6 11.5 copy-start.52
  996.4 9.8 copy-start.51
  1087.8 56.7 %all-gather.19.cloned.1.call-start = ((), (), s32[]{:S(2)}) async-start(), calls=%async_computation.10 | async-start | bytes 1310720 | tf_op jit(solution)/shard_map/all_gather | solution.py:320
  1120.3 12.4 %copy-start.69 = (f32[2,4,64,512]{3,2,1,0:T(8,128)S(1)}, f32[2,4,64,512]{3,2,1,0:T(8,128)}, u32[]{:S(2)}) copy-start(f32[2,4,64,512]{3,2,1,0:T(8,128)} %param.41) | copy-start | bytes 3145732
  1134.0 10.5 copy-start.71
  1134.0 12.9 %copy-start.1 = (bf16[512,1024]{1,0:T(8,128)(2,1)S(1)}, bf16[512,1024]{1,0:T(8,128)(2,1)}, u32[]{:S(2)}) copy-start(bf16[512,1024]{1,0:T(8,128)(2,1)} %param.48) | copy-start | bytes 3145732
  (124 other events, 367.7 us)
Sparse Core Ops, SparseCore 0:
  475.4 202.3 all-reduce.42
  1087.9 25.4 all-gather.16
  1116.0 28.5 all-gather.18
Sparse Core Ops, SparseCore 1:
  486.1 66.8 reduce-scatter.7
  555.1 52.1 reduce-scatter.5
  609.5 54.6 reduce-scatter.3
  817.5 27.1 all-gather.14
  846.9 46.2 all-gather.10
  895.4 45.5 all-gather.12
where the time goes:
time: 1160 us
  matrix products  518 us (45%)
  other arithmetic  198 us (17%)
  blocking collectives  198 us (17%)
  waiting for transfers between devices  120 us (10%)
  local copies, waits for them, and re-layouts  87 us (8%)
  between operations  27.1 us (2%)
    psum x1, blocking collectives, local(): attn_sum, up_sum, down_sum = lax.psum((attn_sum, up_sum, down_sum), 'dp')  110 us
    dot_general x15, matrix products, orthogonal(): matrix = 3.4445 * matrix + jnp.matmul(poly_term, matrix, precision=HIGHEST)  94.2 us
    dot_general x15, matrix products, orthogonal(): gram_matrix = jnp.matmul(matrix, matrix.T, precision=HIGHEST)  91.3 us
    psum x1, waiting for transfers between devices, local(): lax.psum((grad_in, grad_out, grad_vectors, grad_outer, loss_here), ('seg'...  70.8 us
    dot_general x15, matrix products, forward(): jnp.einsum(form, left.astype(jnp.bfloat16), right.astype(jnp.bfloat16), p...  69.8 us
    dot_general x4, matrix products, attention_layer(): mixed = mix_product(weights, values).reshape(length, width)  62.2 us
    convert_element_type x2, other arithmetic, attention_layer(): scores = low_back(score_product(queries, keys_all) * HEAD_DIM ** (-0.5))  56.2 us
    psum x1, blocking collectives, local(): lax.psum((grad_in, grad_out, grad_vectors, grad_outer, loss_here), ('seg'...  52.8 us
  transfers between devices with their start and end apart: 11, of which 4 were waited for; matrix products, arithmetic and copies ran while one was open for 18% of the time, Pallas kernels for 0%

commit v1 on v0

--- a/solution.py
+++ b/solution.py
@@ -1,16 +1,508 @@
+import functools
+import math
+
 import jax
 import jax.numpy as jnp
 from jax import lax
+from jax.experimental import pallas as pl
+from jax.experimental.pallas import tpu as pltpu
 from jax.sharding import PartitionSpec as P
 
 D = 512
 HEAD_DIM = 64
+HEADS = D // HEAD_DIM
 FF = 2048
 LAYERS = 2
 STEP = 10
-
-
-HIGHEST = lax.Precision.HIGHEST
+SEG = 512
+HALF = 256
+PAIR = 2 * HEAD_DIM
+TILE = 512
+VMEM_LIMIT = 56 * 1024 * 1024
+GELU_SCALE = math.sqrt(2.0 / math.pi)
+
+f32 = jnp.float32
+bf16 = jnp.bfloat16
+
+
+def dot_nn(left, right):
+    return lax.dot_general(left, right, (((1,), (0,)), ((), ())), preferred_element_type=f32)
+
+
+def dot_nt(left, right):
+    return lax.dot_general(left, right, (((1,), (1,)), ((), ())), preferred_element_type=f32)
+
+
+def dot_tn(left, right):
+    return lax.dot_general(left, right, (((0,), (0,)), ((), ())), preferred_element_type=f32)
+
+
+def normalised(values):
+    centred = values - jnp.mean(values, -1, keepdims=True)
+    scale = lax.rsqrt(jnp.mean(centred * centred, -1, keepdims=True) + 1e-05)
+    return centred * scale, scale
+
+
+def norm_back(grad, gain, unit, scale):
+    part = grad * gain
+    mean_part = jnp.mean(part, -1, keepdims=True)
+    mean_unit = jnp.mean(part * unit, -1, keepdims=True)
+    return scale * (part - mean_part - unit * mean_unit)
+
+
+def column_sum(values):
+    return jnp.sum(values, 0, keepdims=True)
+
+
+def head_masks():
+    lane = lax.broadcasted_iota(jnp.int32, (1, PAIR), 1)
+    return (lane < HEAD_DIM).astype(bf16), (lane >= HEAD_DIM).astype(bf16)
+
+
+def pair_lanes(pair):
+    return pl.ds(pl.multiple_of(pair * PAIR, PAIR), PAIR)
+
+
+def forward_kernel(
+    bias_ref,
+    x_ref,
+    mem_ref,
+    attn_ref,
+    up_ref,
+    down_ref,
+    vec_ref,
+    *refs,
+):
+    hid_ref, hid16_ref, keyin_ref, q_ref, k_ref, v_ref, lse_ref, mixed_ref, after_ref, act_s, lse_s = refs[-11:]
+    x = x_ref[...]
+    own_unit, _ = normalised(x)
+    gain, shift = vec_ref[0:1, :], vec_ref[1:2, :]
+    normed = (own_unit * gain + shift).astype(bf16)
+    mem_unit, _ = normalised(mem_ref[...].astype(f32))
+    mem_normed = (mem_unit * gain + shift).astype(bf16)
+    keyin_ref[0:SEG, :] = mem_normed
+    keyin_ref[SEG:, :] = normed
+    q_ref[...] = (dot_nn(normed, attn_ref[0]) + vec_ref[4:5, :]).astype(bf16) * jnp.asarray(HEAD_DIM**-0.5, bf16)
+    k_ref[0:SEG, :] = dot_nn(mem_normed, attn_ref[1]).astype(bf16)
+    k_ref[SEG:, :] = dot_nn(normed, attn_ref[1]).astype(bf16)
+    v_ref[0:SEG, :] = (dot_nn(mem_normed, attn_ref[2]) + vec_ref[5:6, :]).astype(bf16)
+    v_ref[SEG:, :] = (dot_nn(normed, attn_ref[2]) + vec_ref[5:6, :]).astype(bf16)
+    first, second = head_masks()
+    memory_bias = bias_ref[0]
+    lane = lax.broadcasted_iota(jnp.int32, (HALF, PAIR), 1)
+    query_pos = lax.broadcasted_iota(jnp.int32, (2 * HALF, HALF), 0) % HALF
+    key_pos = lax.broadcasted_iota(jnp.int32, (2 * HALF, HALF), 1)
+    diagonal = key_pos <= query_pos
+    lse_s[...] = jnp.zeros_like(lse_s)
+
+    def pair_body(pair, carry):
+        lanes = pair_lanes(pair)
+        for block in range(2):
+            rows = slice(block * HALF, (block + 1) * HALF)
+            q_pair = q_ref[rows, lanes]
+            q_both = jnp.concatenate([q_pair * first, q_pair * second], 0)
+            spans = [(0, SEG, 0)]
+            if block:
+                spans.append((SEG, SEG + HALF, 1))
+            spans.append((SEG + block * HALF, SEG + (block + 1) * HALF, 2))
+            scores = []
+            for low, high, kind in spans:
+                part = dot_nt(q_both, k_ref[low:high, lanes])
+                if kind == 0:
+                    part = part + memory_bias
+                if kind == 2:
+                    part = jnp.where(diagonal, part, -1e30)
+                scores.append(part)
+            most = functools.reduce(jnp.maximum, [jnp.max(part, -1, keepdims=True) for part in scores])
+            weights = [jnp.exp(part - most) for part in scores]
+            total = functools.reduce(jnp.add, [jnp.sum(part, -1, keepdims=True) for part in weights])
+            mixed = functools.reduce(
+                jnp.add,
+                [
+                    dot_nn(part.astype(bf16), v_ref[low:high, lanes])
+                    for part, (low, high, kind) in zip(weights, spans)
+                ],
+            )
+            mixed = mixed / total
+            mixed_ref[rows, lanes] = jnp.where(lane < HEAD_DIM, mixed[:HALF], mixed[HALF:]).astype(bf16)
+            lse = most + jnp.log(total)
+            kept = jnp.where(lane == 2 * pair, lse[:HALF], lse_s[rows, :])
+            lse_s[rows, :] = jnp.where(lane == 2 * pair + 1, lse[HALF:], kept)
+        return carry
+
+    lax.fori_loop(0, HEADS // 2, pair_body, 0)
+    lse_ref[...] = jnp.transpose(lse_s[...])[0:HEADS, :]
+    after = x + (dot_nn(mixed_ref[...], attn_ref[3]) + vec_ref[6:7, :])
+    after_ref[...] = after
+    unit, _ = normalised(after)
+    normed_two = (unit * vec_ref[2:3, :] + vec_ref[3:4, :]).astype(bf16)
+    for tile in range(FF // TILE):
+        columns = slice(tile * TILE, (tile + 1) * TILE)
+        inner = dot_nn(normed_two, up_ref[:, columns]) + vec_ref[8 + tile : 9 + tile, :]
+        act_s[:, columns] = (
+            0.5 * inner * (1.0 + jnp.tanh(GELU_SCALE * (inner + 0.044715 * inner * inner * inner)))
+        ).astype(bf16)
+    hidden = after + (dot_nn(act_s[...], down_ref[...]) + vec_ref[7:8, :])
+    hid_ref[...] = hidden
+    hid16_ref[...] = hidden.astype(bf16)
+
+
+SAVED = (
+    ((SEG, D), f32),
+    ((2 * SEG, D), bf16),
+    ((SEG, D), bf16),
+    ((2 * SEG, D), bf16),
+    ((2 * SEG, D), bf16),
+    ((HEADS, SEG), f32),
+    ((SEG, D), bf16),
+    ((SEG, D), f32),
+)
+
+
+def whole_spec(shape):
+    return pl.BlockSpec(shape, lambda *_: (0,) * len(shape))
+
+
+def stream_spec(shape, stream=None):
+    zeros = (0,) * len(shape)
+    if stream is None:
+        return pl.BlockSpec((None,) + shape, lambda i: (i,) + zeros)
+    return pl.BlockSpec((None,) + shape, lambda i: (stream,) + zeros)
+
+
+def forward_layer(stream, streams, bias, hidden, memory, attn, upper, lower, vectors, earlier):
+    saved_shapes = [jax.ShapeDtypeStruct((streams,) + shape, dtype) for shape, dtype in SAVED]
+    saved_specs = [stream_spec(shape, stream) for shape, dtype in SAVED]
+    out_shape = [saved_shapes[0], jax.ShapeDtypeStruct((SEG, D), bf16)] + saved_shapes[1:]
+    out_specs = [saved_specs[0], whole_spec((SEG, D))] + saved_specs[1:]
+    operands = [bias, hidden, memory, attn, upper, lower, vectors]
+    in_specs = [
+        pl.BlockSpec(memory_space=pltpu.SMEM),
+        stream_spec((SEG, D), stream),
+        whole_spec((SEG, D)),
+        whole_spec(attn.shape),
+        whole_spec(upper.shape),
+        whole_spec(lower.shape),
+        whole_spec(vectors.shape),
+    ]
+    aliases = {}
+    if earlier is not None:
+        for place, array in enumerate(earlier):
+            aliases[len(operands)] = place if place == 0 else place + 1
+            operands.append(array)
+            in_specs.append(pl.BlockSpec(memory_space=pl.ANY))
+    out = pl.pallas_call(
+        forward_kernel,
+        grid=(1,),
+        out_shape=out_shape,
+        in_specs=in_specs,
+        out_specs=out_specs,
+        scratch_shapes=[pltpu.VMEM((SEG, FF), bf16), pltpu.VMEM((SEG, PAIR), f32)],
+        input_output_aliases=aliases,
+        compiler_params=pltpu.CompilerParams(vmem_limit_bytes=VMEM_LIMIT),
+        cost_estimate=pl.CostEstimate(flops=10**10, bytes_accessed=2 * 10**7, transcendentals=10**7),
+        name="layer_forward",
+    )(*operands)
+    return [out[0]] + list(out[2:]), out[1]
+
+
+def head_kernel(scale, x_ref, target_ref, weight_ref, out_ref, outer_ref, bias_ref, g_ref, dout_ref, douter_ref, loss_ref, acc_s):
+    step = pl.program_id(0)
+
+    @pl.when(step == 0)
+    def _():
+        acc_s[...] = jnp.zeros_like(acc_s)
+        douter_ref[...] = jnp.zeros_like(douter_ref)
+        loss_ref[...] = jnp.zeros_like(loss_ref)
+
+    unit, rscale = normalised(x_ref[...])
+    gain = outer_ref[1:2, :]
+    normed = (unit * gain + outer_ref[2:3, :]).astype(bf16)
+    logits = dot_nn(normed, out_ref[...]) + bias_ref[...]
+    most = jnp.max(logits, -1, keepdims=True)
+    powers = jnp.exp(logits - most)
+    total = jnp.sum(powers, -1, keepdims=True)
+    chosen = lax.broadcasted_iota(jnp.int32, logits.shape, 1) == target_ref[...]
+    picked = jnp.sum(jnp.where(chosen, logits, 0.0), -1, keepdims=True)
+    weight = weight_ref[...]
+    loss_ref[...] += jnp.sum(weight * (most + jnp.log(total) - picked), 0, keepdims=True)
+    spread = weight * scale
+    dlogits = (powers * (spread / total) - jnp.where(chosen, spread, 0.0)).astype(bf16)
+    acc_s[...] += dot_tn(normed, dlogits)
+    bias_grad = column_sum(dlogits.astype(f32))
+    dnormed = dot_nt(dlogits, out_ref[...])
+    g_ref[...] = norm_back(dnormed, gain, unit, rscale)
+    douter_ref[1:2, :] += column_sum(dnormed * unit)
+    douter_ref[2:3, :] += column_sum(dnormed)
+    douter_ref[3:4, :] += bias_grad[:, :D]
+    douter_ref[4:5, :] += bias_grad[:, D:]
+
+    @pl.when(step == pl.num_programs(0) - 1)
+    def _():
+        dout_ref[...] = acc_s[...]
+
+
+def head(hidden, targets, weighting, out_weight, outer_vectors, scale):
+    streams = hidden.shape[0]
+    codes = out_weight.shape[1]
+    bias = outer_vectors[3:].reshape(1, codes)
+    return pl.pallas_call(
+        functools.partial(head_kernel, scale),
+        grid=(streams,),
+        out_shape=[
+            jax.ShapeDtypeStruct((streams, SEG, D), f32),
+            jax.ShapeDtypeStruct((D, codes), f32),
+            jax.ShapeDtypeStruct((8, D), f32),
+            jax.ShapeDtypeStruct((1, 1), f32),
+        ],
+        in_specs=[
+            stream_spec((SEG, D)),
+            stream_spec((SEG, 1)),
+            stream_spec((SEG, 1)),
+            whole_spec((D, codes)),
+            whole_spec(outer_vectors.shape),
+            whole_spec((1, codes)),
+        ],
+        out_specs=[stream_spec((SEG, D)), whole_spec((D, codes)), whole_spec((8, D)), whole_spec((1, 1))],
+        scratch_shapes=[pltpu.VMEM((D, codes), f32)],
+        compiler_params=pltpu.CompilerParams(vmem_limit_bytes=VMEM_LIMIT),
+        cost_estimate=pl.CostEstimate(flops=33 * 10**8, bytes_accessed=10**7, transcendentals=10**6),
+        name="head",
+    )(hidden, targets[..., None], weighting[..., None], out_weight, outer_vectors, bias)
+
+
+def feed_back_kernel(g_ref, after_ref, up_ref, down_ref, vec_ref, dafter_ref, dup_ref, ddown_ref, dvec_ref, up_s, down_s, act_s, inner_s):
+    step = pl.program_id(0)
+
+    @pl.when(step == 0)
+    def _():
+        up_s[...] = jnp.zeros_like(up_s)
+        down_s[...] = jnp.zeros_like(down_s)
+        dvec_ref[...] = jnp.zeros_like(dvec_ref)
+
+    grad = g_ref[...]
+    branch = grad.astype(bf16)
+    dvec_ref[2:3, :] += column_sum(branch.astype(f32))
+    unit, scale = normalised(after_ref[...])
+    gain = vec_ref[2:3, :]
+    normed = (unit * gain + vec_ref[3:4, :]).astype(bf16)
+    for tile in range(FF // TILE):
+        columns = slice(tile * TILE, (tile + 1) * TILE)
+        inner = dot_nn(normed, up_ref[:, columns]) + vec_ref[8 + tile : 9 + tile, :]
+        dact = dot_nt(branch, down_ref[columns, :])
+        square = inner * inner
+        bent = jnp.tanh(GELU_SCALE * (inner + 0.044715 * square * inner))
+        half = 0.5 * (1.0 + bent)
+        act_s[:, columns] = (inner * half).astype(bf16)
+        slope = half + (0.5 * GELU_SCALE) * inner * (1.0 - bent * bent) * (1.0 + 0.134145 * square)
+        dinner = (dact * slope).astype(bf16)
+        inner_s[:, columns] = dinner
+        dvec_ref[4 + tile : 5 + tile, :] += column_sum(dinner.astype(f32))
+    dnormed = dot_nt(inner_s[...], up_ref[...])
+    dvec_ref[0:1, :] += column_sum(dnormed * unit)
+    dvec_ref[1:2, :] += column_sum(dnormed)
+    dafter_ref[...] = grad + norm_back(dnormed, gain, unit, scale)
+    normed_t = jnp.transpose(normed)
+    branch_t = jnp.transpose(branch)
+    up_s[...] += dot_nn(normed_t, inner_s[...])
+    down_s[...] += dot_nn(branch_t, act_s[...])
+
+    @pl.when(step == pl.num_programs(0) - 1)
+    def _():
+        dup_ref[...] = up_s[...].astype(bf16)
+        ddown_ref[...] = jnp.transpose(down_s[...].astype(bf16))
+
+
+def feed_back(grad, after, upper, lower, vectors):
+    streams = grad.shape[0]
+    return pl.pallas_call(
+        feed_back_kernel,
+        grid=(streams,),
+        out_shape=[
+            jax.ShapeDtypeStruct((streams, SEG, D), f32),
+            jax.ShapeDtypeStruct((D, FF), bf16),
+            jax.ShapeDtypeStruct((FF, D), bf16),
+            jax.ShapeDtypeStruct((8, D), f32),
+        ],
+        in_specs=[
+            stream_spec((SEG, D)),
+            stream_spec((SEG, D)),
+            whole_spec(upper.shape),
+            whole_spec(lower.shape),
+            whole_spec(vectors.shape),
+        ],
+        out_specs=[stream_spec((SEG, D)), whole_spec((D, FF)), whole_spec((FF, D)), whole_spec((8, D))],
+        scratch_shapes=[
+            pltpu.VMEM((D, FF), f32),
+            pltpu.VMEM((D, FF), f32),
+            pltpu.VMEM((SEG, FF), bf16),
+            pltpu.VMEM((SEG, FF), bf16),
+        ],
+        compiler_params=pltpu.CompilerParams(vmem_limit_bytes=VMEM_LIMIT),
+        cost_estimate=pl.CostEstimate(flops=11 * 10**9, bytes_accessed=2 * 10**7, transcendentals=2 * 10**6),
+        name="feed_back",
+    )(grad, after, upper, lower, vectors)
+
+
+def attend_back_kernel(
+    bias_ref,
+    dafter_ref,
+    x_ref,
+    mem_ref,
+    keyin_ref,
+    q_ref,
+    k_ref,
+    v_ref,
+    lse_ref,
+    mixed_ref,
+    attn_ref,
+    vec_ref,
+    dx_ref,
+    dattn_ref,
+    dvec_ref,
+    attn_s,
+    dmixed_s,
+    dq_s,
+    dk_s,
+    dv_s,
+    ds_s,
+    delta_s,
+):
+    step = pl.program_id(0)
+
+    @pl.when(step == 0)
+    def _():
+        attn_s[...] = jnp.zeros_like(attn_s)
+        dvec_ref[...] = jnp.zeros_like(dvec_ref)
+
+    dafter = dafter_ref[...]
+    branch = dafter.astype(bf16)
+    dvec_ref[4:5, :] += column_sum(branch.astype(f32))
+    dmixed = dot_nt(branch, attn_ref[3]).astype(bf16)
+    dmixed_s[...] = dmixed
+    attn_s[3] += dot_nn(jnp.transpose(mixed_ref[...]), branch)
+    product = dmixed.astype(f32) * mixed_ref[...].astype(f32)
+    high = product.astype(bf16)
+    rest = (product - high.astype(f32)).astype(bf16)
+    owner = lax.broadcasted_iota(jnp.int32, (HEADS, D), 1) // HEAD_DIM
+    pick = (owner == lax.broadcasted_iota(jnp.int32, (HEADS, D), 0)).astype(bf16)
+    delta_s[...] = dot_nt(pick, high) + dot_nt(pick, rest)
+    first, second = head_masks()
+    memory_bias = bias_ref[0]
+    key_pos = lax.broadcasted_iota(jnp.int32, (HALF, 2 * HALF), 0)
+    query_pos = lax.broadcasted_iota(jnp.int32, (HALF, 2 * HALF), 1) % HALF
+    diagonal = key_pos <= query_pos
+    head_row = lax.broadcasted_iota(jnp.int32, (PAIR, HALF), 0)
+
+    def pair_body(pair, carry):
+        lanes = pair_lanes(pair)
+        q_pair, do_pair = q_ref[:, lanes], dmixed_s[:, lanes]
+
+        def spread(value):
+            return jnp.concatenate(
+                [value[:HALF] * first, value[:HALF] * second, value[HALF:] * first, value[HALF:] * second], 0
+            )
+
+        q_all, do_all = spread(q_pair), spread(do_pair)
+
+        def rows_of(ref):
+            one, two = ref[pl.ds(2 * pair, 1), :], ref[pl.ds(2 * pair + 1, 1), :]
+            return jnp.concatenate([one[:, :HALF], two[:, :HALF], one[:, HALF:], two[:, HALF:]], 1)
+
+        lse_all, delta_all = rows_of(lse_ref), rows_of(delta_s)
+        for block in range(4):
+            keys = slice(block * HALF, (block + 1) * HALF)
+            start = 2 * HALF if block == 3 else 0
+            scores = dot_nt(k_ref[keys, lanes], q_all[start:])
+            if block < 2:
+                scores = scores + memory_bias
+            weights = jnp.exp(scores - lse_all[:, start:])
+            if block == 2:
+                weights = jnp.concatenate(
+                    [jnp.where(diagonal, weights[:, : 2 * HALF], 0.0), weights[:, 2 * HALF :]], 1
+                )
+            if block == 3:
+                weights = jnp.where(diagonal, weights, 0.0)
+            dweights = dot_nt(v_ref[keys, lanes], do_all[start:])
+            dscores = (weights * (dweights - delta_all[:, start:])).astype(bf16)
+            dv_s[keys, lanes] = dot_nn(weights.astype(bf16), do_all[start:]).astype(bf16)
+            dk_s[keys, lanes] = dot_nn(dscores, q_all[start:]).astype(bf16)
+            ds_s[keys, start:] = dscores
+        k_t = jnp.transpose(k_ref[:, lanes])
+        for block in range(2):
+            seen = SEG + (block + 1) * HALF
+            grads = dot_nn(k_t[:, :seen], ds_s[:seen, block * 2 * HALF : (block + 1) * 2 * HALF])
+            grads = jnp.where(head_row < HEAD_DIM, grads[:, :HALF], grads[:, HALF:])
+            dq_s[block * HALF : (block + 1) * HALF, lanes] = (
+                jnp.transpose(grads) * (HEAD_DIM**-0.5)
+            ).astype(bf16)
+        return carry
+
+    lax.fori_loop(0, HEADS // 2, pair_body, 0)
+    dq, dk, dv = dq_s[...], dk_s[...], dv_s[...]
+    keyin_t = jnp.transpose(keyin_ref[...])
+    attn_s[0] += dot_nn(keyin_t[:, SEG:], dq)
+    attn_s[1] += dot_nn(keyin_t, dk)
+    attn_s[2] += dot_nn(keyin_t, dv)
+    dvec_ref[2:3, :] += column_sum(dq.astype(f32))
+    dvec_ref[3:4, :] += column_sum(dv.astype(f32))
+    dkeyin = dot_nt(dk, attn_ref[1]) + dot_nt(dv, attn_ref[2])
+    dmem = dkeyin[:SEG]
+    down = dkeyin[SEG:] + dot_nt(dq, attn_ref[0])
+    gain = vec_ref[0:1, :]
+    unit, scale = normalised(x_ref[...])
+    mem_unit, _ = normalised(mem_ref[...].astype(f32))
+    dvec_ref[0:1, :] += column_sum(down * unit + dmem * mem_unit)
+    dvec_ref[1:2, :] += column_sum(down + dmem)
+    dx_ref[...] = dafter + norm_back(down, gain, unit, scale)
+
+    @pl.when(step == pl.num_programs(0) - 1)
+    def _():
+        dattn_ref[...] = attn_s[...].astype(bf16)
+
+
+def attend_back(bias, dafter, x, memory, saved, attn, vectors):
+    streams = dafter.shape[0]
+    keyin, q, k, v, lse, mixed = saved
+    return pl.pallas_call(
+        attend_back_kernel,
+        grid=(streams,),
+        out_shape=[
+            jax.ShapeDtypeStruct((streams, SEG, D), f32),
+            jax.ShapeDtypeStruct((4, D, D), bf16),
+            jax.ShapeDtypeStruct((8, D), f32),
+        ],
+        in_specs=[
+            pl.BlockSpec(memory_space=pltpu.SMEM),
+            stream_spec((SEG, D)),
+            stream_spec((SEG, D)),
+            stream_spec((SEG, D)),
+            stream_spec((2 * SEG, D)),
+            stream_spec((SEG, D)),
+            stream_spec((2 * SEG, D)),
+            stream_spec((2 * SEG, D)),
+            stream_spec((HEADS, SEG)),
+            stream_spec((SEG, D)),
+            whole_spec(attn.shape),
+            whole_spec(vectors.shape),
+        ],
+        out_specs=[stream_spec((SEG, D)), whole_spec((4, D, D)), whole_spec((8, D))],
+        scratch_shapes=[
+            pltpu.VMEM((4, D, D), f32),
+            pltpu.VMEM((SEG, D), bf16),
+            pltpu.VMEM((SEG, D), bf16),
+            pltpu.VMEM((2 * SEG, D), bf16),
+            pltpu.VMEM((2 * SEG, D), bf16),
+            pltpu.VMEM((2 * SEG, 2 * SEG), bf16),
+            pltpu.VMEM((HEADS, SEG), f32),
+        ],
+        compiler_params=pltpu.CompilerParams(vmem_limit_bytes=VMEM_LIMIT),
+        cost_estimate=pl.CostEstimate(flops=3 * 10**10, bytes_accessed=2 * 10**7, transcendentals=10**7),
+        name="attend_back",
+    )(bias, dafter, x, memory, keyin, q, k, v, lse, mixed, attn, vectors)
+
+
+HIGH = lax.Precision.HIGH
 
 
 def from_behind(value, axis, steps):
@@ -25,108 +517,6 @@
         return part.astype(jnp.bfloat16) if part.dtype == jnp.float32 else part
 
     return jax.tree.map(short, value)
-
-
-def rounders():
-
-    def round_value(value):
-        return lax.optimization_barrier(value.astype(jnp.bfloat16)).astype(jnp.float32)
-
-    def plain_value(value):
-        return value
-
-    rounded = jax.custom_vjp(round_value)
-    passed = jax.custom_vjp(plain_value)
-
-    def keep_round(value):
-        return (round_value(value), None)
-
-    def pass_grad(kept, grad):
-        return (grad,)
-
-    def keep_plain(value):
-        return (value, None)
-
-    def round_grad(kept, grad):
-        return (round_value(grad),)
-
-    rounded.defvjp(keep_round, pass_grad)
-    passed.defvjp(keep_plain, round_grad)
-    return (rounded, passed)
-
-
-def half_product(form, left_form, right_form):
-
-    def forward(left, right):
-        return jnp.einsum(
-            form,
-            left.astype(jnp.bfloat16),
-            right.astype(jnp.bfloat16),
-            preferred_element_type=jnp.float32,
-        )
-
-    product = jax.custom_vjp(forward)
-
-    def keep_both(left, right):
-        return (forward(left, right), (left, right))
-
-    def back_both(kept, grad):
-        left, right = kept
-        grad_half = grad.astype(jnp.bfloat16)
-        grad_left = jnp.einsum(
-            left_form, grad_half, right.astype(jnp.bfloat16), preferred_element_type=jnp.float32
-        )
-        grad_right = jnp.einsum(
-            right_form, left.astype(jnp.bfloat16), grad_half, preferred_element_type=jnp.float32
-        )
-        return (grad_left, grad_right)
-
-    product.defvjp(keep_both, back_both)
-    return product
-
-
-def layer_norm(values, gain, shift):
-    centred = values - jnp.mean(values, -1, keepdims=True)
-    spread = jnp.mean(centred * centred, -1, keepdims=True)
-    return centred * lax.rsqrt(spread + 1e-05) * gain + shift
-
-
-def attention_layer(hidden, memory, has_memory, attn, upper, lower, vectors):
-    low, low_back = rounders()
-    matmul = half_product("qd,de->qe", "qe,de->qd", "qd,qe->de")
-    score_product = half_product("qhd,khd->hqk", "hqk,khd->qhd", "qhd,hqk->khd")
-    mix_product = half_product("hqk,khd->qhd", "qhd,khd->hqk", "hqk,qhd->khd")
-    length, width = hidden.shape
-    heads = width // HEAD_DIM
-    normed = low(layer_norm(hidden, vectors[0], vectors[1]))
-    memory_normed = low(layer_norm(memory, vectors[0], vectors[1]))
-    keyin = jnp.concatenate([memory_normed, normed], 0)
-    queries = low(low_back(matmul(normed, attn[0]) + vectors[4])).reshape(length, heads, HEAD_DIM)
-    keys_all = low(low_back(matmul(keyin, attn[1]))).reshape(2 * length, heads, HEAD_DIM)
-    values = low(low_back(matmul(keyin, attn[2]) + vectors[5])).reshape(2 * length, heads, HEAD_DIM)
-    scores = low_back(score_product(queries, keys_all) * HEAD_DIM ** (-0.5))
-    query_pos = jnp.arange(length)[:, None]
-    key_pos = jnp.arange(2 * length)[None, :]
-    allowed = jnp.where(key_pos < length, has_memory, key_pos - length <= query_pos)
-    scores = jnp.where(allowed[None], scores, -1e30)
-    weights = low(jax.nn.softmax(scores, -1))
-    mixed = mix_product(weights, values).reshape(length, width)
-    mixed = low(low_back(mixed))
-    after_attn = hidden + low_back(matmul(mixed, attn[3]) + vectors[6])
-    normed_two = low(layer_norm(after_attn, vectors[2], vectors[3]))
-    inner = low_back(matmul(normed_two, upper) + vectors[8:].reshape(-1))
-    active = low(jax.nn.gelu(inner))
-    return after_attn + low_back(matmul(active, lower) + vectors[7])
-
-
-def head_loss(hidden, out_weight, outer_vectors, targets, weighting):
-    low, low_back = rounders()
-    matmul = half_product("sqd,de->sqe", "sqe,de->sqd", "sqd,sqe->de")
-    normed = low(layer_norm(hidden, outer_vectors[1], outer_vectors[2]))
-    logits = low_back(matmul(normed, out_weight) + outer_vectors[3:].reshape(-1))
-    log_probs = jax.nn.log_softmax(logits, -1)
-    picked = jnp.take_along_axis(log_probs, targets[..., None], -1)[..., 0]
-    return -jnp.sum(picked * weighting)
 
 
 def adamw(weight, moment, second, grad, rate, decay):
@@ -144,11 +534,11 @@
         matrix = matrix.T
     matrix = matrix / (jnp.sqrt(jnp.sum(matrix * matrix)) + 1e-07)
     for sweep in range(5):
-        gram_matrix = jnp.matmul(matrix, matrix.T, precision=HIGHEST)
+        gram_matrix = jnp.matmul(matrix, matrix.T, precision=HIGH)
         poly_term = -4.775 * gram_matrix + 2.0315 * jnp.matmul(
-            gram_matrix, gram_matrix, precision=HIGHEST
+            gram_matrix, gram_matrix, precision=HIGH
         )
-        matrix = 3.4445 * matrix + jnp.matmul(poly_term, matrix, precision=HIGHEST)
+        matrix = 3.4445 * matrix + jnp.matmul(poly_term, matrix, precision=HIGH)
     return matrix.T if flipped else matrix
 
 
@@ -204,53 +594,64 @@
     up_copy,
     down_copy,
 ):
-    has_memory = lax.axis_index("seg") > 0
+    segment = lax.axis_index("seg")
     stream_total = frames.shape[0] * lax.axis_size("dp")
+    streams = frames.shape[0]
+    behind = from_behind(frames, "seg", 1)
     local_counts = jnp.sum(speech_mask, 1)
-    every_count = lax.all_gather(local_counts[None], "seg", axis=0, tiled=True)
-    inverse = 1.0 / jnp.sum(every_count, 0).astype(jnp.float32)
-    weighting = speech_mask.astype(jnp.float32) * inverse[:, None]
-    frames_float = frames.astype(jnp.float32)
-    attn_weight = attn_copy.astype(jnp.float32)
-    up_weight = up_copy.astype(jnp.float32)
-    down_weight = down_copy.astype(jnp.float32)
-    out_weight = out_copy.astype(jnp.float32)
-    hidden, embed_back = jax.vjp(
-        lambda weight, outer: jnp.matmul(frames_float, weight, precision=HIGHEST) + outer[0],
-        in_copy.astype(jnp.float32),
-        outer_vectors,
-    )
-    mapped = jax.vmap(attention_layer, (0, 0, None, None, None, None, None))
-    pullbacks = []
+    counts = lax.psum(local_counts, "seg")
+    weighting = speech_mask.astype(f32) / counts.astype(f32)[:, None]
+    bias = jnp.where(segment > 0, 0.0, -1e30).astype(f32)[None]
+    hidden = jnp.dot(frames, in_copy, preferred_element_type=f32) + outer_vectors[0]
+    memory = (jnp.dot(behind, in_copy, preferred_element_type=f32) + outer_vectors[0]).astype(bf16)
+    memory = [memory[stream] for stream in range(streams)]
+    kept = []
     for depth in range(LAYERS):
-        memory = from_behind(hidden.astype(jnp.bfloat16), "seg", 1).astype(jnp.float32)
-        hidden, pullback = jax.vjp(
-            lambda rows, attn, upper, lower, vectors, held=memory: mapped(
-                rows, held, has_memory, attn, upper, lower, vectors
-            ),
-            hidden,
-            attn_weight[depth],
-            up_weight[depth],
-            down_weight[depth],
-            layer_vectors[depth],
-        )
-        pullbacks.append(pullback)
-    loss_here, head_back = jax.vjp(
-        lambda rows, weight, outer: head_loss(rows, weight, outer, targets, weighting),
-        hidden,
-        out_weight,
-        outer_vectors,
-    )
-    grad_hidden, grad_out, grad_outer = head_back(jnp.ones_like(loss_here) / stream_total)
+        saved, passed = None, []
+        for stream in range(streams):
+            saved, short = forward_layer(
+                stream,
+                streams,
+                bias,
+                hidden,
+                memory[stream],
+                attn_copy[depth],
+                up_copy[depth],
+                down_copy[depth],
+                layer_vectors[depth],
+                saved,
+            )
+            if depth + 1 < LAYERS:
+                passed.append(from_behind(short, "seg", 1))
+        kept.append((hidden, jnp.stack(memory), saved))
+        hidden = saved[0]
+        memory = passed
+    grad_hidden, grad_out, head_outer, loss_here = head(
+        hidden, targets, weighting, out_copy, outer_vectors, 1.0 / stream_total
+    )
+    loss_here = loss_here[0, 0]
     attn_grads, up_grads, down_grads, vector_grads = ([], [], [], [])
     for depth in reversed(range(LAYERS)):
-        grad_hidden, grad_attn, grad_up, grad_down, grad_vector = pullbacks[depth](grad_hidden)
+        entering, held, saved = kept[depth]
+        dafter, grad_up, grad_down, feed_vec = feed_back(
+            grad_hidden, saved[7], up_copy[depth], down_copy[depth], layer_vectors[depth]
+        )
+        grad_hidden, grad_attn, attn_vec = attend_back(
+            bias, dafter, entering, held, saved[1:7], attn_copy[depth], layer_vectors[depth]
+        )
         attn_grads.insert(0, grad_attn)
         up_grads.insert(0, grad_up)
         down_grads.insert(0, grad_down)
-        vector_grads.insert(0, grad_vector)
-    grad_in, grad_outer_low = embed_back(grad_hidden)
-    grad_outer = grad_outer + grad_outer_low
+        vector_grads.insert(
+            0,
+            jnp.concatenate([attn_vec[0:2], feed_vec[0:2], attn_vec[2:5], feed_vec[2:3], feed_vec[4:8]], 0),
+        )
+    rows = grad_hidden.reshape(streams * SEG, D)
+    rows_high = rows.astype(bf16)
+    rows_rest = (rows - rows_high.astype(f32)).astype(bf16)
+    frame_rows = frames.reshape(streams * SEG, frames.shape[2])
+    grad_in = dot_tn(frame_rows, rows_high) + dot_tn(frame_rows, rows_rest)
+    grad_outer = jnp.concatenate([jnp.sum(rows, 0, keepdims=True), head_outer[1:5]], 0)
     grad_vectors = jnp.stack(vector_grads)
     grad_in, grad_out, grad_vectors, grad_outer, loss_sum = lax.psum(
         (grad_in, grad_out, grad_vectors, grad_outer, loss_here), ("seg", "dp")

time: 1160 us -> 960 us (0.83)
  matrix products: 518 us -> 135 us
  Pallas kernels: 0 us -> 201 us
  waiting for transfers between devices: 120 us -> 319 us
  other arithmetic: 198 us -> 65.5 us
  blocking collectives: 198 us -> 153 us
  local copies, waits for them, and re-layouts: 87 us -> 45.2 us
    dot_general x96 -> x49, matrix products: 480 us -> 135 us  [the longest x15 60.6 us: orthogonal(): gram_matrix = jnp.matmul(matrix, matrix.T, precision=HIGH)]
    pallas_call x0 -> x9, Pallas kernels: none -> 201 us  [the longest x2 71.9 us: attend_back(): pl.pallas_call(attend_back_kernel, grid=(streams,), out_shape=[jax.ShapeD...]
    convert_element_type x16 -> x2, other arithmetic: 107 us -> 2.62 us  [the longest x1 2.61 us: local(): attn_sum, up_sum, down_sum = (lax.psum_scatter(attn_local.astype(jnp.bflo...]
    unnamed x9 -> x11, waiting for transfers between devices: 0.15 us -> 53.5 us
    reduce_scatter x1, waiting for transfers between devices: 0.02 us -> 50.4 us  [local(): lax.psum_scatter(attn_local.astype(jnp.bfloat16), 'seg', scatter_dimensio...]
    psum x0 -> x1, waiting for transfers between devices: none -> 50.1 us  [local(): attn_sum, up_sum, down_sum = lax.psum((attn_sum, up_sum, down_sum), 'dp')]
    reduce_scatter x1, waiting for transfers between devices: 0.03 us -> 49.4 us  [local(): lax.psum_scatter(down_local.astype(jnp.bfloat16), 'seg', scatter_dimensio...]
    sub x2 -> x0, matrix products: 37.9 us -> none  [attention_layer(): weights = low(jax.nn.softmax(scores, -1))]
  transfers between devices with their start and end apart: 11 -> 13, of which waited for: 4 -> 8; matrix products, arithmetic and copies ran while one was open for 18% -> 24% of each run, Pallas kernels for 0% -> 8%
where the time goes in v1:
time: 960 us; the launch traced here: 952 us
  waiting for transfers between devices  319 us (33%)
  Pallas kernels  201 us (21%)
  blocking collectives  153 us (16%)
  matrix products  135 us (14%)
  other arithmetic  65.5 us (7%)
  local copies, waits for them, and re-layouts  45.2 us (5%)
  between operations  23.8 us (2%)
    psum x1, waiting for transfers between devices, local(): lax.psum((grad_in, grad_out, grad_vectors, grad_outer, loss_here), ('seg'...  84.7 us
    psum x1, blocking collectives, local(): attn_sum, up_sum, down_sum = lax.psum((attn_sum, up_sum, down_sum), 'dp')  72 us
    pallas_call x2, Pallas kernels, attend_back(): pl.pallas_call(attend_back_kernel, grid=(streams,), out_shape=[jax.ShapeD...  71.9 us
    pallas_call x4, Pallas kernels, forward_layer(): pl.pallas_call(forward_kernel, grid=(1,), out_shape=out_shape, in_specs=i...  71.6 us
    dot_general x15, matrix products, orthogonal(): gram_matrix = jnp.matmul(matrix, matrix.T, precision=HIGH)  60.6 us
    unnamed x11, waiting for transfers between devices  53.5 us
    reduce_scatter x1, waiting for transfers between devices, local(): lax.psum_scatter(attn_local.astype(jnp.bfloat16), 'seg', scatter_dimensio...  50.4 us
    psum x1, waiting for transfers between devices, local(): attn_sum, up_sum, down_sum = lax.psum((attn_sum, up_sum, down_sum), 'dp')  50.1 us
  transfers between devices with their start and end apart: 13, of which 8 were waited for; matrix products, arithmetic and copies ran while one was open for 24% of the time, Pallas kernels for 8%

profile of v1, /device:TPU:0, one launch (start us, length us, event | category | flops | bytes accessed | tf_op | source)
XLA Modules:
  0.0 952.3 jit_solution(14776692959025243811)
XLA Ops:
  11.1 4.6 slice_bitcast_fusion
  21.9 10.2 %psum.70 = s32[2]{0:T(128)S(1)} all-reduce(s32[2]{0:T(128)S(1)} %reduce_sum.108), channel_id=1, replica_groups=mesh['seg'=8,'dp'=4] {'seg'}, use_global_device_ids=true, to_apply=%region_1.0 | all-reduce | flops 2 | bytes 16 | tf_op jit(solution)/shard_map/psum | solution.py:602
  38.9 17.8 %layer_forward.4 = (f32[2,512,512]{2,1,0:T(8,128)}, bf16[512,512]{1,0:T(8,128)(2,1)}, bf16[2,1024,512]{2,1,0:T(8,128)(2,1)}, bf16[2,512,512]{2,1,0:T(8,128)(2,1)...) custom-call(f32[1]{0:T(128)} %bitcast.bias_ref, ...), custom_call_target="tpu_custom_call" | custom-call | flops 10000000000 | bytes 20000000 | tf_op jit(solution)/shard_map/layer_forward/pallas_call | solution.py:194
  58.3 17.8 %layer_forward.5 = (f32[2,512,512]{2,1,0:T(8,128)}, bf16[512,512]{1,0:T(8,128)(2,1)}, bf16[2,1024,512]{2,1,0:T(8,128)(2,1)}, bf16[2,512,512]{2,1,0:T(8,128)(2,1)...) custom-call(f32[1]{0:T(128)} %bitcast.bias_ref, ...), custom_call_target="tpu_custom_call", output_to_operand_aliasing={{0}: (7, {}), {2}: (8, {}), {3}: (9, {}), {4}: (10, {}), {5... | custom-call | flops 10000000000 | bytes 20000000 | tf_op jit(solution)/shard_map/layer_forward/pallas_call | solution.py:194
  76.1 4.2 collective-permute-start.1
  81.2 18.3 %layer_forward.6 = (f32[2,512,512]{2,1,0:T(8,128)}, bf16[512,512]{1,0:T(8,128)(2,1)}, bf16[2,1024,512]{2,1,0:T(8,128)(2,1)}, bf16[2,512,512]{2,1,0:T(8,128)(2,1)...) custom-call(f32[1]{0:T(128)} %bitcast.bias_ref, ...), custom_call_target="tpu_custom_call" | custom-call | flops 10000000000 | bytes 20000000 | tf_op jit(solution)/shard_map/layer_forward/pallas_call | solution.py:194
  100.2 17.8 %layer_forward.7 = (f32[2,512,512]{2,1,0:T(8,128)}, bf16[512,512]{1,0:T(8,128)(2,1)}, bf16[2,1024,512]{2,1,0:T(8,128)(2,1)}, bf16[2,512,512]{2,1,0:T(8,128)(2,1)...) custom-call(f32[1]{0:T(128)} %bitcast.bias_ref, ...), custom_call_target="tpu_custom_call", output_to_operand_aliasing={{0}: (7, {}), {2}: (8, {}), {3}: (9, {}), {4}: (10, {}), {5... | custom-call | flops 10000000000 | bytes 20000000 | tf_op jit(solution)/shard_map/layer_forward/pallas_call | solution.py:194
  118.0 10.9 %head.1 = (f32[2,512,512]{2,1,0:T(8,128)}, f32[512,1024]{1,0:T(8,128)}, f32[8,512]{1,0:T(8,128)}, f32[1,1]{1,0:T(1,128)}) custom-call(f32[2,512,512]{2,1,0:T(8,128)} %get-tuple-element.96.x_ref, s32[2,512,1]{2,1,0:T(8,128)} %copy.152.target_ref, f32[2,512,1]{2,1,0:T(8,128)} %copy.153.weight_ref, bf16[512,1024]{1,0:T(8,128)(2,1)} %out_ref.1, ...), custom_call_target="tpu_custom_call" | custom-call | flops 3300000000 | bytes 10000000 | tf_op jit(solution)/shard_map/head/pallas_call | solution.py:249
  129.0 22.8 %feed_back.2 = (f32[2,512,512]{2,1,0:T(8,128)}, bf16[512,2048]{1,0:T(8,128)(2,1)}, bf16[2048,512]{1,0:T(8,128)(2,1)}, f32[8,512]{1,0:T(8,128)}) custom-call(f32[2,512,512]{2,1,0:T(8,128)} %get-tuple-element.98.g_ref, f32[2,512,512]{2,1,0:T(8,128)} %get-tuple-element.99.after_ref, bf16[512,2048]{1,0:T(8,128)(2,1)} %get-tuple-element.253.up_ref, ...), custom_call_target="tpu_custom_call" | custom-call | flops 11000000512 | bytes 20000000 | tf_op jit(solution)/shard_map/feed_back/pallas_call | solution.py:318
  152.8 35.8 %attend_back.2 = (f32[2,512,512]{2,1,0:T(8,128)}, bf16[4,512,512]{2,1,0:T(8,128)(2,1)}, f32[8,512]{1,0:T(8,128)}) custom-call(f32[1]{0:T(128)} %bitcast.bias_ref, f32[2,512,512]{2,1,0:T(8,128)} %get-tuple-element.100.dafter_ref, f32[2,512,512]{2,1,0:T(8,128)} %get-tuple-element.85.x_ref, bf16[2,512,512]{2,1,0:T(8,128)(2,1)} %pad_maximum_fusion.3.mem_ref, ...), custom_call_target="tpu_custom_call" | custom-call | flops 30000001024 | bytes 20000000 | tf_op jit(solution)/shard_map/attend_back/pallas_call | solution.py:467
  188.7 23.5 %feed_back.3 = (f32[2,512,512]{2,1,0:T(8,128)}, bf16[512,2048]{1,0:T(8,128)(2,1)}, bf16[2048,512]{1,0:T(8,128)(2,1)}, f32[8,512]{1,0:T(8,128)}) custom-call(f32[2,512,512]{2,1,0:T(8,128)} %get-tuple-element.107.g_ref, f32[2,512,512]{2,1,0:T(8,128)} %get-tuple-element.108.after_ref, bf16[512,2048]{1,0:T(8,128)(2,1)} %get-tuple-element.254.up_ref, ...), custom_call_target="tpu_custom_call" | custom-call | flops 11000000512 | bytes 20000000 | tf_op jit(solution)/shard_map/feed_back/pallas_call | solution.py:318
  214.2 6.3 copy.154
  220.6 36.1 %attend_back.3 = (f32[2,512,512]{2,1,0:T(8,128)}, bf16[4,512,512]{2,1,0:T(8,128)(2,1)}, f32[8,512]{1,0:T(8,128)}) custom-call(f32[1]{0:T(128)} %bitcast.bias_ref, f32[2,512,512]{2,1,0:T(8,128)} %get-tuple-element.109.dafter_ref, f32[2,512,512]{2,1,0:T(8,128)} %convolution_add_fusion.x_ref, bf16[2,512,512]{2,1,0:T(8,128)(2,1)} %copy-done.5, ...), custom_call_target="tpu_custom_call" | custom-call | flops 30000001024 | bytes 20000000 | tf_op jit(solution)/shard_map/attend_back/pallas_call | solution.py:467
  262.2 53.3 %all-reduce.13.cloned.1.call-done = bf16[2,512,2048]{2,0,1:T(2,128)(2,1)} async-done(((bf16[2,512,2048]{2,0,1:T(2,128)(2,1)}), bf16[2,512,2048]{2,0,1:T(2,128)(2,1)}) %all-reduce.13.cloned.1.call-update) | async-done | bytes 4194320
  318.2 4.6 pad_maximum_fusion.2
  322.8 4.6 pad_maximum_fusion
  329.5 41.2 %all-reduce.3 = (f32[]{:T(128)}, f32[2,12,512]{2,1,0:T(8,128)S(1)}, f32[5,512]{1,0:T(8,128)S(1)}) all-reduce(f32[]{:T(128)} %bitcast.15, f32[2,12,512]{2,1,0:T(8,128)S(1)} %pad_maximum_fusion.4, f32[5,512]{1,0:T(8,128)S(1)} %pad_maximum_fusion.5), channel_id=1, replica_groups=mesh['seg'=8,'dp'=4] {'seg','dp'}, use_global_device_ids=true, to_apply=%region_2.3 | all-reduce | flops 14849 | bytes 118792 | tf_op jit(solution)/shard_map/psum | solution.py:656
  371.9 84.7 %all-reduce.15.cloned.1.call-done = (f32[80,512]{1,0:T(8,128)}, f32[512,1024]{1,0:T(8,128)}) async-done(((f32[80,512]{1,0:T(8,128)}, f32[512,1024]{1,0:T(8,128)}), (f32[80,512]{1,0:T(8,128)}, f32[512,1024]{1,0:T(8,128)})) %all-reduce.15.cloned.1.call-update) | async-done | bytes 2261008 | tf_op jit(solution)/shard_map/psum | solution.py:656
  462.8 50.1 %all-reduce.11.cloned.1.call-done = f32[2,64,2048]{2,0,1:T(2,128)} async-done(((f32[2,64,2048]{2,0,1:T(2,128)}), f32[2,64,2048]{2,0,1:T(2,128)}) %all-reduce.11.cloned.1.call-update) | async-done | bytes 1048592 | tf_op jit(solution)/shard_map/psum | solution.py:676
  515.8 49.4 %reduce-scatter.5.cloned.1.call-done = bf16[2,256,512]{2,1,0:T(8,128)(2,1)} async-done(((bf16[2,2048,512]{2,1,0:T(8,128)(2,1)}), bf16[2,256,512]{2,1,0:T(8,128)(2,1)}) %reduce-scatter.5.cloned.1.call-update) | async-done | bytes 524304 | tf_op jit(solution)/shard_map/reduce_scatter | solution.py:672
  565.2 50.4 %reduce-scatter.3.cloned.1.call-done = bf16[8,64,512]{2,1,0:T(8,128)(2,1)} async-done(((bf16[8,512,512]{2,1,0:T(8,128)(2,1)}), bf16[8,64,512]{2,1,0:T(8,128)(2,1)}) %reduce-scatter.3.cloned.1.call-update) | async-done | bytes 524304 | tf_op jit(solution)/shard_map/reduce_scatter | solution.py:666
  615.7 72.0 %all-reduce.16 = (f32[8,64,512]{2,1,0:T(8,128)S(1)}, f32[2,256,512]{2,1,0:T(8,128)S(1)}) all-reduce(bf16[8,64,512]{2,1,0:T(8,128)(2,1)} %reduce-scatter.3.cloned.1.call-done, bf16[2,256,512]{2,1,0:T(8,128)(2,1)} %reduce-scatter.5.cloned.1.call-done), channel_id=1, replica_groups=mesh['seg'=8,'dp'=4] {'dp'}, use_global_device_ids=true, to_apply=%region_4.5 | all-reduce | flops 524288 | bytes 3145728 | tf_op jit(solution)/shard_map/psum | solution.py:676
  692.0 18.1 %psum.75 = f32[]{:T(128)} all-reduce(f32[]{:T(128)S(6)} %add.269), channel_id=1, replica_groups=mesh['seg'=8,'dp'=4] {'seg'}, use_global_device_ids=true, to_apply=%region_12.13 | all-reduce | flops 1 | bytes 8 | tf_op jit(solution)/shard_map/psum | solution.py:680
  724.0 7.8 fusion.140
  732.7 6.4 all-gather.14.cloned.1.call-done
  767.9 20.2 %all-gather.12.cloned.1.call-done = f32[1,2048,512]{2,1,0:T(8,128)} async-done(((f32[1,256,512]{2,1,0:T(8,128)}), f32[1,2048,512]{2,1,0:T(8,128)}) %all-gather.12.cloned.1.call-update) | async-done | bytes 4194320 | tf_op jit(solution)/shard_map/all_gather | solution.py:713
  788.1 3.9 multiply_reduce_fusion
  792.7 10.7 %fusion.2 = f32[512,512]{1,0:T(8,128)S(1)} fusion(f32[1,2048,512]{2,1,0:T(8,128)} %all-gather.12.cloned.1.call-done, f32[]{:T(128)S(6)} %add.320), kind=kOutput, calls=%fused_computation.5 | convolution fusion | flops 3222274048 | bytes 5242884 | tf_op jit(solution)/shard_map/vmap()/dot_general | solution.py:537
  804.5 3.5 bitcast_add_fusion.3
  812.5 3.7 bitcast_add_fusion.2
  820.7 3.5 bitcast_add_fusion.1
  824.2 3.7 fusion.10
  829.0 3.5 bitcast_add_fusion
  832.5 3.5 fusion.6
  837.0 3.9 fusion.43
  841.8 11.4 %multiply_reduce_fusion.1 = f32[]{:T(128)} fusion(f32[1,512,2048]{2,0,1:T(1,128)} %all-gather.10.cloned.1.call-done), kind=kLoop, calls=%fused_computation.53 | loop fusion | flops 2097151 | bytes 4194308 | tf_op jit(solution)/shard_map/vmap()/reduce_sum | solution.py:535
  854.0 10.9 %copy.161 = f32[1,512,2048]{1,2,0:T(8,128)} copy(f32[1,512,2048]{2,0,1:T(1,128)} %all-gather.10.cloned.1.call-done) | data formatting | bytes 8388608 | tf_op jit(solution)/shard_map/all_gather | solution.py:712
  864.9 10.8 %fusion.38 = f32[512,512]{1,0:T(8,128)S(1)} fusion(f32[1,512,2048]{1,2,0:T(8,128)} %copy.161, f32[]{:T(128)S(6)} %add.308), kind=kOutput, calls=%fused_computation.50 | convolution fusion | flops 3222274048 | bytes 5242884 | tf_op jit(solution)/shard_map/vmap()/dot_general | solution.py:537
  876.7 3.5 bitcast_add_fusion.7
  884.8 3.7 bitcast_add_fusion.6
  888.5 3.5 fusion.30
  893.0 3.5 bitcast_add_fusion.5
  896.6 3.9 fusion.26
  901.5 3.5 bitcast_add_fusion.4
  909.5 3.7 fusion.40
  914.8 4.2 fusion.153
  921.0 11.9 %all-gather.1 = bf16[8,64,512]{2,1,0:T(8,128)(2,1)S(1)} all-gather(bf16[2,64,512]{2,1,0:T(8,128)(2,1)S(1)} %fusion.121), channel_id=3, replica_groups=mesh['seg'=8,'dp'=4] {'dp'}, dimensions={0}, use_global_device_ids=true | all-gather | bytes 655360 | tf_op jit(solution)/shard_map/all_gather | solution.py:719
  937.1 4.7 all-gather.16.cloned.1.call-done
  (207 shorter events, 120.2 us)
Async XLA Ops:
  7.2 27.7 %copy-start = (bf16[80,512]{1,0:T(8,128)(2,1)S(1)}, bf16[80,512]{1,0:T(8,128)(2,1)}, u32[]{:S(2)}) copy-start(bf16[80,512]{1,0:T(8,128)(2,1)} %param.47) | copy-start | bytes 245764
  7.2 308.3 %all-reduce.13.cloned.1.call-start = ((), (), s32[]{:S(2)}) async-start(), calls=%async_computation.10 | async-start | bytes 8388608
  7.3 30.0 %collective-permute-start = (bf16[2,512,80]{1,2,0:T(8,128)(2,1)}, bf16[2,512,80]{1,2,0:T(8,128)(2,1)S(1)}, u32[]{:S(2)}, u32[]{:S(2)}) collective-permute-start(bf16[2,512,80]{1,2,0:T(8,128)(2,1)} %param.26), channel_id=1, source_target_pairs={{0,4},{4,8},{8,12},{12,16},{16,20},{20,24},{24,28},{1,5},{5,9},{9,... | collective-permute-start | bytes 491528 | tf_op jit(solution)/shard_map/ppermute | solution.py:511
  11.1 4.6 copy-start.6
  15.7 3.7 copy-start.7
  19.4 2.3 copy-start.34
  19.4 2.4 copy-start.24
  19.4 13.8 %copy-start.39 = (s32[2,512]{1,0:T(2,128)S(1)}, s32[2,512]{1,0:T(2,128)}, u32[]{:S(2)}) copy-start(s32[2,512]{1,0:T(2,128)} %param.28) | copy-start | bytes 12292
  19.4 15.4 %copy-start.15 = (bf16[2,512,80]{1,2,0:T(8,128)(2,1)S(1)}, bf16[2,512,80]{1,2,0:T(8,128)(2,1)}, u32[]{:S(2)}) copy-start(bf16[2,512,80]{1,2,0:T(8,128)(2,1)} %param.26) | copy-start | bytes 491524
  37.7 19.0 %copy-start.5 = (bf16[2,512,512]{2,1,0:T(8,128)(2,1)}, bf16[2,512,512]{2,1,0:T(8,128)(2,1)S(1)}, u32[]{:S(2)}) copy-start(bf16[2,512,512]{2,1,0:T(8,128)(2,1)S(1)} %add_convert_fusion.mem_ref) | copy-start | bytes 3145732
  56.7 23.6 %collective-permute-start.2 = (bf16[512,512]{1,0:T(8,128)(2,1)}, bf16[512,512]{1,0:T(8,128)(2,1)S(1)}, u32[]{:S(2)}, u32[]{:S(2)}) collective-permute-start(bf16[512,512]{1,0:T(8,128)(2,1)} %get-tuple-element.87), channel_id=1, source_target_pairs={{0,4},{4,8},{8,12},{12,16},{16,20},{20,24},{24,28},{1,5},{5,9},{9,... | collective-permute-start | bytes 1572872 | tf_op jit(solution)/shard_map/ppermute | solution.py:511
  76.1 23.3 %collective-permute-start.1 = (bf16[512,512]{1,0:T(8,128)(2,1)}, bf16[512,512]{1,0:T(8,128)(2,1)S(1)}, u32[]{:S(2)}, u32[]{:S(2)}) collective-permute-start(bf16[512,512]{1,0:T(8,128)(2,1)} %get-tuple-element.86), channel_id=1, source_target_pairs={{0,4},{4,8},{8,12},{12,16},{16,20},{20,24},{24,28},{1,5},{5,9},{9,... | collective-permute-start | bytes 1572872 | tf_op jit(solution)/shard_map/ppermute | solution.py:511
  128.9 22.8 %copy-start.21 = (bf16[512,512]{1,0:T(8,128)(2,1)S(1)}, bf16[512,512]{1,0:T(8,128)(2,1)}, u32[]{:S(2)}) copy-start(bf16[512,512]{1,0:T(8,128)(2,1)} %copy-done.20) | copy-start | bytes 1572868
  129.0 22.8 %copy-start.23 = (bf16[512,512]{1,0:T(8,128)(2,1)S(1)}, bf16[512,512]{1,0:T(8,128)(2,1)}, u32[]{:S(2)}) copy-start(bf16[512,512]{1,0:T(8,128)(2,1)} %copy-done.22) | copy-start | bytes 1572868
  188.7 23.6 %copy-start.13 = (bf16[512,2048]{1,0:T(8,128)(2,1)S(1)}, bf16[512,2048]{1,0:T(8,128)(2,1)}, u32[]{:S(2)}) copy-start(bf16[512,2048]{1,0:T(8,128)(2,1)} %get-tuple-element.119) | copy-start | bytes 6291460
  220.6 236.0 %all-reduce.15.cloned.1.call-start = ((), (), s32[]{:S(2)}) async-start(), calls=%async_computation.11 | async-start | bytes 4521984 | tf_op jit(solution)/shard_map/psum | solution.py:656
  256.7 2.9 copy-start.3
  260.7 252.3 %all-reduce.11.cloned.1.call-start = ((), (), s32[]{:S(2)}) async-start(), calls=%async_computation.3 | async-start | bytes 2097152 | tf_op jit(solution)/shard_map/psum | solution.py:676
  318.1 247.1 %reduce-scatter.5.cloned.1.call-start = ((), (), s32[]{:S(2)}) async-start(), calls=%async_computation.4 | async-start | bytes 4718592 | tf_op jit(solution)/shard_map/reduce_scatter | solution.py:672
  322.8 292.9 %reduce-scatter.3.cloned.1.call-start = ((), (), s32[]{:S(2)}) async-start(), calls=%async_computation.2 | async-start | bytes 4718592 | tf_op jit(solution)/shard_map/reduce_scatter | solution.py:666
  327.5 411.7 %all-gather.14.cloned.1.call-start = ((), (), s32[]{:S(2)}) async-start(), calls=%async_computation.7 | async-start | bytes 2359296 | tf_op jit(solution)/shard_map/all_gather | solution.py:711
  327.6 1.7 copy-start.35
  327.6 1.7 copy-start.40
  712.7 2.6 copy-start.11
  712.8 75.3 %all-gather.12.cloned.1.call-start = ((), (), s32[]{:S(2)}) async-start(), calls=%async_computation.6 | async-start | bytes 4718592 | tf_op jit(solution)/shard_map/all_gather | solution.py:713
  714.3 3.4 copy-start.10
  715.3 126.6 %all-gather.10.cloned.1.call-start = ((), (), s32[]{:S(2)}) async-start(), calls=%async_computation.5 | async-start | bytes 4718592 | tf_op jit(solution)/shard_map/all_gather | solution.py:712
  715.3 4.0 copy-start.25
  715.4 4.0 copy-start.29
  715.4 4.0 copy-start.30
  717.8 5.5 copy-start.31
  717.8 5.5 copy-start.32
  717.8 5.5 copy-start.33
  717.8 6.1 copy-start.4
  722.8 211.5 %all-gather.18.cloned.1.call-start = ((), (), s32[]{:S(2)}) async-start(), calls=%async_computation.9 | async-start | bytes 1310720 | tf_op jit(solution)/shard_map/all_gather | solution.py:721
  723.9 7.9 copy-start.19
  723.9 7.9 copy-start.26
  723.9 7.9 copy-start.27
  723.9 7.9 copy-start.28
  739.2 2.2 copy-start.12
  792.7 11.8 %copy-start.8 = (f32[1,2048,512]{2,1,0:T(8,128)S(1)}, f32[1,2048,512]{2,1,0:T(8,128)}, u32[]{:S(2)}) copy-start(f32[1,2048,512]{2,1,0:T(8,128)} %all-gather.12.cloned.1.call-done) | copy-start | bytes 12582916
  841.8 100.0 %all-gather.16.cloned.1.call-start = ((), (), s32[]{:S(2)}) async-start(), calls=%async_computation.8 | async-start | bytes 1310720 | tf_op jit(solution)/shard_map/all_gather | solution.py:720
  864.9 11.8 %copy-start.9 = (f32[1,512,2048]{1,2,0:T(8,128)S(1)}, f32[1,512,2048]{1,2,0:T(8,128)}, u32[]{:S(2)}) copy-start(f32[1,512,2048]{1,2,0:T(8,128)} %copy.161) | copy-start | bytes 12582916
  914.8 4.2 copy-start.2
  920.9 12.1 %copy-start.16 = (f32[2,4,64,512]{3,2,1,0:T(8,128)S(1)}, f32[2,4,64,512]{3,2,1,0:T(8,128)}, u32[]{:S(2)}) copy-start(f32[2,4,64,512]{3,2,1,0:T(8,128)} %param.41) | copy-start | bytes 3145732
  932.9 1.7 copy-start.17
  934.3 7.4 copy-start.18
  934.7 9.5 copy-start.1
  (7 other events, 8.8 us)
Sparse Core Ops, SparseCore 0:
  220.7 94.7 all-reduce.12
  321.8 134.7 all-reduce.14
  460.5 52.3 all-reduce.10
  515.2 49.9 reduce-scatter.4
  567.5 48.1 reduce-scatter.2
  712.9 26.2 all-gather.13
  741.4 46.6 all-gather.11
  790.3 45.8 all-gather.9
  841.9 25.3 all-gather.17
  914.9 26.8 all-gather.15

commit v2 on v1

--- a/solution.py
+++ b/solution.py
@@ -309,7 +309,8 @@
 
     @pl.when(step == pl.num_programs(0) - 1)
     def _():
-        dup_ref[...] = up_s[...].astype(bf16)
+        for tile in range(FF // TILE):
+            dup_ref[tile] = up_s[:, tile * TILE : (tile + 1) * TILE].astype(bf16)
         ddown_ref[...] = jnp.transpose(down_s[...].astype(bf16))
 
 
@@ -320,7 +321,7 @@
         grid=(streams,),
         out_shape=[
             jax.ShapeDtypeStruct((streams, SEG, D), f32),
-            jax.ShapeDtypeStruct((D, FF), bf16),
+            jax.ShapeDtypeStruct((FF // TILE, D, TILE), bf16),
             jax.ShapeDtypeStruct((FF, D), bf16),
             jax.ShapeDtypeStruct((8, D), f32),
         ],
@@ -331,7 +332,12 @@
             whole_spec(lower.shape),
             whole_spec(vectors.shape),
         ],
-        out_specs=[stream_spec((SEG, D)), whole_spec((D, FF)), whole_spec((FF, D)), whole_spec((8, D))],
+        out_specs=[
+            stream_spec((SEG, D)),
+            whole_spec((FF // TILE, D, TILE)),
+            whole_spec((FF, D)),
+            whole_spec((8, D)),
+        ],
         scratch_shapes=[
             pltpu.VMEM((D, FF), f32),
             pltpu.VMEM((D, FF), f32),
@@ -502,21 +508,10 @@
     )(bias, dafter, x, memory, keyin, q, k, v, lse, mixed, attn, vectors)
 
 
-HIGH = lax.Precision.HIGH
-
-
 def from_behind(value, axis, steps):
     count = lax.axis_size(axis)
     leading, last = (max(0, -steps), min(count, count - steps))
     return lax.ppermute(value, axis, [(source, source + steps) for source in range(leading, last)])
-
-
-def shortened(value):
-
-    def short(part):
-        return part.astype(jnp.bfloat16) if part.dtype == jnp.float32 else part
-
-    return jax.tree.map(short, value)
 
 
 def adamw(weight, moment, second, grad, rate, decay):
@@ -528,42 +523,583 @@
     return (weight, moment, second)
 
 
-def orthogonal(matrix):
-    flipped = matrix.shape[0] > matrix.shape[1]
-    if flipped:
-        matrix = matrix.T
-    matrix = matrix / (jnp.sqrt(jnp.sum(matrix * matrix)) + 1e-07)
-    for sweep in range(5):
-        gram_matrix = jnp.matmul(matrix, matrix.T, precision=HIGH)
-        poly_term = -4.775 * gram_matrix + 2.0315 * jnp.matmul(
-            gram_matrix, gram_matrix, precision=HIGH
+GROUPS = 4
+UNITS = 6
+SMALL = 112
+
+
+def peers():
+    count = {"seg": lax.axis_size("seg"), "dp": lax.axis_size("dp")}
+    seg, dp = lax.axis_index("seg"), lax.axis_index("dp")
+    core, x, y = seg % 2, dp % 2, (dp // 2) % 2
+    across_core = {"seg": seg + 1 - 2 * core}
+    across_x = {"dp": dp + 1 - 2 * x}
+    across_y = {"dp": dp + 2 - 4 * y}
+    across_both = {"dp": dp + 3 - 2 * x - 4 * y}
+    far = []
+    step = GROUPS
+    while step < count["dp"]:
+        far.append({"dp": dp + step - 2 * step * ((dp // step) % 2)})
+        step *= 2
+    return seg, dp, core, x, y, across_core, (across_x, across_y, across_both), far
+
+
+def others(seg, count):
+    return [lax.rem(seg + step, count) for step in range(1, count)]
+
+
+def greet(seg, count, near, far):
+    barrier = pltpu.get_barrier_semaphore()
+    targets = [{"seg": other} for other in others(seg, count)] + list(near) + list(far)
+    for target in targets:
+        pl.semaphore_signal(barrier, inc=1, device_id=target, device_id_type=pl.DeviceIdType.MESH)
+    pl.semaphore_wait(barrier, len(targets))
+
+
+def remote(source, target, send, recv, device):
+    return pltpu.make_async_remote_copy(
+        src_ref=source,
+        dst_ref=target,
+        send_sem=send,
+        recv_sem=recv,
+        device_id=device,
+        device_id_type=pl.DeviceIdType.MESH,
+    )
+
+
+def wait_bytes(ref, sem):
+    pltpu.make_async_copy(ref, ref, sem).wait()
+
+
+def plus(left, right):
+    return (left.astype(f32) + right.astype(f32)).astype(bf16)
+
+
+def owners(count):
+    attn, feed = count // 4 - 1, count // 4
+    return (
+        (0, 1, 2 * attn, 0),
+        (1, 1, 2 * attn + 1, 0),
+        (2, 2, 2 * feed, 0),
+        (4, 2, 2 * feed + 1, 2),
+    )
+
+
+def reduce_kernel(
+    count,
+    attn0,
+    attn1,
+    up0,
+    up1,
+    down0,
+    down1,
+    small_ref,
+    whole_ref,
+    every_ref,
+    small_out,
+    square_out,
+    mine,
+    got0,
+    got1,
+    got2,
+    got3,
+    goth,
+    small_core,
+    small_s,
+    small_got,
+    sq_seg,
+    sq_dp,
+    load_sem,
+    send0,
+    recv0,
+    send1,
+    recv1,
+    send2,
+    recv2,
+    send3,
+    recv3,
+    sendh,
+    recvh,
+    small_send,
+    small_recv,
+    every_send,
+    every_recv,
+    whole_send,
+    whole_recv,
+    half_sem,
+    sq_send,
+    sq_recv,
+    sqd_send,
+    sqd_recv,
+):
+    seg, dp, core, x, y, across_core, near, far = peers()
+    across_x, across_y, across_both = near
+    planes = count // 2
+    plane = seg // 2
+    group = 2 * y + x
+
+    def pieces(row):
+        return (
+            (attn0.at[:, :, row], (slice(None), slice(None), 0)),
+            (attn1.at[:, :, row], (slice(None), slice(None), 1)),
+            (up0.at[:, row], (0, 0, slice(2, 6))),
+            (up1.at[:, row], (0, 1, slice(2, 6))),
+            (down0.at[row], (1, 0, slice(2, 6))),
+            (down1.at[row], (1, 1, slice(2, 6))),
         )
-        matrix = 3.4445 * matrix + jnp.matmul(poly_term, matrix, precision=HIGH)
-    return matrix.T if flipped else matrix
-
-
-def owner_layout(stack, offset, owner_count):
-    total_count = stack.shape[0]
-    slot_count = -(-total_count // owner_count)
-    filler = jnp.zeros((slot_count * owner_count - total_count,) + stack.shape[1:], stack.dtype)
-    rolled = jnp.roll(jnp.concatenate([stack, filler], 0), offset, 0)
-    return rolled.reshape((slot_count, owner_count) + stack.shape[1:])
-
-
-def to_owner(stack, offset, owner_count, owner):
-    return lax.dynamic_index_in_dim(
-        owner_layout(stack, offset, owner_count), owner, 1, keepdims=False
-    )
-
-
-def from_owner(gathered, offset, total_count):
-    owner_count, slot_count = (gathered.shape[0], gathered.shape[1])
-    flat = jnp.swapaxes(gathered, 0, 1).reshape((slot_count * owner_count,) + gathered.shape[2:])
-    return jnp.roll(flat, -offset, 0)[:total_count]
-
-
-def own_rows(whole, row_count):
-    return lax.dynamic_slice_in_dim(whole, lax.axis_index("seg") * row_count, row_count, 1)
+
+    order = [lax.rem(plane + 1 + step, planes) for step in range(planes)]
+    for step in range(planes):
+        for source, place in pieces(2 * order[step] + core):
+            pltpu.make_async_copy(source, mine.at[(step,) + place], load_sem.at[step]).start()
+    greet(seg, count, near, far)
+    for step in range(planes):
+        for source, place in pieces(2 * order[step] + 1 - core):
+            remote(source, got0.at[(step,) + place], send0.at[step], recv0.at[step], across_core).start()
+
+    def small_steps():
+        copy = remote(small_ref, small_core, small_send.at[0], small_recv.at[0], across_core)
+        copy.start()
+        yield
+        copy.wait()
+        small_s[...] = small_ref[...] + small_core[...]
+        half = pl.ds(pl.multiple_of(core * (SMALL // 2), 8), SMALL // 2)
+        targets = [across_x, across_y] + far
+        step = 1
+        while step < planes:
+            targets.append({"seg": seg + 2 * step - 4 * step * ((plane // step) % 2)})
+            step *= 2
+        for place, target in enumerate(targets):
+            copy = remote(
+                small_s.at[half],
+                small_got.at[place],
+                small_send.at[place + 1],
+                small_recv.at[place + 1],
+                target,
+            )
+            copy.start()
+            yield
+            copy.wait()
+            small_s[half, :] += small_got[place]
+        small_out[half, :] = small_s[half, :]
+        last = len(targets) + 1
+        copy = remote(small_out.at[half], small_out.at[half], small_send.at[last], small_recv.at[last], across_core)
+        copy.start()
+        yield
+        copy.wait()
+
+    small_run = small_steps()
+    next(small_run)
+
+    def first_of(step):
+        return (
+            remote(mine.at[step, :, 1 - x, 0:3], got1.at[step, 0], send1.at[step, 0], recv1.at[step, 0], across_x),
+            remote(mine.at[step, 1 - y, :, 3:6], got1.at[step, 1], send1.at[step, 1], recv1.at[step, 1], across_y),
+        )
+
+    def second_of(step):
+        return (
+            remote(mine.at[step, 1 - y, x, 0:3], got2.at[step, 0], send2.at[step, 0], recv2.at[step, 0], across_y),
+            remote(mine.at[step, y, 1 - x, 3:6], got2.at[step, 1], send2.at[step, 1], recv2.at[step, 1], across_x),
+        )
+
+    def third_of(step):
+        return remote(
+            mine.at[step, y, x],
+            got3.at[plane],
+            send3.at[step],
+            recv3.at[plane],
+            {"seg": 2 * order[step] + core},
+        )
+
+    def begin(step):
+        wait_bytes(mine.at[step], load_sem.at[step])
+        wait_bytes(got0.at[step], recv0.at[step])
+
+        def body(place, carry):
+            mine[step, place // 2, place % 2] = plus(mine[step, place // 2, place % 2], got0[step, place // 2, place % 2])
+            return carry
+
+        lax.fori_loop(0, GROUPS, body, 0)
+        for copy in first_of(step):
+            copy.start()
+
+    def middle(step):
+        for copy in first_of(step):
+            copy.wait_recv()
+        for place in range(2):
+            mine[step, place, x, 0:3] = plus(mine[step, place, x, 0:3], got1[step, 0, place])
+            mine[step, y, place, 3:6] = plus(mine[step, y, place, 3:6], got1[step, 1, place])
+        for copy in second_of(step):
+            copy.start()
+
+    def end(step):
+        for copy in second_of(step):
+            copy.wait_recv()
+        mine[step, y, x, 0:3] = plus(mine[step, y, x, 0:3], got2[step, 0])
+        mine[step, y, x, 3:6] = plus(mine[step, y, x, 3:6], got2[step, 1])
+        for place, target in enumerate(far):
+            copy = remote(
+                mine.at[step, y, x], goth.at[place, step], sendh.at[place, step], recvh.at[place, step], target
+            )
+            copy.start()
+            copy.wait()
+            mine[step, y, x] = plus(mine[step, y, x], goth[place, step])
+        if step < planes - 1:
+            third_of(step).start()
+
+    for step in range(planes + 2):
+        if step < planes:
+            begin(step)
+        if 1 <= step <= planes:
+            middle(step - 1)
+        if step >= 2:
+            end(step - 2)
+        next(small_run, None)
+    for _ in small_run:
+        pass
+
+    total = mine[planes - 1, y, x].astype(f32)
+    for step in range(1, planes):
+        sender = lax.rem(plane + step, planes)
+        wait_bytes(got3.at[sender], recv3.at[sender])
+        total = total + got3[sender].astype(f32)
+    every_ref[group] = total.astype(bf16)
+    square = jnp.sum(jnp.sum(jnp.sum(total * total, 0), 0, keepdims=True), 1, keepdims=True)
+    sq_seg[seg] = jnp.broadcast_to(square, (8, 128))
+
+    roles = owners(count)
+
+    def gift(place):
+        first, width, owner, spot = roles[place]
+        return remote(
+            every_ref.at[group, first : first + width],
+            whole_ref.at[seg, spot : spot + width],
+            whole_send.at[place],
+            whole_recv.at[seg],
+            {"seg": owner},
+        )
+
+    for place, (first, width, owner, spot) in enumerate(roles):
+
+        @pl.when(seg != owner)
+        def _():
+            gift(place).start()
+
+        @pl.when(seg == owner)
+        def _():
+            whole_ref[seg, spot : spot + width] = every_ref[group, first : first + width]
+
+    for step, other in enumerate(others(seg, count)):
+        remote(sq_seg.at[seg], sq_seg.at[seg], sq_send.at[step], sq_recv.at[seg], {"seg": other}).start()
+    for place, target in enumerate(near):
+        remote(
+            every_ref.at[group], every_ref.at[group], every_send.at[place], every_recv.at[place], target
+        ).start()
+    for other in others(seg, count):
+        wait_bytes(sq_seg.at[other], sq_recv.at[other])
+    sq_dp[group] = jnp.sum(sq_seg[...], 0)
+    for place, target in enumerate(near):
+        remote(sq_dp.at[group], sq_dp.at[group], sqd_send.at[place], sqd_recv.at[place], target).start()
+    for place, target in enumerate(near):
+        remote(sq_dp.at[group], sq_dp.at[group], sqd_send.at[place], sqd_recv.at[place], target).wait()
+    square_out[...] = jnp.sum(sq_dp[...], 0)
+
+    for place, (first, width, owner, spot) in enumerate(roles):
+
+        @pl.when(seg == owner)
+        def _():
+            for other in others(seg, count):
+                wait_bytes(whole_ref.at[other, spot : spot + width], whole_recv.at[other])
+            if width == 2:
+                span = slice(spot, spot + width)
+                copy = remote(
+                    whole_ref.at[:, span], whole_ref.at[:, span], half_sem.at[0], half_sem.at[1], across_core
+                )
+                copy.start()
+                copy.wait()
+
+    for step in range(planes):
+        wait_bytes(mine.at[step], send0.at[step])
+        for copy in first_of(step) + second_of(step):
+            copy.wait_send()
+        if step < planes - 1:
+            third_of(step).wait_send()
+    for place, (first, width, owner, spot) in enumerate(roles):
+
+        @pl.when(seg != owner)
+        def _():
+            gift(place).wait_send()
+
+    for step in range(count - 1):
+        wait_bytes(sq_seg.at[0], sq_send.at[step])
+    for place, target in enumerate(near):
+        remote(
+            every_ref.at[group], every_ref.at[group], every_send.at[place], every_recv.at[place], target
+        ).wait()
+
+
+def reduce_grads(count, dp_count, attn, up, down, small):
+    rows = D // count
+    planes = count // 2
+    far = max(1, dp_count.bit_length() - 3)
+    shape = (UNITS, rows, D)
+    attn = [grad.reshape(2, 2, count, rows, D) for grad in attn]
+    up = [grad.reshape(4, count, rows, D) for grad in up]
+    down = [grad.reshape(count, 4, rows, D) for grad in down]
+    stages = 2 + planes.bit_length() + max(0, dp_count.bit_length() - 3)
+    dma = pltpu.SemaphoreType.DMA
+    return pl.pallas_call(
+        functools.partial(reduce_kernel, count),
+        out_shape=[
+            jax.ShapeDtypeStruct((count, 4, rows, D), bf16),
+            jax.ShapeDtypeStruct((GROUPS,) + shape, bf16),
+            jax.ShapeDtypeStruct((SMALL, D), f32),
+            jax.ShapeDtypeStruct((8, 128), f32),
+        ],
+        in_specs=[pl.BlockSpec(memory_space=pl.ANY)] * 6 + [pl.BlockSpec(memory_space=pltpu.VMEM)],
+        out_specs=[pl.BlockSpec(memory_space=pltpu.VMEM)] * 4,
+        scratch_shapes=[
+            pltpu.VMEM((planes, 2, 2) + shape, bf16),
+            pltpu.VMEM((planes, 2, 2) + shape, bf16),
+            pltpu.VMEM((planes, 2, 2, 3, rows, D), bf16),
+            pltpu.VMEM((planes, 2, 3, rows, D), bf16),
+            pltpu.VMEM((planes,) + shape, bf16),
+            pltpu.VMEM((far, planes) + shape, bf16),
+            pltpu.VMEM((SMALL, D), f32),
+            pltpu.VMEM((SMALL, D), f32),
+            pltpu.VMEM((stages, SMALL // 2, D), f32),
+            pltpu.VMEM((count, 8, 128), f32),
+            pltpu.VMEM((GROUPS, 8, 128), f32),
+            dma((planes,)),
+            dma((planes,)),
+            dma((planes,)),
+            dma((planes, 2)),
+            dma((planes, 2)),
+            dma((planes, 2)),
+            dma((planes, 2)),
+            dma((planes,)),
+            dma((planes,)),
+            dma((far, planes)),
+            dma((far, planes)),
+            dma((stages + 2,)),
+            dma((stages + 2,)),
+            dma((3,)),
+            dma((3,)),
+            dma((4,)),
+            dma((count,)),
+            dma((2,)),
+            dma((count,)),
+            dma((count,)),
+            dma((3,)),
+            dma((3,)),
+        ],
+        compiler_params=pltpu.CompilerParams(
+            collective_id=1, has_side_effects=True, vmem_limit_bytes=VMEM_LIMIT
+        ),
+        cost_estimate=pl.CostEstimate(flops=10**8, bytes_accessed=2 * 10**8, transcendentals=0),
+        name="reduce_grads",
+    )(*attn, *up, *down, small)
+
+
+def halves(value):
+    high = value.astype(bf16)
+    return high, (value - high.astype(f32)).astype(bf16)
+
+
+def times(left, right):
+    (left_high, left_low), (right_high, right_low) = left, right
+    return dot_nn(
+        jnp.concatenate([left_high, left_high, left_low], 1),
+        jnp.concatenate([right_high, right_low, right_high], 0),
+    )
+
+
+def times_t(left, right):
+    (left_high, left_low), (right_high, right_low) = left, right
+    return dot_nt(
+        jnp.concatenate([left_high, left_high, left_low], 1),
+        jnp.concatenate([right_high, right_low, right_high], 1),
+    )
+
+
+def muon_kernel(role_ref, clip_ref, whole_ref, mom_ref, out_ref, x_s, q_s, gram_s, high_s, low_s):
+    count, rows = whole_ref.shape[0], whole_ref.shape[2]
+    core = role_ref[1]
+    clip = clip_ref[0]
+    eye = (
+        lax.broadcasted_iota(jnp.int32, (D, D), 0) == lax.broadcasted_iota(jnp.int32, (D, D), 1)
+    ).astype(f32)
+
+    @pl.when(role_ref[0] == 1)
+    def _():
+        start = 0.5 * mom_ref[:, core] + clip * whole_ref[:, 0].astype(f32)
+        start = start.reshape(D, D)
+        size = jnp.sum(jnp.sum(start * start, 0, keepdims=True), 1, keepdims=True)
+        x_s[...] = start / (jnp.sqrt(size) + 1e-07)
+
+        def sweep(_, carry):
+            value = x_s[...]
+            both = halves(value)
+            gram = times_t(both, both)
+            gram_both = halves(gram)
+            poly = -4.775 * gram + 2.0315 * times(gram_both, gram_both)
+            x_s[...] = 3.4445 * value + times(halves(poly), both)
+            return carry
+
+        lax.fori_loop(0, 5, sweep, 0)
+        out_ref[:, 0] = x_s[...].astype(bf16).reshape(count, rows, D)
+
+    @pl.when(role_ref[0] == 2)
+    def _():
+        gram_s[...] = jnp.zeros_like(gram_s)
+
+        def gather(tile, size):
+            value = 0.5 * mom_ref[:, 2 + tile] + clip * whole_ref[:, tile].astype(f32)
+            value = value.reshape(D, D)
+            high, low = halves(value)
+            high_s[tile] = high
+            low_s[tile] = low
+
+            @pl.when(role_ref[2] == 1)
+            def _():
+                high_s[tile] = jnp.transpose(high_s[tile])
+                low_s[tile] = jnp.transpose(low_s[tile])
+
+            both = high_s[tile], low_s[tile]
+            gram_s[...] += times_t(both, both)
+            return size + jnp.sum(jnp.sum(value * value, 0, keepdims=True), 1, keepdims=True)
+
+        size = lax.fori_loop(0, 4, gather, jnp.zeros((1, 1), f32))
+        scale = 1.0 / (jnp.sqrt(size) + 1e-07)
+        gram_s[...] = gram_s[...] * (scale * scale)
+
+        def poly_of(gram, gram_both):
+            return 3.4445 * eye - 4.775 * gram + 2.0315 * times(gram_both, gram_both)
+
+        def advance(gram_both, poly_both):
+            gram_s[...] = times(halves(times(gram_both, poly_both)), poly_both)
+
+        gram = gram_s[...]
+        gram_both = halves(gram)
+        poly = poly_of(gram, gram_both)
+        q_s[...] = poly
+        advance(gram_both, halves(poly))
+
+        def sweep(_, carry):
+            gram = gram_s[...]
+            gram_both = halves(gram)
+            poly_both = halves(poly_of(gram, gram_both))
+            q_s[...] = times(halves(q_s[...]), poly_both)
+            advance(gram_both, poly_both)
+            return carry
+
+        lax.fori_loop(0, 3, sweep, 0)
+        gram = gram_s[...]
+        last = times(halves(q_s[...]), halves(poly_of(gram, halves(gram)))) * scale
+        last_both = halves(last)
+
+        def finish(step, carry):
+            tile = 2 * core + step
+            x_s[...] = times(last_both, (high_s[tile], low_s[tile]))
+
+            @pl.when(role_ref[2] == 1)
+            def _():
+                x_s[...] = jnp.transpose(x_s[...])
+
+            out_ref[:, step] = x_s[...].astype(bf16).reshape(count, rows, D)
+            return carry
+
+        lax.fori_loop(0, 2, finish, 0)
+
+
+def muon(role, clip, whole, momenta):
+    count, _, rows, _ = whole.shape
+    return pl.pallas_call(
+        muon_kernel,
+        out_shape=jax.ShapeDtypeStruct((count, 2, rows, D), bf16),
+        in_specs=[
+            pl.BlockSpec(memory_space=pltpu.SMEM),
+            pl.BlockSpec(memory_space=pltpu.SMEM),
+            pl.BlockSpec(memory_space=pltpu.VMEM),
+            pl.BlockSpec(memory_space=pltpu.VMEM),
+        ],
+        out_specs=pl.BlockSpec(memory_space=pltpu.VMEM),
+        scratch_shapes=[
+            pltpu.VMEM((D, D), f32),
+            pltpu.VMEM((D, D), f32),
+            pltpu.VMEM((D, D), f32),
+            pltpu.VMEM((4, D, D), bf16),
+            pltpu.VMEM((4, D, D), bf16),
+        ],
+        compiler_params=pltpu.CompilerParams(vmem_limit_bytes=VMEM_LIMIT),
+        cost_estimate=pl.CostEstimate(flops=2 * 10**10, bytes_accessed=10**7, transcendentals=0),
+        name="muon",
+    )(role, clip, whole, momenta)
+
+
+def spread_kernel(count, made_ref, every_ref, send, recv, on_send, on_recv):
+    seg, dp, core, x, y, across_core, near, far = peers()
+    group = 2 * y + x
+    greet(seg, count, near, ())
+    roles = owners(count)
+
+    def gift(place, other):
+        first, width, owner, spot = roles[place]
+        return remote(
+            made_ref.at[other, 0:width],
+            every_ref.at[group, first : first + width],
+            send.at[other],
+            recv.at[place],
+            {"seg": other},
+        )
+
+    def onward(place, side):
+        first, width, owner, spot = roles[place]
+        block = every_ref.at[group, first : first + width]
+        return remote(block, block, on_send.at[side, place], on_recv.at[side, place], near[side])
+
+    for place, (first, width, owner, spot) in enumerate(roles):
+
+        @pl.when(seg == owner)
+        def _():
+            for other in others(seg, count):
+                gift(place, other).start()
+            every_ref[group, first : first + width] = made_ref[seg, 0:width]
+
+    for place, (first, width, owner, spot) in enumerate(roles):
+
+        @pl.when(seg != owner)
+        def _():
+            wait_bytes(every_ref.at[group, first : first + width], recv.at[place])
+
+        for side in range(3):
+            onward(place, side).start()
+    for place, (first, width, owner, spot) in enumerate(roles):
+        for side in range(3):
+            onward(place, side).wait()
+
+        @pl.when(seg == owner)
+        def _():
+            for other in others(seg, count):
+                gift(place, other).wait_send()
+
+
+def spread(count, made):
+    rows = made.shape[2]
+    dma = pltpu.SemaphoreType.DMA
+    return pl.pallas_call(
+        functools.partial(spread_kernel, count),
+        out_shape=jax.ShapeDtypeStruct((GROUPS, UNITS, rows, D), bf16),
+        in_specs=[pl.BlockSpec(memory_space=pltpu.VMEM)],
+        out_specs=pl.BlockSpec(memory_space=pltpu.VMEM),
+        scratch_shapes=[dma((count,)), dma((4,)), dma((3, 4)), dma((3, 4))],
+        compiler_params=pltpu.CompilerParams(
+            collective_id=2, has_side_effects=True, vmem_limit_bytes=VMEM_LIMIT
+        ),
+        cost_estimate=pl.CostEstimate(flops=10**6, bytes_accessed=4 * 10**7, transcendentals=0),
+        name="spread",
+    )(made)
 
 
 def local(
@@ -598,6 +1134,23 @@
     stream_total = frames.shape[0] * lax.axis_size("dp")
     streams = frames.shape[0]
     behind = from_behind(frames, "seg", 1)
+    group = lax.axis_index("dp") % GROUPS
+    block = D // lax.axis_size("seg")
+    feeds = jnp.concatenate(
+        [
+            jnp.swapaxes(up_momentum.reshape(LAYERS, block, 4, D), 1, 2),
+            down_momentum.reshape(LAYERS, 4, block, D),
+        ],
+        0,
+    )
+    owned = jnp.concatenate(
+        [
+            lax.dynamic_index_in_dim(attn_momentum, group, 1, keepdims=False),
+            lax.dynamic_index_in_dim(feeds, group, 0, keepdims=False),
+        ],
+        0,
+    )
+    momenta = lax.all_gather(owned, "seg", axis=0, tiled=False)
     local_counts = jnp.sum(speech_mask, 1)
     counts = lax.psum(local_counts, "seg")
     weighting = speech_mask.astype(f32) / counts.astype(f32)[:, None]
@@ -653,39 +1206,46 @@
     grad_in = dot_tn(frame_rows, rows_high) + dot_tn(frame_rows, rows_rest)
     grad_outer = jnp.concatenate([jnp.sum(rows, 0, keepdims=True), head_outer[1:5]], 0)
     grad_vectors = jnp.stack(vector_grads)
-    grad_in, grad_out, grad_vectors, grad_outer, loss_sum = lax.psum(
-        (grad_in, grad_out, grad_vectors, grad_outer, loss_here), ("seg", "dp")
-    )
-    attn_local = jnp.stack(attn_grads).reshape(4 * LAYERS, D, D)
-    up_local = jnp.stack(up_grads)
-    down_local = jnp.stack(down_grads)
-    offsets = (0, 4 * LAYERS, 5 * LAYERS)
-    owner = lax.axis_index("dp")
-    owner_count = lax.axis_size("dp")
-    attn_sum, up_sum, down_sum = (
-        lax.psum_scatter(
-            attn_local.astype(jnp.bfloat16), "seg", scatter_dimension=1, tiled=True
-        ).astype(jnp.float32),
-        lax.psum_scatter(
-            up_local.astype(jnp.bfloat16), "seg", scatter_dimension=1, tiled=True
-        ).astype(jnp.float32),
-        lax.psum_scatter(
-            down_local.astype(jnp.bfloat16), "seg", scatter_dimension=1, tiled=True
-        ).astype(jnp.float32),
-    )
-    attn_sum, up_sum, down_sum = lax.psum((attn_sum, up_sum, down_sum), "dp")
-    shard_squares = (
-        jnp.sum(attn_sum * attn_sum) + jnp.sum(up_sum * up_sum) + jnp.sum(down_sum * down_sum)
-    )
-    matrix_squares = lax.psum(shard_squares, "seg")
+    grad_out = lax.psum(grad_out, ("seg", "dp"))
+    count, dp_count = lax.axis_size("seg"), lax.axis_size("dp")
+    rows = D // count
+    small = jnp.concatenate(
+        [
+            grad_in,
+            grad_vectors.reshape(-1, D),
+            grad_outer,
+            jnp.full((1, D), loss_here),
+            jnp.zeros((SMALL - 110, D), f32),
+        ],
+        0,
+    )
+    whole, every, small, squares = reduce_grads(count, dp_count, attn_grads, up_grads, down_grads, small)
+    grad_in, grad_vectors, grad_outer = small[0:80], small[80:104].reshape(layer_vectors.shape), small[104:109]
+    loss_sum = small[109, 0]
     small_squares = (
         jnp.sum(grad_in * grad_in)
         + jnp.sum(grad_out * grad_out)
         + jnp.sum(grad_vectors * grad_vectors)
         + jnp.sum(grad_outer * grad_outer)
     )
-    grad_norm = jnp.sqrt(matrix_squares + small_squares)
+    grad_norm = jnp.sqrt(squares[0, 0] + small_squares)
     clip = jnp.minimum(1.0, 0.25 / (grad_norm + 1e-06))
+    plane, core = segment // 2, segment % 2
+    kind = jnp.where(plane == count // 4 - 1, 1, jnp.where(plane == count // 4, 2, 0))
+    role = jnp.stack([kind, core, (group >= 2).astype(jnp.int32), core]).astype(jnp.int32)
+    made = muon(role, clip[None], whole, momenta)
+    updates = spread(count, made)
+
+    def arranged(blocks):
+        attn_part = jnp.swapaxes(blocks[:, 0:2], 0, 1)
+        up_part = jnp.swapaxes(blocks[0:2, 2:6], 1, 2).reshape(ff_up.shape)
+        down_part = blocks[2:4, 2:6].reshape(ff_down.shape)
+        return attn_part.astype(f32), up_part.astype(f32), down_part.astype(f32)
+
+    attn_sum, up_sum, down_sum = arranged(every)
+    attn_mom = 0.5 * attn_momentum + clip * attn_sum
+    up_mom = 0.5 * up_momentum + clip * up_sum
+    down_mom = 0.5 * down_momentum + clip * down_sum
     in_new, in_moment_new, in_second_new = adamw(
         in_proj, in_moment, in_second, grad_in * clip, 0.05, 0.01
     )
@@ -698,32 +1258,8 @@
     outer_new, outer_moment_new, outer_second_new = adamw(
         outer_vectors, outer_moment, outer_second, grad_outer * clip, 0.25, 0.0
     )
-    block_rows = attn_momentum.shape[2]
-    attn_old = attn_momentum.reshape(4 * LAYERS, block_rows, D)
-    row_counts = (block_rows, up_momentum.shape[1], down_momentum.shape[1])
-    attn_mom = 0.5 * attn_old + clip * attn_sum
-    up_mom = 0.5 * up_momentum + clip * up_sum
-    down_mom = 0.5 * down_momentum + clip * down_sum
-    owned_attn = to_owner(attn_mom, offsets[0], owner_count, owner)
-    owned_up = to_owner(up_mom, offsets[1], owner_count, owner)
-    owned_down = to_owner(down_mom, offsets[2], owner_count, owner)
-    whole_attn, whole_up, whole_down = (
-        lax.all_gather(owned_attn, "seg", axis=1, tiled=True),
-        lax.all_gather(owned_up, "seg", axis=1, tiled=True),
-        lax.all_gather(owned_down, "seg", axis=1, tiled=True),
-    )
-    part_attn = own_rows(jax.vmap(orthogonal)(whole_attn), row_counts[0])
-    part_up = own_rows(jax.vmap(orthogonal)(whole_up), row_counts[1])
-    part_down = own_rows(jax.vmap(orthogonal)(whole_down), row_counts[2])
-    back_attn, back_up, back_down = (
-        lax.all_gather(shortened(part_attn[None]), "dp", axis=0, tiled=True),
-        lax.all_gather(shortened(part_up[None]), "dp", axis=0, tiled=True),
-        lax.all_gather(shortened(part_down[None]), "dp", axis=0, tiled=True),
-    )
-    attn_update = from_owner(back_attn, offsets[0], 4 * LAYERS)
-    up_update = from_owner(back_up, offsets[1], LAYERS)
-    down_update = from_owner(back_down, offsets[2], LAYERS)
-    attn_new = attn_proj * (1.0 - 0.3 * 0.01) - 0.3 * attn_update.reshape(attn_proj.shape)
+    attn_update, up_update, down_update = arranged(updates)
+    attn_new = attn_proj * (1.0 - 0.3 * 0.01) - 0.3 * attn_update
     up_new = ff_up * (1.0 - 0.3 * 0.01) - 0.3 * max(1.0, FF / D) ** 0.5 * up_update
     down_new = ff_down * (1.0 - 0.3 * 0.01) - 0.3 * max(1.0, D / FF) ** 0.5 * down_update
     return (
@@ -742,7 +1278,7 @@
         outer_moment_new,
         outer_second_new,
         attn_new,
-        attn_mom.reshape(attn_proj.shape),
+        attn_mom,
         up_new,
         up_mom,
         down_new,

time: 960 us -> 485 us (0.51)
  waiting for transfers between devices: 319 us -> 0.04 us
  Pallas kernels: 201 us -> 367 us
  blocking collectives: 153 us -> 10.2 us
  matrix products: 135 us -> 2.87 us
  other arithmetic: 65.5 us -> 33.2 us
  local copies, waits for them, and re-layouts: 45.2 us -> 35.2 us
    pallas_call x0 -> x3, Pallas kernels: none -> 166 us  [the longest x1 105 us: reduce_grads(): pl.pallas_call(functools.partial(reduce_kernel, count), out_shape=[jax.Sh...]
    psum x2 -> x1, waiting for transfers between devices: 135 us -> 0.01 us  [local(): grad_out = lax.psum(grad_out, ('seg', 'dp'))]
    psum x3 -> x0, blocking collectives: 131 us -> none  [the longest x1 72 us: local(): attn_sum, up_sum, down_sum = lax.psum((attn_sum, up_sum, down_sum), 'dp')]
    dot_general x45 -> x0, matrix products: 129 us -> none  [the longest x15 60.6 us: orthogonal(): gram_matrix = jnp.matmul(matrix, matrix.T, precision=HIGH)]
    reduce_scatter x2 -> x0, waiting for transfers between devices: 99.8 us -> none  [the longest x1 50.4 us: local(): lax.psum_scatter(attn_local.astype(jnp.bfloat16), 'seg', scatter_dimensio...]
    unnamed x11 -> x2, waiting for transfers between devices: 53.5 us -> 0.03 us
    all_gather x5 -> x1, waiting for transfers between devices: 31.3 us -> 0.01 us  [local(): momenta = lax.all_gather(owned, 'seg', axis=0, tiled=False)]
    reduce_sum x6 -> x0, other arithmetic: 22 us -> none  [the longest x3 17.4 us: orthogonal(): matrix = matrix / (jnp.sqrt(jnp.sum(matrix * matrix)) + 1e-07)]
  transfers between devices with their start and end apart: 13 -> 5, of which waited for: 8 -> 0; matrix products, arithmetic and copies ran while one was open for 24% -> 12% of each run, Pallas kernels for 8% -> 54%
where the time goes in v2:
time: 485 us; the launch traced here: 478 us
  Pallas kernels  367 us (76%)
  local copies, waits for them, and re-layouts  35.2 us (7%)
  other arithmetic  33.2 us (7%)
  between operations  21 us (4%)
  blocking collectives  10.2 us (2%)
  starting transfers between devices  8.47 us (2%)
    pallas_call x1, Pallas kernels, reduce_grads(): pl.pallas_call(functools.partial(reduce_kernel, count), out_shape=[jax.Sh...  105 us
    pallas_call x2, Pallas kernels, attend_back(): pl.pallas_call(attend_back_kernel, grid=(streams,), out_shape=[jax.ShapeD...  72.3 us
    pallas_call x4, Pallas kernels, forward_layer(): pl.pallas_call(forward_kernel, grid=(1,), out_shape=out_shape, in_specs=i...  71.2 us
    pallas_call x1, Pallas kernels, spread(): pl.pallas_call(functools.partial(spread_kernel, count), out_shape=jax.Sha...  57.1 us
    pallas_call x2, Pallas kernels, feed_back(): pl.pallas_call(feed_back_kernel, grid=(streams,), out_shape=[jax.ShapeDty...  45.7 us
    pallas_call x1, Pallas kernels, head(): pl.pallas_call(functools.partial(head_kernel, scale), grid=(streams,), ou...  11 us
    unnamed x71, local copies, waits for them, and re-layouts  10.9 us
    psum x1, blocking collectives, local(): counts = lax.psum(local_counts, 'seg')  10.2 us
  transfers between devices with their start and end apart: 5, of which 0 were waited for; matrix products, arithmetic and copies ran while one was open for 12% of the time, Pallas kernels for 54%

profile of v2, /device:TPU:0, one launch (start us, length us, event | category | flops | bytes accessed | tf_op | source)
XLA Modules:
  0.0 477.6 jit_solution(3320243577616807723)
XLA Ops:
  8.1 2.4 collective-permute-start
  11.9 4.7 slice_bitcast_fusion
  16.6 2.7 slice_bitcast_fusion.1
  19.3 1.0 copy-done.7
  20.3 2.3 slice_bitcast_fusion.2
  22.7 10.2 %psum.14 = s32[2]{0:T(128)S(1)} all-reduce(s32[2]{0:T(128)S(1)} %reduce_sum.54), channel_id=1, replica_groups=mesh['seg'=8,'dp'=4] {'seg'}, use_global_device_ids=true, to_apply=%region_1.2 | all-reduce | flops 2 | bytes 16 | tf_op jit(solution)/shard_map/psum | solution.py:1155
  33.1 1.0 copy.99.weight_ref
  34.1 1.0 copy.98.target_ref
  35.7 1.8 convolution_add_fusion.x_ref
  38.6 1.1 slice_bitcast_fusion.6
  39.8 17.7 %layer_forward.4 = (f32[2,512,512]{2,1,0:T(8,128)}, bf16[512,512]{1,0:T(8,128)(2,1)}, bf16[2,1024,512]{2,1,0:T(8,128)(2,1)}, bf16[2,512,512]{2,1,0:T(8,128)(2,1)...) custom-call(f32[1]{0:T(128)} %bitcast.bias_ref, ...), custom_call_target="tpu_custom_call" | custom-call | flops 10000000000 | bytes 20000000 | tf_op jit(solution)/shard_map/layer_forward/pallas_call | solution.py:194
  57.5 1.8 collective-permute-start.2
  59.3 17.8 %layer_forward.5 = (f32[2,512,512]{2,1,0:T(8,128)}, bf16[512,512]{1,0:T(8,128)(2,1)}, bf16[2,1024,512]{2,1,0:T(8,128)(2,1)}, bf16[2,512,512]{2,1,0:T(8,128)(2,1)...) custom-call(f32[1]{0:T(128)} %bitcast.bias_ref, ...), custom_call_target="tpu_custom_call", output_to_operand_aliasing={{0}: (7, {}), {2}: (8, {}), {3}: (9, {}), {4}: (10, {}), {5... | custom-call | flops 10000000000 | bytes 20000000 | tf_op jit(solution)/shard_map/layer_forward/pallas_call | solution.py:194
  77.1 4.2 collective-permute-start.1
  82.1 18.0 %layer_forward.6 = (f32[2,512,512]{2,1,0:T(8,128)}, bf16[512,512]{1,0:T(8,128)(2,1)}, bf16[2,1024,512]{2,1,0:T(8,128)(2,1)}, bf16[2,512,512]{2,1,0:T(8,128)(2,1)...) custom-call(f32[1]{0:T(128)} %bitcast.bias_ref, ...), custom_call_target="tpu_custom_call" | custom-call | flops 10000000000 | bytes 20000000 | tf_op jit(solution)/shard_map/layer_forward/pallas_call | solution.py:194
  100.9 17.7 %layer_forward.7 = (f32[2,512,512]{2,1,0:T(8,128)}, bf16[512,512]{1,0:T(8,128)(2,1)}, bf16[2,1024,512]{2,1,0:T(8,128)(2,1)}, bf16[2,512,512]{2,1,0:T(8,128)(2,1)...) custom-call(f32[1]{0:T(128)} %bitcast.bias_ref, ...), custom_call_target="tpu_custom_call", output_to_operand_aliasing={{0}: (7, {}), {2}: (8, {}), {3}: (9, {}), {4}: (10, {}), {5... | custom-call | flops 10000000000 | bytes 20000000 | tf_op jit(solution)/shard_map/layer_forward/pallas_call | solution.py:194
  118.7 11.0 %head.1 = (f32[2,512,512]{2,1,0:T(8,128)}, f32[512,1024]{1,0:T(8,128)}, f32[8,512]{1,0:T(8,128)}, f32[1,1]{1,0:T(1,128)}) custom-call(f32[2,512,512]{2,1,0:T(8,128)} %get-tuple-element.100.x_ref, s32[2,512,1]{2,1,0:T(8,128)} %copy.98.target_ref, f32[2,512,1]{2,1,0:T(8,128)} %copy.99.weight_ref, bf16[512,1024]{1,0:T(8,128)(2,1)} %out_ref.1, ...), custom_call_target="tpu_custom_call" | custom-call | flops 3300000000 | bytes 10000000 | tf_op jit(solution)/shard_map/head/pallas_call | solution.py:249
  129.7 1.1 copy-done.8
  130.9 1.0 dynamic-slice_bitcast_fusion
  132.1 1.0 pad_maximum_fusion.1
  133.7 1.1 pad_maximum_fusion.mem_ref
  134.8 22.8 %feed_back.2 = (f32[2,512,512]{2,1,0:T(8,128)}, bf16[4,512,512]{2,1,0:T(8,128)(2,1)}, bf16[2048,512]{1,0:T(8,128)(2,1)}, f32[8,512]{1,0:T(8,128)}) custom-call(f32[2,512,512]{2,1,0:T(8,128)} %get-tuple-element.101.g_ref, f32[2,512,512]{2,1,0:T(8,128)} %get-tuple-element.102.after_ref, bf16[512,2048]{1,0:T(8,128)(2,1)} %get-tuple-element.229.up_ref, ...), custom_call_target="tpu_custom_call" | custom-call | flops 11000000512 | bytes 20000000 | tf_op jit(solution)/shard_map/feed_back/pallas_call | solution.py:319
  157.6 36.3 %attend_back.2 = (f32[2,512,512]{2,1,0:T(8,128)}, bf16[4,512,512]{2,1,0:T(8,128)(2,1)}, f32[8,512]{1,0:T(8,128)}) custom-call(f32[1]{0:T(128)} %bitcast.bias_ref, f32[2,512,512]{2,1,0:T(8,128)} %get-tuple-element.103.dafter_ref, f32[2,512,512]{2,1,0:T(8,128)} %get-tuple-element.89.x_ref, bf16[2,512,512]{2,1,0:T(8,128)(2,1)} %pad_maximum_fusion.mem_ref, ...), custom_call_target="tpu_custom_call" | custom-call | flops 30000001024 | bytes 20000000 | tf_op jit(solution)/shard_map/attend_back/pallas_call | solution.py:473
  193.8 22.9 %feed_back.3 = (f32[2,512,512]{2,1,0:T(8,128)}, bf16[4,512,512]{2,1,0:T(8,128)(2,1)}, bf16[2048,512]{1,0:T(8,128)(2,1)}, f32[8,512]{1,0:T(8,128)}) custom-call(f32[2,512,512]{2,1,0:T(8,128)} %get-tuple-element.110.g_ref, f32[2,512,512]{2,1,0:T(8,128)} %get-tuple-element.111.after_ref, bf16[512,2048]{1,0:T(8,128)(2,1)} %get-tuple-element.230.up_ref, ...), custom_call_target="tpu_custom_call" | custom-call | flops 11000000512 | bytes 20000000 | tf_op jit(solution)/shard_map/feed_back/pallas_call | solution.py:319
  216.8 36.0 %attend_back.3 = (f32[2,512,512]{2,1,0:T(8,128)}, bf16[4,512,512]{2,1,0:T(8,128)(2,1)}, f32[8,512]{1,0:T(8,128)}) custom-call(f32[1]{0:T(128)} %bitcast.bias_ref, f32[2,512,512]{2,1,0:T(8,128)} %get-tuple-element.112.dafter_ref, f32[2,512,512]{2,1,0:T(8,128)} %convolution_add_fusion.x_ref, bf16[2,512,512]{2,1,0:T(8,128)(2,1)} %copy-done.5, ...), custom_call_target="tpu_custom_call" | custom-call | flops 30000001024 | bytes 20000000 | tf_op jit(solution)/shard_map/attend_back/pallas_call | solution.py:473
  255.3 1.8 reduce_sum.55
  258.4 2.7 concatenate.17.small_ref
  261.1 104.6 %reduce_grads.1 = (bf16[8,4,64,512]{3,2,1,0:T(8,128)(2,1)}, bf16[4,6,64,512]{3,2,1,0:T(8,128)(2,1)}, f32[112,512]{1,0:T(8,128)}, f32[8,128]{1,0:T(8,128)}) custom-call(bf16[2,2,8,64,512]{4,3,2,1,0:T(8,128)(2,1)} %bitcast.107, bf16[2,2,8,64,512]{4,3,2,1,0:T(8,128)(2,1)} %bitcast.104, bf16[4,8,64,512]{3,2,1,0:T(8,128)(2,1)} %bitcast.105, ...), custom_call_target="tpu_custom_call" | custom-call | flops 100000000 | bytes 200000000 | tf_op jit(solution)/shard_map/reduce_grads/pallas_call | solution.py:852
  365.7 1.2 slice.146
  366.9 1.2 slice.145
  368.1 1.3 multiply_reduce_fusion.3
  369.4 1.4 multiply_reduce_fusion.2
  370.8 1.6 multiply_reduce_fusion.1
  372.4 2.7 multiply_reduce_fusion
  378.4 1.6 convert_multiply_fusion
  380.1 1.3 bitcast_add_fusion.1
  381.5 1.1 copy.112
  384.0 0.9 fusion.10
  387.5 2.1 fusion.18
  389.6 1.2 bitcast_add_fusion
  390.9 7.1 %fusion.16 = (bf16[512,1024]{1,0:T(8,128)(2,1)}, f32[512,1024]{1,0:T(8,128)}, f32[512,1024]{1,0:T(8,128)}, f32[512,1024]{1,0:T(8,128)}) fusion(f32[512,1024]{1,0:T(8,128)S(1)} %copy-done.10, f32[512,1024]{1,0:T(8,128)S(1)} %copy-done.3, f32[]{:T(128)} %min.3, f32[512,1024]{1,0:T(8,128)} %param.32, f32[512,1024]{1,0:T(8,128)} %param.34), kind=kLoop, calls=%fused_computation.74 | loop fusion | flops 7340032 | bytes 15728644 | tf_op jit(solution)/shard_map/convert_element_type | solution.py:1287
  397.9 4.7 muon.1.made_ref
  402.7 57.1 %spread.1 = bf16[4,6,64,512]{3,2,1,0:T(8,128)(2,1)} custom-call(bf16[8,2,64,512]{3,2,1,0:T(8,128)(2,1)} %muon.1.made_ref), custom_call_target="tpu_custom_call" | custom-call | flops 1000000 | bytes 40000000 | tf_op jit(solution)/shard_map/spread/pallas_call | solution.py:1091
  459.8 1.6 convert_multiply_fusion.1
  461.5 1.3 fusion.15
  462.8 1.1 copy.111
  464.7 1.4 fusion.13
  466.8 1.6 fusion.14
  (109 shorter events, 15.4 us)
Async XLA Ops:
  8.0 27.7 %copy-start = (bf16[80,512]{1,0:T(8,128)(2,1)S(1)}, bf16[80,512]{1,0:T(8,128)(2,1)}, u32[]{:S(2)}) copy-start(bf16[80,512]{1,0:T(8,128)(2,1)} %param.47) | copy-start | bytes 245764
  8.1 364.3 %all-reduce.2.cloned.1.call-start = ((), (), s32[]{:S(2)}) async-start(), calls=%async_computation | async-start | bytes 4194304 | tf_op jit(solution)/shard_map/psum | solution.py:1209
  8.1 30.1 %collective-permute-start = (bf16[2,512,80]{1,2,0:T(8,128)(2,1)}, bf16[2,512,80]{1,2,0:T(8,128)(2,1)S(1)}, u32[]{:S(2)}, u32[]{:S(2)}) collective-permute-start(bf16[2,512,80]{1,2,0:T(8,128)(2,1)} %param.26), channel_id=1, source_target_pairs={{0,4},{4,8},{8,12},{12,16},{16,20},{20,24},{24,28},{1,5},{5,9},{9,... | collective-permute-start | bytes 491528 | tf_op jit(solution)/shard_map/ppermute | solution.py:514
  11.9 4.7 copy-start.6
  16.6 3.7 copy-start.7
  20.3 2.3 copy-start.25
  20.3 2.4 copy-start.21
  20.3 13.8 %copy-start.29 = (s32[2,512]{1,0:T(2,128)S(1)}, s32[2,512]{1,0:T(2,128)}, u32[]{:S(2)}) copy-start(s32[2,512]{1,0:T(2,128)} %param.28) | copy-start | bytes 12292
  20.3 15.4 %copy-start.12 = (bf16[2,512,80]{1,2,0:T(8,128)(2,1)S(1)}, bf16[2,512,80]{1,2,0:T(8,128)(2,1)}, u32[]{:S(2)}) copy-start(bf16[2,512,80]{1,2,0:T(8,128)(2,1)} %param.26) | copy-start | bytes 491524
  38.6 18.9 %copy-start.5 = (bf16[2,512,512]{2,1,0:T(8,128)(2,1)}, bf16[2,512,512]{2,1,0:T(8,128)(2,1)S(1)}, u32[]{:S(2)}) copy-start(bf16[2,512,512]{2,1,0:T(8,128)(2,1)S(1)} %add_convert_fusion.mem_ref) | copy-start | bytes 3145732
  57.5 23.8 %collective-permute-start.2 = (bf16[512,512]{1,0:T(8,128)(2,1)}, bf16[512,512]{1,0:T(8,128)(2,1)S(1)}, u32[]{:S(2)}, u32[]{:S(2)}) collective-permute-start(bf16[512,512]{1,0:T(8,128)(2,1)} %get-tuple-element.91), channel_id=1, source_target_pairs={{0,4},{4,8},{8,12},{12,16},{16,20},{20,24},{24,28},{1,5},{5,9},{9,... | collective-permute-start | bytes 1572872 | tf_op jit(solution)/shard_map/ppermute | solution.py:514
  77.1 23.0 %collective-permute-start.1 = (bf16[512,512]{1,0:T(8,128)(2,1)}, bf16[512,512]{1,0:T(8,128)(2,1)S(1)}, u32[]{:S(2)}, u32[]{:S(2)}) collective-permute-start(bf16[512,512]{1,0:T(8,128)(2,1)} %get-tuple-element.90), channel_id=1, source_target_pairs={{0,4},{4,8},{8,12},{12,16},{16,20},{20,24},{24,28},{1,5},{5,9},{9,... | collective-permute-start | bytes 1572872 | tf_op jit(solution)/shard_map/ppermute | solution.py:514
  81.4 0.8 copy-start.17
  100.1 0.8 copy-start.19
  129.6 1.2 copy-start.8
  129.6 2.3 copy-start.4
  129.7 268.3 %all-gather.3.cloned.1.call-start = ((), (), s32[]{:S(2)}) async-start(), calls=%async_computation.1 | async-start | bytes 7077888 | tf_op jit(solution)/shard_map/all_gather | solution.py:1153
  131.9 1.8 copy-start.18
  131.9 1.8 copy-start.20
  216.8 37.7 %copy-start.27 = (f32[8,512]{1,0:T(8,128)S(1)}, f32[8,512]{1,0:T(8,128)}, u32[]{:S(2)}) copy-start(f32[8,512]{1,0:T(8,128)} %get-tuple-element.127) | copy-start | bytes 49156
  216.8 37.7 %copy-start.28 = (f32[8,512]{1,0:T(8,128)S(1)}, f32[8,512]{1,0:T(8,128)}, u32[]{:S(2)}) copy-start(f32[8,512]{1,0:T(8,128)} %get-tuple-element.128) | copy-start | bytes 49156
  216.8 37.7 %copy-start.26 = (f32[8,512]{1,0:T(8,128)S(1)}, f32[8,512]{1,0:T(8,128)}, u32[]{:S(2)}) copy-start(f32[8,512]{1,0:T(8,128)} %get-tuple-element.129) | copy-start | bytes 49156
  252.8 4.2 copy-start.30
  252.9 4.2 copy-start.2
  378.4 1.7 copy-start.11
  380.1 2.4 copy-start.16
  381.4 5.4 %copy-start.22 = (f32[5,512]{1,0:T(8,128)S(1)}, f32[5,512]{1,0:T(8,128)}, u32[]{:S(2)}) copy-start(f32[5,512]{1,0:T(8,128)} %outer_ref.1) | copy-start | bytes 30724
  381.4 5.4 %copy-start.23 = (f32[5,512]{1,0:T(8,128)S(1)}, f32[5,512]{1,0:T(8,128)}, u32[]{:S(2)}) copy-start(f32[5,512]{1,0:T(8,128)} %param.39) | copy-start | bytes 30724
  381.5 5.4 %copy-start.24 = (f32[5,512]{1,0:T(8,128)S(1)}, f32[5,512]{1,0:T(8,128)}, u32[]{:S(2)}) copy-start(f32[5,512]{1,0:T(8,128)} %param.40) | copy-start | bytes 30724
  387.5 3.4 copy-start.3
  387.5 3.4 copy-start.10
  459.8 1.7 copy-start.13
  462.8 1.9 copy-start.14
  464.7 1.4 copy-start.9
  464.7 2.1 copy-start.15
  466.2 2.3 copy-start.1
Sparse Core Ops, SparseCore 0:
  129.8 187.6 all-reduce.1
Sparse Core Ops, SparseCore 1:
  133.2 66.2 all-gather.2

commit v3 on v2

--- a/solution.py
+++ b/solution.py
@@ -170,7 +170,12 @@
     return pl.BlockSpec((None,) + shape, lambda i: (stream,) + zeros)
 
 
-def forward_layer(stream, streams, bias, hidden, memory, attn, upper, lower, vectors, earlier):
+def layer_spec(shape, depth):
+    zeros = (0,) * len(shape)
+    return pl.BlockSpec((None,) + shape, lambda *_: (depth,) + zeros)
+
+
+def forward_layer(depth, stream, streams, bias, hidden, memory, attn, upper, lower, vectors, earlier):
     saved_shapes = [jax.ShapeDtypeStruct((streams,) + shape, dtype) for shape, dtype in SAVED]
     saved_specs = [stream_spec(shape, stream) for shape, dtype in SAVED]
     out_shape = [saved_shapes[0], jax.ShapeDtypeStruct((SEG, D), bf16)] + saved_shapes[1:]
@@ -179,11 +184,11 @@
     in_specs = [
         pl.BlockSpec(memory_space=pltpu.SMEM),
         stream_spec((SEG, D), stream),
-        whole_spec((SEG, D)),
-        whole_spec(attn.shape),
-        whole_spec(upper.shape),
-        whole_spec(lower.shape),
-        whole_spec(vectors.shape),
+        stream_spec((SEG, D), stream) if memory.ndim == 3 else whole_spec((SEG, D)),
+        layer_spec(attn.shape[1:], depth),
+        layer_spec(upper.shape[1:], depth),
+        layer_spec(lower.shape[1:], depth),
+        layer_spec(vectors.shape[1:], depth),
     ]
     aliases = {}
     if earlier is not None:
@@ -206,14 +211,13 @@
     return [out[0]] + list(out[2:]), out[1]
 
 
-def head_kernel(scale, x_ref, target_ref, weight_ref, out_ref, outer_ref, bias_ref, g_ref, dout_ref, douter_ref, loss_ref, acc_s):
+def head_kernel(scale, x_ref, target_ref, mask_ref, total_ref, out_ref, outer_ref, bias_ref, mom_ref, g_ref, dout_ref, douter_ref, acc_s):
     step = pl.program_id(0)
 
     @pl.when(step == 0)
     def _():
         acc_s[...] = jnp.zeros_like(acc_s)
         douter_ref[...] = jnp.zeros_like(douter_ref)
-        loss_ref[...] = jnp.zeros_like(loss_ref)
 
     unit, rscale = normalised(x_ref[...])
     gain = outer_ref[1:2, :]
@@ -222,13 +226,16 @@
     most = jnp.max(logits, -1, keepdims=True)
     powers = jnp.exp(logits - most)
     total = jnp.sum(powers, -1, keepdims=True)
-    chosen = lax.broadcasted_iota(jnp.int32, logits.shape, 1) == target_ref[...]
+    target_row = target_ref[pl.ds(step, 1), :].astype(f32)
+    weight_row = mask_ref[pl.ds(step, 1), :].astype(f32) * (1.0 / total_ref[pl.ds(step, 1), 0:1])
+    columns = jnp.transpose(jnp.concatenate([target_row, weight_row, jnp.zeros((6, SEG), f32)], 0))
+    target, weight = columns[:, 0:1].astype(jnp.int32), columns[:, 1:2]
+    chosen = lax.broadcasted_iota(jnp.int32, logits.shape, 1) == target
     picked = jnp.sum(jnp.where(chosen, logits, 0.0), -1, keepdims=True)
-    weight = weight_ref[...]
-    loss_ref[...] += jnp.sum(weight * (most + jnp.log(total) - picked), 0, keepdims=True)
+    loss = jnp.sum(weight * (most + jnp.log(total) - picked), 0, keepdims=True)
     spread = weight * scale
     dlogits = (powers * (spread / total) - jnp.where(chosen, spread, 0.0)).astype(bf16)
-    acc_s[...] += dot_tn(normed, dlogits)
+    acc_s[...] += dot_nn(jnp.transpose(normed), dlogits)
     bias_grad = column_sum(dlogits.astype(f32))
     dnormed = dot_nt(dlogits, out_ref[...])
     g_ref[...] = norm_back(dnormed, gain, unit, rscale)
@@ -236,13 +243,14 @@
     douter_ref[2:3, :] += column_sum(dnormed)
     douter_ref[3:4, :] += bias_grad[:, :D]
     douter_ref[4:5, :] += bias_grad[:, D:]
+    douter_ref[5:6, :] += jnp.broadcast_to(loss, (1, D))
 
     @pl.when(step == pl.num_programs(0) - 1)
     def _():
         dout_ref[...] = acc_s[...]
 
 
-def head(hidden, targets, weighting, out_weight, outer_vectors, scale):
+def head(hidden, targets, mask, totals, out_weight, outer_vectors, scale, momenta):
     streams = hidden.shape[0]
     codes = out_weight.shape[1]
     bias = outer_vectors[3:].reshape(1, codes)
@@ -253,22 +261,23 @@
             jax.ShapeDtypeStruct((streams, SEG, D), f32),
             jax.ShapeDtypeStruct((D, codes), f32),
             jax.ShapeDtypeStruct((8, D), f32),
-            jax.ShapeDtypeStruct((1, 1), f32),
         ],
         in_specs=[
             stream_spec((SEG, D)),
-            stream_spec((SEG, 1)),
-            stream_spec((SEG, 1)),
+            whole_spec((streams, SEG)),
+            whole_spec((streams, SEG)),
+            whole_spec((8, 128)),
             whole_spec((D, codes)),
             whole_spec(outer_vectors.shape),
             whole_spec((1, codes)),
+            pl.BlockSpec(memory_space=pl.ANY),
         ],
-        out_specs=[stream_spec((SEG, D)), whole_spec((D, codes)), whole_spec((8, D)), whole_spec((1, 1))],
+        out_specs=[stream_spec((SEG, D)), whole_spec((D, codes)), whole_spec((8, D))],
         scratch_shapes=[pltpu.VMEM((D, codes), f32)],
         compiler_params=pltpu.CompilerParams(vmem_limit_bytes=VMEM_LIMIT),
         cost_estimate=pl.CostEstimate(flops=33 * 10**8, bytes_accessed=10**7, transcendentals=10**6),
         name="head",
-    )(hidden, targets[..., None], weighting[..., None], out_weight, outer_vectors, bias)
+    )(hidden, targets, mask, totals, out_weight, outer_vectors, bias, momenta)
 
 
 def feed_back_kernel(g_ref, after_ref, up_ref, down_ref, vec_ref, dafter_ref, dup_ref, ddown_ref, dvec_ref, up_s, down_s, act_s, inner_s):
@@ -314,7 +323,7 @@
         ddown_ref[...] = jnp.transpose(down_s[...].astype(bf16))
 
 
-def feed_back(grad, after, upper, lower, vectors):
+def feed_back(depth, grad, after, upper, lower, vectors):
     streams = grad.shape[0]
     return pl.pallas_call(
         feed_back_kernel,
@@ -328,9 +337,9 @@
         in_specs=[
             stream_spec((SEG, D)),
             stream_spec((SEG, D)),
-            whole_spec(upper.shape),
-            whole_spec(lower.shape),
-            whole_spec(vectors.shape),
+            layer_spec(upper.shape[1:], depth),
+            layer_spec(lower.shape[1:], depth),
+            layer_spec(vectors.shape[1:], depth),
         ],
         out_specs=[
             stream_spec((SEG, D)),
@@ -351,6 +360,7 @@
 
 
 def attend_back_kernel(
+    lowest,
     bias_ref,
     dafter_ref,
     x_ref,
@@ -363,9 +373,11 @@
     mixed_ref,
     attn_ref,
     vec_ref,
+    frames_ref,
     dx_ref,
     dattn_ref,
     dvec_ref,
+    din_ref,
     attn_s,
     dmixed_s,
     dq_s,
@@ -380,6 +392,7 @@
     def _():
         attn_s[...] = jnp.zeros_like(attn_s)
         dvec_ref[...] = jnp.zeros_like(dvec_ref)
+        din_ref[...] = jnp.zeros_like(din_ref)
 
     dafter = dafter_ref[...]
     branch = dafter.astype(bf16)
@@ -460,23 +473,31 @@
     mem_unit, _ = normalised(mem_ref[...].astype(f32))
     dvec_ref[0:1, :] += column_sum(down * unit + dmem * mem_unit)
     dvec_ref[1:2, :] += column_sum(down + dmem)
-    dx_ref[...] = dafter + norm_back(down, gain, unit, scale)
+    dx = dafter + norm_back(down, gain, unit, scale)
+    dx_ref[...] = dx
+    if lowest:
+        dx_high = dx.astype(bf16)
+        dx_rest = (dx - dx_high.astype(f32)).astype(bf16)
+        din_ref[...] += dot_nn(frames_ref[...], dx_high) + dot_nn(frames_ref[...], dx_rest)
+        dvec_ref[5:6, :] += column_sum(dx)
 
     @pl.when(step == pl.num_programs(0) - 1)
     def _():
         dattn_ref[...] = attn_s[...].astype(bf16)
 
 
-def attend_back(bias, dafter, x, memory, saved, attn, vectors):
+def attend_back(depth, bias, dafter, x, memory, saved, attn, vectors, frames):
     streams = dafter.shape[0]
     keyin, q, k, v, lse, mixed = saved
+    inputs = frames.shape[1]
     return pl.pallas_call(
-        attend_back_kernel,
+        functools.partial(attend_back_kernel, depth == 0),
         grid=(streams,),
         out_shape=[
             jax.ShapeDtypeStruct((streams, SEG, D), f32),
             jax.ShapeDtypeStruct((4, D, D), bf16),
             jax.ShapeDtypeStruct((8, D), f32),
+            jax.ShapeDtypeStruct((inputs, D), f32),
         ],
         in_specs=[
             pl.BlockSpec(memory_space=pltpu.SMEM),
@@ -489,10 +510,16 @@
             stream_spec((2 * SEG, D)),
             stream_spec((HEADS, SEG)),
             stream_spec((SEG, D)),
-            whole_spec(attn.shape),
-            whole_spec(vectors.shape),
+            layer_spec(attn.shape[1:], depth),
+            layer_spec(vectors.shape[1:], depth),
+            stream_spec((inputs, SEG)),
         ],
-        out_specs=[stream_spec((SEG, D)), whole_spec((4, D, D)), whole_spec((8, D))],
+        out_specs=[
+            stream_spec((SEG, D)),
+            whole_spec((4, D, D)),
+            whole_spec((8, D)),
+            whole_spec((inputs, D)),
+        ],
         scratch_shapes=[
             pltpu.VMEM((4, D, D), f32),
             pltpu.VMEM((SEG, D), bf16),
@@ -505,7 +532,7 @@
         compiler_params=pltpu.CompilerParams(vmem_limit_bytes=VMEM_LIMIT),
         cost_estimate=pl.CostEstimate(flops=3 * 10**10, bytes_accessed=2 * 10**7, transcendentals=10**7),
         name="attend_back",
-    )(bias, dafter, x, memory, keyin, q, k, v, lse, mixed, attn, vectors)
+    )(bias, dafter, x, memory, keyin, q, k, v, lse, mixed, attn, vectors, frames)
 
 
 def from_behind(value, axis, steps):
@@ -525,7 +552,7 @@
 
 GROUPS = 4
 UNITS = 6
-SMALL = 112
+SMALL = 128
 
 
 def peers():
@@ -593,7 +620,12 @@
     up1,
     down0,
     down1,
-    small_ref,
+    din_ref,
+    vec0_ref,
+    vec1_ref,
+    vec2_ref,
+    vec3_ref,
+    outer_ref,
     whole_ref,
     every_ref,
     small_out,
@@ -604,6 +636,7 @@
     got2,
     got3,
     goth,
+    small_ref,
     small_core,
     small_s,
     small_got,
@@ -642,8 +675,8 @@
         return (
             (attn0.at[:, :, row], (slice(None), slice(None), 0)),
             (attn1.at[:, :, row], (slice(None), slice(None), 1)),
-            (up0.at[:, row], (0, 0, slice(2, 6))),
-            (up1.at[:, row], (0, 1, slice(2, 6))),
+            (up1.at[:, row], (0, 0, slice(2, 6))),
+            (up0.at[:, row], (0, 1, slice(2, 6))),
             (down0.at[row], (1, 0, slice(2, 6))),
             (down1.at[row], (1, 1, slice(2, 6))),
         )
@@ -652,6 +685,11 @@
     for step in range(planes):
         for source, place in pieces(2 * order[step] + core):
             pltpu.make_async_copy(source, mine.at[(step,) + place], load_sem.at[step]).start()
+    inputs = din_ref.shape[0]
+    small_ref[0:inputs, :] = din_ref[...]
+    for place, ref in enumerate((vec0_ref, vec1_ref, vec2_ref, vec3_ref, outer_ref)):
+        small_ref[inputs + 8 * place : inputs + 8 * place + 8, :] = ref[...]
+    small_ref[inputs + 40 :, :] = jnp.zeros((SMALL - inputs - 40, D), f32)
     greet(seg, count, near, far)
     for step in range(planes):
         for source, place in pieces(2 * order[step] + 1 - core):
@@ -803,7 +841,11 @@
         remote(sq_dp.at[group], sq_dp.at[group], sqd_send.at[place], sqd_recv.at[place], target).start()
     for place, target in enumerate(near):
         remote(sq_dp.at[group], sq_dp.at[group], sqd_send.at[place], sqd_recv.at[place], target).wait()
-    square_out[...] = jnp.sum(sq_dp[...], 0)
+    sums = small_out[...]
+    is_loss = lax.broadcasted_iota(jnp.int32, (SMALL, D), 0) == inputs + 37
+    sums = jnp.where(is_loss, 0.0, sums)
+    small_square = jnp.sum(jnp.sum(sums * sums, 0, keepdims=True), 1, keepdims=True)
+    square_out[...] = jnp.sum(sq_dp[...], 0) + jnp.broadcast_to(small_square, (8, 128))
 
     for place, (first, width, owner, spot) in enumerate(roles):
 
@@ -839,7 +881,7 @@
         ).wait()
 
 
-def reduce_grads(count, dp_count, attn, up, down, small):
+def reduce_grads(count, dp_count, attn, up, down, pieces):
     rows = D // count
     planes = count // 2
     far = max(1, dp_count.bit_length() - 3)
@@ -857,7 +899,7 @@
             jax.ShapeDtypeStruct((SMALL, D), f32),
             jax.ShapeDtypeStruct((8, 128), f32),
         ],
-        in_specs=[pl.BlockSpec(memory_space=pl.ANY)] * 6 + [pl.BlockSpec(memory_space=pltpu.VMEM)],
+        in_specs=[pl.BlockSpec(memory_space=pl.ANY)] * 6 + [pl.BlockSpec(memory_space=pltpu.VMEM)] * 6,
         out_specs=[pl.BlockSpec(memory_space=pltpu.VMEM)] * 4,
         scratch_shapes=[
             pltpu.VMEM((planes, 2, 2) + shape, bf16),
@@ -866,6 +908,7 @@
             pltpu.VMEM((planes, 2, 3, rows, D), bf16),
             pltpu.VMEM((planes,) + shape, bf16),
             pltpu.VMEM((far, planes) + shape, bf16),
+            pltpu.VMEM((SMALL, D), f32),
             pltpu.VMEM((SMALL, D), f32),
             pltpu.VMEM((SMALL, D), f32),
             pltpu.VMEM((stages, SMALL // 2, D), f32),
@@ -899,7 +942,7 @@
         ),
         cost_estimate=pl.CostEstimate(flops=10**8, bytes_accessed=2 * 10**8, transcendentals=0),
         name="reduce_grads",
-    )(*attn, *up, *down, small)
+    )(*attn, *up, *down, *pieces)
 
 
 def halves(value):
@@ -923,18 +966,25 @@
     )
 
 
-def muon_kernel(role_ref, clip_ref, whole_ref, mom_ref, out_ref, x_s, q_s, gram_s, high_s, low_s):
+def clip_of(norm):
+    return jnp.minimum(1.0, 0.25 / (norm + 1e-06))
+
+
+def muon_kernel(role_ref, square_ref, dout_ref, whole_ref, mom_ref, out_ref, norm_ref, x_s, q_s, gram_s, high_s, low_s):
     count, rows = whole_ref.shape[0], whole_ref.shape[2]
     core = role_ref[1]
-    clip = clip_ref[0]
+    dout = dout_ref[...]
+    norm = jnp.sqrt(square_ref[0:1, 0:1] + jnp.sum(jnp.sum(dout * dout, 0, keepdims=True), 1, keepdims=True))
+    norm_ref[...] = jnp.broadcast_to(norm, norm_ref.shape)
+    clip = clip_of(norm)
     eye = (
         lax.broadcasted_iota(jnp.int32, (D, D), 0) == lax.broadcasted_iota(jnp.int32, (D, D), 1)
     ).astype(f32)
 
     @pl.when(role_ref[0] == 1)
     def _():
-        start = 0.5 * mom_ref[:, core] + clip * whole_ref[:, 0].astype(f32)
-        start = start.reshape(D, D)
+        start = (0.5 * mom_ref[:, core].astype(f32)).reshape(D, D)
+        start = start + clip * whole_ref[:, 0].astype(f32).reshape(D, D)
         size = jnp.sum(jnp.sum(start * start, 0, keepdims=True), 1, keepdims=True)
         x_s[...] = start / (jnp.sqrt(size) + 1e-07)
 
@@ -955,8 +1005,8 @@
         gram_s[...] = jnp.zeros_like(gram_s)
 
         def gather(tile, size):
-            value = 0.5 * mom_ref[:, 2 + tile] + clip * whole_ref[:, tile].astype(f32)
-            value = value.reshape(D, D)
+            value = (0.5 * mom_ref[:, 2 + tile].astype(f32)).reshape(D, D)
+            value = value + clip * whole_ref[:, tile].astype(f32).reshape(D, D)
             high, low = halves(value)
             high_s[tile] = high
             low_s[tile] = low
@@ -1013,18 +1063,13 @@
         lax.fori_loop(0, 2, finish, 0)
 
 
-def muon(role, clip, whole, momenta):
+def muon(role, squares, dout, whole, momenta):
     count, _, rows, _ = whole.shape
     return pl.pallas_call(
         muon_kernel,
-        out_shape=jax.ShapeDtypeStruct((count, 2, rows, D), bf16),
-        in_specs=[
-            pl.BlockSpec(memory_space=pltpu.SMEM),
-            pl.BlockSpec(memory_space=pltpu.SMEM),
-            pl.BlockSpec(memory_space=pltpu.VMEM),
-            pl.BlockSpec(memory_space=pltpu.VMEM),
-        ],
-        out_specs=pl.BlockSpec(memory_space=pltpu.VMEM),
+        out_shape=[jax.ShapeDtypeStruct((count, 2, rows, D), bf16), jax.ShapeDtypeStruct((8, 128), f32)],
+        in_specs=[pl.BlockSpec(memory_space=pltpu.SMEM)] + [pl.BlockSpec(memory_space=pltpu.VMEM)] * 4,
+        out_specs=[pl.BlockSpec(memory_space=pltpu.VMEM)] * 2,
         scratch_shapes=[
             pltpu.VMEM((D, D), f32),
             pltpu.VMEM((D, D), f32),
@@ -1035,7 +1080,7 @@
         compiler_params=pltpu.CompilerParams(vmem_limit_bytes=VMEM_LIMIT),
         cost_estimate=pl.CostEstimate(flops=2 * 10**10, bytes_accessed=10**7, transcendentals=0),
         name="muon",
-    )(role, clip, whole, momenta)
+    )(role, squares, dout, whole, momenta)
 
 
 def spread_kernel(count, made_ref, every_ref, send, recv, on_send, on_recv):
@@ -1100,6 +1145,259 @@
         cost_estimate=pl.CostEstimate(flops=10**6, bytes_accessed=4 * 10**7, transcendentals=0),
         name="spread",
     )(made)
+
+
+def embed_kernel(
+    count,
+    frames_ref,
+    mask_ref,
+    in_ref,
+    outer_ref,
+    x_ref,
+    mem_ref,
+    total_ref,
+    got_s,
+    count_s,
+    frame_send,
+    frame_recv,
+    count_send,
+    count_recv,
+):
+    seg = lax.axis_index("seg")
+    after, before = lax.rem(seg + 1, count), lax.rem(seg + count - 1, count)
+    streams = frames_ref.shape[0]
+    tally = jnp.sum(mask_ref[...].astype(f32), 1, keepdims=True)
+    count_s[seg] = jnp.broadcast_to(
+        jnp.concatenate([tally, jnp.zeros((8 - streams, 1), f32)], 0), (8, 128)
+    )
+    greet(seg, count, (), ())
+    frame_copy = remote(frames_ref, got_s, frame_send.at[0], frame_recv.at[0], {"seg": after})
+    frame_copy.start()
+    for step, other in enumerate(others(seg, count)):
+        remote(count_s.at[seg], count_s.at[seg], count_send.at[step], count_recv.at[seg], {"seg": other}).start()
+    weight, shift = in_ref[...], outer_ref[0:1, :]
+    for stream in range(streams):
+        x_ref[stream] = dot_nn(jnp.transpose(frames_ref[stream]), weight) + shift
+    frame_copy.wait()
+    for stream in range(streams):
+        mem_ref[stream] = (dot_nn(jnp.transpose(got_s[stream]), weight) + shift).astype(bf16)
+    for other in others(seg, count):
+        wait_bytes(count_s.at[other], count_recv.at[other])
+    total_ref[...] = jnp.sum(count_s[...], 0)
+    for step in range(count - 1):
+        wait_bytes(count_s.at[0], count_send.at[step])
+
+
+def embed(count, frames, mask, in_weight, outer_vectors):
+    streams = frames.shape[0]
+    dma = pltpu.SemaphoreType.DMA
+    return pl.pallas_call(
+        functools.partial(embed_kernel, count),
+        out_shape=[
+            jax.ShapeDtypeStruct((streams, SEG, D), f32),
+            jax.ShapeDtypeStruct((streams, SEG, D), bf16),
+            jax.ShapeDtypeStruct((8, 128), f32),
+        ],
+        in_specs=[pl.BlockSpec(memory_space=pltpu.VMEM)] * 4,
+        out_specs=[pl.BlockSpec(memory_space=pltpu.VMEM)] * 3,
+        scratch_shapes=[
+            pltpu.VMEM(frames.shape, bf16),
+            pltpu.VMEM((count, 8, 128), f32),
+            dma((1,)),
+            dma((1,)),
+            dma((count,)),
+            dma((count,)),
+        ],
+        compiler_params=pltpu.CompilerParams(
+            collective_id=3, has_side_effects=True, vmem_limit_bytes=VMEM_LIMIT
+        ),
+        cost_estimate=pl.CostEstimate(flops=2 * 10**8, bytes_accessed=4 * 10**6, transcendentals=0),
+        name="embed",
+    )(frames, mask, in_weight, outer_vectors)
+
+
+FEED_UP = (1, 0)
+FEED_DOWN = (2, 3)
+KEEP = 1.0 - 0.3 * 0.01
+
+
+def finish_kernel(norm_ref, every_ref, update_ref, dout_ref, small_ref, *refs):
+    (
+        attn_ref,
+        attn_mom_ref,
+        up_ref,
+        up_mom_ref,
+        down_ref,
+        down_mom_ref,
+        out_ref,
+        out_mom_ref,
+        out_sec_ref,
+        in_ref,
+        in_mom_ref,
+        in_sec_ref,
+        vec_ref,
+        vec_mom_ref,
+        vec_sec_ref,
+        outer_ref,
+        outer_mom_ref,
+        outer_sec_ref,
+        attn_new,
+        attn_mom_new,
+        attn_copy_new,
+        up_new,
+        up_mom_new,
+        up_copy_new,
+        down_new,
+        down_mom_new,
+        down_copy_new,
+        out_new,
+        out_mom_new,
+        out_sec_new,
+        out_copy_new,
+        in_new,
+        in_mom_new,
+        in_sec_new,
+        in_copy_new,
+        vec_new,
+        vec_mom_new,
+        vec_sec_new,
+        outer_new,
+        outer_mom_new,
+        outer_sec_new,
+    ) = refs
+    clip = clip_of(norm_ref[0:1, 0:1])
+
+    def muon_step(weight, momentum, grad, update, scale):
+        weight = weight * KEEP - (0.3 * scale) * update.astype(f32)
+        return weight, 0.5 * momentum + clip * grad.astype(f32)
+
+    up_scale, down_scale = max(1.0, FF / D) ** 0.5, max(1.0, D / FF) ** 0.5
+    for depth in range(LAYERS):
+        for kind in range(4):
+            weight, momentum = muon_step(
+                attn_ref[depth, kind],
+                attn_mom_ref[depth, kind],
+                every_ref[kind, depth],
+                update_ref[kind, depth],
+                1.0,
+            )
+            attn_new[depth, kind] = weight
+            attn_mom_new[depth, kind] = momentum
+            attn_copy_new[depth, kind] = weight.astype(bf16)
+            columns = slice(kind * TILE, (kind + 1) * TILE)
+            weight, momentum = muon_step(
+                up_ref[depth, :, columns],
+                up_mom_ref[depth, :, columns],
+                every_ref[FEED_UP[depth], 2 + kind],
+                update_ref[FEED_UP[depth], 2 + kind],
+                up_scale,
+            )
+            up_new[depth, :, columns] = weight
+            up_mom_new[depth, :, columns] = momentum
+            up_copy_new[depth, :, columns] = weight.astype(bf16)
+            weight, momentum = muon_step(
+                down_ref[depth, kind],
+                down_mom_ref[depth, kind],
+                every_ref[FEED_DOWN[depth], 2 + kind],
+                update_ref[FEED_DOWN[depth], 2 + kind],
+                down_scale,
+            )
+            down_new[depth, kind] = weight
+            down_mom_new[depth, kind] = momentum
+            down_copy_new[depth, kind] = weight.astype(bf16)
+    weight, moment, second = adamw(out_ref[...], out_mom_ref[...], out_sec_ref[...], dout_ref[...] * clip, 0.05, 0.01)
+    out_new[...] = weight
+    out_mom_new[...] = moment
+    out_sec_new[...] = second
+    out_copy_new[...] = weight.astype(bf16)
+
+    @pl.when(pl.program_id(0) == 0)
+    def _():
+        inputs = in_ref.shape[0]
+        weight, moment, second = adamw(
+            in_ref[...], in_mom_ref[...], in_sec_ref[...], small_ref[0:inputs, :] * clip, 0.05, 0.01
+        )
+        in_new[...] = weight
+        in_mom_new[...] = moment
+        in_sec_new[...] = second
+        in_copy_new[...] = weight.astype(bf16)
+
+        def rows_of(first, last, base):
+            return small_ref[inputs + base + first : inputs + base + last, :]
+
+        for depth in range(LAYERS):
+            base = 16 * depth
+            for low, high, grad in (
+                (0, 2, rows_of(0, 2, base)),
+                (2, 4, rows_of(0, 2, base + 8)),
+                (4, 7, rows_of(2, 5, base)),
+                (7, 8, rows_of(2, 3, base + 8)),
+                (8, 12, rows_of(4, 8, base + 8)),
+            ):
+                weight, moment, second = adamw(
+                    vec_ref[depth, low:high],
+                    vec_mom_ref[depth, low:high],
+                    vec_sec_ref[depth, low:high],
+                    grad * clip,
+                    0.25,
+                    0.0,
+                )
+                vec_new[depth, low:high] = weight
+                vec_mom_new[depth, low:high] = moment
+                vec_sec_new[depth, low:high] = second
+        for low, high, grad in ((0, 1, rows_of(5, 6, 0)), (1, 5, rows_of(1, 5, 32))):
+            weight, moment, second = adamw(
+                outer_ref[low:high, :], outer_mom_ref[low:high, :], outer_sec_ref[low:high, :], grad * clip, 0.25, 0.0
+            )
+            outer_new[low:high, :] = weight
+            outer_mom_new[low:high, :] = moment
+            outer_sec_new[low:high, :] = second
+
+
+def finish(rows, norm, every, updates, dout, small, arrays):
+    steps = rows // 16
+    attn, _, up, _, down, _, out, _, _, inp, _, _, vec, _, _, outer, _, _ = arrays
+    codes = out.shape[1]
+    blocks = pl.BlockSpec((GROUPS, UNITS, 16, D), lambda i: (0, 0, i, 0))
+    attn_spec = pl.BlockSpec((LAYERS, 4, 16, D), lambda i: (0, 0, i, 0))
+    up_spec = pl.BlockSpec((LAYERS, 16, FF), lambda i: (0, i, 0))
+    out_spec = pl.BlockSpec((D // steps, codes), lambda i: (i, 0))
+    in_spec, vec_spec, outer_spec = whole_spec(inp.shape), whole_spec(vec.shape), whole_spec(outer.shape)
+
+    def like(array, dtype=f32):
+        return jax.ShapeDtypeStruct(array.shape, dtype)
+
+    return pl.pallas_call(
+        finish_kernel,
+        grid=(steps,),
+        out_shape=[like(attn), like(attn), like(attn, bf16)]
+        + [like(up), like(up), like(up, bf16)]
+        + [like(down), like(down), like(down, bf16)]
+        + [like(out)] * 3
+        + [like(out, bf16)]
+        + [like(inp)] * 3
+        + [like(inp, bf16)]
+        + [like(vec)] * 3
+        + [like(outer)] * 3,
+        in_specs=[whole_spec((8, 128)), blocks, blocks, out_spec, whole_spec(small.shape)]
+        + [attn_spec] * 2
+        + [up_spec] * 2
+        + [attn_spec] * 2
+        + [out_spec] * 3
+        + [in_spec] * 3
+        + [vec_spec] * 3
+        + [outer_spec] * 3,
+        out_specs=[attn_spec] * 3
+        + [up_spec] * 3
+        + [attn_spec] * 3
+        + [out_spec] * 4
+        + [in_spec] * 4
+        + [vec_spec] * 3
+        + [outer_spec] * 3,
+        compiler_params=pltpu.CompilerParams(vmem_limit_bytes=VMEM_LIMIT),
+        cost_estimate=pl.CostEstimate(flops=10**8, bytes_accessed=4 * 10**7, transcendentals=0),
+        name="finish",
+    )(norm, every, updates, dout, small, *arrays)
 
 
 def local(
@@ -1131,17 +1429,18 @@
     down_copy,
 ):
     segment = lax.axis_index("seg")
-    stream_total = frames.shape[0] * lax.axis_size("dp")
+    count, dp_count = lax.axis_size("seg"), lax.axis_size("dp")
+    rows = D // count
     streams = frames.shape[0]
-    behind = from_behind(frames, "seg", 1)
+    stream_total = streams * dp_count
     group = lax.axis_index("dp") % GROUPS
-    block = D // lax.axis_size("seg")
-    feeds = jnp.concatenate(
+    feeds = jnp.stack(
         [
-            jnp.swapaxes(up_momentum.reshape(LAYERS, block, 4, D), 1, 2),
-            down_momentum.reshape(LAYERS, 4, block, D),
-        ],
-        0,
+            jnp.swapaxes(up_momentum[1].reshape(rows, 4, D), 0, 1),
+            jnp.swapaxes(up_momentum[0].reshape(rows, 4, D), 0, 1),
+            down_momentum[0].reshape(4, rows, D),
+            down_momentum[1].reshape(4, rows, D),
+        ]
     )
     owned = jnp.concatenate(
         [
@@ -1149,122 +1448,116 @@
             lax.dynamic_index_in_dim(feeds, group, 0, keepdims=False),
         ],
         0,
-    )
+    ).astype(bf16)
     momenta = lax.all_gather(owned, "seg", axis=0, tiled=False)
-    local_counts = jnp.sum(speech_mask, 1)
-    counts = lax.psum(local_counts, "seg")
-    weighting = speech_mask.astype(f32) / counts.astype(f32)[:, None]
+    frames_t = jnp.swapaxes(frames, 1, 2)
     bias = jnp.where(segment > 0, 0.0, -1e30).astype(f32)[None]
-    hidden = jnp.dot(frames, in_copy, preferred_element_type=f32) + outer_vectors[0]
-    memory = (jnp.dot(behind, in_copy, preferred_element_type=f32) + outer_vectors[0]).astype(bf16)
-    memory = [memory[stream] for stream in range(streams)]
+    hidden, memory, totals = embed(count, frames_t, speech_mask, in_copy, outer_vectors)
+    memory = [memory] * streams
     kept = []
     for depth in range(LAYERS):
         saved, passed = None, []
         for stream in range(streams):
             saved, short = forward_layer(
+                depth,
                 stream,
                 streams,
                 bias,
                 hidden,
                 memory[stream],
-                attn_copy[depth],
-                up_copy[depth],
-                down_copy[depth],
-                layer_vectors[depth],
+                attn_copy,
+                up_copy,
+                down_copy,
+                layer_vectors,
                 saved,
             )
             if depth + 1 < LAYERS:
                 passed.append(from_behind(short, "seg", 1))
-        kept.append((hidden, jnp.stack(memory), saved))
+        kept.append((hidden, memory[0] if depth == 0 else jnp.stack(memory), saved))
         hidden = saved[0]
         memory = passed
-    grad_hidden, grad_out, head_outer, loss_here = head(
-        hidden, targets, weighting, out_copy, outer_vectors, 1.0 / stream_total
+    grad_hidden, grad_out, head_outer = head(
+        hidden, targets, speech_mask, totals, out_copy, outer_vectors, 1.0 / stream_total, momenta
     )
-    loss_here = loss_here[0, 0]
+    grad_out = lax.psum(grad_out, ("seg", "dp"))
     attn_grads, up_grads, down_grads, vector_grads = ([], [], [], [])
     for depth in reversed(range(LAYERS)):
         entering, held, saved = kept[depth]
         dafter, grad_up, grad_down, feed_vec = feed_back(
-            grad_hidden, saved[7], up_copy[depth], down_copy[depth], layer_vectors[depth]
+            depth, grad_hidden, saved[7], up_copy, down_copy, layer_vectors
         )
-        grad_hidden, grad_attn, attn_vec = attend_back(
-            bias, dafter, entering, held, saved[1:7], attn_copy[depth], layer_vectors[depth]
+        grad_hidden, grad_attn, attn_vec, grad_in = attend_back(
+            depth, bias, dafter, entering, held, saved[1:7], attn_copy, layer_vectors, frames_t
         )
         attn_grads.insert(0, grad_attn)
         up_grads.insert(0, grad_up)
         down_grads.insert(0, grad_down)
-        vector_grads.insert(
-            0,
-            jnp.concatenate([attn_vec[0:2], feed_vec[0:2], attn_vec[2:5], feed_vec[2:3], feed_vec[4:8]], 0),
-        )
-    rows = grad_hidden.reshape(streams * SEG, D)
-    rows_high = rows.astype(bf16)
-    rows_rest = (rows - rows_high.astype(f32)).astype(bf16)
-    frame_rows = frames.reshape(streams * SEG, frames.shape[2])
-    grad_in = dot_tn(frame_rows, rows_high) + dot_tn(frame_rows, rows_rest)
-    grad_outer = jnp.concatenate([jnp.sum(rows, 0, keepdims=True), head_outer[1:5]], 0)
-    grad_vectors = jnp.stack(vector_grads)
-    grad_out = lax.psum(grad_out, ("seg", "dp"))
-    count, dp_count = lax.axis_size("seg"), lax.axis_size("dp")
-    rows = D // count
-    small = jnp.concatenate(
-        [
-            grad_in,
-            grad_vectors.reshape(-1, D),
-            grad_outer,
-            jnp.full((1, D), loss_here),
-            jnp.zeros((SMALL - 110, D), f32),
-        ],
-        0,
+        vector_grads = [attn_vec, feed_vec] + vector_grads
+    whole, every, small, squares = reduce_grads(
+        count, dp_count, attn_grads, up_grads, down_grads, [grad_in] + vector_grads + [head_outer]
     )
-    whole, every, small, squares = reduce_grads(count, dp_count, attn_grads, up_grads, down_grads, small)
-    grad_in, grad_vectors, grad_outer = small[0:80], small[80:104].reshape(layer_vectors.shape), small[104:109]
-    loss_sum = small[109, 0]
-    small_squares = (
-        jnp.sum(grad_in * grad_in)
-        + jnp.sum(grad_out * grad_out)
-        + jnp.sum(grad_vectors * grad_vectors)
-        + jnp.sum(grad_outer * grad_outer)
-    )
-    grad_norm = jnp.sqrt(squares[0, 0] + small_squares)
-    clip = jnp.minimum(1.0, 0.25 / (grad_norm + 1e-06))
+    loss_sum = small[grad_in.shape[0] + 37, 0]
     plane, core = segment // 2, segment % 2
     kind = jnp.where(plane == count // 4 - 1, 1, jnp.where(plane == count // 4, 2, 0))
     role = jnp.stack([kind, core, (group >= 2).astype(jnp.int32), core]).astype(jnp.int32)
-    made = muon(role, clip[None], whole, momenta)
+    made, norm = muon(role, squares, grad_out, whole, momenta)
     updates = spread(count, made)
-
-    def arranged(blocks):
-        attn_part = jnp.swapaxes(blocks[:, 0:2], 0, 1)
-        up_part = jnp.swapaxes(blocks[0:2, 2:6], 1, 2).reshape(ff_up.shape)
-        down_part = blocks[2:4, 2:6].reshape(ff_down.shape)
-        return attn_part.astype(f32), up_part.astype(f32), down_part.astype(f32)
-
-    attn_sum, up_sum, down_sum = arranged(every)
-    attn_mom = 0.5 * attn_momentum + clip * attn_sum
-    up_mom = 0.5 * up_momentum + clip * up_sum
-    down_mom = 0.5 * down_momentum + clip * down_sum
-    in_new, in_moment_new, in_second_new = adamw(
-        in_proj, in_moment, in_second, grad_in * clip, 0.05, 0.01
+    split = (LAYERS, 4, rows, D)
+    (
+        attn_new,
+        attn_mom,
+        attn_copy_new,
+        up_new,
+        up_mom,
+        up_copy_new,
+        down_new,
+        down_mom,
+        down_copy_new,
+        out_new,
+        out_moment_new,
+        out_second_new,
+        out_copy_new,
+        in_new,
+        in_moment_new,
+        in_second_new,
+        in_copy_new,
+        vectors_new,
+        vectors_moment_new,
+        vectors_second_new,
+        outer_new,
+        outer_moment_new,
+        outer_second_new,
+    ) = finish(
+        rows,
+        norm,
+        every,
+        updates,
+        grad_out,
+        small,
+        [
+            attn_proj,
+            attn_momentum,
+            ff_up,
+            up_momentum,
+            ff_down.reshape(split),
+            down_momentum.reshape(split),
+            out_proj,
+            out_moment,
+            out_second,
+            in_proj,
+            in_moment,
+            in_second,
+            layer_vectors,
+            vectors_moment,
+            vectors_second,
+            outer_vectors,
+            outer_moment,
+            outer_second,
+        ],
     )
-    out_new, out_moment_new, out_second_new = adamw(
-        out_proj, out_moment, out_second, grad_out * clip, 0.05, 0.01
-    )
-    vectors_new, vectors_moment_new, vectors_second_new = adamw(
-        layer_vectors, vectors_moment, vectors_second, grad_vectors * clip, 0.25, 0.0
-    )
-    outer_new, outer_moment_new, outer_second_new = adamw(
-        outer_vectors, outer_moment, outer_second, grad_outer * clip, 0.25, 0.0
-    )
-    attn_update, up_update, down_update = arranged(updates)
-    attn_new = attn_proj * (1.0 - 0.3 * 0.01) - 0.3 * attn_update
-    up_new = ff_up * (1.0 - 0.3 * 0.01) - 0.3 * max(1.0, FF / D) ** 0.5 * up_update
-    down_new = ff_down * (1.0 - 0.3 * 0.01) - 0.3 * max(1.0, D / FF) ** 0.5 * down_update
     return (
         loss_sum,
-        grad_norm,
+        norm[0, 0],
         in_new,
         in_moment_new,
         in_second_new,
@@ -1281,13 +1574,13 @@
         attn_mom,
         up_new,
         up_mom,
-        down_new,
-        down_mom,
-        in_new.astype(jnp.bfloat16),
-        out_new.astype(jnp.bfloat16),
-        attn_new.astype(jnp.bfloat16),
-        up_new.astype(jnp.bfloat16),
-        down_new.astype(jnp.bfloat16),
+        down_new.reshape(ff_down.shape),
+        down_mom.reshape(ff_down.shape),
+        in_copy_new,
+        out_copy_new,
+        attn_copy_new,
+        up_copy_new,
+        down_copy_new.reshape(ff_down.shape),
     )
 
 

time: 485 us -> 441 us (0.909)
  other arithmetic: 33.2 us -> 2.65 us
  Pallas kernels: 367 us -> 396 us
  local copies, waits for them, and re-layouts: 35.2 us -> 14.3 us
  blocking collectives: 10.2 us -> 0 us
  between operations: 21 us -> 14.8 us
    pallas_call x3 -> x5, Pallas kernels: 77.1 us -> 103 us  [the longest x2 73 us: attend_back(): pl.pallas_call(functools.partial(attend_back_kernel, depth == 0), grid=(s...]
    convert_element_type x6 -> x0, other arithmetic: 13.6 us -> none  [the longest x1 7.08 us: local(): out_new.astype(jnp.bfloat16)]
    squeeze x6 -> x0, local copies, waits for them, and re-layouts: 12.4 us -> none  [the longest x1 4.69 us: local(): down_copy[depth]]
    psum x1 -> x0, blocking collectives: 10.2 us -> none  [local(): counts = lax.psum(local_counts, 'seg')]
    reduce_sum x6 -> x0, other arithmetic: 8.94 us -> none  [the longest x1 2.73 us: local(): jnp.sum(grad_out * grad_out)]
    unnamed x71 -> x21, local copies, waits for them, and re-layouts: 10.9 us -> 7.89 us
  transfers between devices with their start and end apart: 5 -> 4, of which waited for: 0 -> 0; matrix products, arithmetic and copies ran while one was open for 12% -> 1% of each run, Pallas kernels for 54% -> 71%
where the time goes in v3:
time: 441 us; the launch traced here: 434 us
  Pallas kernels  396 us (90%)
  between operations  14.8 us (3%)
  local copies, waits for them, and re-layouts  14.3 us (3%)
  starting transfers between devices  5.99 us (1%)
    pallas_call x1, Pallas kernels, reduce_grads(): pl.pallas_call(functools.partial(reduce_kernel, count), out_shape=[jax.Sh...  107 us
    pallas_call x2, Pallas kernels, attend_back(): pl.pallas_call(functools.partial(attend_back_kernel, depth == 0), grid=(s...  73 us
    pallas_call x4, Pallas kernels, forward_layer(): pl.pallas_call(forward_kernel, grid=(1,), out_shape=out_shape, in_specs=i...  71.3 us
    pallas_call x1, Pallas kernels, spread(): pl.pallas_call(functools.partial(spread_kernel, count), out_shape=jax.Sha...  58 us
    pallas_call x2, Pallas kernels, feed_back(): pl.pallas_call(feed_back_kernel, grid=(streams,), out_shape=[jax.ShapeDty...  45.6 us
    pallas_call x1, Pallas kernels, finish(): pl.pallas_call(finish_kernel, grid=(steps,), out_shape=[like(attn), like(...  13.3 us
    pallas_call x1, Pallas kernels, embed(): pl.pallas_call(functools.partial(embed_kernel, count), out_shape=[jax.Sha...  12.1 us
    pallas_call x1, Pallas kernels, head(): pl.pallas_call(functools.partial(head_kernel, scale), grid=(streams,), ou...  10.7 us
  transfers between devices with their start and end apart: 4, of which 0 were waited for; matrix products, arithmetic and copies ran while one was open for 1% of the time, Pallas kernels for 71%

profile of v3, /device:TPU:0, one launch (start us, length us, event | category | flops | bytes accessed | tf_op | source)
XLA Modules:
  0.0 433.6 jit_solution(18279859344156682773)
XLA Ops:
  7.2 0.0 copy-start
  7.2 0.0 all-gather.2.cloned.1.call-start
  7.3 1.3 fusion.4
  8.6 0.2 reshape_squeeze.6
  8.8 0.2 reshape_squeeze.7
  9.0 0.1 fusion.5
  9.1 0.2 copy.120
  9.3 0.2 copy.121
  9.5 0.0 copy-start.3
  9.5 1.0 dynamic-slice_convert_fusion
  10.5 0.1 copy.137
  10.6 0.6 fusion.3
  11.3 0.3 pad_maximum_fusion.1
  11.5 0.9 copy.122
  12.4 0.0 all-gather.2.cloned.1.call-update
  12.4 0.0 all-reduce.2.cloned.1.call-start
  12.5 0.6 copy.116.vec_ref.refs_12_
  13.1 12.1 %embed.1 = (f32[2,512,512]{2,1,0:T(8,128)}, bf16[2,512,512]{2,1,0:T(8,128)(2,1)}, f32[8,128]{1,0:T(8,128)}) custom-call(bf16[2,80,512]{2,1,0:T(8,128)(2,1)} %bitcast.54, s32[2,512]{1,0:T(2,128)} %mask_ref.3, bf16[80,512]{1,0:T(8,128)(2,1)} %in_ref.1, f32[5,512]{1,0:T(8,128)} %refs_15_.1), custom_call_target="tpu_custom_call" | custom-call | flops 200000000 | bytes 4000000 | tf_op jit(solution)/shard_map/embed/pallas_call | solution.py:1194
  25.2 17.8 %layer_forward.4 = (f32[2,512,512]{2,1,0:T(8,128)}, bf16[512,512]{1,0:T(8,128)(2,1)}, bf16[2,1024,512]{2,1,0:T(8,128)(2,1)}, bf16[2,512,512]{2,1,0:T(8,128)(2,1)...) custom-call(f32[1]{0:T(128)} %bitcast.bias_ref, ...), custom_call_target="tpu_custom_call" | custom-call | flops 10000000000 | bytes 20000000 | tf_op jit(solution)/shard_map/layer_forward/pallas_call | solution.py:199
  43.0 2.2 collective-permute-start.1
  45.2 0.0 copy-start.4
  45.3 0.0 copy-start.5
  45.3 17.8 %layer_forward.5 = (f32[2,512,512]{2,1,0:T(8,128)}, bf16[512,512]{1,0:T(8,128)(2,1)}, bf16[2,1024,512]{2,1,0:T(8,128)(2,1)}, bf16[2,512,512]{2,1,0:T(8,128)(2,1)...) custom-call(f32[1]{0:T(128)} %bitcast.bias_ref, ...), custom_call_target="tpu_custom_call", output_to_operand_aliasing={{0}: (7, {}), {2}: (8, {}), {3}: (9, {}), {4}: (10, {}), {5... | custom-call | flops 10000000000 | bytes 20000000 | tf_op jit(solution)/shard_map/layer_forward/pallas_call | solution.py:199
  63.1 3.7 collective-permute-start
  66.8 0.7 slice_bitcast_fusion
  67.5 0.6 copy.134
  68.1 0.6 copy.128.refs_13_
  68.7 0.6 copy.129.refs_14_
  69.4 0.6 pad_add_fusion.role_ref
  70.0 1.2 pad_maximum_fusion.mem_ref
  71.2 17.9 %layer_forward.6 = (f32[2,512,512]{2,1,0:T(8,128)}, bf16[512,512]{1,0:T(8,128)(2,1)}, bf16[2,1024,512]{2,1,0:T(8,128)(2,1)}, bf16[2,512,512]{2,1,0:T(8,128)(2,1)...) custom-call(f32[1]{0:T(128)} %bitcast.bias_ref, ...), custom_call_target="tpu_custom_call" | custom-call | flops 10000000000 | bytes 20000000 | tf_op jit(solution)/shard_map/layer_forward/pallas_call | solution.py:199
  89.1 17.8 %layer_forward.7 = (f32[2,512,512]{2,1,0:T(8,128)}, bf16[512,512]{1,0:T(8,128)(2,1)}, bf16[2,1024,512]{2,1,0:T(8,128)(2,1)}, bf16[2,512,512]{2,1,0:T(8,128)(2,1)...) custom-call(f32[1]{0:T(128)} %bitcast.bias_ref, ...), custom_call_target="tpu_custom_call", output_to_operand_aliasing={{0}: (7, {}), {2}: (8, {}), {3}: (9, {}), {4}: (10, {}), {5... | custom-call | flops 10000000000 | bytes 20000000 | tf_op jit(solution)/shard_map/layer_forward/pallas_call | solution.py:199
  106.9 0.0 all-gather.2.cloned.1.call-done.mom_ref
  106.9 10.7 %head.1 = (f32[2,512,512]{2,1,0:T(8,128)}, f32[512,1024]{1,0:T(8,128)}, f32[8,512]{1,0:T(8,128)}) custom-call(f32[2,512,512]{2,1,0:T(8,128)} %get-tuple-element.129.x_ref, s32[2,512]{1,0:T(2,128)} %target_ref.1, s32[2,512]{1,0:T(2,128)} %mask_ref.3, f32[8,128]{1,0:T(8,128)} %get-tuple-element.130.total_ref, bf16[512,1024]{1,0:T(8,128)(2,1)} %out_ref.1, ...), custom_call_target="tpu_custom_call" | custom-call | flops 3300000000 | bytes 10000000 | tf_op jit(solution)/shard_map/head/pallas_call | solution.py:257
  117.7 0.0 all-reduce.2.cloned.1.call-update
  117.7 22.7 %feed_back.2 = (f32[2,512,512]{2,1,0:T(8,128)}, bf16[4,512,512]{2,1,0:T(8,128)(2,1)}, bf16[2048,512]{1,0:T(8,128)(2,1)}, f32[8,512]{1,0:T(8,128)}) custom-call(f32[2,512,512]{2,1,0:T(8,128)} %get-tuple-element.131.g_ref, f32[2,512,512]{2,1,0:T(8,128)} %get-tuple-element.132.after_ref, bf16[2,512,2048]{2,1,0:T(8,128)(2,1)} %up_ref.11, ...), custom_call_target="tpu_custom_call" | custom-call | flops 11000000512 | bytes 20000000 | tf_op jit(solution)/shard_map/feed_back/pallas_call | solution.py:328
  140.4 36.2 %attend_back.2 = (f32[2,512,512]{2,1,0:T(8,128)}, bf16[4,512,512]{2,1,0:T(8,128)(2,1)}, f32[8,512]{1,0:T(8,128)}, f32[80,512]{1,0:T(8,128)}) custom-call(f32[1]{0:T(128)} %bitcast.bias_ref, f32[2,512,512]{2,1,0:T(8,128)} %get-tuple-element.133.dafter_ref, f32[2,512,512]{2,1,0:T(8,128)} %get-tuple-element.118.x_ref, ...), custom_call_target="tpu_custom_call" | custom-call | flops 30000001024 | bytes 20000000 | tf_op jit(solution)/shard_map/attend_back/pallas_call | solution.py:493
  176.6 22.9 %feed_back.3 = (f32[2,512,512]{2,1,0:T(8,128)}, bf16[4,512,512]{2,1,0:T(8,128)(2,1)}, bf16[2048,512]{1,0:T(8,128)(2,1)}, f32[8,512]{1,0:T(8,128)}) custom-call(f32[2,512,512]{2,1,0:T(8,128)} %get-tuple-element.140.g_ref, f32[2,512,512]{2,1,0:T(8,128)} %get-tuple-element.141.after_ref, bf16[2,512,2048]{2,1,0:T(8,128)(2,1)} %up_ref.11, ...), custom_call_target="tpu_custom_call" | custom-call | flops 11000000512 | bytes 20000000 | tf_op jit(solution)/shard_map/feed_back/pallas_call | solution.py:328
  199.5 36.8 %attend_back.3 = (f32[2,512,512]{2,1,0:T(8,128)}, bf16[4,512,512]{2,1,0:T(8,128)(2,1)}, f32[8,512]{1,0:T(8,128)}, f32[80,512]{1,0:T(8,128)}) custom-call(f32[1]{0:T(128)} %bitcast.bias_ref, f32[2,512,512]{2,1,0:T(8,128)} %get-tuple-element.142.dafter_ref, f32[2,512,512]{2,1,0:T(8,128)} %get-tuple-element.108.x_ref, ...), custom_call_target="tpu_custom_call" | custom-call | flops 30000001024 | bytes 20000000 | tf_op jit(solution)/shard_map/attend_back/pallas_call | solution.py:493
  236.3 107.1 %reduce_grads.1 = (bf16[8,4,64,512]{3,2,1,0:T(8,128)(2,1)}, bf16[4,6,64,512]{3,2,1,0:T(8,128)(2,1)}, f32[128,512]{1,0:T(8,128)}, f32[8,128]{1,0:T(8,128)}) custom-call(bf16[2,2,8,64,512]{4,3,2,1,0:T(8,128)(2,1)} %bitcast.41, bf16[2,2,8,64,512]{4,3,2,1,0:T(8,128)(2,1)} %bitcast.38, bf16[4,8,64,512]{3,2,1,0:T(8,128)(2,1)} %bitcast.39, ...), custom_call_target="tpu_custom_call" | custom-call | flops 100000000 | bytes 200000000 | tf_op jit(solution)/shard_map/reduce_grads/pallas_call | solution.py:894
  343.4 1.2 slice.26
  344.6 4.7 %muon.1 = (bf16[8,2,64,512]{3,2,1,0:T(8,128)(2,1)}, f32[8,128]{1,0:T(8,128)}) custom-call(s32[4]{0:T(128)} %pad_add_fusion.role_ref, f32[8,128]{1,0:T(8,128)} %get-tuple-element.162.square_ref, f32[512,1024]{1,0:T(8,128)} %all-reduce.2.cloned.1.call-done.dout_ref, bf16[8,4,64,512]{3,2,1,0:T(8,128)(2,1)} %get-tuple-element.164.whole_ref, ...), custom_call_target="tpu_custom_call" | custom-call | flops 20000000000 | bytes 10000000 | tf_op jit(solution)/shard_map/muon/pallas_call | solution.py:1068
  349.3 58.0 %spread.1.update_ref = bf16[4,6,64,512]{3,2,1,0:T(8,128)(2,1)} custom-call(bf16[8,2,64,512]{3,2,1,0:T(8,128)(2,1)} %get-tuple-element.167.made_ref), custom_call_target="tpu_custom_call" | custom-call | flops 1000000 | bytes 40000000 | tf_op jit(solution)/shard_map/spread/pallas_call | solution.py:1136
  407.4 1.2 slice.27
  408.6 13.3 %finish.1 = (f32[2,4,64,512]{3,2,1,0:T(8,128)}, f32[2,4,64,512]{3,2,1,0:T(8,128)}, bf16[2,4,64,512]{3,2,1,0:T(8,128)(2,1)}, f32[2,64,2048]{2,1,0:T(8,128)}, f32[...) custom-call(f32[8,128]{1,0:T(8,128)} %get-tuple-element.165.norm_ref, ...), custom_call_target="tpu_custom_call" | custom-call | flops 100000000 | bytes 40000000 | tf_op jit(solution)/shard_map/finish/pallas_call | solution.py:1370
  421.9 1.5 copy.130
  423.4 1.5 copy.131
  424.8 1.5 copy.132
  (11 shorter events, 0.0 us)
Async XLA Ops:
  7.2 1.8 copy-start
  7.2 99.7 %all-gather.2.cloned.1.call-start = ((), (), s32[]{:S(2)}) async-start(), calls=%async_computation | async-start | bytes 3538944 | tf_op jit(solution)/shard_map/all_gather | solution.py:1452
  9.5 3.0 copy-start.3
  12.4 332.2 %all-reduce.2.cloned.1.call-start = ((), (), s32[]{:S(2)}) async-start(), calls=%async_computation.1 | async-start | bytes 4194304 | tf_op jit(solution)/shard_map/psum | solution.py:1482
  43.0 27.0 %collective-permute-start.1 = (bf16[512,512]{1,0:T(8,128)(2,1)}, bf16[512,512]{1,0:T(8,128)(2,1)S(1)}, u32[]{:S(2)}, u32[]{:S(2)}) collective-permute-start(bf16[512,512]{1,0:T(8,128)(2,1)} %get-tuple-element.120), channel_id=1, source_target_pairs={{0,4},{4,8},{8,12},{12,16},{16,20},{20,24},{24,28},{1,5},{5,9},{9,... | collective-permute-start | bytes 1572872 | tf_op jit(solution)/shard_map/ppermute | solution.py:541
  45.2 22.9 %copy-start.4 = (f32[2,12,512]{2,0,1:T(2,128)S(1)}, f32[2,12,512]{2,0,1:T(2,128)}, u32[]{:S(2)}) copy-start(f32[2,12,512]{2,0,1:T(2,128)} %param.36) | copy-start | bytes 147460
  45.3 23.5 %copy-start.5 = (f32[2,12,512]{2,0,1:T(2,128)S(1)}, f32[2,12,512]{2,0,1:T(2,128)}, u32[]{:S(2)}) copy-start(f32[2,12,512]{2,0,1:T(2,128)} %param.37) | copy-start | bytes 147460
  63.1 6.9 %collective-permute-start = (bf16[512,512]{1,0:T(8,128)(2,1)}, bf16[512,512]{1,0:T(8,128)(2,1)S(1)}, u32[]{:S(2)}, u32[]{:S(2)}) collective-permute-start(bf16[512,512]{1,0:T(8,128)(2,1)} %get-tuple-element.119), channel_id=1, source_target_pairs={{0,4},{4,8},{8,12},{12,16},{16,20},{20,24},{24,28},{1,5},{5,9},{9,... | collective-permute-start | bytes 1572872 | tf_op jit(solution)/shard_map/ppermute | solution.py:541
  70.0 1.2 copy-start.1
  70.0 19.1 %copy-start.2 = (bf16[512,512]{1,0:T(8,128)(2,1)}, bf16[512,512]{1,0:T(8,128)(2,1)S(1)}, u32[]{:S(2)}) copy-start(bf16[512,512]{1,0:T(8,128)(2,1)S(1)} %collective-permute-done.mem_ref) | copy-start | bytes 1572868
Sparse Core Ops, SparseCore 0:
  12.5 40.9 all-gather.1
  117.8 138.6 all-reduce.1

commit v4 on v3

--- a/solution.py
+++ b/solution.py
@@ -280,8 +280,21 @@
     )(hidden, targets, mask, totals, out_weight, outer_vectors, bias, momenta)
 
 
-def feed_back_kernel(g_ref, after_ref, up_ref, down_ref, vec_ref, dafter_ref, dup_ref, ddown_ref, dvec_ref, up_s, down_s, act_s, inner_s):
+def feed_back_kernel(streams, carried, g_ref, after_ref, up_ref, down_ref, vec_ref, *refs):
     step = pl.program_id(0)
+    tiles = FF // TILE
+    if carried:
+        grad_ref, refs = refs[0], refs[1:]
+        dafter_ref, dup_ref, ddown_ref, dvec_ref, done_ref, up_s, down_s, act_s, inner_s = refs[:9]
+        carry = AttnCarry(grad_ref, refs[9 : 9 + CARRY_REFS], refs[9 + CARRY_REFS :])
+
+        @pl.when(step == 0)
+        def _():
+            hail(carry.targets)
+            carry.load_all()
+
+    else:
+        dafter_ref, dup_ref, ddown_ref, dvec_ref, up_s, down_s, act_s, inner_s = refs
 
     @pl.when(step == 0)
     def _():
@@ -307,6 +320,15 @@
         dinner = (dact * slope).astype(bf16)
         inner_s[:, columns] = dinner
         dvec_ref[4 + tile : 5 + tile, :] += column_sum(dinner.astype(f32))
+        if carried:
+            if tile == 0:
+
+                @pl.when(step == 0)
+                def _():
+                    meet(carry.targets)
+                    carry.send_all()
+
+            carry.tick(tiles * step + tile - 1)
     dnormed = dot_nt(inner_s[...], up_ref[...])
     dvec_ref[0:1, :] += column_sum(dnormed * unit)
     dvec_ref[1:2, :] += column_sum(dnormed)
@@ -321,46 +343,66 @@
         for tile in range(FF // TILE):
             dup_ref[tile] = up_s[:, tile * TILE : (tile + 1) * TILE].astype(bf16)
         ddown_ref[...] = jnp.transpose(down_s[...].astype(bf16))
-
-
-def feed_back(depth, grad, after, upper, lower, vectors):
+        if carried:
+            for time in range(tiles * streams - 1, carry.planes + 2):
+                carry.tick(time)
+            carry.finish(done_ref)
+
+
+def feed_back(depth, grad, after, upper, lower, vectors, count, dp_count, attn_grad=None):
     streams = grad.shape[0]
+    rows = D // count
+    carried = attn_grad is not None
+    in_specs = [
+        stream_spec((SEG, D)),
+        stream_spec((SEG, D)),
+        layer_spec(upper.shape[1:], depth),
+        layer_spec(lower.shape[1:], depth),
+        layer_spec(vectors.shape[1:], depth),
+    ]
+    out_shape = [
+        jax.ShapeDtypeStruct((streams, SEG, D), f32),
+        jax.ShapeDtypeStruct((FF // TILE, D, TILE), bf16),
+        jax.ShapeDtypeStruct((FF, D), bf16),
+        jax.ShapeDtypeStruct((8, D), f32),
+    ]
+    out_specs = [
+        stream_spec((SEG, D)),
+        whole_spec((FF // TILE, D, TILE)),
+        whole_spec((FF, D)),
+        whole_spec((8, D)),
+    ]
+    scratch = [
+        pltpu.VMEM((D, FF), f32),
+        pltpu.VMEM((D, FF), f32),
+        pltpu.VMEM((SEG, FF), bf16),
+        pltpu.VMEM((SEG, FF), bf16),
+    ]
+    operands = [grad, after, upper, lower, vectors]
+    params = {}
+    if carried:
+        in_specs.append(pl.BlockSpec(memory_space=pl.ANY))
+        operands.append(attn_grad.reshape(2, 2, count, rows, D))
+        out_shape.append(jax.ShapeDtypeStruct((rows, D), bf16))
+        out_specs.append(whole_spec((rows, D)))
+        scratch = scratch + carry_scratch("attn", count, dp_count)
+        params = {"collective_id": 6, "has_side_effects": True}
     return pl.pallas_call(
-        feed_back_kernel,
+        functools.partial(feed_back_kernel, streams, carried),
         grid=(streams,),
-        out_shape=[
-            jax.ShapeDtypeStruct((streams, SEG, D), f32),
-            jax.ShapeDtypeStruct((FF // TILE, D, TILE), bf16),
-            jax.ShapeDtypeStruct((FF, D), bf16),
-            jax.ShapeDtypeStruct((8, D), f32),
-        ],
-        in_specs=[
-            stream_spec((SEG, D)),
-            stream_spec((SEG, D)),
-            layer_spec(upper.shape[1:], depth),
-            layer_spec(lower.shape[1:], depth),
-            layer_spec(vectors.shape[1:], depth),
-        ],
-        out_specs=[
-            stream_spec((SEG, D)),
-            whole_spec((FF // TILE, D, TILE)),
-            whole_spec((FF, D)),
-            whole_spec((8, D)),
-        ],
-        scratch_shapes=[
-            pltpu.VMEM((D, FF), f32),
-            pltpu.VMEM((D, FF), f32),
-            pltpu.VMEM((SEG, FF), bf16),
-            pltpu.VMEM((SEG, FF), bf16),
-        ],
-        compiler_params=pltpu.CompilerParams(vmem_limit_bytes=VMEM_LIMIT),
+        out_shape=out_shape,
+        in_specs=in_specs,
+        out_specs=out_specs,
+        scratch_shapes=scratch,
+        compiler_params=pltpu.CompilerParams(vmem_limit_bytes=VMEM_LIMIT, **params),
         cost_estimate=pl.CostEstimate(flops=11 * 10**9, bytes_accessed=2 * 10**7, transcendentals=2 * 10**6),
         name="feed_back",
-    )(grad, after, upper, lower, vectors)
+    )(*operands)
 
 
 def attend_back_kernel(
-    lowest,
+    streams,
+    depth,
     bias_ref,
     dafter_ref,
     x_ref,
@@ -374,10 +416,13 @@
     attn_ref,
     vec_ref,
     frames_ref,
+    dup_ref,
+    ddown_ref,
     dx_ref,
     dattn_ref,
     dvec_ref,
     din_ref,
+    done_ref,
     attn_s,
     dmixed_s,
     dq_s,
@@ -385,11 +430,16 @@
     dv_s,
     ds_s,
     delta_s,
+    *refs,
 ):
     step = pl.program_id(0)
+    pairs = HEADS // 2
+    carry = FeedCarry(depth, dup_ref, ddown_ref, refs[:CARRY_REFS], refs[CARRY_REFS:])
 
     @pl.when(step == 0)
     def _():
+        hail(carry.targets)
+        carry.load_all()
         attn_s[...] = jnp.zeros_like(attn_s)
         dvec_ref[...] = jnp.zeros_like(dvec_ref)
         din_ref[...] = jnp.zeros_like(din_ref)
@@ -413,7 +463,12 @@
     diagonal = key_pos <= query_pos
     head_row = lax.broadcasted_iota(jnp.int32, (PAIR, HALF), 0)
 
-    def pair_body(pair, carry):
+    @pl.when(step == 0)
+    def _():
+        meet(carry.targets)
+        carry.send_all()
+
+    def pair_body(pair, state):
         lanes = pair_lanes(pair)
         q_pair, do_pair = q_ref[:, lanes], dmixed_s[:, lanes]
 
@@ -455,9 +510,10 @@
             dq_s[block * HALF : (block + 1) * HALF, lanes] = (
                 jnp.transpose(grads) * (HEAD_DIM**-0.5)
             ).astype(bf16)
-        return carry
-
-    lax.fori_loop(0, HEADS // 2, pair_body, 0)
+        carry.tick(pairs * step + pair)
+        return state
+
+    lax.fori_loop(0, pairs, pair_body, 0)
     dq, dk, dv = dq_s[...], dk_s[...], dv_s[...]
     keyin_t = jnp.transpose(keyin_ref[...])
     attn_s[0] += dot_nn(keyin_t[:, SEG:], dq)
@@ -475,7 +531,7 @@
     dvec_ref[1:2, :] += column_sum(down + dmem)
     dx = dafter + norm_back(down, gain, unit, scale)
     dx_ref[...] = dx
-    if lowest:
+    if depth == 0:
         dx_high = dx.astype(bf16)
         dx_rest = (dx - dx_high.astype(f32)).astype(bf16)
         din_ref[...] += dot_nn(frames_ref[...], dx_high) + dot_nn(frames_ref[...], dx_rest)
@@ -484,20 +540,26 @@
     @pl.when(step == pl.num_programs(0) - 1)
     def _():
         dattn_ref[...] = attn_s[...].astype(bf16)
-
-
-def attend_back(depth, bias, dafter, x, memory, saved, attn, vectors, frames):
+        for time in range(pairs * streams, carry.planes + 2):
+            carry.tick(time)
+        carry.finish(done_ref)
+
+
+def attend_back(depth, bias, dafter, x, memory, saved, attn, vectors, frames, up_grad, down_grad, count, dp_count):
     streams = dafter.shape[0]
     keyin, q, k, v, lse, mixed = saved
     inputs = frames.shape[1]
+    rows = D // count
+    up_grad, down_grad = up_grad.reshape(4, count, rows, D), down_grad.reshape(count, 4, rows, D)
     return pl.pallas_call(
-        functools.partial(attend_back_kernel, depth == 0),
+        functools.partial(attend_back_kernel, streams, depth),
         grid=(streams,),
         out_shape=[
             jax.ShapeDtypeStruct((streams, SEG, D), f32),
             jax.ShapeDtypeStruct((4, D, D), bf16),
             jax.ShapeDtypeStruct((8, D), f32),
             jax.ShapeDtypeStruct((inputs, D), f32),
+            jax.ShapeDtypeStruct((4, rows, D), bf16),
         ],
         in_specs=[
             pl.BlockSpec(memory_space=pltpu.SMEM),
@@ -513,12 +575,15 @@
             layer_spec(attn.shape[1:], depth),
             layer_spec(vectors.shape[1:], depth),
             stream_spec((inputs, SEG)),
+            pl.BlockSpec(memory_space=pl.ANY),
+            pl.BlockSpec(memory_space=pl.ANY),
         ],
         out_specs=[
             stream_spec((SEG, D)),
             whole_spec((4, D, D)),
             whole_spec((8, D)),
             whole_spec((inputs, D)),
+            whole_spec((4, rows, D)),
         ],
         scratch_shapes=[
             pltpu.VMEM((4, D, D), f32),
@@ -528,11 +593,14 @@
             pltpu.VMEM((2 * SEG, D), bf16),
             pltpu.VMEM((2 * SEG, 2 * SEG), bf16),
             pltpu.VMEM((HEADS, SEG), f32),
-        ],
-        compiler_params=pltpu.CompilerParams(vmem_limit_bytes=VMEM_LIMIT),
+        ]
+        + carry_scratch("feed", count, dp_count),
+        compiler_params=pltpu.CompilerParams(
+            collective_id=4 + depth, has_side_effects=True, vmem_limit_bytes=VMEM_LIMIT
+        ),
         cost_estimate=pl.CostEstimate(flops=3 * 10**10, bytes_accessed=2 * 10**7, transcendentals=10**7),
         name="attend_back",
-    )(bias, dafter, x, memory, keyin, q, k, v, lse, mixed, attn, vectors, frames)
+    )(bias, dafter, x, memory, keyin, q, k, v, lse, mixed, attn, vectors, frames, up_grad, down_grad)
 
 
 def from_behind(value, axis, steps):
@@ -575,12 +643,20 @@
     return [lax.rem(seg + step, count) for step in range(1, count)]
 
 
-def greet(seg, count, near, far):
+def hail(targets):
     barrier = pltpu.get_barrier_semaphore()
-    targets = [{"seg": other} for other in others(seg, count)] + list(near) + list(far)
     for target in targets:
         pl.semaphore_signal(barrier, inc=1, device_id=target, device_id_type=pl.DeviceIdType.MESH)
-    pl.semaphore_wait(barrier, len(targets))
+
+
+def meet(targets):
+    pl.semaphore_wait(pltpu.get_barrier_semaphore(), len(targets))
+
+
+def greet(seg, count, near, far):
+    targets = [{"seg": other} for other in others(seg, count)] + list(near) + list(far)
+    hail(targets)
+    meet(targets)
 
 
 def remote(source, target, send, recv, device):
@@ -612,14 +688,286 @@
     )
 
 
+class Carry:
+    def __init__(self, refs, sems):
+        self.mine, self.got0, self.got1, self.got2, self.got3, self.goth = refs
+        (
+            self.load,
+            self.send0,
+            self.recv0,
+            self.send1,
+            self.recv1,
+            self.send2,
+            self.recv2,
+            self.send3,
+            self.recv3,
+            self.sendh,
+            self.recvh,
+        ) = sems
+        self.seg, self.dp, self.core, self.x, self.y, self.across_core, near, self.far = peers()
+        self.across_x, self.across_y, _ = near
+        self.planes = self.mine.shape[0]
+        self.plane = self.seg // 2
+        self.targets = [self.across_core, self.across_x, self.across_y] + self.far
+        for step in range(1, self.planes):
+            self.targets.append({"seg": 2 * lax.rem(self.plane + step, self.planes) + self.core})
+
+    def block(self, step):
+        return lax.rem(self.plane + 1 + step, self.planes)
+
+    def load_all(self):
+        for step in range(self.planes):
+            for source, place in self.pieces(2 * self.block(step) + self.core):
+                pltpu.make_async_copy(source, self.mine.at[(step,) + place], self.load.at[step]).start()
+
+    def send_all(self):
+        for step in range(self.planes):
+            for source, place in self.pieces(2 * self.block(step) + 1 - self.core):
+                remote(
+                    source, self.got0.at[(step,) + place], self.send0.at[step], self.recv0.at[step], self.across_core
+                ).start()
+
+    def begin(self, step):
+        wait_bytes(self.mine.at[step], self.load.at[step])
+        wait_bytes(self.got0.at[step], self.recv0.at[step])
+        for place in range(2):
+            self.mine[step, place] = plus(self.mine[step, place], self.got0[step, place])
+        for copy in self.first(step):
+            copy.start()
+
+    def across(self, place, step):
+        return remote(
+            self.held(step),
+            self.goth.at[place, step],
+            self.sendh.at[place, step],
+            self.recvh.at[place, step],
+            self.far[place],
+        )
+
+    def third(self, step):
+        return remote(
+            self.held(step),
+            self.got3.at[self.plane],
+            self.send3.at[step],
+            self.recv3.at[self.plane],
+            {"seg": 2 * self.block(step) + self.core},
+        )
+
+    def onward(self, step):
+        for place in range(len(self.far)):
+            copy = self.across(place, step)
+            copy.start()
+            copy.wait()
+            held = self.held(step)
+            held[...] = plus(held[...], self.goth[place, step])
+
+        @pl.when(step < self.planes - 1)
+        def _():
+            self.third(step).start()
+
+    def total(self):
+        value = self.held(self.planes - 1)[...].astype(f32)
+        for step in range(1, self.planes):
+            sender = lax.rem(self.plane + step, self.planes)
+            wait_bytes(self.got3.at[sender], self.recv3.at[sender])
+            value = value + self.got3[sender].astype(f32)
+        return value
+
+    def tick(self, time):
+        planes = self.planes
+
+        @pl.when((time >= 0) & (time < planes))
+        def _():
+            self.begin(time)
+
+        @pl.when((time >= 1) & (time < planes + 1))
+        def _():
+            self.middle(time - 1)
+
+        @pl.when((time >= 2) & (time < planes + 2))
+        def _():
+            self.end(time - 2)
+
+
+class AttnCarry(Carry):
+    def __init__(self, source, refs, sems):
+        super().__init__(refs, sems)
+        self.source = source
+
+    def pieces(self, row):
+        return ((self.source.at[:, :, row], ()),)
+
+    def held(self, step):
+        return self.mine.at[step, self.y, self.x]
+
+    def first(self, step):
+        return (
+            remote(
+                self.mine.at[step, :, 1 - self.x],
+                self.got1.at[step],
+                self.send1.at[step],
+                self.recv1.at[step],
+                self.across_x,
+            ),
+        )
+
+    def second(self, step):
+        return remote(
+            self.mine.at[step, 1 - self.y, self.x],
+            self.got2.at[step],
+            self.send2.at[step],
+            self.recv2.at[step],
+            self.across_y,
+        )
+
+    def middle(self, step):
+        for copy in self.first(step):
+            copy.wait_recv()
+        for place in range(2):
+            self.mine[step, place, self.x] = plus(self.mine[step, place, self.x], self.got1[step, place])
+        self.second(step).start()
+
+    def end(self, step):
+        self.second(step).wait_recv()
+        self.mine[step, self.y, self.x] = plus(self.mine[step, self.y, self.x], self.got2[step])
+        self.onward(step)
+
+    def finish(self, out_ref):
+        value = self.total()
+        out_ref[...] = value.astype(bf16)
+        self.drain()
+
+    def drain(self):
+        for step in range(self.planes):
+            wait_bytes(self.mine.at[step], self.send0.at[step])
+            for copy in self.first(step):
+                copy.wait_send()
+            self.second(step).wait_send()
+            if step < self.planes - 1:
+                self.third(step).wait_send()
+
+
+class FeedCarry(Carry):
+    def __init__(self, depth, up, down, refs, sems):
+        super().__init__(refs, sems)
+        self.up, self.down = up, down
+        self.owner = (self.x == self.y) if depth == 1 else (self.x != self.y)
+        self.keep = self.x if depth == 1 else 1 - self.x
+
+    def pieces(self, row):
+        return ((self.up.at[:, row], (0,)), (self.down.at[row], (1,)))
+
+    def held(self, step):
+        return self.mine.at[step, self.y]
+
+    def first(self, step):
+        return (
+            remote(
+                self.mine.at[step, 1 - self.keep, 0:2],
+                self.got1.at[step, 0],
+                self.send1.at[step, 0],
+                self.recv1.at[step, 0],
+                self.across_x,
+            ),
+            remote(
+                self.mine.at[step, 1 - self.y, 2:4],
+                self.got1.at[step, 1],
+                self.send1.at[step, 1],
+                self.recv1.at[step, 1],
+                self.across_y,
+            ),
+        )
+
+    def second(self, step):
+        return (
+            remote(
+                self.mine.at[step, self.keep, 0:2],
+                self.got2.at[step, 0],
+                self.send2.at[step, 0],
+                self.recv2.at[step, 0],
+                self.across_y,
+            ),
+            remote(
+                self.mine.at[step, self.y, 2:4],
+                self.got2.at[step, 1],
+                self.send2.at[step, 1],
+                self.recv2.at[step, 1],
+                self.across_x,
+            ),
+        )
+
+    def middle(self, step):
+        for copy in self.first(step):
+            copy.wait_recv()
+        self.mine[step, self.keep, 0:2] = plus(self.mine[step, self.keep, 0:2], self.got1[step, 0])
+        self.mine[step, self.y, 2:4] = plus(self.mine[step, self.y, 2:4], self.got1[step, 1])
+
+        @pl.when(jnp.logical_not(self.owner))
+        def _():
+            for copy in self.second(step):
+                copy.start()
+
+    def end(self, step):
+        @pl.when(self.owner)
+        def _():
+            for place in range(2):
+                wait_bytes(self.got2.at[step, place], self.recv2.at[step, place])
+                span = slice(2 * place, 2 * place + 2)
+                self.mine[step, self.y, span] = plus(self.mine[step, self.y, span], self.got2[step, place])
+            self.onward(step)
+
+    def finish(self, out_ref):
+        @pl.when(self.owner)
+        def _():
+            out_ref[...] = self.total().astype(bf16)
+            for step in range(self.planes - 1):
+                self.third(step).wait_send()
+
+        @pl.when(jnp.logical_not(self.owner))
+        def _():
+            out_ref[...] = jnp.zeros_like(out_ref)
+            for step in range(self.planes):
+                for copy in self.second(step):
+                    copy.wait_send()
+
+        for step in range(self.planes):
+            wait_bytes(self.mine.at[step], self.send0.at[step])
+            for copy in self.first(step):
+                copy.wait_send()
+
+
+CARRY_REFS = 6
+CARRY_SEMS = 11
+
+
+def carry_scratch(kind, count, dp_count):
+    rows, planes = D // count, count // 2
+    far = max(1, dp_count.bit_length() - 3)
+    dma = pltpu.SemaphoreType.DMA
+    if kind == "attn":
+        shapes = ((planes, 2, 2), (planes, 2, 2), (planes, 2), (planes,), (planes,), (far, planes))
+        pair = (planes,)
+    else:
+        shapes = (
+            (planes, 2, 4),
+            (planes, 2, 4),
+            (planes, 2, 2),
+            (planes, 2, 2),
+            (planes, 4),
+            (far, planes, 4),
+        )
+        pair = (planes, 2)
+    one = (planes,)
+    sems = (one, one, one, pair, pair, pair, pair, one, one, (far, planes), (far, planes))
+    return [pltpu.VMEM(shape + (rows, D), bf16) for shape in shapes] + [dma(shape) for shape in sems]
+
+
 def reduce_kernel(
     count,
-    attn0,
-    attn1,
-    up0,
-    up1,
-    down0,
-    down1,
+    attn_grad_ref,
+    attn_done_ref,
+    feed_low_ref,
+    feed_high_ref,
     din_ref,
     vec0_ref,
     vec1_ref,
@@ -627,36 +975,17 @@
     vec3_ref,
     outer_ref,
     whole_ref,
-    every_ref,
+    own_ref,
     small_out,
     square_out,
-    mine,
-    got0,
-    got1,
-    got2,
-    got3,
-    goth,
     small_ref,
     small_core,
     small_s,
     small_got,
     sq_seg,
     sq_dp,
-    load_sem,
-    send0,
-    recv0,
-    send1,
-    recv1,
-    send2,
-    recv2,
-    send3,
-    recv3,
-    sendh,
-    recvh,
     small_send,
     small_recv,
-    every_send,
-    every_recv,
     whole_send,
     whole_recv,
     half_sem,
@@ -664,36 +993,34 @@
     sq_recv,
     sqd_send,
     sqd_recv,
+    *refs,
 ):
+    carry = AttnCarry(attn_grad_ref, refs[:CARRY_REFS], refs[CARRY_REFS:])
     seg, dp, core, x, y, across_core, near, far = peers()
     across_x, across_y, across_both = near
     planes = count // 2
     plane = seg // 2
     group = 2 * y + x
-
-    def pieces(row):
-        return (
-            (attn0.at[:, :, row], (slice(None), slice(None), 0)),
-            (attn1.at[:, :, row], (slice(None), slice(None), 1)),
-            (up1.at[:, row], (0, 0, slice(2, 6))),
-            (up0.at[:, row], (0, 1, slice(2, 6))),
-            (down0.at[row], (1, 0, slice(2, 6))),
-            (down1.at[row], (1, 1, slice(2, 6))),
-        )
-
-    order = [lax.rem(plane + 1 + step, planes) for step in range(planes)]
-    for step in range(planes):
-        for source, place in pieces(2 * order[step] + core):
-            pltpu.make_async_copy(source, mine.at[(step,) + place], load_sem.at[step]).start()
+    targets = [{"seg": other} for other in others(seg, count)] + list(near) + list(far)
+    hail(targets)
+    carry.load_all()
+    own_ref[1] = attn_done_ref[...]
+
+    @pl.when(x == y)
+    def _():
+        own_ref[2:6] = feed_high_ref[...]
+
+    @pl.when(x != y)
+    def _():
+        own_ref[2:6] = feed_low_ref[...]
+
     inputs = din_ref.shape[0]
     small_ref[0:inputs, :] = din_ref[...]
     for place, ref in enumerate((vec0_ref, vec1_ref, vec2_ref, vec3_ref, outer_ref)):
         small_ref[inputs + 8 * place : inputs + 8 * place + 8, :] = ref[...]
     small_ref[inputs + 40 :, :] = jnp.zeros((SMALL - inputs - 40, D), f32)
-    greet(seg, count, near, far)
-    for step in range(planes):
-        for source, place in pieces(2 * order[step] + 1 - core):
-            remote(source, got0.at[(step,) + place], send0.at[step], recv0.at[step], across_core).start()
+    meet(targets)
+    carry.send_all()
 
     def small_steps():
         copy = remote(small_ref, small_core, small_send.at[0], small_recv.at[0], across_core)
@@ -728,97 +1055,20 @@
 
     small_run = small_steps()
     next(small_run)
-
-    def first_of(step):
-        return (
-            remote(mine.at[step, :, 1 - x, 0:3], got1.at[step, 0], send1.at[step, 0], recv1.at[step, 0], across_x),
-            remote(mine.at[step, 1 - y, :, 3:6], got1.at[step, 1], send1.at[step, 1], recv1.at[step, 1], across_y),
-        )
-
-    def second_of(step):
-        return (
-            remote(mine.at[step, 1 - y, x, 0:3], got2.at[step, 0], send2.at[step, 0], recv2.at[step, 0], across_y),
-            remote(mine.at[step, y, 1 - x, 3:6], got2.at[step, 1], send2.at[step, 1], recv2.at[step, 1], across_x),
-        )
-
-    def third_of(step):
-        return remote(
-            mine.at[step, y, x],
-            got3.at[plane],
-            send3.at[step],
-            recv3.at[plane],
-            {"seg": 2 * order[step] + core},
-        )
-
-    def begin(step):
-        wait_bytes(mine.at[step], load_sem.at[step])
-        wait_bytes(got0.at[step], recv0.at[step])
-
-        def body(place, carry):
-            mine[step, place // 2, place % 2] = plus(mine[step, place // 2, place % 2], got0[step, place // 2, place % 2])
-            return carry
-
-        lax.fori_loop(0, GROUPS, body, 0)
-        for copy in first_of(step):
-            copy.start()
-
-    def middle(step):
-        for copy in first_of(step):
-            copy.wait_recv()
-        for place in range(2):
-            mine[step, place, x, 0:3] = plus(mine[step, place, x, 0:3], got1[step, 0, place])
-            mine[step, y, place, 3:6] = plus(mine[step, y, place, 3:6], got1[step, 1, place])
-        for copy in second_of(step):
-            copy.start()
-
-    def end(step):
-        for copy in second_of(step):
-            copy.wait_recv()
-        mine[step, y, x, 0:3] = plus(mine[step, y, x, 0:3], got2[step, 0])
-        mine[step, y, x, 3:6] = plus(mine[step, y, x, 3:6], got2[step, 1])
-        for place, target in enumerate(far):
-            copy = remote(
-                mine.at[step, y, x], goth.at[place, step], sendh.at[place, step], recvh.at[place, step], target
-            )
-            copy.start()
-            copy.wait()
-            mine[step, y, x] = plus(mine[step, y, x], goth[place, step])
-        if step < planes - 1:
-            third_of(step).start()
-
-    for step in range(planes + 2):
-        if step < planes:
-            begin(step)
-        if 1 <= step <= planes:
-            middle(step - 1)
-        if step >= 2:
-            end(step - 2)
-        next(small_run, None)
-    for _ in small_run:
-        pass
-
-    total = mine[planes - 1, y, x].astype(f32)
-    for step in range(1, planes):
-        sender = lax.rem(plane + step, planes)
-        wait_bytes(got3.at[sender], recv3.at[sender])
-        total = total + got3[sender].astype(f32)
-    every_ref[group] = total.astype(bf16)
-    square = jnp.sum(jnp.sum(jnp.sum(total * total, 0), 0, keepdims=True), 1, keepdims=True)
-    sq_seg[seg] = jnp.broadcast_to(square, (8, 128))
-
     roles = owners(count)
 
     def gift(place):
         first, width, owner, spot = roles[place]
         return remote(
-            every_ref.at[group, first : first + width],
+            own_ref.at[first : first + width],
             whole_ref.at[seg, spot : spot + width],
             whole_send.at[place],
             whole_recv.at[seg],
             {"seg": owner},
         )
 
-    for place, (first, width, owner, spot) in enumerate(roles):
+    def give(place):
+        first, width, owner, spot = roles[place]
 
         @pl.when(seg != owner)
         def _():
@@ -826,25 +1076,40 @@
 
         @pl.when(seg == owner)
         def _():
-            whole_ref[seg, spot : spot + width] = every_ref[group, first : first + width]
-
+            whole_ref[seg, spot : spot + width] = own_ref[first : first + width]
+
+    for place in (2, 3, 1):
+        give(place)
+    for time in range(planes + 2):
+        if time < planes:
+            carry.begin(time)
+        if 1 <= time <= planes:
+            carry.middle(time - 1)
+        if time >= 2:
+            carry.end(time - 2)
+        next(small_run, None)
+    for _ in small_run:
+        pass
+    own_ref[0] = carry.total().astype(bf16)
+    give(0)
+    square = jnp.zeros((1, 1), f32)
+    for unit in range(UNITS):
+        value = own_ref[unit].astype(f32)
+        square = square + jnp.sum(jnp.sum(value * value, 0, keepdims=True), 1, keepdims=True)
+    sq_seg[seg] = jnp.broadcast_to(square, (8, 128))
     for step, other in enumerate(others(seg, count)):
         remote(sq_seg.at[seg], sq_seg.at[seg], sq_send.at[step], sq_recv.at[seg], {"seg": other}).start()
-    for place, target in enumerate(near):
-        remote(
-            every_ref.at[group], every_ref.at[group], every_send.at[place], every_recv.at[place], target
-        ).start()
     for other in others(seg, count):
         wait_bytes(sq_seg.at[other], sq_recv.at[other])
     sq_dp[group] = jnp.sum(sq_seg[...], 0)
     for place, target in enumerate(near):
         remote(sq_dp.at[group], sq_dp.at[group], sqd_send.at[place], sqd_recv.at[place], target).start()
-    for place, target in enumerate(near):
-        remote(sq_dp.at[group], sq_dp.at[group], sqd_send.at[place], sqd_recv.at[place], target).wait()
     sums = small_out[...]
     is_loss = lax.broadcasted_iota(jnp.int32, (SMALL, D), 0) == inputs + 37
     sums = jnp.where(is_loss, 0.0, sums)
     small_square = jnp.sum(jnp.sum(sums * sums, 0, keepdims=True), 1, keepdims=True)
+    for place, target in enumerate(near):
+        remote(sq_dp.at[group], sq_dp.at[group], sqd_send.at[place], sqd_recv.at[place], target).wait()
     square_out[...] = jnp.sum(sq_dp[...], 0) + jnp.broadcast_to(small_square, (8, 128))
 
     for place, (first, width, owner, spot) in enumerate(roles):
@@ -861,12 +1126,7 @@
                 copy.start()
                 copy.wait()
 
-    for step in range(planes):
-        wait_bytes(mine.at[step], send0.at[step])
-        for copy in first_of(step) + second_of(step):
-            copy.wait_send()
-        if step < planes - 1:
-            third_of(step).wait_send()
+    carry.drain()
     for place, (first, width, owner, spot) in enumerate(roles):
 
         @pl.when(seg != owner)
@@ -875,60 +1135,33 @@
 
     for step in range(count - 1):
         wait_bytes(sq_seg.at[0], sq_send.at[step])
-    for place, target in enumerate(near):
-        remote(
-            every_ref.at[group], every_ref.at[group], every_send.at[place], every_recv.at[place], target
-        ).wait()
-
-
-def reduce_grads(count, dp_count, attn, up, down, pieces):
+
+
+def reduce_grads(count, dp_count, attn, done, feed_low, feed_high, pieces):
     rows = D // count
     planes = count // 2
-    far = max(1, dp_count.bit_length() - 3)
-    shape = (UNITS, rows, D)
-    attn = [grad.reshape(2, 2, count, rows, D) for grad in attn]
-    up = [grad.reshape(4, count, rows, D) for grad in up]
-    down = [grad.reshape(count, 4, rows, D) for grad in down]
     stages = 2 + planes.bit_length() + max(0, dp_count.bit_length() - 3)
     dma = pltpu.SemaphoreType.DMA
+    vmem = pl.BlockSpec(memory_space=pltpu.VMEM)
     return pl.pallas_call(
         functools.partial(reduce_kernel, count),
         out_shape=[
             jax.ShapeDtypeStruct((count, 4, rows, D), bf16),
-            jax.ShapeDtypeStruct((GROUPS,) + shape, bf16),
+            jax.ShapeDtypeStruct((UNITS, rows, D), bf16),
             jax.ShapeDtypeStruct((SMALL, D), f32),
             jax.ShapeDtypeStruct((8, 128), f32),
         ],
-        in_specs=[pl.BlockSpec(memory_space=pl.ANY)] * 6 + [pl.BlockSpec(memory_space=pltpu.VMEM)] * 6,
-        out_specs=[pl.BlockSpec(memory_space=pltpu.VMEM)] * 4,
+        in_specs=[pl.BlockSpec(memory_space=pl.ANY)] + [vmem] * 9,
+        out_specs=[vmem] * 4,
         scratch_shapes=[
-            pltpu.VMEM((planes, 2, 2) + shape, bf16),
-            pltpu.VMEM((planes, 2, 2) + shape, bf16),
-            pltpu.VMEM((planes, 2, 2, 3, rows, D), bf16),
-            pltpu.VMEM((planes, 2, 3, rows, D), bf16),
-            pltpu.VMEM((planes,) + shape, bf16),
-            pltpu.VMEM((far, planes) + shape, bf16),
             pltpu.VMEM((SMALL, D), f32),
             pltpu.VMEM((SMALL, D), f32),
             pltpu.VMEM((SMALL, D), f32),
             pltpu.VMEM((stages, SMALL // 2, D), f32),
             pltpu.VMEM((count, 8, 128), f32),
             pltpu.VMEM((GROUPS, 8, 128), f32),
-            dma((planes,)),
-            dma((planes,)),
-            dma((planes,)),
-            dma((planes, 2)),
-            dma((planes, 2)),
-            dma((planes, 2)),
-            dma((planes, 2)),
-            dma((planes,)),
-            dma((planes,)),
-            dma((far, planes)),
-            dma((far, planes)),
             dma((stages + 2,)),
             dma((stages + 2,)),
-            dma((3,)),
-            dma((3,)),
             dma((4,)),
             dma((count,)),
             dma((2,)),
@@ -936,13 +1169,14 @@
             dma((count,)),
             dma((3,)),
             dma((3,)),
-        ],
+        ]
+        + carry_scratch("attn", count, dp_count),
         compiler_params=pltpu.CompilerParams(
             collective_id=1, has_side_effects=True, vmem_limit_bytes=VMEM_LIMIT
         ),
-        cost_estimate=pl.CostEstimate(flops=10**8, bytes_accessed=2 * 10**8, transcendentals=0),
+        cost_estimate=pl.CostEstimate(flops=10**8, bytes_accessed=10**8, transcendentals=0),
         name="reduce_grads",
-    )(*attn, *up, *down, *pieces)
+    )(attn.reshape(2, 2, count, rows, D), done, feed_low, feed_high, *pieces)
 
 
 def halves(value):
@@ -1083,7 +1317,7 @@
     )(role, squares, dout, whole, momenta)
 
 
-def spread_kernel(count, made_ref, every_ref, send, recv, on_send, on_recv):
+def spread_kernel(count, made_ref, own_ref, update_ref, every_ref, send, recv, on_send, on_recv, own_send, own_recv):
     seg, dp, core, x, y, across_core, near, far = peers()
     group = 2 * y + x
     greet(seg, count, near, ())
@@ -1093,7 +1327,7 @@
         first, width, owner, spot = roles[place]
         return remote(
             made_ref.at[other, 0:width],
-            every_ref.at[group, first : first + width],
+            update_ref.at[group, first : first + width],
             send.at[other],
             recv.at[place],
             {"seg": other},
@@ -1101,8 +1335,11 @@
 
     def onward(place, side):
         first, width, owner, spot = roles[place]
-        block = every_ref.at[group, first : first + width]
+        block = update_ref.at[group, first : first + width]
         return remote(block, block, on_send.at[side, place], on_recv.at[side, place], near[side])
+
+    def own_rows(side):
+        return remote(own_ref, every_ref.at[group], own_send.at[side], own_recv.at[side], near[side])
 
     for place, (first, width, owner, spot) in enumerate(roles):
 
@@ -1110,16 +1347,21 @@
         def _():
             for other in others(seg, count):
                 gift(place, other).start()
-            every_ref[group, first : first + width] = made_ref[seg, 0:width]
-
+            update_ref[group, first : first + width] = made_ref[seg, 0:width]
+
+    for side in range(3):
+        own_rows(side).start()
+    every_ref[group] = own_ref[...]
     for place, (first, width, owner, spot) in enumerate(roles):
 
         @pl.when(seg != owner)
         def _():
-            wait_bytes(every_ref.at[group, first : first + width], recv.at[place])
+            wait_bytes(update_ref.at[group, first : first + width], recv.at[place])
 
         for side in range(3):
             onward(place, side).start()
+    for side in range(3):
+        own_rows(side).wait()
     for place, (first, width, owner, spot) in enumerate(roles):
         for side in range(3):
             onward(place, side).wait()
@@ -1130,21 +1372,22 @@
                 gift(place, other).wait_send()
 
 
-def spread(count, made):
+def spread(count, made, own):
     rows = made.shape[2]
     dma = pltpu.SemaphoreType.DMA
+    vmem = pl.BlockSpec(memory_space=pltpu.VMEM)
     return pl.pallas_call(
         functools.partial(spread_kernel, count),
-        out_shape=jax.ShapeDtypeStruct((GROUPS, UNITS, rows, D), bf16),
-        in_specs=[pl.BlockSpec(memory_space=pltpu.VMEM)],
-        out_specs=pl.BlockSpec(memory_space=pltpu.VMEM),
-        scratch_shapes=[dma((count,)), dma((4,)), dma((3, 4)), dma((3, 4))],
+        out_shape=[jax.ShapeDtypeStruct((GROUPS, UNITS, rows, D), bf16)] * 2,
+        in_specs=[vmem] * 2,
+        out_specs=[vmem] * 2,
+        scratch_shapes=[dma((count,)), dma((4,)), dma((3, 4)), dma((3, 4)), dma((3,)), dma((3,))],
         compiler_params=pltpu.CompilerParams(
             collective_id=2, has_side_effects=True, vmem_limit_bytes=VMEM_LIMIT
         ),
         cost_estimate=pl.CostEstimate(flops=10**6, bytes_accessed=4 * 10**7, transcendentals=0),
         name="spread",
-    )(made)
+    )(made, own)
 
 
 def embed_kernel(
@@ -1480,28 +1723,47 @@
         hidden, targets, speech_mask, totals, out_copy, outer_vectors, 1.0 / stream_total, momenta
     )
     grad_out = lax.psum(grad_out, ("seg", "dp"))
-    attn_grads, up_grads, down_grads, vector_grads = ([], [], [], [])
+    vector_grads, feed_done = [], [None, None]
+    grad_attn = None
+    attn_done = None
     for depth in reversed(range(LAYERS)):
         entering, held, saved = kept[depth]
-        dafter, grad_up, grad_down, feed_vec = feed_back(
-            depth, grad_hidden, saved[7], up_copy, down_copy, layer_vectors
+        dafter, grad_up, grad_down, feed_vec, *done = feed_back(
+            depth, grad_hidden, saved[7], up_copy, down_copy, layer_vectors, count, dp_count, grad_attn
         )
-        grad_hidden, grad_attn, attn_vec, grad_in = attend_back(
-            depth, bias, dafter, entering, held, saved[1:7], attn_copy, layer_vectors, frames_t
+        if done:
+            attn_done = done[0]
+        grad_hidden, grad_attn, attn_vec, grad_in, feed_done[depth] = attend_back(
+            depth,
+            bias,
+            dafter,
+            entering,
+            held,
+            saved[1:7],
+            attn_copy,
+            layer_vectors,
+            frames_t,
+            grad_up,
+            grad_down,
+            count,
+            dp_count,
         )
-        attn_grads.insert(0, grad_attn)
-        up_grads.insert(0, grad_up)
-        down_grads.insert(0, grad_down)
         vector_grads = [attn_vec, feed_vec] + vector_grads
-    whole, every, small, squares = reduce_grads(
-        count, dp_count, attn_grads, up_grads, down_grads, [grad_in] + vector_grads + [head_outer]
+    whole, own, small, squares = reduce_grads(
+        count,
+        dp_count,
+        grad_attn,
+        attn_done,
+        feed_done[0],
+        feed_done[1],
+        [grad_in] + vector_grads + [head_outer],
     )
     loss_sum = small[grad_in.shape[0] + 37, 0]
     plane, core = segment // 2, segment % 2
     kind = jnp.where(plane == count // 4 - 1, 1, jnp.where(plane == count // 4, 2, 0))
     role = jnp.stack([kind, core, (group >= 2).astype(jnp.int32), core]).astype(jnp.int32)
     made, norm = muon(role, squares, grad_out, whole, momenta)
-    updates = spread(count, made)
+    updates, every = spread(count, made, own)
     split = (LAYERS, 4, rows, D)
     (
         attn_new,

time: 441 us -> 433 us (0.982)
  Pallas kernels: 396 us -> 389 us
    pallas_call x1, Pallas kernels: 107 us -> 49.7 us  [reduce_grads(): pl.pallas_call(functools.partial(reduce_kernel, count), out_shape=[jax.Sh...]
    pallas_call x5, Pallas kernels: 177 us -> 227 us  [the longest x2 98.2 us: attend_back(): pl.pallas_call(functools.partial(attend_back_kernel, streams, depth), gri...]
  transfers between devices with their start and end apart: 4 -> 4, of which waited for: 0 -> 0; matrix products, arithmetic and copies ran while one was open for 1% -> 1% of each run, Pallas kernels for 71% -> 68%
where the time goes in v4:
time: 433 us; the launch traced here: 426 us
  Pallas kernels  389 us (90%)
  between operations  14.6 us (3%)
  local copies, waits for them, and re-layouts  14.3 us (3%)
  starting transfers between devices  5.7 us (1%)
    pallas_call x2, Pallas kernels, attend_back(): pl.pallas_call(functools.partial(attend_back_kernel, streams, depth), gri...  98.2 us
    pallas_call x4, Pallas kernels, forward_layer(): pl.pallas_call(forward_kernel, grid=(1,), out_shape=out_shape, in_specs=i...  71.3 us
    pallas_call x1, Pallas kernels, spread(): pl.pallas_call(functools.partial(spread_kernel, count), out_shape=[jax.Sh...  68.6 us
    pallas_call x2, Pallas kernels, feed_back(): pl.pallas_call(functools.partial(feed_back_kernel, streams, carried), gri...  60 us
    pallas_call x1, Pallas kernels, reduce_grads(): pl.pallas_call(functools.partial(reduce_kernel, count), out_shape=[jax.Sh...  49.7 us
    pallas_call x1, Pallas kernels, finish(): pl.pallas_call(finish_kernel, grid=(steps,), out_shape=[like(attn), like(...  13.4 us
    pallas_call x1, Pallas kernels, embed(): pl.pallas_call(functools.partial(embed_kernel, count), out_shape=[jax.Sha...  12.1 us
    pallas_call x1, Pallas kernels, head(): pl.pallas_call(functools.partial(head_kernel, scale), grid=(streams,), ou...  10.8 us
  transfers between devices with their start and end apart: 4, of which 0 were waited for; matrix products, arithmetic and copies ran while one was open for 1% of the time, Pallas kernels for 68%

profile of v4, /device:TPU:0, one launch (start us, length us, event | category | flops | bytes accessed | tf_op | source)
XLA Modules:
  0.0 425.9 jit_solution(497449564508783390)
XLA Ops:
  7.2 0.0 copy-start
  7.2 0.0 all-gather.2.cloned.1.call-start
  7.3 1.3 fusion.4
  8.6 0.2 reshape_squeeze.6
  8.8 0.2 reshape_squeeze.7
  9.0 0.1 fusion.5
  9.1 0.2 copy.120
  9.3 0.2 copy.121
  9.5 0.0 copy-start.3
  9.5 1.0 dynamic-slice_convert_fusion
  10.5 0.1 copy.137
  10.6 0.6 fusion.3
  11.3 0.3 pad_maximum_fusion.1
  11.5 0.9 copy.122
  12.4 0.0 all-gather.2.cloned.1.call-update
  12.4 0.0 all-reduce.2.cloned.1.call-start
  12.5 0.6 copy.116.vec_ref.refs_12_
  13.1 12.1 %embed.1 = (f32[2,512,512]{2,1,0:T(8,128)}, bf16[2,512,512]{2,1,0:T(8,128)(2,1)}, f32[8,128]{1,0:T(8,128)}) custom-call(bf16[2,80,512]{2,1,0:T(8,128)(2,1)} %bitcast.49, s32[2,512]{1,0:T(2,128)} %mask_ref.3, bf16[80,512]{1,0:T(8,128)(2,1)} %in_ref.1, f32[5,512]{1,0:T(8,128)} %refs_15_.1), custom_call_target="tpu_custom_call" | custom-call | flops 200000000 | bytes 4000000 | tf_op jit(solution)/shard_map/embed/pallas_call | solution.py:1437
  25.2 17.8 %layer_forward.4 = (f32[2,512,512]{2,1,0:T(8,128)}, bf16[512,512]{1,0:T(8,128)(2,1)}, bf16[2,1024,512]{2,1,0:T(8,128)(2,1)}, bf16[2,512,512]{2,1,0:T(8,128)(2,1)...) custom-call(f32[1]{0:T(128)} %bitcast.bias_ref, ...), custom_call_target="tpu_custom_call" | custom-call | flops 10000000000 | bytes 20000000 | tf_op jit(solution)/shard_map/layer_forward/pallas_call | solution.py:199
  42.9 1.9 collective-permute-start.1
  44.9 0.0 copy-start.4
  44.9 0.0 copy-start.5
  44.9 17.8 %layer_forward.5 = (f32[2,512,512]{2,1,0:T(8,128)}, bf16[512,512]{1,0:T(8,128)(2,1)}, bf16[2,1024,512]{2,1,0:T(8,128)(2,1)}, bf16[2,512,512]{2,1,0:T(8,128)(2,1)...) custom-call(f32[1]{0:T(128)} %bitcast.bias_ref, ...), custom_call_target="tpu_custom_call", output_to_operand_aliasing={{0}: (7, {}), {2}: (8, {}), {3}: (9, {}), {4}: (10, {}), {5... | custom-call | flops 10000000000 | bytes 20000000 | tf_op jit(solution)/shard_map/layer_forward/pallas_call | solution.py:199
  62.7 3.7 collective-permute-start
  66.4 0.7 slice_bitcast_fusion
  67.1 0.6 copy.134
  67.7 0.6 copy.128.refs_13_
  68.4 0.6 copy.129.refs_14_
  69.0 0.6 pad_add_fusion.role_ref
  69.6 1.2 pad_maximum_fusion.mem_ref
  70.8 17.9 %layer_forward.6 = (f32[2,512,512]{2,1,0:T(8,128)}, bf16[512,512]{1,0:T(8,128)(2,1)}, bf16[2,1024,512]{2,1,0:T(8,128)(2,1)}, bf16[2,512,512]{2,1,0:T(8,128)(2,1)...) custom-call(f32[1]{0:T(128)} %bitcast.bias_ref, ...), custom_call_target="tpu_custom_call" | custom-call | flops 10000000000 | bytes 20000000 | tf_op jit(solution)/shard_map/layer_forward/pallas_call | solution.py:199
  88.7 17.8 %layer_forward.7 = (f32[2,512,512]{2,1,0:T(8,128)}, bf16[512,512]{1,0:T(8,128)(2,1)}, bf16[2,1024,512]{2,1,0:T(8,128)(2,1)}, bf16[2,512,512]{2,1,0:T(8,128)(2,1)...) custom-call(f32[1]{0:T(128)} %bitcast.bias_ref, ...), custom_call_target="tpu_custom_call", output_to_operand_aliasing={{0}: (7, {}), {2}: (8, {}), {3}: (9, {}), {4}: (10, {}), {5... | custom-call | flops 10000000000 | bytes 20000000 | tf_op jit(solution)/shard_map/layer_forward/pallas_call | solution.py:199
  106.5 0.0 all-gather.2.cloned.1.call-done.mom_ref
  106.5 10.8 %head.1 = (f32[2,512,512]{2,1,0:T(8,128)}, f32[512,1024]{1,0:T(8,128)}, f32[8,512]{1,0:T(8,128)}) custom-call(f32[2,512,512]{2,1,0:T(8,128)} %get-tuple-element.134.x_ref, s32[2,512]{1,0:T(2,128)} %target_ref.1, s32[2,512]{1,0:T(2,128)} %mask_ref.3, f32[8,128]{1,0:T(8,128)} %get-tuple-element.135.total_ref, bf16[512,1024]{1,0:T(8,128)(2,1)} %out_ref.1, ...), custom_call_target="tpu_custom_call" | custom-call | flops 3300000000 | bytes 10000000 | tf_op jit(solution)/shard_map/head/pallas_call | solution.py:257
  117.3 0.0 all-reduce.2.cloned.1.call-update
  117.4 22.7 %feed_back.2 = (f32[2,512,512]{2,1,0:T(8,128)}, bf16[4,512,512]{2,1,0:T(8,128)(2,1)}, bf16[2048,512]{1,0:T(8,128)(2,1)}, f32[8,512]{1,0:T(8,128)}) custom-call(f32[2,512,512]{2,1,0:T(8,128)} %get-tuple-element.136.g_ref, f32[2,512,512]{2,1,0:T(8,128)} %get-tuple-element.137.after_ref, bf16[2,512,2048]{2,1,0:T(8,128)(2,1)} %up_ref.11, ...), custom_call_target="tpu_custom_call" | custom-call | flops 11000000512 | bytes 20000000 | tf_op jit(solution)/shard_map/feed_back/pallas_call | solution.py:390
  140.1 54.8 %attend_back.2 = (f32[2,512,512]{2,1,0:T(8,128)}, bf16[4,512,512]{2,1,0:T(8,128)(2,1)}, f32[8,512]{1,0:T(8,128)}, f32[80,512]{1,0:T(8,128)}, bf16[4,64,512]{2,1,0:T(8,128)(2,1)}) custom-call(f32[1]{0:T(128)} %bitcast.bias_ref, f32[2,512,512]{2,1,0:T(8,128)} %get-tuple-element.138.dafter_ref, f32[2,512,512]{2,1,0:T(8,128)} %get-tuple-element.123.x_ref, ...), custom_call_target="tpu_custom_call" | custom-call | flops 30000001024 | bytes 20000000 | tf_op jit(solution)/shard_map/attend_back/pallas_call | solution.py:554
  194.9 37.3 %feed_back.3 = (f32[2,512,512]{2,1,0:T(8,128)}, bf16[4,512,512]{2,1,0:T(8,128)(2,1)}, bf16[2048,512]{1,0:T(8,128)(2,1)}, f32[8,512]{1,0:T(8,128)}, bf16[64,512]{1,0:T(8,128)(2,1)}) custom-call(f32[2,512,512]{2,1,0:T(8,128)} %get-tuple-element.147.g_ref, f32[2,512,512]{2,1,0:T(8,128)} %get-tuple-element.148.after_ref, bf16[2,512,2048]{2,1,0:T(8,128)(2,1)} %up_ref.11, ...), custom_call_target="tpu_custom_call" | custom-call | flops 11000000512 | bytes 20000000 | tf_op jit(solution)/shard_map/feed_back/pallas_call | solution.py:390
  232.2 43.4 %attend_back.3 = (f32[2,512,512]{2,1,0:T(8,128)}, bf16[4,512,512]{2,1,0:T(8,128)(2,1)}, f32[8,512]{1,0:T(8,128)}, f32[80,512]{1,0:T(8,128)}, bf16[4,64,512]{2,1,0:T(8,128)(2,1)}) custom-call(f32[1]{0:T(128)} %bitcast.bias_ref, f32[2,512,512]{2,1,0:T(8,128)} %get-tuple-element.150.dafter_ref, f32[2,512,512]{2,1,0:T(8,128)} %get-tuple-element.113.x_ref, ...), custom_call_target="tpu_custom_call" | custom-call | flops 30000001024 | bytes 20000000 | tf_op jit(solution)/shard_map/attend_back/pallas_call | solution.py:554
  275.6 49.7 %reduce_grads.1 = (bf16[8,4,64,512]{3,2,1,0:T(8,128)(2,1)}, bf16[6,64,512]{2,1,0:T(8,128)(2,1)}, f32[128,512]{1,0:T(8,128)}, f32[8,128]{1,0:T(8,128)}) custom-call(bf16[2,2,8,64,512]{4,3,2,1,0:T(8,128)(2,1)} %bitcast.36, bf16[64,512]{1,0:T(8,128)(2,1)} %get-tuple-element.160.attn_done_ref, bf16[4,64,512]{2,1,0:T(8,128)(2,1)} %get-tuple-element.161.feed_low_ref, ...), custom_call_target="tpu_custom_call" | custom-call | flops 100000000 | bytes 100000000 | tf_op jit(solution)/shard_map/reduce_grads/pallas_call | solution.py:1146
  325.3 1.2 slice.26
  326.5 4.7 %muon.1 = (bf16[8,2,64,512]{3,2,1,0:T(8,128)(2,1)}, f32[8,128]{1,0:T(8,128)}) custom-call(s32[4]{0:T(128)} %pad_add_fusion.role_ref, f32[8,128]{1,0:T(8,128)} %get-tuple-element.170.square_ref, f32[512,1024]{1,0:T(8,128)} %all-reduce.2.cloned.1.call-done.dout_ref, bf16[8,4,64,512]{3,2,1,0:T(8,128)(2,1)} %get-tuple-element.172.whole_ref, ...), custom_call_target="tpu_custom_call" | custom-call | flops 20000000000 | bytes 10000000 | tf_op jit(solution)/shard_map/muon/pallas_call | solution.py:1302
  331.1 1.2 slice.27
  332.3 68.6 %spread.1 = (bf16[4,6,64,512]{3,2,1,0:T(8,128)(2,1)}, bf16[4,6,64,512]{3,2,1,0:T(8,128)(2,1)}) custom-call(bf16[8,2,64,512]{3,2,1,0:T(8,128)(2,1)} %get-tuple-element.174.made_ref, bf16[6,64,512]{2,1,0:T(8,128)(2,1)} %get-tuple-element.175.own_ref), custom_call_target="tpu_custom_call" | custom-call | flops 1000000 | bytes 40000000 | tf_op jit(solution)/shard_map/spread/pallas_call | solution.py:1379
  400.9 13.4 %finish.1 = (f32[2,4,64,512]{3,2,1,0:T(8,128)}, f32[2,4,64,512]{3,2,1,0:T(8,128)}, bf16[2,4,64,512]{3,2,1,0:T(8,128)(2,1)}, f32[2,64,2048]{2,1,0:T(8,128)}, f32[...) custom-call(f32[8,128]{1,0:T(8,128)} %get-tuple-element.173.norm_ref, ...), custom_call_target="tpu_custom_call" | custom-call | flops 100000000 | bytes 40000000 | tf_op jit(solution)/shard_map/finish/pallas_call | solution.py:1613
  414.3 1.5 copy.130
  415.8 1.5 copy.131
  417.3 1.5 copy.132
  (11 shorter events, 0.0 us)
Async XLA Ops:
  7.2 1.8 copy-start
  7.2 99.3 %all-gather.2.cloned.1.call-start = ((), (), s32[]{:S(2)}) async-start(), calls=%async_computation | async-start | bytes 3538944 | tf_op jit(solution)/shard_map/all_gather | solution.py:1695
  9.5 3.0 copy-start.3
  12.4 314.1 %all-reduce.2.cloned.1.call-start = ((), (), s32[]{:S(2)}) async-start(), calls=%async_computation.1 | async-start | bytes 4194304 | tf_op jit(solution)/shard_map/psum | solution.py:1725
  42.9 26.6 %collective-permute-start.1 = (bf16[512,512]{1,0:T(8,128)(2,1)}, bf16[512,512]{1,0:T(8,128)(2,1)S(1)}, u32[]{:S(2)}, u32[]{:S(2)}) collective-permute-start(bf16[512,512]{1,0:T(8,128)(2,1)} %get-tuple-element.125), channel_id=1, source_target_pairs={{0,4},{4,8},{8,12},{12,16},{16,20},{20,24},{24,28},{1,5},{5,9},{9,... | collective-permute-start | bytes 1572872 | tf_op jit(solution)/shard_map/ppermute | solution.py:609
  44.9 22.9 %copy-start.4 = (f32[2,12,512]{2,0,1:T(2,128)S(1)}, f32[2,12,512]{2,0,1:T(2,128)}, u32[]{:S(2)}) copy-start(f32[2,12,512]{2,0,1:T(2,128)} %param.36) | copy-start | bytes 147460
  44.9 23.5 %copy-start.5 = (f32[2,12,512]{2,0,1:T(2,128)S(1)}, f32[2,12,512]{2,0,1:T(2,128)}, u32[]{:S(2)}) copy-start(f32[2,12,512]{2,0,1:T(2,128)} %param.37) | copy-start | bytes 147460
  62.7 6.9 %collective-permute-start = (bf16[512,512]{1,0:T(8,128)(2,1)}, bf16[512,512]{1,0:T(8,128)(2,1)S(1)}, u32[]{:S(2)}, u32[]{:S(2)}) collective-permute-start(bf16[512,512]{1,0:T(8,128)(2,1)} %get-tuple-element.124), channel_id=1, source_target_pairs={{0,4},{4,8},{8,12},{12,16},{16,20},{20,24},{24,28},{1,5},{5,9},{9,... | collective-permute-start | bytes 1572872 | tf_op jit(solution)/shard_map/ppermute | solution.py:609
  69.6 1.2 copy-start.1
  69.6 19.2 %copy-start.2 = (bf16[512,512]{1,0:T(8,128)(2,1)}, bf16[512,512]{1,0:T(8,128)(2,1)S(1)}, u32[]{:S(2)}) copy-start(bf16[512,512]{1,0:T(8,128)(2,1)S(1)} %collective-permute-done.mem_ref) | copy-start | bytes 1572868
Sparse Core Ops, SparseCore 0:
  12.5 40.9 all-gather.1
  117.5 143.5 all-reduce.1

commit v5 on v4

--- a/solution.py
+++ b/solution.py
@@ -73,7 +73,8 @@
     vec_ref,
     *refs,
 ):
-    hid_ref, hid16_ref, keyin_ref, q_ref, k_ref, v_ref, lse_ref, mixed_ref, after_ref, act_s, lse_s = refs[-11:]
+    hid_ref, hid16_ref, keyin_ref, q_ref, k_ref, v_ref, lse_ref, mixed_ref, after_ref, kept_ref, act_s, lse_s = refs[-12:]
+    kept_ref[...] = mem_ref[...]
     x = x_ref[...]
     own_unit, _ = normalised(x)
     gain, shift = vec_ref[0:1, :], vec_ref[1:2, :]
@@ -156,6 +157,7 @@
     ((HEADS, SEG), f32),
     ((SEG, D), bf16),
     ((SEG, D), f32),
+    ((SEG, D), bf16),
 )
 
 
@@ -247,7 +249,12 @@
 
     @pl.when(step == pl.num_programs(0) - 1)
     def _():
-        dout_ref[...] = acc_s[...]
+        half = D // 2
+        for right in range(2):
+            for low in range(2):
+                dout_ref[right, low] = acc_s[
+                    low * half : (low + 1) * half, right * D : (right + 1) * D
+                ]
 
 
 def head(hidden, targets, mask, totals, out_weight, outer_vectors, scale, momenta):
@@ -259,7 +266,7 @@
         grid=(streams,),
         out_shape=[
             jax.ShapeDtypeStruct((streams, SEG, D), f32),
-            jax.ShapeDtypeStruct((D, codes), f32),
+            jax.ShapeDtypeStruct((2, 2, D // 2, D), f32),
             jax.ShapeDtypeStruct((8, D), f32),
         ],
         in_specs=[
@@ -272,7 +279,7 @@
             whole_spec((1, codes)),
             pl.BlockSpec(memory_space=pl.ANY),
         ],
-        out_specs=[stream_spec((SEG, D)), whole_spec((D, codes)), whole_spec((8, D))],
+        out_specs=[stream_spec((SEG, D)), whole_spec((2, 2, D // 2, D)), whole_spec((8, D))],
         scratch_shapes=[pltpu.VMEM((D, codes), f32)],
         compiler_params=pltpu.CompilerParams(vmem_limit_bytes=VMEM_LIMIT),
         cost_estimate=pl.CostEstimate(flops=33 * 10**8, bytes_accessed=10**7, transcendentals=10**6),
@@ -280,21 +287,18 @@
     )(hidden, targets, mask, totals, out_weight, outer_vectors, bias, momenta)
 
 
-def feed_back_kernel(streams, carried, g_ref, after_ref, up_ref, down_ref, vec_ref, *refs):
+def feed_back_kernel(streams, g_ref, after_ref, up_ref, down_ref, vec_ref, *refs):
     step = pl.program_id(0)
-    tiles = FF // TILE
-    if carried:
-        grad_ref, refs = refs[0], refs[1:]
-        dafter_ref, dup_ref, ddown_ref, dvec_ref, done_ref, up_s, down_s, act_s, inner_s = refs[:9]
-        carry = AttnCarry(grad_ref, refs[9 : 9 + CARRY_REFS], refs[9 + CARRY_REFS :])
-
-        @pl.when(step == 0)
-        def _():
-            hail(carry.targets)
-            carry.load_all()
-
-    else:
-        dafter_ref, dup_ref, ddown_ref, dvec_ref, up_s, down_s, act_s, inner_s = refs
+    grad_ref, dafter_ref, dup_ref, ddown_ref, dvec_ref, done_ref, up_s, down_s, act_s, inner_s = refs[:10]
+    carry = AttnCarry(grad_ref, refs[10 : 10 + CARRY_REFS], refs[10 + CARRY_REFS :])
+
+    def beat(place):
+        carry.tick(4 * step + place, 4 * streams, 2)
+
+    @pl.when(step == 0)
+    def _():
+        hail(carry.targets)
+        carry.load_all()
 
     @pl.when(step == 0)
     def _():
@@ -308,6 +312,12 @@
     unit, scale = normalised(after_ref[...])
     gain = vec_ref[2:3, :]
     normed = (unit * gain + vec_ref[3:4, :]).astype(bf16)
+
+    @pl.when(step == 0)
+    def _():
+        meet(carry.targets)
+        carry.send_all()
+
     for tile in range(FF // TILE):
         columns = slice(tile * TILE, (tile + 1) * TILE)
         inner = dot_nn(normed, up_ref[:, columns]) + vec_ref[8 + tile : 9 + tile, :]
@@ -320,39 +330,31 @@
         dinner = (dact * slope).astype(bf16)
         inner_s[:, columns] = dinner
         dvec_ref[4 + tile : 5 + tile, :] += column_sum(dinner.astype(f32))
-        if carried:
-            if tile == 0:
-
-                @pl.when(step == 0)
-                def _():
-                    meet(carry.targets)
-                    carry.send_all()
-
-            carry.tick(tiles * step + tile - 1)
+        if tile % 2:
+            beat(tile // 2)
     dnormed = dot_nt(inner_s[...], up_ref[...])
     dvec_ref[0:1, :] += column_sum(dnormed * unit)
     dvec_ref[1:2, :] += column_sum(dnormed)
     dafter_ref[...] = grad + norm_back(dnormed, gain, unit, scale)
+    beat(2)
     normed_t = jnp.transpose(normed)
     branch_t = jnp.transpose(branch)
     up_s[...] += dot_nn(normed_t, inner_s[...])
     down_s[...] += dot_nn(branch_t, act_s[...])
+    beat(3)
 
     @pl.when(step == pl.num_programs(0) - 1)
     def _():
         for tile in range(FF // TILE):
             dup_ref[tile] = up_s[:, tile * TILE : (tile + 1) * TILE].astype(bf16)
         ddown_ref[...] = jnp.transpose(down_s[...].astype(bf16))
-        if carried:
-            for time in range(tiles * streams - 1, carry.planes + 2):
-                carry.tick(time)
-            carry.finish(done_ref)
-
-
-def feed_back(depth, grad, after, upper, lower, vectors, count, dp_count, attn_grad=None):
+        carry.rest(4 * streams, 2)
+        carry.finish(done_ref)
+
+
+def feed_back(depth, grad, after, upper, lower, vectors, count, dp_count, attn_grad):
     streams = grad.shape[0]
-    rows = D // count
-    carried = attn_grad is not None
+    rows = attn_grad.shape[0] // (GROUPS * count)
     in_specs = [
         stream_spec((SEG, D)),
         stream_spec((SEG, D)),
@@ -379,16 +381,14 @@
         pltpu.VMEM((SEG, FF), bf16),
     ]
     operands = [grad, after, upper, lower, vectors]
-    params = {}
-    if carried:
-        in_specs.append(pl.BlockSpec(memory_space=pl.ANY))
-        operands.append(attn_grad.reshape(2, 2, count, rows, D))
-        out_shape.append(jax.ShapeDtypeStruct((rows, D), bf16))
-        out_specs.append(whole_spec((rows, D)))
-        scratch = scratch + carry_scratch("attn", count, dp_count)
-        params = {"collective_id": 6, "has_side_effects": True}
+    in_specs.append(pl.BlockSpec(memory_space=pl.ANY))
+    operands.append(attn_grad.reshape(2, 2, count, rows, D))
+    out_shape.append(jax.ShapeDtypeStruct((rows, D), bf16))
+    out_specs.append(whole_spec((rows, D)))
+    scratch = scratch + carry_scratch("attn", rows, count, dp_count, attn_grad.dtype)
+    params = {"collective_id": 6 + depth, "has_side_effects": True}
     return pl.pallas_call(
-        functools.partial(feed_back_kernel, streams, carried),
+        functools.partial(feed_back_kernel, streams),
         grid=(streams,),
         out_shape=out_shape,
         in_specs=in_specs,
@@ -510,7 +510,7 @@
             dq_s[block * HALF : (block + 1) * HALF, lanes] = (
                 jnp.transpose(grads) * (HEAD_DIM**-0.5)
             ).astype(bf16)
-        carry.tick(pairs * step + pair)
+        carry.tick(pairs * step + pair, pairs * streams, 1)
         return state
 
     lax.fori_loop(0, pairs, pair_body, 0)
@@ -540,8 +540,7 @@
     @pl.when(step == pl.num_programs(0) - 1)
     def _():
         dattn_ref[...] = attn_s[...].astype(bf16)
-        for time in range(pairs * streams, carry.planes + 2):
-            carry.tick(time)
+        carry.rest(pairs * streams, 1)
         carry.finish(done_ref)
 
 
@@ -594,7 +593,7 @@
             pltpu.VMEM((2 * SEG, 2 * SEG), bf16),
             pltpu.VMEM((HEADS, SEG), f32),
         ]
-        + carry_scratch("feed", count, dp_count),
+        + carry_scratch("feed", rows, count, dp_count),
         compiler_params=pltpu.CompilerParams(
             collective_id=4 + depth, has_side_effects=True, vmem_limit_bytes=VMEM_LIMIT
         ),
@@ -675,7 +674,7 @@
 
 
 def plus(left, right):
-    return (left.astype(f32) + right.astype(f32)).astype(bf16)
+    return (left.astype(f32) + right.astype(f32)).astype(left.dtype)
 
 
 def owners(count):
@@ -686,6 +685,13 @@
         (2, 2, 2 * feed, 0),
         (4, 2, 2 * feed + 1, 2),
     )
+
+
+def lowest_bit(mask, planes):
+    bit = 1
+    while bit < planes and not mask & bit:
+        bit *= 2
+    return bit
 
 
 class Carry:
@@ -709,20 +715,32 @@
         self.planes = self.mine.shape[0]
         self.plane = self.seg // 2
         self.targets = [self.across_core, self.across_x, self.across_y] + self.far
-        for step in range(1, self.planes):
-            self.targets.append({"seg": 2 * lax.rem(self.plane + step, self.planes) + self.core})
-
-    def block(self, step):
-        return lax.rem(self.plane + 1 + step, self.planes)
+        bit = 1
+        while bit < self.planes:
+            self.targets.append({"seg": 2 * self.toggled(bit) + self.core})
+            bit *= 2
+
+        places = []
+        for low in range(self.planes.bit_length()):
+            places += [mask for mask in reversed(range(self.planes)) if lowest_bit(mask, self.planes) == 1 << low]
+        self.order = places
+
+    def toggled(self, mask):
+        place, bit = self.plane, 1
+        while bit <= mask:
+            if mask & bit:
+                place = place + bit - 2 * bit * ((self.plane // bit) % 2)
+            bit *= 2
+        return place
 
     def load_all(self):
         for step in range(self.planes):
-            for source, place in self.pieces(2 * self.block(step) + self.core):
+            for source, place in self.pieces(2 * self.toggled(self.order[step]) + self.core):
                 pltpu.make_async_copy(source, self.mine.at[(step,) + place], self.load.at[step]).start()
 
     def send_all(self):
         for step in range(self.planes):
-            for source, place in self.pieces(2 * self.block(step) + 1 - self.core):
+            for source, place in self.pieces(2 * self.toggled(self.order[step]) + 1 - self.core):
                 remote(
                     source, self.got0.at[(step,) + place], self.send0.at[step], self.recv0.at[step], self.across_core
                 ).start()
@@ -745,48 +763,56 @@
         )
 
     def third(self, step):
+        mask = self.order[step]
         return remote(
             self.held(step),
-            self.got3.at[self.plane],
+            self.got3.at[mask],
             self.send3.at[step],
-            self.recv3.at[self.plane],
-            {"seg": 2 * self.block(step) + self.core},
+            self.recv3.at[mask],
+            {"seg": 2 * self.toggled(lowest_bit(mask, self.planes)) + self.core},
         )
 
     def onward(self, step):
+        held = self.held(step)
         for place in range(len(self.far)):
             copy = self.across(place, step)
             copy.start()
             copy.wait()
-            held = self.held(step)
             held[...] = plus(held[...], self.goth[place, step])
-
-        @pl.when(step < self.planes - 1)
-        def _():
+        mask, bit = self.order[step], 1
+        value = held[...].astype(f32)
+        while bit < lowest_bit(mask, self.planes):
+            wait_bytes(self.got3.at[mask + bit], self.recv3.at[mask + bit])
+            value = value + self.got3[mask + bit].astype(f32)
+            bit *= 2
+        held[...] = value.astype(held.dtype)
+        if mask:
             self.third(step).start()
 
     def total(self):
-        value = self.held(self.planes - 1)[...].astype(f32)
-        for step in range(1, self.planes):
-            sender = lax.rem(self.plane + step, self.planes)
-            wait_bytes(self.got3.at[sender], self.recv3.at[sender])
-            value = value + self.got3[sender].astype(f32)
-        return value
-
-    def tick(self, time):
+        return self.held(self.planes - 1)[...]
+
+    def actions(self, time, slack):
         planes = self.planes
-
-        @pl.when((time >= 0) & (time < planes))
-        def _():
-            self.begin(time)
-
-        @pl.when((time >= 1) & (time < planes + 1))
-        def _():
-            self.middle(time - 1)
-
-        @pl.when((time >= 2) & (time < planes + 2))
-        def _():
-            self.end(time - 2)
+        started = range(2) if time == 0 else range(time + 1, time + 2)
+        for step in started:
+            if step < planes:
+                self.begin(step)
+        if 0 <= time - slack < planes:
+            self.middle(time - slack)
+        if 0 <= time - slack - 2 < planes:
+            self.end(time - slack - 2)
+
+    def tick(self, time, last, slack):
+        for place in range(last):
+
+            @pl.when(time == place)
+            def _():
+                self.actions(place, slack)
+
+    def rest(self, first, slack):
+        for time in range(first, self.planes + slack + 2):
+            self.actions(time, slack)
 
 
 class AttnCarry(Carry):
@@ -833,8 +859,7 @@
         self.onward(step)
 
     def finish(self, out_ref):
-        value = self.total()
-        out_ref[...] = value.astype(bf16)
+        out_ref[...] = self.total().astype(out_ref.dtype)
         self.drain()
 
     def drain(self):
@@ -919,7 +944,7 @@
     def finish(self, out_ref):
         @pl.when(self.owner)
         def _():
-            out_ref[...] = self.total().astype(bf16)
+            out_ref[...] = self.total().astype(out_ref.dtype)
             for step in range(self.planes - 1):
                 self.third(step).wait_send()
 
@@ -940,8 +965,8 @@
 CARRY_SEMS = 11
 
 
-def carry_scratch(kind, count, dp_count):
-    rows, planes = D // count, count // 2
+def carry_scratch(kind, rows, count, dp_count, dtype=bf16):
+    planes = count // 2
     far = max(1, dp_count.bit_length() - 3)
     dma = pltpu.SemaphoreType.DMA
     if kind == "attn":
@@ -959,7 +984,7 @@
         pair = (planes, 2)
     one = (planes,)
     sems = (one, one, one, pair, pair, pair, pair, one, one, (far, planes), (far, planes))
-    return [pltpu.VMEM(shape + (rows, D), bf16) for shape in shapes] + [dma(shape) for shape in sems]
+    return [pltpu.VMEM(shape + (rows, D), dtype) for shape in shapes] + [dma(shape) for shape in sems]
 
 
 def reduce_kernel(
@@ -968,6 +993,7 @@
     attn_done_ref,
     feed_low_ref,
     feed_high_ref,
+    dout_ref,
     din_ref,
     vec0_ref,
     vec1_ref,
@@ -1080,19 +1106,15 @@
 
     for place in (2, 3, 1):
         give(place)
-    for time in range(planes + 2):
-        if time < planes:
-            carry.begin(time)
-        if 1 <= time <= planes:
-            carry.middle(time - 1)
-        if time >= 2:
-            carry.end(time - 2)
+    for time in range(planes + 3):
+        carry.actions(time, 1)
         next(small_run, None)
+    own_ref[0] = carry.total()
+    give(0)
     for _ in small_run:
         pass
-    own_ref[0] = carry.total().astype(bf16)
-    give(0)
-    square = jnp.zeros((1, 1), f32)
+    shard = dout_ref[...].astype(f32)
+    square = jnp.sum(jnp.sum(shard * shard, 0, keepdims=True), 1, keepdims=True)
     for unit in range(UNITS):
         value = own_ref[unit].astype(f32)
         square = square + jnp.sum(jnp.sum(value * value, 0, keepdims=True), 1, keepdims=True)
@@ -1137,7 +1159,7 @@
         wait_bytes(sq_seg.at[0], sq_send.at[step])
 
 
-def reduce_grads(count, dp_count, attn, done, feed_low, feed_high, pieces):
+def reduce_grads(count, dp_count, attn, done, feed_low, feed_high, dout, pieces):
     rows = D // count
     planes = count // 2
     stages = 2 + planes.bit_length() + max(0, dp_count.bit_length() - 3)
@@ -1151,7 +1173,7 @@
             jax.ShapeDtypeStruct((SMALL, D), f32),
             jax.ShapeDtypeStruct((8, 128), f32),
         ],
-        in_specs=[pl.BlockSpec(memory_space=pl.ANY)] + [vmem] * 9,
+        in_specs=[pl.BlockSpec(memory_space=pl.ANY)] + [vmem] * 10,
         out_specs=[vmem] * 4,
         scratch_shapes=[
             pltpu.VMEM((SMALL, D), f32),
@@ -1170,13 +1192,13 @@
             dma((3,)),
             dma((3,)),
         ]
-        + carry_scratch("attn", count, dp_count),
+        + carry_scratch("attn", rows, count, dp_count),
         compiler_params=pltpu.CompilerParams(
             collective_id=1, has_side_effects=True, vmem_limit_bytes=VMEM_LIMIT
         ),
         cost_estimate=pl.CostEstimate(flops=10**8, bytes_accessed=10**8, transcendentals=0),
         name="reduce_grads",
-    )(attn.reshape(2, 2, count, rows, D), done, feed_low, feed_high, *pieces)
+    )(attn.reshape(2, 2, count, rows, D), done, feed_low, feed_high, dout, *pieces)
 
 
 def halves(value):
@@ -1204,18 +1226,71 @@
     return jnp.minimum(1.0, 0.25 / (norm + 1e-06))
 
 
-def muon_kernel(role_ref, square_ref, dout_ref, whole_ref, mom_ref, out_ref, norm_ref, x_s, q_s, gram_s, high_s, low_s):
-    count, rows = whole_ref.shape[0], whole_ref.shape[2]
-    core = role_ref[1]
-    dout = dout_ref[...]
-    norm = jnp.sqrt(square_ref[0:1, 0:1] + jnp.sum(jnp.sum(dout * dout, 0, keepdims=True), 1, keepdims=True))
+def muon_kernel(
+    count,
+    square_ref,
+    whole_ref,
+    mom_ref,
+    own_ref,
+    update_ref,
+    every_ref,
+    norm_ref,
+    made_ref,
+    x_s,
+    q_s,
+    gram_s,
+    high_s,
+    low_s,
+    send,
+    recv,
+    on_send,
+    on_recv,
+    own_send,
+    own_recv,
+):
+    seg, dp, core, x, y, across_core, near, far = peers()
+    group = 2 * y + x
+    plane = seg // 2
+    targets = [{"seg": other} for other in others(seg, count)] + list(near)
+    hail(targets)
+    is_down = group >= 2
+    norm = jnp.sqrt(square_ref[0:1, 0:1])
     norm_ref[...] = jnp.broadcast_to(norm, norm_ref.shape)
     clip = clip_of(norm)
     eye = (
         lax.broadcasted_iota(jnp.int32, (D, D), 0) == lax.broadcasted_iota(jnp.int32, (D, D), 1)
     ).astype(f32)
-
-    @pl.when(role_ref[0] == 1)
+    rows = whole_ref.shape[2]
+    makers = [attn for _, _, attn, _ in owners(count)]
+    units = [makers[0], makers[1], makers[2], makers[2], makers[3], makers[3]]
+
+    def own_rows(side):
+        return remote(own_ref, every_ref.at[group], own_send.at[side], own_recv.at[side], near[side])
+
+    def gift(unit, slot, other):
+        return remote(
+            made_ref.at[other, slot],
+            update_ref.at[group, unit],
+            send.at[slot, other],
+            recv.at[unit],
+            {"seg": other},
+        )
+
+    def give(unit, slot):
+        for other in others(seg, count):
+            gift(unit, slot, other).start()
+        update_ref[group, unit] = made_ref[seg, slot]
+
+    def onward(unit, side):
+        block = update_ref.at[group, unit]
+        return remote(block, block, on_send.at[side, unit], on_recv.at[side, unit], near[side])
+
+    meet(targets)
+    for side in range(3):
+        own_rows(side).start()
+    every_ref[group] = own_ref[...]
+
+    @pl.when(plane == count // 4 - 1)
     def _():
         start = (0.5 * mom_ref[:, core].astype(f32)).reshape(D, D)
         start = start + clip * whole_ref[:, 0].astype(f32).reshape(D, D)
@@ -1232,9 +1307,14 @@
             return carry
 
         lax.fori_loop(0, 5, sweep, 0)
-        out_ref[:, 0] = x_s[...].astype(bf16).reshape(count, rows, D)
-
-    @pl.when(role_ref[0] == 2)
+        made_ref[:, 0] = x_s[...].astype(bf16).reshape(count, rows, D)
+        for unit in range(2):
+
+            @pl.when(core == unit)
+            def _():
+                give(unit, 0)
+
+    @pl.when(plane == count // 4)
     def _():
         gram_s[...] = jnp.zeros_like(gram_s)
 
@@ -1245,7 +1325,7 @@
             high_s[tile] = high
             low_s[tile] = low
 
-            @pl.when(role_ref[2] == 1)
+            @pl.when(is_down)
             def _():
                 high_s[tile] = jnp.transpose(high_s[tile])
                 low_s[tile] = jnp.transpose(low_s[tile])
@@ -1282,112 +1362,72 @@
         gram = gram_s[...]
         last = times(halves(q_s[...]), halves(poly_of(gram, halves(gram)))) * scale
         last_both = halves(last)
-
-        def finish(step, carry):
-            tile = 2 * core + step
+        for slot in range(2):
+            tile = 2 * core + slot
             x_s[...] = times(last_both, (high_s[tile], low_s[tile]))
 
-            @pl.when(role_ref[2] == 1)
+            @pl.when(is_down)
             def _():
                 x_s[...] = jnp.transpose(x_s[...])
 
-            out_ref[:, step] = x_s[...].astype(bf16).reshape(count, rows, D)
-            return carry
-
-        lax.fori_loop(0, 2, finish, 0)
-
-
-def muon(role, squares, dout, whole, momenta):
-    count, _, rows, _ = whole.shape
+            made_ref[:, slot] = x_s[...].astype(bf16).reshape(count, rows, D)
+            for half in range(2):
+
+                @pl.when(core == half)
+                def _():
+                    give(2 + 2 * half + slot, slot)
+
+    for unit in (0, 1, 2, 4, 3, 5):
+
+        @pl.when(seg != units[unit])
+        def _():
+            wait_bytes(update_ref.at[group, unit], recv.at[unit])
+
+        for side in range(3):
+            onward(unit, side).start()
+    for side in range(3):
+        own_rows(side).wait()
+    for unit in range(UNITS):
+        for side in range(3):
+            onward(unit, side).wait()
+
+        @pl.when(seg == units[unit])
+        def _():
+            slot = 0 if unit < 2 else unit % 2
+            for other in others(seg, count):
+                gift(unit, slot, other).wait_send()
+
+
+def muon(count, squares, whole, momenta, own):
+    rows = whole.shape[2]
+    dma = pltpu.SemaphoreType.DMA
+    vmem = pl.BlockSpec(memory_space=pltpu.VMEM)
+    blocks = jax.ShapeDtypeStruct((GROUPS, UNITS, rows, D), bf16)
     return pl.pallas_call(
-        muon_kernel,
-        out_shape=[jax.ShapeDtypeStruct((count, 2, rows, D), bf16), jax.ShapeDtypeStruct((8, 128), f32)],
-        in_specs=[pl.BlockSpec(memory_space=pltpu.SMEM)] + [pl.BlockSpec(memory_space=pltpu.VMEM)] * 4,
-        out_specs=[pl.BlockSpec(memory_space=pltpu.VMEM)] * 2,
+        functools.partial(muon_kernel, count),
+        out_shape=[blocks, blocks, jax.ShapeDtypeStruct((8, 128), f32)],
+        in_specs=[vmem] * 4,
+        out_specs=[vmem] * 3,
         scratch_shapes=[
+            pltpu.VMEM((count, 2, rows, D), bf16),
             pltpu.VMEM((D, D), f32),
             pltpu.VMEM((D, D), f32),
             pltpu.VMEM((D, D), f32),
             pltpu.VMEM((4, D, D), bf16),
             pltpu.VMEM((4, D, D), bf16),
+            dma((2, count)),
+            dma((UNITS,)),
+            dma((3, UNITS)),
+            dma((3, UNITS)),
+            dma((3,)),
+            dma((3,)),
         ],
-        compiler_params=pltpu.CompilerParams(vmem_limit_bytes=VMEM_LIMIT),
-        cost_estimate=pl.CostEstimate(flops=2 * 10**10, bytes_accessed=10**7, transcendentals=0),
-        name="muon",
-    )(role, squares, dout, whole, momenta)
-
-
-def spread_kernel(count, made_ref, own_ref, update_ref, every_ref, send, recv, on_send, on_recv, own_send, own_recv):
-    seg, dp, core, x, y, across_core, near, far = peers()
-    group = 2 * y + x
-    greet(seg, count, near, ())
-    roles = owners(count)
-
-    def gift(place, other):
-        first, width, owner, spot = roles[place]
-        return remote(
-            made_ref.at[other, 0:width],
-            update_ref.at[group, first : first + width],
-            send.at[other],
-            recv.at[place],
-            {"seg": other},
-        )
-
-    def onward(place, side):
-        first, width, owner, spot = roles[place]
-        block = update_ref.at[group, first : first + width]
-        return remote(block, block, on_send.at[side, place], on_recv.at[side, place], near[side])
-
-    def own_rows(side):
-        return remote(own_ref, every_ref.at[group], own_send.at[side], own_recv.at[side], near[side])
-
-    for place, (first, width, owner, spot) in enumerate(roles):
-
-        @pl.when(seg == owner)
-        def _():
-            for other in others(seg, count):
-                gift(place, other).start()
-            update_ref[group, first : first + width] = made_ref[seg, 0:width]
-
-    for side in range(3):
-        own_rows(side).start()
-    every_ref[group] = own_ref[...]
-    for place, (first, width, owner, spot) in enumerate(roles):
-
-        @pl.when(seg != owner)
-        def _():
-            wait_bytes(update_ref.at[group, first : first + width], recv.at[place])
-
-        for side in range(3):
-            onward(place, side).start()
-    for side in range(3):
-        own_rows(side).wait()
-    for place, (first, width, owner, spot) in enumerate(roles):
-        for side in range(3):
-            onward(place, side).wait()
-
-        @pl.when(seg == owner)
-        def _():
-            for other in others(seg, count):
-                gift(place, other).wait_send()
-
-
-def spread(count, made, own):
-    rows = made.shape[2]
-    dma = pltpu.SemaphoreType.DMA
-    vmem = pl.BlockSpec(memory_space=pltpu.VMEM)
-    return pl.pallas_call(
-        functools.partial(spread_kernel, count),
-        out_shape=[jax.ShapeDtypeStruct((GROUPS, UNITS, rows, D), bf16)] * 2,
-        in_specs=[vmem] * 2,
-        out_specs=[vmem] * 2,
-        scratch_shapes=[dma((count,)), dma((4,)), dma((3, 4)), dma((3, 4)), dma((3,)), dma((3,))],
         compiler_params=pltpu.CompilerParams(
             collective_id=2, has_side_effects=True, vmem_limit_bytes=VMEM_LIMIT
         ),
-        cost_estimate=pl.CostEstimate(flops=10**6, bytes_accessed=4 * 10**7, transcendentals=0),
-        name="spread",
-    )(made, own)
+        cost_estimate=pl.CostEstimate(flops=2 * 10**10, bytes_accessed=4 * 10**7, transcendentals=0),
+        name="muon",
+    )(squares, whole, momenta, own)
 
 
 def embed_kernel(
@@ -1507,6 +1547,8 @@
         outer_new,
         outer_mom_new,
         outer_sec_new,
+        loss_new,
+        norm_new,
     ) = refs
     clip = clip_of(norm_ref[0:1, 0:1])
 
@@ -1548,11 +1590,21 @@
             down_new[depth, kind] = weight
             down_mom_new[depth, kind] = momentum
             down_copy_new[depth, kind] = weight.astype(bf16)
-    weight, moment, second = adamw(out_ref[...], out_mom_ref[...], out_sec_ref[...], dout_ref[...] * clip, 0.05, 0.01)
-    out_new[...] = weight
-    out_mom_new[...] = moment
-    out_sec_new[...] = second
-    out_copy_new[...] = weight.astype(bf16)
+    for low in range(2):
+        for right in range(2):
+            columns = slice(right * D, (right + 1) * D)
+            weight, moment, second = adamw(
+                out_ref[low, :, columns],
+                out_mom_ref[low, :, columns],
+                out_sec_ref[low, :, columns],
+                dout_ref[2 * right + low].astype(f32) * clip,
+                0.05,
+                0.01,
+            )
+            out_new[low, :, columns] = weight
+            out_mom_new[low, :, columns] = moment
+            out_sec_new[low, :, columns] = second
+            out_copy_new[low, :, columns] = weight.astype(bf16)
 
     @pl.when(pl.program_id(0) == 0)
     def _():
@@ -1565,6 +1617,9 @@
         in_sec_new[...] = second
         in_copy_new[...] = weight.astype(bf16)
 
+        norm_new[...] = norm_ref[0:1, 0:1]
+        loss_new[...] = small_ref[inputs + 37 : inputs + 38, 0:1]
+
         def rows_of(first, last, base):
             return small_ref[inputs + base + first : inputs + base + last, :]
 
@@ -1578,16 +1633,16 @@
                 (8, 12, rows_of(4, 8, base + 8)),
             ):
                 weight, moment, second = adamw(
-                    vec_ref[depth, low:high],
-                    vec_mom_ref[depth, low:high],
-                    vec_sec_ref[depth, low:high],
+                    vec_ref[low:high, depth],
+                    vec_mom_ref[low:high, depth],
+                    vec_sec_ref[low:high, depth],
                     grad * clip,
                     0.25,
                     0.0,
                 )
-                vec_new[depth, low:high] = weight
-                vec_mom_new[depth, low:high] = moment
-                vec_sec_new[depth, low:high] = second
+                vec_new[low:high, depth] = weight
+                vec_mom_new[low:high, depth] = moment
+                vec_sec_new[low:high, depth] = second
         for low, high, grad in ((0, 1, rows_of(5, 6, 0)), (1, 5, rows_of(1, 5, 32))):
             weight, moment, second = adamw(
                 outer_ref[low:high, :], outer_mom_ref[low:high, :], outer_sec_ref[low:high, :], grad * clip, 0.25, 0.0
@@ -1600,11 +1655,13 @@
 def finish(rows, norm, every, updates, dout, small, arrays):
     steps = rows // 16
     attn, _, up, _, down, _, out, _, _, inp, _, _, vec, _, _, outer, _, _ = arrays
-    codes = out.shape[1]
+    codes = out.shape[2]
+    part = out.shape[1] // steps
     blocks = pl.BlockSpec((GROUPS, UNITS, 16, D), lambda i: (0, 0, i, 0))
     attn_spec = pl.BlockSpec((LAYERS, 4, 16, D), lambda i: (0, 0, i, 0))
     up_spec = pl.BlockSpec((LAYERS, 16, FF), lambda i: (0, i, 0))
-    out_spec = pl.BlockSpec((D // steps, codes), lambda i: (i, 0))
+    out_spec = pl.BlockSpec((2, part, codes), lambda i: (0, i, 0))
+    dout_spec = pl.BlockSpec((GROUPS, part, D), lambda i: (0, i, 0))
     in_spec, vec_spec, outer_spec = whole_spec(inp.shape), whole_spec(vec.shape), whole_spec(outer.shape)
 
     def like(array, dtype=f32):
@@ -1621,8 +1678,9 @@
         + [like(inp)] * 3
         + [like(inp, bf16)]
         + [like(vec)] * 3
-        + [like(outer)] * 3,
-        in_specs=[whole_spec((8, 128)), blocks, blocks, out_spec, whole_spec(small.shape)]
+        + [like(outer)] * 3
+        + [jax.ShapeDtypeStruct((1, 1), f32)] * 2,
+        in_specs=[whole_spec((8, 128)), blocks, blocks, dout_spec, whole_spec(small.shape)]
         + [attn_spec] * 2
         + [up_spec] * 2
         + [attn_spec] * 2
@@ -1636,7 +1694,8 @@
         + [out_spec] * 4
         + [in_spec] * 4
         + [vec_spec] * 3
-        + [outer_spec] * 3,
+        + [outer_spec] * 3
+        + [whole_spec((1, 1))] * 2,
         compiler_params=pltpu.CompilerParams(vmem_limit_bytes=VMEM_LIMIT),
         cost_estimate=pl.CostEstimate(flops=10**8, bytes_accessed=4 * 10**7, transcendentals=0),
         name="finish",
@@ -1716,23 +1775,21 @@
             )
             if depth + 1 < LAYERS:
                 passed.append(from_behind(short, "seg", 1))
-        kept.append((hidden, memory[0] if depth == 0 else jnp.stack(memory), saved))
+        kept.append((hidden, saved[8], saved))
         hidden = saved[0]
         memory = passed
     grad_hidden, grad_out, head_outer = head(
         hidden, targets, speech_mask, totals, out_copy, outer_vectors, 1.0 / stream_total, momenta
     )
-    grad_out = lax.psum(grad_out, ("seg", "dp"))
     vector_grads, feed_done = [], [None, None]
-    grad_attn = None
-    attn_done = None
+    carried = grad_out.reshape(GROUPS * D // 2, D)
+    carried_done = []
     for depth in reversed(range(LAYERS)):
         entering, held, saved = kept[depth]
-        dafter, grad_up, grad_down, feed_vec, *done = feed_back(
-            depth, grad_hidden, saved[7], up_copy, down_copy, layer_vectors, count, dp_count, grad_attn
+        dafter, grad_up, grad_down, feed_vec, done = feed_back(
+            depth, grad_hidden, saved[7], up_copy, down_copy, layer_vectors, count, dp_count, carried
         )
-        if done:
-            attn_done = done[0]
+        carried_done.append(done)
         grad_hidden, grad_attn, attn_vec, grad_in, feed_done[depth] = attend_back(
             depth,
             bias,
@@ -1748,7 +1805,11 @@
             count,
             dp_count,
         )
+        carried = grad_attn.reshape(4 * D, D)
         vector_grads = [attn_vec, feed_vec] + vector_grads
+    out_done, attn_done = carried_done
+    every_out = lax.all_gather(out_done, ("dp", "seg"), axis=0, tiled=True)[: GROUPS * D // 2]
+    every_out = every_out.reshape(GROUPS, D // 2, D)
     whole, own, small, squares = reduce_grads(
         count,
         dp_count,
@@ -1756,15 +1817,12 @@
         attn_done,
         feed_done[0],
         feed_done[1],
+        out_done,
         [grad_in] + vector_grads + [head_outer],
     )
-    loss_sum = small[grad_in.shape[0] + 37, 0]
-    plane, core = segment // 2, segment % 2
-    kind = jnp.where(plane == count // 4 - 1, 1, jnp.where(plane == count // 4, 2, 0))
-    role = jnp.stack([kind, core, (group >= 2).astype(jnp.int32), core]).astype(jnp.int32)
-    made, norm = muon(role, squares, grad_out, whole, momenta)
-    updates, every = spread(count, made, own)
+    updates, every, norm = muon(count, squares, whole, momenta, own)
     split = (LAYERS, 4, rows, D)
+    halved = (2, D // 2, out_proj.shape[1])
     (
         attn_new,
         attn_mom,
@@ -1789,12 +1847,14 @@
         outer_new,
         outer_moment_new,
         outer_second_new,
+        loss_sum,
+        norm,
     ) = finish(
         rows,
         norm,
         every,
         updates,
-        grad_out,
+        every_out,
         small,
         [
             attn_proj,
@@ -1803,32 +1863,32 @@
             up_momentum,
             ff_down.reshape(split),
             down_momentum.reshape(split),
-            out_proj,
-            out_moment,
-            out_second,
+            out_proj.reshape(halved),
+            out_moment.reshape(halved),
+            out_second.reshape(halved),
             in_proj,
             in_moment,
             in_second,
-            layer_vectors,
-            vectors_moment,
-            vectors_second,
+            jnp.swapaxes(layer_vectors, 0, 1),
+            jnp.swapaxes(vectors_moment, 0, 1),
+            jnp.swapaxes(vectors_second, 0, 1),
             outer_vectors,
             outer_moment,
             outer_second,
         ],
     )
     return (
-        loss_sum,
-        norm[0, 0],
+        loss_sum.reshape(()),
+        norm.reshape(()),
         in_new,
         in_moment_new,
         in_second_new,
-        out_new,
-        out_moment_new,
-        out_second_new,
-        vectors_new,
-        vectors_moment_new,
-        vectors_second_new,
+        out_new.reshape(out_proj.shape),
+        out_moment_new.reshape(out_proj.shape),
+        out_second_new.reshape(out_proj.shape),
+        jnp.swapaxes(vectors_new, 0, 1),
+        jnp.swapaxes(vectors_moment_new, 0, 1),
+        jnp.swapaxes(vectors_second_new, 0, 1),
         outer_new,
         outer_moment_new,
         outer_second_new,
@@ -1839,7 +1899,7 @@
         down_new.reshape(ff_down.shape),
         down_mom.reshape(ff_down.shape),
         in_copy_new,
-        out_copy_new,
+        out_copy_new.reshape(out_proj.shape),
         attn_copy_new,
         up_copy_new,
         down_copy_new.reshape(ff_down.shape),

time: 433 us -> 410 us (0.947)
  Pallas kernels: 389 us -> 373 us
  local copies, waits for them, and re-layouts: 14.3 us -> 7.71 us
    pallas_call x4 -> x3, Pallas kernels: 133 us -> 111 us  [the longest x2 60.3 us: feed_back(): pl.pallas_call(functools.partial(feed_back_kernel, streams), grid=(stream...]
    pallas_call x1, Pallas kernels: 49.7 us -> 57.4 us  [reduce_grads(): pl.pallas_call(functools.partial(reduce_kernel, count), out_shape=[jax.Sh...]
  transfers between devices with their start and end apart: 4 -> 4, of which waited for: 0 -> 0; matrix products, arithmetic and copies ran while one was open for 1% -> 0% of each run, Pallas kernels for 68% -> 79%
where the time goes in v5:
time: 410 us; the launch traced here: 402 us
  Pallas kernels  373 us (91%)
  between operations  14.8 us (4%)
  local copies, waits for them, and re-layouts  7.71 us (2%)
  starting transfers between devices  6.06 us (1%)
    pallas_call x2, Pallas kernels, attend_back(): pl.pallas_call(functools.partial(attend_back_kernel, streams, depth), gri...  97.2 us
    pallas_call x4, Pallas kernels, forward_layer(): pl.pallas_call(forward_kernel, grid=(1,), out_shape=out_shape, in_specs=i...  71.5 us
    pallas_call x2, Pallas kernels, feed_back(): pl.pallas_call(functools.partial(feed_back_kernel, streams), grid=(stream...  60.3 us
    pallas_call x1, Pallas kernels, reduce_grads(): pl.pallas_call(functools.partial(reduce_kernel, count), out_shape=[jax.Sh...  57.4 us
    pallas_call x1, Pallas kernels, muon(): pl.pallas_call(functools.partial(muon_kernel, count), out_shape=[blocks,...  50.6 us
    pallas_call x1, Pallas kernels, finish(): pl.pallas_call(finish_kernel, grid=(steps,), out_shape=[like(attn), like(...  13 us
    pallas_call x1, Pallas kernels, embed(): pl.pallas_call(functools.partial(embed_kernel, count), out_shape=[jax.Sha...  12.1 us
    pallas_call x1, Pallas kernels, head(): pl.pallas_call(functools.partial(head_kernel, scale), grid=(streams,), ou...  10.5 us
  transfers between devices with their start and end apart: 4, of which 0 were waited for; matrix products, arithmetic and copies ran while one was open for 0% of the time, Pallas kernels for 79%

profile of v5, /device:TPU:0, one launch (start us, length us, event | category | flops | bytes accessed | tf_op | source)
XLA Modules:
  0.0 402.0 jit_solution(16526199680222440915)
XLA Ops:
  7.2 0.0 copy-start
  7.2 0.0 all-gather.3.cloned.1.call-start
  7.3 1.3 fusion.4
  8.6 0.2 reshape_squeeze.6
  8.8 0.2 reshape_squeeze.7
  9.0 0.0 copy-done
  9.0 0.1 fusion.5
  9.1 0.2 copy.104
  9.3 0.2 copy.105
  9.5 0.0 copy-start.1
  9.5 1.0 dynamic-slice_convert_fusion
  10.5 0.1 copy.115
  10.6 0.6 fusion.3
  11.3 0.3 pad_maximum_fusion
  11.5 0.9 copy.106
  12.4 0.0 all-gather.3.cloned.1.call-update
  12.4 0.0 all-gather.5.cloned.1.call-start
  12.5 0.0 copy-done.1
  12.5 0.6 copy.100.vec_ref
  13.1 12.1 %embed.1 = (f32[2,512,512]{2,1,0:T(8,128)}, bf16[2,512,512]{2,1,0:T(8,128)(2,1)}, f32[8,128]{1,0:T(8,128)}) custom-call(bf16[2,80,512]{2,1,0:T(8,128)(2,1)} %bitcast.68, s32[2,512]{1,0:T(2,128)} %mask_ref.3, bf16[80,512]{1,0:T(8,128)(2,1)} %in_ref.1, f32[5,512]{1,0:T(8,128)} %refs_15_.1), custom_call_target="tpu_custom_call" | custom-call | flops 200000000 | bytes 4000000 | tf_op jit(solution)/shard_map/embed/pallas_call | solution.py:1477
  25.2 17.8 %layer_forward.4 = (f32[2,512,512]{2,1,0:T(8,128)}, bf16[512,512]{1,0:T(8,128)(2,1)}, bf16[2,1024,512]{2,1,0:T(8,128)(2,1)}, bf16[2,512,512]{2,1,0:T(8,128)(2,1)...) custom-call(f32[1]{0:T(128)} %bitcast.bias_ref, ...), custom_call_target="tpu_custom_call" | custom-call | flops 10000000000 | bytes 20000000 | tf_op jit(solution)/shard_map/layer_forward/pallas_call | solution.py:201
  43.0 2.2 collective-permute-start.1
  45.3 17.8 %layer_forward.5 = (f32[2,512,512]{2,1,0:T(8,128)}, bf16[512,512]{1,0:T(8,128)(2,1)}, bf16[2,1024,512]{2,1,0:T(8,128)(2,1)}, bf16[2,512,512]{2,1,0:T(8,128)(2,1)...) custom-call(f32[1]{0:T(128)} %bitcast.bias_ref, ...), custom_call_target="tpu_custom_call", output_to_operand_aliasing={{0}: (7, {}), {2}: (8, {}), {3}: (9, {}), {4}: (10, {}), {5... | custom-call | flops 10000000000 | bytes 20000000 | tf_op jit(solution)/shard_map/layer_forward/pallas_call | solution.py:201
  63.1 3.7 collective-permute-start
  66.9 0.7 slice_bitcast_fusion
  67.6 0.6 copy.112
  68.2 0.0 collective-permute-done.1.mem_ref
  68.2 0.0 copy-start.2
  68.2 0.8 copy-done.2
  69.0 18.0 %layer_forward.6 = (f32[2,512,512]{2,1,0:T(8,128)}, bf16[512,512]{1,0:T(8,128)(2,1)}, bf16[2,1024,512]{2,1,0:T(8,128)(2,1)}, bf16[2,512,512]{2,1,0:T(8,128)(2,1)...) custom-call(f32[1]{0:T(128)} %bitcast.bias_ref, ...), custom_call_target="tpu_custom_call" | custom-call | flops 10000000000 | bytes 20000000 | tf_op jit(solution)/shard_map/layer_forward/pallas_call | solution.py:201
  87.0 0.0 collective-permute-done.mem_ref
  87.0 0.0 copy-start.3
  87.0 0.8 copy-done.3
  87.8 17.8 %layer_forward.7 = (f32[2,512,512]{2,1,0:T(8,128)}, bf16[512,512]{1,0:T(8,128)(2,1)}, bf16[2,1024,512]{2,1,0:T(8,128)(2,1)}, bf16[2,512,512]{2,1,0:T(8,128)(2,1)...) custom-call(f32[1]{0:T(128)} %bitcast.bias_ref, ...), custom_call_target="tpu_custom_call", output_to_operand_aliasing={{0}: (7, {}), {2}: (8, {}), {3}: (9, {}), {4}: (10, {}), {5... | custom-call | flops 10000000000 | bytes 20000000 | tf_op jit(solution)/shard_map/layer_forward/pallas_call | solution.py:201
  105.6 0.0 all-gather.3.cloned.1.call-done.mom_ref
  105.6 10.5 %head.1 = (f32[2,512,512]{2,1,0:T(8,128)}, f32[2,2,256,512]{3,2,1,0:T(8,128)}, f32[8,512]{1,0:T(8,128)}) custom-call(f32[2,512,512]{2,1,0:T(8,128)} %get-tuple-element.142.x_ref, s32[2,512]{1,0:T(2,128)} %target_ref.1, s32[2,512]{1,0:T(2,128)} %mask_ref.3, f32[8,128]{1,0:T(8,128)} %get-tuple-element.143.total_ref, bf16[512,1024]{1,0:T(8,128)(2,1)} %out_ref.1, ...), custom_call_target="tpu_custom_call" | custom-call | flops 3300000000 | bytes 10000000 | tf_op jit(solution)/shard_map/head/pallas_call | solution.py:264
  116.2 30.8 %feed_back.2 = (f32[2,512,512]{2,1,0:T(8,128)}, bf16[4,512,512]{2,1,0:T(8,128)(2,1)}, bf16[2048,512]{1,0:T(8,128)(2,1)}, f32[8,512]{1,0:T(8,128)}, bf16[32,512]{1,0:T(8,128)(2,1)}) custom-call(f32[2,512,512]{2,1,0:T(8,128)} %get-tuple-element.144.g_ref, f32[2,512,512]{2,1,0:T(8,128)} %get-tuple-element.145.after_ref, bf16[2,512,2048]{2,1,0:T(8,128)(2,1)} %up_ref.11, ...), custom_call_target="tpu_custom_call" | custom-call | flops 11000000512 | bytes 20000000 | tf_op jit(solution)/shard_map/feed_back/pallas_call | solution.py:390
  147.0 0.0 all-gather.5.cloned.1.call-update
  147.0 54.7 %attend_back.2 = (f32[2,512,512]{2,1,0:T(8,128)}, bf16[4,512,512]{2,1,0:T(8,128)(2,1)}, f32[8,512]{1,0:T(8,128)}, f32[80,512]{1,0:T(8,128)}, bf16[4,64,512]{2,1,0:T(8,128)(2,1)}) custom-call(f32[1]{0:T(128)} %bitcast.bias_ref, f32[2,512,512]{2,1,0:T(8,128)} %get-tuple-element.147.dafter_ref, f32[2,512,512]{2,1,0:T(8,128)} %get-tuple-element.130.x_ref, ...), custom_call_target="tpu_custom_call" | custom-call | flops 30000001024 | bytes 20000000 | tf_op jit(solution)/shard_map/attend_back/pallas_call | solution.py:553
  201.7 29.5 %feed_back.3 = (f32[2,512,512]{2,1,0:T(8,128)}, bf16[4,512,512]{2,1,0:T(8,128)(2,1)}, bf16[2048,512]{1,0:T(8,128)(2,1)}, f32[8,512]{1,0:T(8,128)}, bf16[64,512]{1,0:T(8,128)(2,1)}) custom-call(f32[2,512,512]{2,1,0:T(8,128)} %get-tuple-element.157.g_ref, f32[2,512,512]{2,1,0:T(8,128)} %get-tuple-element.158.after_ref, bf16[2,512,2048]{2,1,0:T(8,128)(2,1)} %up_ref.11, ...), custom_call_target="tpu_custom_call" | custom-call | flops 11000000512 | bytes 20000000 | tf_op jit(solution)/shard_map/feed_back/pallas_call | solution.py:390
  231.2 42.5 %attend_back.3 = (f32[2,512,512]{2,1,0:T(8,128)}, bf16[4,512,512]{2,1,0:T(8,128)(2,1)}, f32[8,512]{1,0:T(8,128)}, f32[80,512]{1,0:T(8,128)}, bf16[4,64,512]{2,1,0:T(8,128)(2,1)}) custom-call(f32[1]{0:T(128)} %bitcast.bias_ref, f32[2,512,512]{2,1,0:T(8,128)} %get-tuple-element.160.dafter_ref, f32[2,512,512]{2,1,0:T(8,128)} %get-tuple-element.119.x_ref, ...), custom_call_target="tpu_custom_call" | custom-call | flops 30000001024 | bytes 20000000 | tf_op jit(solution)/shard_map/attend_back/pallas_call | solution.py:553
  273.7 57.4 %reduce_grads.1 = (bf16[8,4,64,512]{3,2,1,0:T(8,128)(2,1)}, bf16[6,64,512]{2,1,0:T(8,128)(2,1)}, f32[128,512]{1,0:T(8,128)}, f32[8,128]{1,0:T(8,128)}) custom-call(bf16[2,2,8,64,512]{4,3,2,1,0:T(8,128)(2,1)} %bitcast.49, bf16[64,512]{1,0:T(8,128)(2,1)} %get-tuple-element.171.attn_done_ref, bf16[4,64,512]{2,1,0:T(8,128)(2,1)} %get-tuple-element.172.feed_low_ref, ...), custom_call_target="tpu_custom_call" | custom-call | flops 100000000 | bytes 100000000 | tf_op jit(solution)/shard_map/reduce_grads/pallas_call | solution.py:1168
  331.1 50.6 %muon.1 = (bf16[4,6,64,512]{3,2,1,0:T(8,128)(2,1)}, bf16[4,6,64,512]{3,2,1,0:T(8,128)(2,1)}, f32[8,128]{1,0:T(8,128)}) custom-call(f32[8,128]{1,0:T(8,128)} %get-tuple-element.181.square_ref, bf16[8,4,64,512]{3,2,1,0:T(8,128)(2,1)} %get-tuple-element.182.whole_ref, bf16[8,6,64,512]{3,2,1,0:T(8,128)(2,1)} %all-gather.3.cloned.1.call-done.mom_ref, ...), custom_call_target="tpu_custom_call" | custom-call | flops 20000000000 | bytes 40000000 | tf_op jit(solution)/shard_map/muon/pallas_call | solution.py:1406
  381.7 0.0 all-gather.5.cloned.1.call-done
  381.7 13.0 %finish.1 = (f32[2,4,64,512]{3,2,1,0:T(8,128)}, f32[2,4,64,512]{3,2,1,0:T(8,128)}, bf16[2,4,64,512]{3,2,1,0:T(8,128)(2,1)}, f32[2,64,2048]{2,1,0:T(8,128)}, f32[...) custom-call(f32[8,128]{1,0:T(8,128)} %get-tuple-element.184.norm_ref, ...), custom_call_target="tpu_custom_call" | custom-call | flops 100000000 | bytes 40000000 | tf_op jit(solution)/shard_map/finish/pallas_call | solution.py:1670
Async XLA Ops:
  7.2 1.8 copy-start
  7.2 98.4 %all-gather.3.cloned.1.call-start = ((), (), s32[]{:S(2)}) async-start(), calls=%async_computation | async-start | bytes 3538944 | tf_op jit(solution)/shard_map/all_gather | solution.py:1754
  9.5 3.0 copy-start.1
  12.4 369.3 %all-gather.5.cloned.1.call-start = ((), (), s32[]{:S(2)}) async-start(), calls=%async_computation.1 | async-start | bytes 1081344 | tf_op jit(solution)/shard_map/all_gather | solution.py:1811
  43.0 25.2 %collective-permute-start.1 = (bf16[512,512]{1,0:T(8,128)(2,1)}, bf16[512,512]{1,0:T(8,128)(2,1)S(1)}, u32[]{:S(2)}, u32[]{:S(2)}) collective-permute-start(bf16[512,512]{1,0:T(8,128)(2,1)} %get-tuple-element.132), channel_id=1, source_target_pairs={{0,4},{4,8},{8,12},{12,16},{16,20},{20,24},{24,28},{1,5},{5,9},{9,... | collective-permute-start | bytes 1572872 | tf_op jit(solution)/shard_map/ppermute | solution.py:608
  63.1 23.9 %collective-permute-start = (bf16[512,512]{1,0:T(8,128)(2,1)}, bf16[512,512]{1,0:T(8,128)(2,1)S(1)}, u32[]{:S(2)}, u32[]{:S(2)}) collective-permute-start(bf16[512,512]{1,0:T(8,128)(2,1)} %get-tuple-element.131), channel_id=1, source_target_pairs={{0,4},{4,8},{8,12},{12,16},{16,20},{20,24},{24,28},{1,5},{5,9},{9,... | collective-permute-start | bytes 1572872 | tf_op jit(solution)/shard_map/ppermute | solution.py:608
  68.2 0.8 copy-start.2
  87.0 0.8 copy-start.3
Sparse Core Ops, SparseCore 0:
  12.5 40.9 all-gather.2
  147.2 52.8 all-gather.4

commit v6 on v5

--- a/solution.py
+++ b/solution.py
@@ -109,13 +109,15 @@
             scores = []
             for low, high, kind in spans:
                 part = dot_nt(q_both, k_ref[low:high, lanes])
-                if kind == 0:
-                    part = part + memory_bias
                 if kind == 2:
                     part = jnp.where(diagonal, part, -1e30)
                 scores.append(part)
-            most = functools.reduce(jnp.maximum, [jnp.max(part, -1, keepdims=True) for part in scores])
-            weights = [jnp.exp(part - most) for part in scores]
+            peaks = [jnp.max(part, -1, keepdims=True) for part in scores]
+            peaks[0] = peaks[0] + memory_bias
+            most = functools.reduce(jnp.maximum, peaks)
+            weights = [
+                jnp.exp(part - (most if place else most - memory_bias)) for place, part in enumerate(scores)
+            ]
             total = functools.reduce(jnp.add, [jnp.sum(part, -1, keepdims=True) for part in weights])
             mixed = functools.reduce(
                 jnp.add,
@@ -289,29 +291,33 @@
 
 def feed_back_kernel(streams, g_ref, after_ref, up_ref, down_ref, vec_ref, *refs):
     step = pl.program_id(0)
-    grad_ref, dafter_ref, dup_ref, ddown_ref, dvec_ref, done_ref, up_s, down_s, act_s, inner_s = refs[:10]
+    grad_ref, dafter_ref, dup_ref, ddown_ref, dvec_ref, done_ref, normed_s, branch_s, act_s, inner_s = refs[:10]
     carry = AttnCarry(grad_ref, refs[10 : 10 + CARRY_REFS], refs[10 + CARRY_REFS :])
-
-    def beat(place):
-        carry.tick(4 * step + place, 4 * streams, 2)
+    planes = carry.planes
+    later = range(1, planes)
+    beats = [
+        [("b", place) for place in range(planes)],
+        [("m", 0)],
+        [("m", place) for place in later] + [("e", 0)],
+        [("e", place) for place in range(1, planes // 2)],
+        [("e", place) for place in range(planes // 2, planes)],
+    ]
 
     @pl.when(step == 0)
     def _():
         hail(carry.targets)
         carry.load_all()
-
-    @pl.when(step == 0)
-    def _():
-        up_s[...] = jnp.zeros_like(up_s)
-        down_s[...] = jnp.zeros_like(down_s)
         dvec_ref[...] = jnp.zeros_like(dvec_ref)
 
+    rows = pl.ds(pl.multiple_of(step * SEG, SEG), SEG)
     grad = g_ref[...]
     branch = grad.astype(bf16)
     dvec_ref[2:3, :] += column_sum(branch.astype(f32))
     unit, scale = normalised(after_ref[...])
     gain = vec_ref[2:3, :]
     normed = (unit * gain + vec_ref[3:4, :]).astype(bf16)
+    normed_s[:, rows] = jnp.transpose(normed)
+    branch_s[:, rows] = jnp.transpose(branch)
 
     @pl.when(step == 0)
     def _():
@@ -323,32 +329,41 @@
         inner = dot_nn(normed, up_ref[:, columns]) + vec_ref[8 + tile : 9 + tile, :]
         dact = dot_nt(branch, down_ref[columns, :])
         square = inner * inner
-        bent = jnp.tanh(GELU_SCALE * (inner + 0.044715 * square * inner))
+        bent = jnp.tanh(inner * (GELU_SCALE + (GELU_SCALE * 0.044715) * square))
         half = 0.5 * (1.0 + bent)
-        act_s[:, columns] = (inner * half).astype(bf16)
-        slope = half + (0.5 * GELU_SCALE) * inner * (1.0 - bent * bent) * (1.0 + 0.134145 * square)
+        act_s[rows, columns] = (inner * half).astype(bf16)
+        slope = half + inner * (half * (1.0 - bent)) * (GELU_SCALE + (GELU_SCALE * 0.134145) * square)
         dinner = (dact * slope).astype(bf16)
-        inner_s[:, columns] = dinner
+        inner_s[rows, columns] = dinner
         dvec_ref[4 + tile : 5 + tile, :] += column_sum(dinner.astype(f32))
-        if tile % 2:
-            beat(tile // 2)
-    dnormed = dot_nt(inner_s[...], up_ref[...])
+
+    @pl.when(step == 0)
+    def _():
+        carry.run(beats[0])
+
+    @pl.when(step == streams - 1)
+    def _():
+        carry.run(beats[2])
+
+    dnormed = dot_nt(inner_s[rows, :], up_ref[...])
     dvec_ref[0:1, :] += column_sum(dnormed * unit)
     dvec_ref[1:2, :] += column_sum(dnormed)
     dafter_ref[...] = grad + norm_back(dnormed, gain, unit, scale)
-    beat(2)
-    normed_t = jnp.transpose(normed)
-    branch_t = jnp.transpose(branch)
-    up_s[...] += dot_nn(normed_t, inner_s[...])
-    down_s[...] += dot_nn(branch_t, act_s[...])
-    beat(3)
-
-    @pl.when(step == pl.num_programs(0) - 1)
+
+    @pl.when(step == 0)
     def _():
+        carry.run(beats[1])
+
+    @pl.when(step == streams - 1)
+    def _():
+        carry.run(beats[3])
         for tile in range(FF // TILE):
-            dup_ref[tile] = up_s[:, tile * TILE : (tile + 1) * TILE].astype(bf16)
-        ddown_ref[...] = jnp.transpose(down_s[...].astype(bf16))
-        carry.rest(4 * streams, 2)
+            columns = slice(tile * TILE, (tile + 1) * TILE)
+            dup_ref[tile] = dot_nn(normed_s[...], inner_s[:, columns]).astype(bf16)
+        carry.run(beats[4])
+        for tile in range(FF // TILE):
+            columns = slice(tile * TILE, (tile + 1) * TILE)
+            ddown_ref[columns, :] = jnp.transpose(dot_nn(branch_s[...], act_s[:, columns]).astype(bf16))
         carry.finish(done_ref)
 
 
@@ -375,10 +390,10 @@
         whole_spec((8, D)),
     ]
     scratch = [
-        pltpu.VMEM((D, FF), f32),
-        pltpu.VMEM((D, FF), f32),
-        pltpu.VMEM((SEG, FF), bf16),
-        pltpu.VMEM((SEG, FF), bf16),
+        pltpu.VMEM((D, streams * SEG), bf16),
+        pltpu.VMEM((D, streams * SEG), bf16),
+        pltpu.VMEM((streams * SEG, FF), bf16),
+        pltpu.VMEM((streams * SEG, FF), bf16),
     ]
     operands = [grad, after, upper, lower, vectors]
     in_specs.append(pl.BlockSpec(memory_space=pl.ANY))
@@ -488,9 +503,8 @@
             keys = slice(block * HALF, (block + 1) * HALF)
             start = 2 * HALF if block == 3 else 0
             scores = dot_nt(k_ref[keys, lanes], q_all[start:])
-            if block < 2:
-                scores = scores + memory_bias
-            weights = jnp.exp(scores - lse_all[:, start:])
+            shift = lse_all - memory_bias if block < 2 else lse_all[:, start:]
+            weights = jnp.exp(scores - shift)
             if block == 2:
                 weights = jnp.concatenate(
                     [jnp.where(diagonal, weights[:, : 2 * HALF], 0.0), weights[:, 2 * HALF :]], 1
@@ -720,10 +734,7 @@
             self.targets.append({"seg": 2 * self.toggled(bit) + self.core})
             bit *= 2
 
-        places = []
-        for low in range(self.planes.bit_length()):
-            places += [mask for mask in reversed(range(self.planes)) if lowest_bit(mask, self.planes) == 1 << low]
-        self.order = places
+        self.order = list(reversed(range(self.planes)))
 
     def toggled(self, mask):
         place, bit = self.plane, 1
@@ -779,18 +790,28 @@
             copy.start()
             copy.wait()
             held[...] = plus(held[...], self.goth[place, step])
-        mask, bit = self.order[step], 1
-        value = held[...].astype(f32)
+        mask = self.order[step]
+        if mask:
+            self.gathered(mask, held)
+            self.third(step).start()
+
+    def gathered(self, mask, held):
+        value, bit = held[...].astype(f32), 1
         while bit < lowest_bit(mask, self.planes):
             wait_bytes(self.got3.at[mask + bit], self.recv3.at[mask + bit])
             value = value + self.got3[mask + bit].astype(f32)
             bit *= 2
         held[...] = value.astype(held.dtype)
-        if mask:
-            self.third(step).start()
 
     def total(self):
-        return self.held(self.planes - 1)[...]
+        held = self.held(self.planes - 1)
+        self.gathered(0, held)
+        return held[...]
+
+    def run(self, acts):
+        for kind, step in acts:
+            if step < self.planes:
+                {"b": self.begin, "m": self.middle, "e": self.end}[kind](step)
 
     def actions(self, time, slack):
         planes = self.planes
@@ -827,35 +848,59 @@
         return self.mine.at[step, self.y, self.x]
 
     def first(self, step):
+        half = self.mine.shape[3] // 2
         return (
             remote(
-                self.mine.at[step, :, 1 - self.x],
-                self.got1.at[step],
-                self.send1.at[step],
-                self.recv1.at[step],
+                self.mine.at[step, :, 1 - self.x, 0:half],
+                self.got1.at[step, 0],
+                self.send1.at[step, 0],
+                self.recv1.at[step, 0],
+                self.across_x,
+            ),
+            remote(
+                self.mine.at[step, 1 - self.y, :, half:],
+                self.got1.at[step, 1],
+                self.send1.at[step, 1],
+                self.recv1.at[step, 1],
+                self.across_y,
+            ),
+        )
+
+    def second(self, step):
+        half = self.mine.shape[3] // 2
+        return (
+            remote(
+                self.mine.at[step, 1 - self.y, self.x, 0:half],
+                self.got2.at[step, 0],
+                self.send2.at[step, 0],
+                self.recv2.at[step, 0],
+                self.across_y,
+            ),
+            remote(
+                self.mine.at[step, self.y, 1 - self.x, half:],
+                self.got2.at[step, 1],
+                self.send2.at[step, 1],
+                self.recv2.at[step, 1],
                 self.across_x,
             ),
         )
 
-    def second(self, step):
-        return remote(
-            self.mine.at[step, 1 - self.y, self.x],
-            self.got2.at[step],
-            self.send2.at[step],
-            self.recv2.at[step],
-            self.across_y,
-        )
-
     def middle(self, step):
+        mine, half = self.mine, self.mine.shape[3] // 2
         for copy in self.first(step):
             copy.wait_recv()
         for place in range(2):
-            self.mine[step, place, self.x] = plus(self.mine[step, place, self.x], self.got1[step, place])
-        self.second(step).start()
+            mine[step, place, self.x, 0:half] = plus(mine[step, place, self.x, 0:half], self.got1[step, 0, place])
+            mine[step, self.y, place, half:] = plus(mine[step, self.y, place, half:], self.got1[step, 1, place])
+        for copy in self.second(step):
+            copy.start()
 
     def end(self, step):
-        self.second(step).wait_recv()
-        self.mine[step, self.y, self.x] = plus(self.mine[step, self.y, self.x], self.got2[step])
+        mine, half = self.mine, self.mine.shape[3] // 2
+        for copy in self.second(step):
+            copy.wait_recv()
+        mine[step, self.y, self.x, 0:half] = plus(mine[step, self.y, self.x, 0:half], self.got2[step, 0])
+        mine[step, self.y, self.x, half:] = plus(mine[step, self.y, self.x, half:], self.got2[step, 1])
         self.onward(step)
 
     def finish(self, out_ref):
@@ -865,9 +910,8 @@
     def drain(self):
         for step in range(self.planes):
             wait_bytes(self.mine.at[step], self.send0.at[step])
-            for copy in self.first(step):
+            for copy in self.first(step) + self.second(step):
                 copy.wait_send()
-            self.second(step).wait_send()
             if step < self.planes - 1:
                 self.third(step).wait_send()
 
@@ -969,22 +1013,29 @@
     planes = count // 2
     far = max(1, dp_count.bit_length() - 3)
     dma = pltpu.SemaphoreType.DMA
+    half = rows // 2
     if kind == "attn":
-        shapes = ((planes, 2, 2), (planes, 2, 2), (planes, 2), (planes,), (planes,), (far, planes))
-        pair = (planes,)
+        shapes = (
+            (planes, 2, 2, rows),
+            (planes, 2, 2, rows),
+            (planes, 2, 2, half),
+            (planes, 2, half),
+            (planes, rows),
+            (far, planes, rows),
+        )
     else:
         shapes = (
-            (planes, 2, 4),
-            (planes, 2, 4),
-            (planes, 2, 2),
-            (planes, 2, 2),
-            (planes, 4),
-            (far, planes, 4),
+            (planes, 2, 4, rows),
+            (planes, 2, 4, rows),
+            (planes, 2, 2, rows),
+            (planes, 2, 2, rows),
+            (planes, 4, rows),
+            (far, planes, 4, rows),
         )
-        pair = (planes, 2)
+    pair = (planes, 2)
     one = (planes,)
     sems = (one, one, one, pair, pair, pair, pair, one, one, (far, planes), (far, planes))
-    return [pltpu.VMEM(shape + (rows, D), dtype) for shape in shapes] + [dma(shape) for shape in sems]
+    return [pltpu.VMEM(shape + (D,), dtype) for shape in shapes] + [dma(shape) for shape in sems]
 
 
 def reduce_kernel(
@@ -1046,8 +1097,6 @@
         small_ref[inputs + 8 * place : inputs + 8 * place + 8, :] = ref[...]
     small_ref[inputs + 40 :, :] = jnp.zeros((SMALL - inputs - 40, D), f32)
     meet(targets)
-    carry.send_all()
-
     def small_steps():
         copy = remote(small_ref, small_core, small_send.at[0], small_recv.at[0], across_core)
         copy.start()
@@ -1081,6 +1130,7 @@
 
     small_run = small_steps()
     next(small_run)
+    carry.send_all()
     roles = owners(count)
 
     def gift(place):
@@ -1106,8 +1156,15 @@
 
     for place in (2, 3, 1):
         give(place)
-    for time in range(planes + 3):
-        carry.actions(time, 1)
+    acts = [
+        [("b", 0), ("b", 1)],
+        [("b", step) for step in range(2, planes)],
+        [("m", 0), ("m", 1)],
+        [("m", step) for step in range(2, planes)] + [("e", 0)],
+    ] + [[("e", step)] for step in range(1, planes)]
+    next(small_run)
+    for part in acts:
+        carry.run(part)
         next(small_run, None)
     own_ref[0] = carry.total()
     give(0)
@@ -1121,6 +1178,20 @@
     sq_seg[seg] = jnp.broadcast_to(square, (8, 128))
     for step, other in enumerate(others(seg, count)):
         remote(sq_seg.at[seg], sq_seg.at[seg], sq_send.at[step], sq_recv.at[seg], {"seg": other}).start()
+
+    def halves_copy(spot):
+        span = slice(spot, spot + 2)
+        return remote(whole_ref.at[:, span], whole_ref.at[:, span], half_sem.at[0], half_sem.at[1], across_core)
+
+    for place, (first, width, owner, spot) in enumerate(roles):
+        if width == 2:
+
+            @pl.when(seg == owner)
+            def _():
+                for other in others(seg, count):
+                    wait_bytes(whole_ref.at[other, spot : spot + width], whole_recv.at[other])
+                halves_copy(spot).start()
+
     for other in others(seg, count):
         wait_bytes(sq_seg.at[other], sq_recv.at[other])
     sq_dp[group] = jnp.sum(sq_seg[...], 0)
@@ -1138,15 +1209,11 @@
 
         @pl.when(seg == owner)
         def _():
-            for other in others(seg, count):
-                wait_bytes(whole_ref.at[other, spot : spot + width], whole_recv.at[other])
             if width == 2:
-                span = slice(spot, spot + width)
-                copy = remote(
-                    whole_ref.at[:, span], whole_ref.at[:, span], half_sem.at[0], half_sem.at[1], across_core
-                )
-                copy.start()
-                copy.wait()
+                halves_copy(spot).wait()
+            else:
+                for other in others(seg, count):
+                    wait_bytes(whole_ref.at[other, spot : spot + width], whole_recv.at[other])
 
     carry.drain()
     for place, (first, width, owner, spot) in enumerate(roles):

time: 410 us -> 389 us (0.949)
  Pallas kernels: 373 us -> 352 us
    pallas_call x1, Pallas kernels: 57.4 us -> 47.2 us  [reduce_grads(): pl.pallas_call(functools.partial(reduce_kernel, count), out_shape=[jax.Sh...]
    pallas_call x2, Pallas kernels: 97.2 us -> 90.4 us  [attend_back(): pl.pallas_call(functools.partial(attend_back_kernel, streams, depth), gri...]
  transfers between devices with their start and end apart: 4 -> 4, of which waited for: 0 -> 0; matrix products, arithmetic and copies ran while one was open for 0% -> 1% of each run, Pallas kernels for 79% -> 78%
where the time goes in v6:
time: 389 us; the launch traced here: 381 us
  Pallas kernels  352 us (90%)
  between operations  14.8 us (4%)
  local copies, waits for them, and re-layouts  7.71 us (2%)
  starting transfers between devices  6.04 us (2%)
    pallas_call x2, Pallas kernels, attend_back(): pl.pallas_call(functools.partial(attend_back_kernel, streams, depth), gri...  90.4 us
    pallas_call x4, Pallas kernels, forward_layer(): pl.pallas_call(forward_kernel, grid=(1,), out_shape=out_shape, in_specs=i...  71.1 us
    pallas_call x2, Pallas kernels, feed_back(): pl.pallas_call(functools.partial(feed_back_kernel, streams), grid=(stream...  58.3 us
    pallas_call x1, Pallas kernels, muon(): pl.pallas_call(functools.partial(muon_kernel, count), out_shape=[blocks,...  49 us
    pallas_call x1, Pallas kernels, reduce_grads(): pl.pallas_call(functools.partial(reduce_kernel, count), out_shape=[jax.Sh...  47.2 us
    pallas_call x1, Pallas kernels, finish(): pl.pallas_call(finish_kernel, grid=(steps,), out_shape=[like(attn), like(...  13 us
    pallas_call x1, Pallas kernels, embed(): pl.pallas_call(functools.partial(embed_kernel, count), out_shape=[jax.Sha...  12.1 us
    pallas_call x1, Pallas kernels, head(): pl.pallas_call(functools.partial(head_kernel, scale), grid=(streams,), ou...  10.5 us
  transfers between devices with their start and end apart: 4, of which 0 were waited for; matrix products, arithmetic and copies ran while one was open for 1% of the time, Pallas kernels for 78%

profile of v6, /device:TPU:0, one launch (start us, length us, event | category | flops | bytes accessed | tf_op | source)
XLA Modules:
  0.0 381.2 jit_solution(721998766611020834)
XLA Ops:
  7.2 0.0 copy-start
  7.2 0.0 all-gather.3.cloned.1.call-start
  7.3 1.3 fusion.4
  8.6 0.2 reshape_squeeze.6
  8.8 0.2 reshape_squeeze.7
  9.0 0.0 copy-done
  9.0 0.1 fusion.5
  9.1 0.2 copy.104
  9.3 0.2 copy.105
  9.5 0.0 copy-start.1
  9.5 1.0 dynamic-slice_convert_fusion
  10.5 0.1 copy.115
  10.6 0.6 fusion.3
  11.3 0.3 pad_maximum_fusion
  11.5 0.9 copy.106
  12.4 0.0 all-gather.3.cloned.1.call-update
  12.4 0.0 all-gather.5.cloned.1.call-start
  12.5 0.0 copy-done.1
  12.5 0.6 copy.100.vec_ref
  13.1 12.1 %embed.1 = (f32[2,512,512]{2,1,0:T(8,128)}, bf16[2,512,512]{2,1,0:T(8,128)(2,1)}, f32[8,128]{1,0:T(8,128)}) custom-call(bf16[2,80,512]{2,1,0:T(8,128)(2,1)} %bitcast.68, s32[2,512]{1,0:T(2,128)} %mask_ref.3, bf16[80,512]{1,0:T(8,128)(2,1)} %in_ref.1, f32[5,512]{1,0:T(8,128)} %refs_15_.1), custom_call_target="tpu_custom_call" | custom-call | flops 200000000 | bytes 4000000 | tf_op jit(solution)/shard_map/embed/pallas_call | solution.py:1544
  25.2 17.8 %layer_forward.4 = (f32[2,512,512]{2,1,0:T(8,128)}, bf16[512,512]{1,0:T(8,128)(2,1)}, bf16[2,1024,512]{2,1,0:T(8,128)(2,1)}, bf16[2,512,512]{2,1,0:T(8,128)(2,1)...) custom-call(f32[1]{0:T(128)} %bitcast.bias_ref, ...), custom_call_target="tpu_custom_call" | custom-call | flops 10000000000 | bytes 20000000 | tf_op jit(solution)/shard_map/layer_forward/pallas_call | solution.py:203
  43.0 2.2 collective-permute-start.1
  45.2 17.8 %layer_forward.5 = (f32[2,512,512]{2,1,0:T(8,128)}, bf16[512,512]{1,0:T(8,128)(2,1)}, bf16[2,1024,512]{2,1,0:T(8,128)(2,1)}, bf16[2,512,512]{2,1,0:T(8,128)(2,1)...) custom-call(f32[1]{0:T(128)} %bitcast.bias_ref, ...), custom_call_target="tpu_custom_call", output_to_operand_aliasing={{0}: (7, {}), {2}: (8, {}), {3}: (9, {}), {4}: (10, {}), {5... | custom-call | flops 10000000000 | bytes 20000000 | tf_op jit(solution)/shard_map/layer_forward/pallas_call | solution.py:203
  63.0 3.7 collective-permute-start
  66.7 0.7 slice_bitcast_fusion
  67.4 0.6 copy.112
  68.0 0.0 collective-permute-done.1.mem_ref
  68.0 0.0 copy-start.2
  68.0 0.8 copy-done.2
  68.8 17.9 %layer_forward.6 = (f32[2,512,512]{2,1,0:T(8,128)}, bf16[512,512]{1,0:T(8,128)(2,1)}, bf16[2,1024,512]{2,1,0:T(8,128)(2,1)}, bf16[2,512,512]{2,1,0:T(8,128)(2,1)...) custom-call(f32[1]{0:T(128)} %bitcast.bias_ref, ...), custom_call_target="tpu_custom_call" | custom-call | flops 10000000000 | bytes 20000000 | tf_op jit(solution)/shard_map/layer_forward/pallas_call | solution.py:203
  86.8 0.0 collective-permute-done.mem_ref
  86.8 0.0 copy-start.3
  86.8 0.8 copy-done.3
  87.6 17.7 %layer_forward.7 = (f32[2,512,512]{2,1,0:T(8,128)}, bf16[512,512]{1,0:T(8,128)(2,1)}, bf16[2,1024,512]{2,1,0:T(8,128)(2,1)}, bf16[2,512,512]{2,1,0:T(8,128)(2,1)...) custom-call(f32[1]{0:T(128)} %bitcast.bias_ref, ...), custom_call_target="tpu_custom_call", output_to_operand_aliasing={{0}: (7, {}), {2}: (8, {}), {3}: (9, {}), {4}: (10, {}), {5... | custom-call | flops 10000000000 | bytes 20000000 | tf_op jit(solution)/shard_map/layer_forward/pallas_call | solution.py:203
  105.3 0.0 all-gather.3.cloned.1.call-done.mom_ref
  105.3 10.5 %head.1 = (f32[2,512,512]{2,1,0:T(8,128)}, f32[2,2,256,512]{3,2,1,0:T(8,128)}, f32[8,512]{1,0:T(8,128)}) custom-call(f32[2,512,512]{2,1,0:T(8,128)} %get-tuple-element.142.x_ref, s32[2,512]{1,0:T(2,128)} %target_ref.1, s32[2,512]{1,0:T(2,128)} %mask_ref.3, f32[8,128]{1,0:T(8,128)} %get-tuple-element.143.total_ref, bf16[512,1024]{1,0:T(8,128)(2,1)} %out_ref.1, ...), custom_call_target="tpu_custom_call" | custom-call | flops 3300000000 | bytes 10000000 | tf_op jit(solution)/shard_map/head/pallas_call | solution.py:266
  115.9 30.0 %feed_back.2 = (f32[2,512,512]{2,1,0:T(8,128)}, bf16[4,512,512]{2,1,0:T(8,128)(2,1)}, bf16[2048,512]{1,0:T(8,128)(2,1)}, f32[8,512]{1,0:T(8,128)}, bf16[32,512]{1,0:T(8,128)(2,1)}) custom-call(f32[2,512,512]{2,1,0:T(8,128)} %get-tuple-element.144.g_ref, f32[2,512,512]{2,1,0:T(8,128)} %get-tuple-element.145.after_ref, bf16[2,512,2048]{2,1,0:T(8,128)(2,1)} %up_ref.11, ...), custom_call_target="tpu_custom_call" | custom-call | flops 11000000512 | bytes 20000000 | tf_op jit(solution)/shard_map/feed_back/pallas_call | solution.py:405
  145.8 0.0 all-gather.5.cloned.1.call-update
  145.9 47.9 %attend_back.2 = (f32[2,512,512]{2,1,0:T(8,128)}, bf16[4,512,512]{2,1,0:T(8,128)(2,1)}, f32[8,512]{1,0:T(8,128)}, f32[80,512]{1,0:T(8,128)}, bf16[4,64,512]{2,1,0:T(8,128)(2,1)}) custom-call(f32[1]{0:T(128)} %bitcast.bias_ref, f32[2,512,512]{2,1,0:T(8,128)} %get-tuple-element.147.dafter_ref, f32[2,512,512]{2,1,0:T(8,128)} %get-tuple-element.130.x_ref, ...), custom_call_target="tpu_custom_call" | custom-call | flops 30000001024 | bytes 20000000 | tf_op jit(solution)/shard_map/attend_back/pallas_call | solution.py:567
  193.8 28.3 %feed_back.3 = (f32[2,512,512]{2,1,0:T(8,128)}, bf16[4,512,512]{2,1,0:T(8,128)(2,1)}, bf16[2048,512]{1,0:T(8,128)(2,1)}, f32[8,512]{1,0:T(8,128)}, bf16[64,512]{1,0:T(8,128)(2,1)}) custom-call(f32[2,512,512]{2,1,0:T(8,128)} %get-tuple-element.157.g_ref, f32[2,512,512]{2,1,0:T(8,128)} %get-tuple-element.158.after_ref, bf16[2,512,2048]{2,1,0:T(8,128)(2,1)} %up_ref.11, ...), custom_call_target="tpu_custom_call" | custom-call | flops 11000000512 | bytes 20000000 | tf_op jit(solution)/shard_map/feed_back/pallas_call | solution.py:405
  222.2 42.4 %attend_back.3 = (f32[2,512,512]{2,1,0:T(8,128)}, bf16[4,512,512]{2,1,0:T(8,128)(2,1)}, f32[8,512]{1,0:T(8,128)}, f32[80,512]{1,0:T(8,128)}, bf16[4,64,512]{2,1,0:T(8,128)(2,1)}) custom-call(f32[1]{0:T(128)} %bitcast.bias_ref, f32[2,512,512]{2,1,0:T(8,128)} %get-tuple-element.160.dafter_ref, f32[2,512,512]{2,1,0:T(8,128)} %get-tuple-element.119.x_ref, ...), custom_call_target="tpu_custom_call" | custom-call | flops 30000001024 | bytes 20000000 | tf_op jit(solution)/shard_map/attend_back/pallas_call | solution.py:567
  264.6 47.2 %reduce_grads.1 = (bf16[8,4,64,512]{3,2,1,0:T(8,128)(2,1)}, bf16[6,64,512]{2,1,0:T(8,128)(2,1)}, f32[128,512]{1,0:T(8,128)}, f32[8,128]{1,0:T(8,128)}) custom-call(bf16[2,2,8,64,512]{4,3,2,1,0:T(8,128)(2,1)} %bitcast.49, bf16[64,512]{1,0:T(8,128)(2,1)} %get-tuple-element.171.attn_done_ref, bf16[4,64,512]{2,1,0:T(8,128)(2,1)} %get-tuple-element.172.feed_low_ref, ...), custom_call_target="tpu_custom_call" | custom-call | flops 100000000 | bytes 100000000 | tf_op jit(solution)/shard_map/reduce_grads/pallas_call | solution.py:1235
  311.9 49.0 %muon.1 = (bf16[4,6,64,512]{3,2,1,0:T(8,128)(2,1)}, bf16[4,6,64,512]{3,2,1,0:T(8,128)(2,1)}, f32[8,128]{1,0:T(8,128)}) custom-call(f32[8,128]{1,0:T(8,128)} %get-tuple-element.181.square_ref, bf16[8,4,64,512]{3,2,1,0:T(8,128)(2,1)} %get-tuple-element.182.whole_ref, bf16[8,6,64,512]{3,2,1,0:T(8,128)(2,1)} %all-gather.3.cloned.1.call-done.mom_ref, ...), custom_call_target="tpu_custom_call" | custom-call | flops 20000000000 | bytes 40000000 | tf_op jit(solution)/shard_map/muon/pallas_call | solution.py:1473
  360.8 0.0 all-gather.5.cloned.1.call-done
  360.8 13.0 %finish.1 = (f32[2,4,64,512]{3,2,1,0:T(8,128)}, f32[2,4,64,512]{3,2,1,0:T(8,128)}, bf16[2,4,64,512]{3,2,1,0:T(8,128)(2,1)}, f32[2,64,2048]{2,1,0:T(8,128)}, f32[...) custom-call(f32[8,128]{1,0:T(8,128)} %get-tuple-element.184.norm_ref, ...), custom_call_target="tpu_custom_call" | custom-call | flops 100000000 | bytes 40000000 | tf_op jit(solution)/shard_map/finish/pallas_call | solution.py:1737
Async XLA Ops:
  7.2 1.8 copy-start
  7.2 98.1 %all-gather.3.cloned.1.call-start = ((), (), s32[]{:S(2)}) async-start(), calls=%async_computation | async-start | bytes 3538944 | tf_op jit(solution)/shard_map/all_gather | solution.py:1821
  9.5 3.0 copy-start.1
  12.4 348.4 %all-gather.5.cloned.1.call-start = ((), (), s32[]{:S(2)}) async-start(), calls=%async_computation.1 | async-start | bytes 1081344 | tf_op jit(solution)/shard_map/all_gather | solution.py:1878
  43.0 25.1 %collective-permute-start.1 = (bf16[512,512]{1,0:T(8,128)(2,1)}, bf16[512,512]{1,0:T(8,128)(2,1)S(1)}, u32[]{:S(2)}, u32[]{:S(2)}) collective-permute-start(bf16[512,512]{1,0:T(8,128)(2,1)} %get-tuple-element.132), channel_id=1, source_target_pairs={{0,4},{4,8},{8,12},{12,16},{16,20},{20,24},{24,28},{1,5},{5,9},{9,... | collective-permute-start | bytes 1572872 | tf_op jit(solution)/shard_map/ppermute | solution.py:622
  63.0 23.8 %collective-permute-start = (bf16[512,512]{1,0:T(8,128)(2,1)}, bf16[512,512]{1,0:T(8,128)(2,1)S(1)}, u32[]{:S(2)}, u32[]{:S(2)}) collective-permute-start(bf16[512,512]{1,0:T(8,128)(2,1)} %get-tuple-element.131), channel_id=1, source_target_pairs={{0,4},{4,8},{8,12},{12,16},{16,20},{20,24},{24,28},{1,5},{5,9},{9,... | collective-permute-start | bytes 1572872 | tf_op jit(solution)/shard_map/ppermute | solution.py:622
  68.0 0.8 copy-start.2
  86.8 0.8 copy-start.3
Sparse Core Ops, SparseCore 0:
  12.5 40.9 all-gather.2
  146.0 53.5 all-gather.4

commit v7 on v6

--- a/solution.py
+++ b/solution.py
@@ -64,6 +64,8 @@
 
 
 def forward_kernel(
+    depth,
+    stream,
     bias_ref,
     x_ref,
     mem_ref,
@@ -73,8 +75,41 @@
     vec_ref,
     *refs,
 ):
-    hid_ref, hid16_ref, keyin_ref, q_ref, k_ref, v_ref, lse_ref, mixed_ref, after_ref, kept_ref, act_s, lse_s = refs[-12:]
-    kept_ref[...] = mem_ref[...]
+    (
+        hid_ref,
+        hid16_ref,
+        keyin_out,
+        q_out,
+        k_out,
+        v_out,
+        lse_ref,
+        mixed_ref,
+        after_ref,
+        kept_out,
+        act_s,
+        lse_s,
+        up_s,
+        down_s,
+        keyin_ref,
+        q_ref,
+        k_ref,
+        v_ref,
+        in_sem,
+        out_sem,
+    ) = refs[-20:]
+    weights_in = (
+        pltpu.make_async_copy(up_ref.at[depth], up_s, in_sem.at[0]),
+        pltpu.make_async_copy(down_ref.at[depth], down_s, in_sem.at[1]),
+    )
+    for copy in weights_in:
+        copy.start()
+    saved_out = [
+        pltpu.make_async_copy(source, target.at[stream], out_sem.at[place])
+        for place, (source, target) in enumerate(
+            ((keyin_ref, keyin_out), (q_ref, q_out), (k_ref, k_out), (v_ref, v_out))
+        )
+    ]
+    kept_out[...] = mem_ref[...]
     x = x_ref[...]
     own_unit, _ = normalised(x)
     gain, shift = vec_ref[0:1, :], vec_ref[1:2, :]
@@ -88,6 +123,8 @@
     k_ref[SEG:, :] = dot_nn(normed, attn_ref[1]).astype(bf16)
     v_ref[0:SEG, :] = (dot_nn(mem_normed, attn_ref[2]) + vec_ref[5:6, :]).astype(bf16)
     v_ref[SEG:, :] = (dot_nn(normed, attn_ref[2]) + vec_ref[5:6, :]).astype(bf16)
+    for copy in saved_out:
+        copy.start()
     first, second = head_masks()
     memory_bias = bias_ref[0]
     lane = lax.broadcasted_iota(jnp.int32, (HALF, PAIR), 1)
@@ -139,15 +176,19 @@
     after_ref[...] = after
     unit, _ = normalised(after)
     normed_two = (unit * vec_ref[2:3, :] + vec_ref[3:4, :]).astype(bf16)
+    for copy in weights_in:
+        copy.wait()
     for tile in range(FF // TILE):
         columns = slice(tile * TILE, (tile + 1) * TILE)
-        inner = dot_nn(normed_two, up_ref[:, columns]) + vec_ref[8 + tile : 9 + tile, :]
+        inner = dot_nn(normed_two, up_s[:, columns]) + vec_ref[8 + tile : 9 + tile, :]
         act_s[:, columns] = (
             0.5 * inner * (1.0 + jnp.tanh(GELU_SCALE * (inner + 0.044715 * inner * inner * inner)))
         ).astype(bf16)
-    hidden = after + (dot_nn(act_s[...], down_ref[...]) + vec_ref[7:8, :])
+    hidden = after + (dot_nn(act_s[...], down_s[...]) + vec_ref[7:8, :])
     hid_ref[...] = hidden
     hid16_ref[...] = hidden.astype(bf16)
+    for copy in saved_out:
+        copy.wait()
 
 
 SAVED = (
@@ -184,14 +225,16 @@
     saved_specs = [stream_spec(shape, stream) for shape, dtype in SAVED]
     out_shape = [saved_shapes[0], jax.ShapeDtypeStruct((SEG, D), bf16)] + saved_shapes[1:]
     out_specs = [saved_specs[0], whole_spec((SEG, D))] + saved_specs[1:]
+    for place in (2, 3, 4, 5):
+        out_specs[place] = pl.BlockSpec(memory_space=pl.ANY)
     operands = [bias, hidden, memory, attn, upper, lower, vectors]
     in_specs = [
         pl.BlockSpec(memory_space=pltpu.SMEM),
         stream_spec((SEG, D), stream),
         stream_spec((SEG, D), stream) if memory.ndim == 3 else whole_spec((SEG, D)),
         layer_spec(attn.shape[1:], depth),
-        layer_spec(upper.shape[1:], depth),
-        layer_spec(lower.shape[1:], depth),
+        pl.BlockSpec(memory_space=pl.ANY),
+        pl.BlockSpec(memory_space=pl.ANY),
         layer_spec(vectors.shape[1:], depth),
     ]
     aliases = {}
@@ -201,12 +244,23 @@
             operands.append(array)
             in_specs.append(pl.BlockSpec(memory_space=pl.ANY))
     out = pl.pallas_call(
-        forward_kernel,
+        functools.partial(forward_kernel, depth, stream),
         grid=(1,),
         out_shape=out_shape,
         in_specs=in_specs,
         out_specs=out_specs,
-        scratch_shapes=[pltpu.VMEM((SEG, FF), bf16), pltpu.VMEM((SEG, PAIR), f32)],
+        scratch_shapes=[
+            pltpu.VMEM((SEG, FF), bf16),
+            pltpu.VMEM((SEG, PAIR), f32),
+            pltpu.VMEM((D, FF), bf16),
+            pltpu.VMEM((FF, D), bf16),
+            pltpu.VMEM((2 * SEG, D), bf16),
+            pltpu.VMEM((SEG, D), bf16),
+            pltpu.VMEM((2 * SEG, D), bf16),
+            pltpu.VMEM((2 * SEG, D), bf16),
+            pltpu.SemaphoreType.DMA((2,)),
+            pltpu.SemaphoreType.DMA((4,)),
+        ],
         input_output_aliases=aliases,
         compiler_params=pltpu.CompilerParams(vmem_limit_bytes=VMEM_LIMIT),
         cost_estimate=pl.CostEstimate(flops=10**10, bytes_accessed=2 * 10**7, transcendentals=10**7),
@@ -215,7 +269,7 @@
     return [out[0]] + list(out[2:]), out[1]
 
 
-def head_kernel(scale, x_ref, target_ref, mask_ref, total_ref, out_ref, outer_ref, bias_ref, mom_ref, g_ref, dout_ref, douter_ref, acc_s):
+def head_kernel(scale, x_ref, target_ref, mask_ref, total_ref, out_ref, outer_ref, mom_ref, g_ref, dout_ref, douter_ref, acc_s):
     step = pl.program_id(0)
 
     @pl.when(step == 0)
@@ -226,7 +280,8 @@
     unit, rscale = normalised(x_ref[...])
     gain = outer_ref[1:2, :]
     normed = (unit * gain + outer_ref[2:3, :]).astype(bf16)
-    logits = dot_nn(normed, out_ref[...]) + bias_ref[...]
+    shift = jnp.concatenate([outer_ref[3:4, :], outer_ref[4:5, :]], 1)
+    logits = dot_nn(normed, out_ref[...]) + shift
     most = jnp.max(logits, -1, keepdims=True)
     powers = jnp.exp(logits - most)
     total = jnp.sum(powers, -1, keepdims=True)
@@ -262,7 +317,6 @@
 def head(hidden, targets, mask, totals, out_weight, outer_vectors, scale, momenta):
     streams = hidden.shape[0]
     codes = out_weight.shape[1]
-    bias = outer_vectors[3:].reshape(1, codes)
     return pl.pallas_call(
         functools.partial(head_kernel, scale),
         grid=(streams,),
@@ -278,7 +332,6 @@
             whole_spec((8, 128)),
             whole_spec((D, codes)),
             whole_spec(outer_vectors.shape),
-            whole_spec((1, codes)),
             pl.BlockSpec(memory_space=pl.ANY),
         ],
         out_specs=[stream_spec((SEG, D)), whole_spec((2, 2, D // 2, D)), whole_spec((8, D))],
@@ -286,7 +339,7 @@
         compiler_params=pltpu.CompilerParams(vmem_limit_bytes=VMEM_LIMIT),
         cost_estimate=pl.CostEstimate(flops=33 * 10**8, bytes_accessed=10**7, transcendentals=10**6),
         name="head",
-    )(hidden, targets, mask, totals, out_weight, outer_vectors, bias, momenta)
+    )(hidden, targets, mask, totals, out_weight, outer_vectors, momenta)
 
 
 def feed_back_kernel(streams, g_ref, after_ref, up_ref, down_ref, vec_ref, *refs):
@@ -449,7 +502,7 @@
 ):
     step = pl.program_id(0)
     pairs = HEADS // 2
-    carry = FeedCarry(depth, dup_ref, ddown_ref, refs[:CARRY_REFS], refs[CARRY_REFS:])
+    carry = FeedCarry(depth, dup_ref, ddown_ref, refs[: CARRY_REFS + 2], refs[CARRY_REFS + 2 :])
 
     @pl.when(step == 0)
     def _():
@@ -918,7 +971,9 @@
 
 class FeedCarry(Carry):
     def __init__(self, depth, up, down, refs, sems):
-        super().__init__(refs, sems)
+        super().__init__(refs[:CARRY_REFS], sems[:CARRY_SEMS])
+        self.sums, self.got4 = refs[CARRY_REFS:]
+        self.send4, self.recv4 = sems[CARRY_SEMS:]
         self.up, self.down = up, down
         self.owner = (self.x == self.y) if depth == 1 else (self.x != self.y)
         self.keep = self.x if depth == 1 else 1 - self.x
@@ -927,7 +982,7 @@
         return ((self.up.at[:, row], (0,)), (self.down.at[row], (1,)))
 
     def held(self, step):
-        return self.mine.at[step, self.y]
+        return self.sums.at[step]
 
     def first(self, step):
         return (
@@ -950,14 +1005,14 @@
     def second(self, step):
         return (
             remote(
-                self.mine.at[step, self.keep, 0:2],
+                self.mine.at[step, self.keep, 1 - self.y],
                 self.got2.at[step, 0],
                 self.send2.at[step, 0],
                 self.recv2.at[step, 0],
                 self.across_y,
             ),
             remote(
-                self.mine.at[step, self.y, 2:4],
+                self.mine.at[step, self.y, 3 - self.x],
                 self.got2.at[step, 1],
                 self.send2.at[step, 1],
                 self.recv2.at[step, 1],
@@ -970,39 +1025,49 @@
             copy.wait_recv()
         self.mine[step, self.keep, 0:2] = plus(self.mine[step, self.keep, 0:2], self.got1[step, 0])
         self.mine[step, self.y, 2:4] = plus(self.mine[step, self.y, 2:4], self.got1[step, 1])
-
-        @pl.when(jnp.logical_not(self.owner))
-        def _():
-            for copy in self.second(step):
-                copy.start()
+        for copy in self.second(step):
+            copy.start()
 
     def end(self, step):
+        for copy in self.second(step):
+            copy.wait_recv()
+        self.sums[step, 0] = plus(self.mine[step, self.keep, self.y], self.got2[step, 0])
+        self.sums[step, 1] = plus(self.mine[step, self.y, 2 + self.x], self.got2[step, 1])
+        self.onward(step)
+
+    def last(self):
+        step = self.planes - 1
+        return (
+            remote(self.sums.at[step, 0], self.got4.at[0], self.send4.at[0], self.recv4.at[0], self.across_y),
+            remote(self.sums.at[step, 1], self.got4.at[1], self.send4.at[1], self.recv4.at[1], self.across_x),
+        )
+
+    def finish(self, out_ref):
+        value = self.total()
+
         @pl.when(self.owner)
         def _():
             for place in range(2):
-                wait_bytes(self.got2.at[step, place], self.recv2.at[step, place])
-                span = slice(2 * place, 2 * place + 2)
-                self.mine[step, self.y, span] = plus(self.mine[step, self.y, span], self.got2[step, place])
-            self.onward(step)
-
-    def finish(self, out_ref):
-        @pl.when(self.owner)
-        def _():
-            out_ref[...] = self.total().astype(out_ref.dtype)
-            for step in range(self.planes - 1):
-                self.third(step).wait_send()
+                wait_bytes(self.got4.at[place], self.recv4.at[place])
+            out_ref[self.y] = value[0]
+            out_ref[1 - self.y] = self.got4[0]
+            out_ref[2 + self.x] = value[1]
+            out_ref[3 - self.x] = self.got4[1]
 
         @pl.when(jnp.logical_not(self.owner))
         def _():
+            for copy in self.last():
+                copy.start()
             out_ref[...] = jnp.zeros_like(out_ref)
-            for step in range(self.planes):
-                for copy in self.second(step):
-                    copy.wait_send()
+            for copy in self.last():
+                copy.wait_send()
 
         for step in range(self.planes):
             wait_bytes(self.mine.at[step], self.send0.at[step])
-            for copy in self.first(step):
+            for copy in self.first(step) + self.second(step):
                 copy.wait_send()
+            if step < self.planes - 1:
+                self.third(step).wait_send()
 
 
 CARRY_REFS = 6
@@ -1028,13 +1093,17 @@
             (planes, 2, 4, rows),
             (planes, 2, 4, rows),
             (planes, 2, 2, rows),
-            (planes, 2, 2, rows),
-            (planes, 4, rows),
-            (far, planes, 4, rows),
+            (planes, 2, rows),
+            (planes, 2, rows),
+            (far, planes, 2, rows),
+            (planes, 2, rows),
+            (2, rows),
         )
     pair = (planes, 2)
     one = (planes,)
     sems = (one, one, one, pair, pair, pair, pair, one, one, (far, planes), (far, planes))
+    if kind == "feed":
+        sems = sems + ((2,), (2,))
     return [pltpu.VMEM(shape + (D,), dtype) for shape in shapes] + [dma(shape) for shape in sems]
 
 
@@ -1281,11 +1350,35 @@
     )
 
 
-def times_t(left, right):
+def mirrored(first, second, third):
+    return jnp.concatenate(
+        [
+            jnp.concatenate([first, second], 1),
+            jnp.concatenate([jnp.transpose(second), third], 1),
+        ],
+        0,
+    )
+
+
+def times_even(left, right):
     (left_high, left_low), (right_high, right_low) = left, right
-    return dot_nt(
-        jnp.concatenate([left_high, left_high, left_low], 1),
-        jnp.concatenate([right_high, right_low, right_high], 1),
+    wide = jnp.concatenate([left_high, left_high, left_low], 1)
+    tall = jnp.concatenate([right_high, right_low, right_high], 0)
+    return mirrored(
+        dot_nn(wide[:HALF], tall[:, :HALF]),
+        dot_nn(wide[:HALF], tall[:, HALF:]),
+        dot_nn(wide[HALF:], tall[:, HALF:]),
+    )
+
+
+def gram_of(both):
+    high, low = both
+    wide = jnp.concatenate([high, high, low], 1)
+    tall = jnp.concatenate([high, low, high], 1)
+    return mirrored(
+        dot_nt(wide[:HALF], tall[:HALF]),
+        dot_nt(wide[:HALF], tall[HALF:]),
+        dot_nt(wide[HALF:], tall[HALF:]),
     )
 
 
@@ -1367,9 +1460,9 @@
         def sweep(_, carry):
             value = x_s[...]
             both = halves(value)
-            gram = times_t(both, both)
+            gram = gram_of(both)
             gram_both = halves(gram)
-            poly = -4.775 * gram + 2.0315 * times(gram_both, gram_both)
+            poly = -4.775 * gram + 2.0315 * times_even(gram_both, gram_both)
             x_s[...] = 3.4445 * value + times(halves(poly), both)
             return carry
 
@@ -1398,7 +1491,7 @@
                 low_s[tile] = jnp.transpose(low_s[tile])
 
             both = high_s[tile], low_s[tile]
-            gram_s[...] += times_t(both, both)
+            gram_s[...] += gram_of(both)
             return size + jnp.sum(jnp.sum(value * value, 0, keepdims=True), 1, keepdims=True)
 
         size = lax.fori_loop(0, 4, gather, jnp.zeros((1, 1), f32))
@@ -1406,10 +1499,10 @@
         gram_s[...] = gram_s[...] * (scale * scale)
 
         def poly_of(gram, gram_both):
-            return 3.4445 * eye - 4.775 * gram + 2.0315 * times(gram_both, gram_both)
+            return 3.4445 * eye - 4.775 * gram + 2.0315 * times_even(gram_both, gram_both)
 
         def advance(gram_both, poly_both):
-            gram_s[...] = times(halves(times(gram_both, poly_both)), poly_both)
+            gram_s[...] = times_even(halves(times_even(gram_both, poly_both)), poly_both)
 
         gram = gram_s[...]
         gram_both = halves(gram)
@@ -1421,13 +1514,13 @@
             gram = gram_s[...]
             gram_both = halves(gram)
             poly_both = halves(poly_of(gram, gram_both))
-            q_s[...] = times(halves(q_s[...]), poly_both)
+            q_s[...] = times_even(halves(q_s[...]), poly_both)
             advance(gram_both, poly_both)
             return carry
 
         lax.fori_loop(0, 3, sweep, 0)
         gram = gram_s[...]
-        last = times(halves(q_s[...]), halves(poly_of(gram, halves(gram)))) * scale
+        last = times_even(halves(q_s[...]), halves(poly_of(gram, halves(gram)))) * scale
         last_both = halves(last)
         for slot in range(2):
             tile = 2 * core + slot
@@ -1503,11 +1596,17 @@
     mask_ref,
     in_ref,
     outer_ref,
+    attn_mom_ref,
+    up_mom_ref,
+    down_mom_ref,
     x_ref,
     mem_ref,
     total_ref,
+    owned_ref,
     got_s,
     count_s,
+    mom_s,
+    mom_sem,
     frame_send,
     frame_recv,
     count_send,
@@ -1516,6 +1615,20 @@
     seg = lax.axis_index("seg")
     after, before = lax.rem(seg + 1, count), lax.rem(seg + count - 1, count)
     streams = frames_ref.shape[0]
+    group = lax.rem(lax.axis_index("dp"), GROUPS)
+    for depth in range(LAYERS):
+        pltpu.make_async_copy(attn_mom_ref.at[depth, group], mom_s.at[depth], mom_sem.at[0]).start()
+
+        @pl.when(group == FEED_UP[depth])
+        def _():
+            for tile in range(4):
+                source = up_mom_ref.at[depth, :, pl.ds(tile * TILE, TILE)]
+                pltpu.make_async_copy(source, mom_s.at[2 + tile], mom_sem.at[0]).start()
+
+        @pl.when(group == FEED_DOWN[depth])
+        def _():
+            pltpu.make_async_copy(down_mom_ref.at[depth], mom_s.at[2:6], mom_sem.at[0]).start()
+
     tally = jnp.sum(mask_ref[...].astype(f32), 1, keepdims=True)
     count_s[seg] = jnp.broadcast_to(
         jnp.concatenate([tally, jnp.zeros((8 - streams, 1), f32)], 0), (8, 128)
@@ -1528,6 +1641,8 @@
     weight, shift = in_ref[...], outer_ref[0:1, :]
     for stream in range(streams):
         x_ref[stream] = dot_nn(jnp.transpose(frames_ref[stream]), weight) + shift
+    wait_bytes(mom_s, mom_sem.at[0])
+    owned_ref[...] = mom_s[...].astype(bf16)
     frame_copy.wait()
     for stream in range(streams):
         mem_ref[stream] = (dot_nn(jnp.transpose(got_s[stream]), weight) + shift).astype(bf16)
@@ -1538,8 +1653,9 @@
         wait_bytes(count_s.at[0], count_send.at[step])
 
 
-def embed(count, frames, mask, in_weight, outer_vectors):
+def embed(count, frames, mask, in_weight, outer_vectors, attn_mom, up_mom, down_mom):
     streams = frames.shape[0]
+    rows = D // count
     dma = pltpu.SemaphoreType.DMA
     return pl.pallas_call(
         functools.partial(embed_kernel, count),
@@ -1547,12 +1663,15 @@
             jax.ShapeDtypeStruct((streams, SEG, D), f32),
             jax.ShapeDtypeStruct((streams, SEG, D), bf16),
             jax.ShapeDtypeStruct((8, 128), f32),
+            jax.ShapeDtypeStruct((UNITS, rows, D), bf16),
         ],
-        in_specs=[pl.BlockSpec(memory_space=pltpu.VMEM)] * 4,
-        out_specs=[pl.BlockSpec(memory_space=pltpu.VMEM)] * 3,
+        in_specs=[pl.BlockSpec(memory_space=pltpu.VMEM)] * 4 + [pl.BlockSpec(memory_space=pl.ANY)] * 3,
+        out_specs=[pl.BlockSpec(memory_space=pltpu.VMEM)] * 4,
         scratch_shapes=[
             pltpu.VMEM(frames.shape, bf16),
             pltpu.VMEM((count, 8, 128), f32),
+            pltpu.VMEM((UNITS, rows, D), f32),
+            dma((1,)),
             dma((1,)),
             dma((1,)),
             dma((count,)),
@@ -1563,7 +1682,7 @@
         ),
         cost_estimate=pl.CostEstimate(flops=2 * 10**8, bytes_accessed=4 * 10**6, transcendentals=0),
         name="embed",
-    )(frames, mask, in_weight, outer_vectors)
+    )(frames, mask, in_weight, outer_vectors, attn_mom, up_mom, down_mom.reshape(LAYERS, 4, rows, D))
 
 
 FEED_UP = (1, 0)
@@ -1802,26 +1921,12 @@
     rows = D // count
     streams = frames.shape[0]
     stream_total = streams * dp_count
-    group = lax.axis_index("dp") % GROUPS
-    feeds = jnp.stack(
-        [
-            jnp.swapaxes(up_momentum[1].reshape(rows, 4, D), 0, 1),
-            jnp.swapaxes(up_momentum[0].reshape(rows, 4, D), 0, 1),
-            down_momentum[0].reshape(4, rows, D),
-            down_momentum[1].reshape(4, rows, D),
-        ]
-    )
-    owned = jnp.concatenate(
-        [
-            lax.dynamic_index_in_dim(attn_momentum, group, 1, keepdims=False),
-            lax.dynamic_index_in_dim(feeds, group, 0, keepdims=False),
-        ],
-        0,
-    ).astype(bf16)
-    momenta = lax.all_gather(owned, "seg", axis=0, tiled=False)
     frames_t = jnp.swapaxes(frames, 1, 2)
     bias = jnp.where(segment > 0, 0.0, -1e30).astype(f32)[None]
-    hidden, memory, totals = embed(count, frames_t, speech_mask, in_copy, outer_vectors)
+    hidden, memory, totals, owned = embed(
+        count, frames_t, speech_mask, in_copy, outer_vectors, attn_momentum, up_momentum, down_momentum
+    )
+    momenta = lax.all_gather(owned, "seg", axis=0, tiled=False)
     memory = [memory] * streams
     kept = []
     for depth in range(LAYERS):

time: 389 us -> 375 us (0.964)
  Pallas kernels: 352 us -> 346 us
  local copies, waits for them, and re-layouts: 7.71 us -> 2.22 us
  transfers between devices with their start and end apart: 4 -> 4, of which waited for: 0 -> 0; matrix products, arithmetic and copies ran while one was open for 1% -> 0% of each run, Pallas kernels for 78% -> 76%
where the time goes in v7:
time: 375 us; the launch traced here: 369 us
  Pallas kernels  346 us (92%)
  between operations  14.7 us (4%)
  starting transfers between devices  6.01 us (2%)
    pallas_call x2, Pallas kernels, attend_back(): pl.pallas_call(functools.partial(attend_back_kernel, streams, depth), gri...  93.6 us
    pallas_call x4, Pallas kernels, forward_layer(): pl.pallas_call(functools.partial(forward_kernel, depth, stream), grid=(1,...  68.2 us
    pallas_call x2, Pallas kernels, feed_back(): pl.pallas_call(functools.partial(feed_back_kernel, streams), grid=(stream...  59.1 us
    pallas_call x1, Pallas kernels, muon(): pl.pallas_call(functools.partial(muon_kernel, count), out_shape=[blocks,...  45.3 us
    pallas_call x1, Pallas kernels, reduce_grads(): pl.pallas_call(functools.partial(reduce_kernel, count), out_shape=[jax.Sh...  43.7 us
    pallas_call x1, Pallas kernels, finish(): pl.pallas_call(finish_kernel, grid=(steps,), out_shape=[like(attn), like(...  13 us
    pallas_call x1, Pallas kernels, embed(): pl.pallas_call(functools.partial(embed_kernel, count), out_shape=[jax.Sha...  12.2 us
    pallas_call x1, Pallas kernels, head(): pl.pallas_call(functools.partial(head_kernel, scale), grid=(streams,), ou...  10.5 us
  transfers between devices with their start and end apart: 4, of which 0 were waited for; matrix products, arithmetic and copies ran while one was open for 0% of the time, Pallas kernels for 76%

profile of v7, /device:TPU:0, one launch (start us, length us, event | category | flops | bytes accessed | tf_op | source)
XLA Modules:
  0.0 368.6 jit_solution(9434558387352948216)
XLA Ops:
  7.2 0.0 copy-start
  7.2 0.0 all-gather.6.cloned.1.call-start
  7.3 12.2 %embed.1 = (f32[2,512,512]{2,1,0:T(8,128)}, bf16[2,512,512]{2,1,0:T(8,128)(2,1)}, f32[8,128]{1,0:T(8,128)}, bf16[6,64,512]{2,1,0:T(8,128)(2,1)}) custom-call(bf16[2,80,512]{2,1,0:T(8,128)(2,1)} %bitcast.40, s32[2,512]{1,0:T(2,128)} %mask_ref.3, bf16[80,512]{1,0:T(8,128)(2,1)} %in_ref.1, f32[5,512]{1,0:T(8,128)} %refs_15_.1, f32[2,4,64,512]{3,2,1,0:T(8,128)} %refs_1_.1, ...), custom_call_target="tpu_custom_call" | custom-call | flops 200000000 | bytes 4000000 | tf_op jit(solution)/shard_map/embed/pallas_call | solution.py:1660
  19.5 0.0 all-gather.6.cloned.1.call-update
  19.5 0.0 all-gather.4.cloned.1.call-start
  19.5 0.0 copy-done
  19.6 0.6 copy.78.vec_ref
  20.2 17.0 %layer_forward.4 = (f32[2,512,512]{2,1,0:T(8,128)}, bf16[512,512]{1,0:T(8,128)(2,1)}, bf16[2,1024,512]{2,1,0:T(8,128)(2,1)}, bf16[2,512,512]{2,1,0:T(8,128)(2,1)...) custom-call(f32[1]{0:T(128)} %bitcast.bias_ref, ...), custom_call_target="tpu_custom_call" | custom-call | flops 10000000000 | bytes 20000000 | tf_op jit(solution)/shard_map/layer_forward/pallas_call | solution.py:246
  37.2 2.2 collective-permute-start.1
  39.4 17.0 %layer_forward.5 = (f32[2,512,512]{2,1,0:T(8,128)}, bf16[512,512]{1,0:T(8,128)(2,1)}, bf16[2,1024,512]{2,1,0:T(8,128)(2,1)}, bf16[2,512,512]{2,1,0:T(8,128)(2,1)...) custom-call(f32[1]{0:T(128)} %bitcast.bias_ref, ...), custom_call_target="tpu_custom_call", output_to_operand_aliasing={{0}: (7, {}), {2}: (8, {}), {3}: (9, {}), {4}: (10, {}), {5... | custom-call | flops 10000000000 | bytes 20000000 | tf_op jit(solution)/shard_map/layer_forward/pallas_call | solution.py:246
  56.5 3.7 %collective-permute-start = (bf16[512,512]{1,0:T(8,128)(2,1)}, bf16[512,512]{1,0:T(8,128)(2,1)S(1)}, u32[]{:S(2)}, u32[]{:S(2)}) collective-permute-start(bf16[512,512]{1,0:T(8,128)(2,1)} %get-tuple-element.132), channel_id=1, source_target_pairs={{0,4},{4,8},{8,12},{12,16},{16,20},{20,24},{24,28},{1,5},{5,9},{9,... | collective-permute-start | bytes 1572872 | tf_op jit(solution)/shard_map/ppermute | solution.py:675
  60.2 0.0 collective-permute-done.1.mem_ref
  60.2 0.0 copy-start.1
  60.2 0.8 copy-done.1
  61.0 17.2 %layer_forward.6 = (f32[2,512,512]{2,1,0:T(8,128)}, bf16[512,512]{1,0:T(8,128)(2,1)}, bf16[2,1024,512]{2,1,0:T(8,128)(2,1)}, bf16[2,512,512]{2,1,0:T(8,128)(2,1)...) custom-call(f32[1]{0:T(128)} %bitcast.bias_ref, ...), custom_call_target="tpu_custom_call" | custom-call | flops 10000000000 | bytes 20000000 | tf_op jit(solution)/shard_map/layer_forward/pallas_call | solution.py:246
  78.1 0.0 collective-permute-done.mem_ref
  78.2 0.0 copy-start.2
  78.2 0.8 copy-done.2
  78.9 17.0 %layer_forward.7 = (f32[2,512,512]{2,1,0:T(8,128)}, bf16[512,512]{1,0:T(8,128)(2,1)}, bf16[2,1024,512]{2,1,0:T(8,128)(2,1)}, bf16[2,512,512]{2,1,0:T(8,128)(2,1)...) custom-call(f32[1]{0:T(128)} %bitcast.bias_ref, ...), custom_call_target="tpu_custom_call", output_to_operand_aliasing={{0}: (7, {}), {2}: (8, {}), {3}: (9, {}), {4}: (10, {}), {5... | custom-call | flops 10000000000 | bytes 20000000 | tf_op jit(solution)/shard_map/layer_forward/pallas_call | solution.py:246
  96.0 0.0 all-gather.6.cloned.1.call-done
  96.0 10.5 %head.1 = (f32[2,512,512]{2,1,0:T(8,128)}, f32[2,2,256,512]{3,2,1,0:T(8,128)}, f32[8,512]{1,0:T(8,128)}) custom-call(f32[2,512,512]{2,1,0:T(8,128)} %get-tuple-element.143.x_ref, s32[2,512]{1,0:T(2,128)} %target_ref.1, s32[2,512]{1,0:T(2,128)} %mask_ref.3, f32[8,128]{1,0:T(8,128)} %get-tuple-element.144.total_ref, bf16[512,1024]{1,0:T(8,128)(2,1)} %out_ref.1, ...), custom_call_target="tpu_custom_call" | custom-call | flops 3300000000 | bytes 10000000 | tf_op jit(solution)/shard_map/head/pallas_call | solution.py:320
  106.5 30.6 %feed_back.2 = (f32[2,512,512]{2,1,0:T(8,128)}, bf16[4,512,512]{2,1,0:T(8,128)(2,1)}, bf16[2048,512]{1,0:T(8,128)(2,1)}, f32[8,512]{1,0:T(8,128)}, bf16[32,512]{1,0:T(8,128)(2,1)}) custom-call(f32[2,512,512]{2,1,0:T(8,128)} %get-tuple-element.146.g_ref, f32[2,512,512]{2,1,0:T(8,128)} %get-tuple-element.147.after_ref, bf16[2,512,2048]{2,1,0:T(8,128)(2,1)} %up_ref.11, ...), custom_call_target="tpu_custom_call" | custom-call | flops 11000000512 | bytes 20000000 | tf_op jit(solution)/shard_map/feed_back/pallas_call | solution.py:458
  137.1 0.0 all-gather.4.cloned.1.call-update
  137.2 47.1 %attend_back.2 = (f32[2,512,512]{2,1,0:T(8,128)}, bf16[4,512,512]{2,1,0:T(8,128)(2,1)}, f32[8,512]{1,0:T(8,128)}, f32[80,512]{1,0:T(8,128)}, bf16[4,64,512]{2,1,0:T(8,128)(2,1)}) custom-call(f32[1]{0:T(128)} %bitcast.bias_ref, f32[2,512,512]{2,1,0:T(8,128)} %get-tuple-element.149.dafter_ref, f32[2,512,512]{2,1,0:T(8,128)} %get-tuple-element.131.x_ref, ...), custom_call_target="tpu_custom_call" | custom-call | flops 30000001024 | bytes 20000000 | tf_op jit(solution)/shard_map/attend_back/pallas_call | solution.py:620
  184.3 28.5 %feed_back.3 = (f32[2,512,512]{2,1,0:T(8,128)}, bf16[4,512,512]{2,1,0:T(8,128)(2,1)}, bf16[2048,512]{1,0:T(8,128)(2,1)}, f32[8,512]{1,0:T(8,128)}, bf16[64,512]{1,0:T(8,128)(2,1)}) custom-call(f32[2,512,512]{2,1,0:T(8,128)} %get-tuple-element.159.g_ref, f32[2,512,512]{2,1,0:T(8,128)} %get-tuple-element.160.after_ref, bf16[2,512,2048]{2,1,0:T(8,128)(2,1)} %up_ref.11, ...), custom_call_target="tpu_custom_call" | custom-call | flops 11000000512 | bytes 20000000 | tf_op jit(solution)/shard_map/feed_back/pallas_call | solution.py:458
  212.7 46.5 %attend_back.3 = (f32[2,512,512]{2,1,0:T(8,128)}, bf16[4,512,512]{2,1,0:T(8,128)(2,1)}, f32[8,512]{1,0:T(8,128)}, f32[80,512]{1,0:T(8,128)}, bf16[4,64,512]{2,1,0:T(8,128)(2,1)}) custom-call(f32[1]{0:T(128)} %bitcast.bias_ref, f32[2,512,512]{2,1,0:T(8,128)} %get-tuple-element.162.dafter_ref, f32[2,512,512]{2,1,0:T(8,128)} %get-tuple-element.120.x_ref, ...), custom_call_target="tpu_custom_call" | custom-call | flops 30000001024 | bytes 20000000 | tf_op jit(solution)/shard_map/attend_back/pallas_call | solution.py:620
  259.2 43.7 %reduce_grads.1 = (bf16[8,4,64,512]{3,2,1,0:T(8,128)(2,1)}, bf16[6,64,512]{2,1,0:T(8,128)(2,1)}, f32[128,512]{1,0:T(8,128)}, f32[8,128]{1,0:T(8,128)}) custom-call(bf16[2,2,8,64,512]{4,3,2,1,0:T(8,128)(2,1)} %bitcast.36, bf16[64,512]{1,0:T(8,128)(2,1)} %get-tuple-element.173.attn_done_ref, bf16[4,64,512]{2,1,0:T(8,128)(2,1)} %get-tuple-element.174.feed_low_ref, ...), custom_call_target="tpu_custom_call" | custom-call | flops 100000000 | bytes 100000000 | tf_op jit(solution)/shard_map/reduce_grads/pallas_call | solution.py:1304
  302.9 45.3 %muon.1 = (bf16[4,6,64,512]{3,2,1,0:T(8,128)(2,1)}, bf16[4,6,64,512]{3,2,1,0:T(8,128)(2,1)}, f32[8,128]{1,0:T(8,128)}) custom-call(f32[8,128]{1,0:T(8,128)} %get-tuple-element.183.square_ref, bf16[8,4,64,512]{3,2,1,0:T(8,128)(2,1)} %get-tuple-element.184.whole_ref, bf16[8,6,64,512]{3,2,1,0:T(8,128)(2,1)} %bitcast.46, ...), custom_call_target="tpu_custom_call" | custom-call | flops 20000000000 | bytes 40000000 | tf_op jit(solution)/shard_map/muon/pallas_call | solution.py:1566
  348.2 0.0 all-gather.4.cloned.1.call-done
  348.2 13.0 %finish.1 = (f32[2,4,64,512]{3,2,1,0:T(8,128)}, f32[2,4,64,512]{3,2,1,0:T(8,128)}, bf16[2,4,64,512]{3,2,1,0:T(8,128)(2,1)}, f32[2,64,2048]{2,1,0:T(8,128)}, f32[...) custom-call(f32[8,128]{1,0:T(8,128)} %get-tuple-element.186.norm_ref, ...), custom_call_target="tpu_custom_call" | custom-call | flops 100000000 | bytes 40000000 | tf_op jit(solution)/shard_map/finish/pallas_call | solution.py:1856
Async XLA Ops:
  7.2 12.4 %copy-start = (f32[2,12,512]{2,0,1:T(2,128)S(1)}, f32[2,12,512]{2,0,1:T(2,128)}, u32[]{:S(2)}) copy-start(f32[2,12,512]{2,0,1:T(2,128)} %param.35) | copy-start | bytes 147460
  7.2 88.8 %all-gather.6.cloned.1.call-start = ((), (), s32[]{:S(2)}) async-start(), calls=%async_computation.1 | async-start | bytes 3538944 | tf_op jit(solution)/shard_map/all_gather | solution.py:1929
  19.5 328.7 %all-gather.4.cloned.1.call-start = ((), (), s32[]{:S(2)}) async-start(), calls=%async_computation | async-start | bytes 1081344 | tf_op jit(solution)/shard_map/all_gather | solution.py:1983
  37.2 23.0 %collective-permute-start.1 = (bf16[512,512]{1,0:T(8,128)(2,1)}, bf16[512,512]{1,0:T(8,128)(2,1)S(1)}, u32[]{:S(2)}, u32[]{:S(2)}) collective-permute-start(bf16[512,512]{1,0:T(8,128)(2,1)} %get-tuple-element.133), channel_id=1, source_target_pairs={{0,4},{4,8},{8,12},{12,16},{16,20},{20,24},{24,28},{1,5},{5,9},{9,... | collective-permute-start | bytes 1572872 | tf_op jit(solution)/shard_map/ppermute | solution.py:675
  56.5 21.7 %collective-permute-start = (bf16[512,512]{1,0:T(8,128)(2,1)}, bf16[512,512]{1,0:T(8,128)(2,1)S(1)}, u32[]{:S(2)}, u32[]{:S(2)}) collective-permute-start(bf16[512,512]{1,0:T(8,128)(2,1)} %get-tuple-element.132), channel_id=1, source_target_pairs={{0,4},{4,8},{8,12},{12,16},{16,20},{20,24},{24,28},{1,5},{5,9},{9,... | collective-permute-start | bytes 1572872 | tf_op jit(solution)/shard_map/ppermute | solution.py:675
  60.2 0.8 copy-start.1
  78.2 0.8 copy-start.2
Sparse Core Ops, SparseCore 0:
  19.6 39.9 all-gather.5
  137.3 53.7 all-gather.3

commit v8 on v7

--- a/solution.py
+++ b/solution.py
@@ -345,15 +345,15 @@
 def feed_back_kernel(streams, g_ref, after_ref, up_ref, down_ref, vec_ref, *refs):
     step = pl.program_id(0)
     grad_ref, dafter_ref, dup_ref, ddown_ref, dvec_ref, done_ref, normed_s, branch_s, act_s, inner_s = refs[:10]
-    carry = AttnCarry(grad_ref, refs[10 : 10 + CARRY_REFS], refs[10 + CARRY_REFS :])
+    carry = AttnCarry(grad_ref, refs[10 : 10 + CARRY_REFS], refs[10 + CARRY_REFS :], done_ref)
     planes = carry.planes
-    later = range(1, planes)
+    early, late = range(planes // 2), range(planes // 2, planes)
     beats = [
         [("b", place) for place in range(planes)],
-        [("m", 0)],
-        [("m", place) for place in later] + [("e", 0)],
-        [("e", place) for place in range(1, planes // 2)],
-        [("e", place) for place in range(planes // 2, planes)],
+        [("m", place) for place in early],
+        [("m", place) for place in late],
+        [("e", place) for place in early],
+        [("e", place) for place in late],
     ]
 
     @pl.when(step == 0)
@@ -396,28 +396,25 @@
 
     @pl.when(step == streams - 1)
     def _():
-        carry.run(beats[2])
+        carry.run(beats[1])
 
     dnormed = dot_nt(inner_s[rows, :], up_ref[...])
     dvec_ref[0:1, :] += column_sum(dnormed * unit)
     dvec_ref[1:2, :] += column_sum(dnormed)
     dafter_ref[...] = grad + norm_back(dnormed, gain, unit, scale)
 
-    @pl.when(step == 0)
-    def _():
-        carry.run(beats[1])
-
     @pl.when(step == streams - 1)
     def _():
+        carry.run(beats[2])
+        for tile in range(FF // TILE):
+            columns = slice(tile * TILE, (tile + 1) * TILE)
+            dup_ref[tile] = dot_nn(normed_s[...], inner_s[:, columns]).astype(bf16)
         carry.run(beats[3])
         for tile in range(FF // TILE):
             columns = slice(tile * TILE, (tile + 1) * TILE)
-            dup_ref[tile] = dot_nn(normed_s[...], inner_s[:, columns]).astype(bf16)
+            ddown_ref[columns, :] = jnp.transpose(dot_nn(branch_s[...], act_s[:, columns]).astype(bf16))
         carry.run(beats[4])
-        for tile in range(FF // TILE):
-            columns = slice(tile * TILE, (tile + 1) * TILE)
-            ddown_ref[columns, :] = jnp.transpose(dot_nn(branch_s[...], act_s[:, columns]).astype(bf16))
-        carry.finish(done_ref)
+        carry.drain()
 
 
 def feed_back(depth, grad, after, upper, lower, vectors, count, dp_count, attn_grad):
@@ -451,8 +448,8 @@
     operands = [grad, after, upper, lower, vectors]
     in_specs.append(pl.BlockSpec(memory_space=pl.ANY))
     operands.append(attn_grad.reshape(2, 2, count, rows, D))
-    out_shape.append(jax.ShapeDtypeStruct((rows, D), bf16))
-    out_specs.append(whole_spec((rows, D)))
+    out_shape.append(jax.ShapeDtypeStruct((count // 2, rows, D), attn_grad.dtype))
+    out_specs.append(whole_spec((count // 2, rows, D)))
     scratch = scratch + carry_scratch("attn", rows, count, dp_count, attn_grad.dtype)
     params = {"collective_id": 6 + depth, "has_side_effects": True}
     return pl.pallas_call(
@@ -486,11 +483,13 @@
     frames_ref,
     dup_ref,
     ddown_ref,
+    sums_ref,
     dx_ref,
     dattn_ref,
     dvec_ref,
     din_ref,
     done_ref,
+    along_ref,
     attn_s,
     dmixed_s,
     dq_s,
@@ -502,12 +501,16 @@
 ):
     step = pl.program_id(0)
     pairs = HEADS // 2
-    carry = FeedCarry(depth, dup_ref, ddown_ref, refs[: CARRY_REFS + 2], refs[CARRY_REFS + 2 :])
+    split = CARRY_REFS + 1 + CARRY_SEMS
+    carry = FeedCarry(depth, dup_ref, ddown_ref, refs[: CARRY_REFS + 1], refs[CARRY_REFS + 1 : split])
+    along = ZCarry(refs[split : split + Z_REFS], refs[split + Z_REFS :])
+    plans, (free, bound) = carry.plans(), along.plans()
 
     @pl.when(step == 0)
     def _():
         hail(carry.targets)
         carry.load_all()
+        along.sums[...] = sums_ref[...]
         attn_s[...] = jnp.zeros_like(attn_s)
         dvec_ref[...] = jnp.zeros_like(dvec_ref)
         din_ref[...] = jnp.zeros_like(din_ref)
@@ -535,6 +538,11 @@
     def _():
         meet(carry.targets)
         carry.send_all()
+        along.run(free)
+
+    @pl.when(step == 1)
+    def _():
+        carry.run(plans[-1])
 
     def pair_body(pair, state):
         lanes = pair_lanes(pair)
@@ -577,7 +585,15 @@
             dq_s[block * HALF : (block + 1) * HALF, lanes] = (
                 jnp.transpose(grads) * (HEAD_DIM**-0.5)
             ).astype(bf16)
-        carry.tick(pairs * step + pair, pairs * streams, 1)
+        for time, acts in enumerate(plans[:-1]):
+            if acts:
+
+                @pl.when(pairs * step + pair == time)
+                def _():
+                    carry.run(acts)
+                    if time == 3:
+                        along.run(bound)
+
         return state
 
     lax.fori_loop(0, pairs, pair_body, 0)
@@ -607,11 +623,11 @@
     @pl.when(step == pl.num_programs(0) - 1)
     def _():
         dattn_ref[...] = attn_s[...].astype(bf16)
-        carry.rest(pairs * streams, 1)
         carry.finish(done_ref)
-
-
-def attend_back(depth, bias, dafter, x, memory, saved, attn, vectors, frames, up_grad, down_grad, count, dp_count):
+        along.finish(along_ref)
+
+
+def attend_back(depth, bias, dafter, x, memory, saved, attn, vectors, frames, up_grad, down_grad, sums, count, dp_count):
     streams = dafter.shape[0]
     keyin, q, k, v, lse, mixed = saved
     inputs = frames.shape[1]
@@ -625,7 +641,8 @@
             jax.ShapeDtypeStruct((4, D, D), bf16),
             jax.ShapeDtypeStruct((8, D), f32),
             jax.ShapeDtypeStruct((inputs, D), f32),
-            jax.ShapeDtypeStruct((4, rows, D), bf16),
+            jax.ShapeDtypeStruct((2, rows, D), bf16),
+            jax.ShapeDtypeStruct(sums.shape[1:], bf16),
         ],
         in_specs=[
             pl.BlockSpec(memory_space=pltpu.SMEM),
@@ -643,13 +660,15 @@
             stream_spec((inputs, SEG)),
             pl.BlockSpec(memory_space=pl.ANY),
             pl.BlockSpec(memory_space=pl.ANY),
+            whole_spec(sums.shape),
         ],
         out_specs=[
             stream_spec((SEG, D)),
             whole_spec((4, D, D)),
             whole_spec((8, D)),
             whole_spec((inputs, D)),
-            whole_spec((4, rows, D)),
+            whole_spec((2, rows, D)),
+            whole_spec(sums.shape[1:]),
         ],
         scratch_shapes=[
             pltpu.VMEM((4, D, D), f32),
@@ -660,13 +679,14 @@
             pltpu.VMEM((2 * SEG, 2 * SEG), bf16),
             pltpu.VMEM((HEADS, SEG), f32),
         ]
-        + carry_scratch("feed", rows, count, dp_count),
+        + carry_scratch("feed", rows, count, dp_count)
+        + z_scratch(sums.shape[1], count, dp_count, sums.dtype),
         compiler_params=pltpu.CompilerParams(
             collective_id=4 + depth, has_side_effects=True, vmem_limit_bytes=VMEM_LIMIT
         ),
         cost_estimate=pl.CostEstimate(flops=3 * 10**10, bytes_accessed=2 * 10**7, transcendentals=10**7),
         name="attend_back",
-    )(bias, dafter, x, memory, keyin, q, k, v, lse, mixed, attn, vectors, frames, up_grad, down_grad)
+    )(bias, dafter, x, memory, keyin, q, k, v, lse, mixed, attn, vectors, frames, up_grad, down_grad, sums)
 
 
 def from_behind(value, axis, steps):
@@ -777,17 +797,19 @@
             self.sendh,
             self.recvh,
         ) = sems
+        self.settle(self.mine.shape[0])
+
+    def settle(self, planes):
         self.seg, self.dp, self.core, self.x, self.y, self.across_core, near, self.far = peers()
         self.across_x, self.across_y, _ = near
-        self.planes = self.mine.shape[0]
+        self.planes = planes
         self.plane = self.seg // 2
         self.targets = [self.across_core, self.across_x, self.across_y] + self.far
         bit = 1
-        while bit < self.planes:
+        while bit < planes:
             self.targets.append({"seg": 2 * self.toggled(bit) + self.core})
             bit *= 2
-
-        self.order = list(reversed(range(self.planes)))
+        self.order = list(reversed(range(planes)))
 
     def toggled(self, mask):
         place, bit = self.plane, 1
@@ -863,36 +885,33 @@
 
     def run(self, acts):
         for kind, step in acts:
-            if step < self.planes:
-                {"b": self.begin, "m": self.middle, "e": self.end}[kind](step)
-
-    def actions(self, time, slack):
-        planes = self.planes
-        started = range(2) if time == 0 else range(time + 1, time + 2)
-        for step in started:
-            if step < planes:
-                self.begin(step)
-        if 0 <= time - slack < planes:
-            self.middle(time - slack)
-        if 0 <= time - slack - 2 < planes:
-            self.end(time - slack - 2)
-
-    def tick(self, time, last, slack):
-        for place in range(last):
-
-            @pl.when(time == place)
-            def _():
-                self.actions(place, slack)
-
-    def rest(self, first, slack):
-        for time in range(first, self.planes + slack + 2):
-            self.actions(time, slack)
+            getattr(self, {"b": "begin", "m": "middle", "e": "end", "z": "onward"}[kind])(step)
+
+
+class ZCarry(Carry):
+    def __init__(self, refs, sems):
+        self.sums, self.got3, self.goth = refs
+        self.send3, self.recv3, self.sendh, self.recvh = sems
+        self.settle(self.sums.shape[0])
+
+    def held(self, step):
+        return self.sums.at[step]
+
+    def plans(self):
+        free = [("z", step) for step in range(self.planes) if self.order[step] % 2]
+        bound = [("z", step) for step in range(self.planes) if self.order[step] and not self.order[step] % 2]
+        return free, bound
+
+    def finish(self, out_ref):
+        out_ref[...] = self.total().astype(out_ref.dtype)
+        for step in range(self.planes - 1):
+            self.third(step).wait_send()
 
 
 class AttnCarry(Carry):
-    def __init__(self, source, refs, sems):
+    def __init__(self, source, refs, sems, sums=None):
         super().__init__(refs, sems)
-        self.source = source
+        self.source, self.sums = source, sums
 
     def pieces(self, row):
         return ((self.source.at[:, :, row], ()),)
@@ -952,30 +971,30 @@
         mine, half = self.mine, self.mine.shape[3] // 2
         for copy in self.second(step):
             copy.wait_recv()
-        mine[step, self.y, self.x, 0:half] = plus(mine[step, self.y, self.x, 0:half], self.got2[step, 0])
-        mine[step, self.y, self.x, half:] = plus(mine[step, self.y, self.x, half:], self.got2[step, 1])
+        upper = plus(mine[step, self.y, self.x, 0:half], self.got2[step, 0])
+        lower = plus(mine[step, self.y, self.x, half:], self.got2[step, 1])
+        if self.sums is not None:
+            self.sums[step, 0:half] = upper
+            self.sums[step, half:] = lower
+            return
+        mine[step, self.y, self.x, 0:half] = upper
+        mine[step, self.y, self.x, half:] = lower
         self.onward(step)
-
-    def finish(self, out_ref):
-        out_ref[...] = self.total().astype(out_ref.dtype)
-        self.drain()
 
     def drain(self):
         for step in range(self.planes):
             wait_bytes(self.mine.at[step], self.send0.at[step])
             for copy in self.first(step) + self.second(step):
                 copy.wait_send()
-            if step < self.planes - 1:
+            if self.sums is None and step < self.planes - 1:
                 self.third(step).wait_send()
 
 
 class FeedCarry(Carry):
     def __init__(self, depth, up, down, refs, sems):
-        super().__init__(refs[:CARRY_REFS], sems[:CARRY_SEMS])
-        self.sums, self.got4 = refs[CARRY_REFS:]
-        self.send4, self.recv4 = sems[CARRY_SEMS:]
+        super().__init__(refs[:CARRY_REFS], sems)
+        (self.sums,) = refs[CARRY_REFS:]
         self.up, self.down = up, down
-        self.owner = (self.x == self.y) if depth == 1 else (self.x != self.y)
         self.keep = self.x if depth == 1 else 1 - self.x
 
     def pieces(self, row):
@@ -1035,33 +1054,22 @@
         self.sums[step, 1] = plus(self.mine[step, self.y, 2 + self.x], self.got2[step, 1])
         self.onward(step)
 
-    def last(self):
-        step = self.planes - 1
+    def plans(self):
+        planes = self.planes
         return (
-            remote(self.sums.at[step, 0], self.got4.at[0], self.send4.at[0], self.recv4.at[0], self.across_y),
-            remote(self.sums.at[step, 1], self.got4.at[1], self.send4.at[1], self.recv4.at[1], self.across_x),
+            [("b", step) for step in range(planes - 1)],
+            [],
+            [("m", 0), ("b", planes - 1)],
+            [("m", 1)],
+            [("m", step) for step in range(3, planes)],
+            [("e", 1)],
+            [("e", 2)],
+            [("e", step) for step in range(3, planes)],
+            [("m", 2), ("e", 0)],
         )
 
     def finish(self, out_ref):
-        value = self.total()
-
-        @pl.when(self.owner)
-        def _():
-            for place in range(2):
-                wait_bytes(self.got4.at[place], self.recv4.at[place])
-            out_ref[self.y] = value[0]
-            out_ref[1 - self.y] = self.got4[0]
-            out_ref[2 + self.x] = value[1]
-            out_ref[3 - self.x] = self.got4[1]
-
-        @pl.when(jnp.logical_not(self.owner))
-        def _():
-            for copy in self.last():
-                copy.start()
-            out_ref[...] = jnp.zeros_like(out_ref)
-            for copy in self.last():
-                copy.wait_send()
-
+        out_ref[...] = self.total()
         for step in range(self.planes):
             wait_bytes(self.mine.at[step], self.send0.at[step])
             for copy in self.first(step) + self.second(step):
@@ -1097,14 +1105,24 @@
             (planes, 2, rows),
             (far, planes, 2, rows),
             (planes, 2, rows),
-            (2, rows),
         )
     pair = (planes, 2)
     one = (planes,)
     sems = (one, one, one, pair, pair, pair, pair, one, one, (far, planes), (far, planes))
-    if kind == "feed":
-        sems = sems + ((2,), (2,))
     return [pltpu.VMEM(shape + (D,), dtype) for shape in shapes] + [dma(shape) for shape in sems]
+
+
+def z_scratch(rows, count, dp_count, dtype):
+    planes = count // 2
+    far = max(1, dp_count.bit_length() - 3)
+    dma = pltpu.SemaphoreType.DMA
+    shapes = ((planes, rows), (planes, rows), (far, planes, rows))
+    sems = ((planes,), (planes,), (far, planes), (far, planes))
+    return [pltpu.VMEM(shape + (D,), dtype) for shape in shapes] + [dma(shape) for shape in sems]
+
+
+Z_REFS = 3
+Z_SEMS = 4
 
 
 def reduce_kernel(
@@ -1130,6 +1148,10 @@
     small_got,
     sq_seg,
     sq_dp,
+    keep_s,
+    give_s,
+    last_send,
+    last_recv,
     small_send,
     small_recv,
     whole_send,
@@ -1154,11 +1176,20 @@
 
     @pl.when(x == y)
     def _():
-        own_ref[2:6] = feed_high_ref[...]
+        keep_s[...] = feed_high_ref[...]
+        give_s[...] = feed_low_ref[...]
 
     @pl.when(x != y)
     def _():
-        own_ref[2:6] = feed_low_ref[...]
+        keep_s[...] = feed_low_ref[...]
+        give_s[...] = feed_high_ref[...]
+
+    own_ref[2 + y] = keep_s[0]
+    own_ref[4 + x] = keep_s[1]
+    last = (
+        remote(give_s.at[0], own_ref.at[2 + y], last_send.at[0], last_recv.at[0], across_y),
+        remote(give_s.at[1], own_ref.at[4 + x], last_send.at[1], last_recv.at[1], across_x),
+    )
 
     inputs = din_ref.shape[0]
     small_ref[0:inputs, :] = din_ref[...]
@@ -1200,6 +1231,8 @@
     small_run = small_steps()
     next(small_run)
     carry.send_all()
+    for copy in last:
+        copy.start()
     roles = owners(count)
 
     def gift(place):
@@ -1223,17 +1256,22 @@
         def _():
             whole_ref[seg, spot : spot + width] = own_ref[first : first + width]
 
-    for place in (2, 3, 1):
-        give(place)
     acts = [
-        [("b", 0), ("b", 1)],
-        [("b", step) for step in range(2, planes)],
-        [("m", 0), ("m", 1)],
-        [("m", step) for step in range(2, planes)] + [("e", 0)],
+        [("b", step) for step in range(planes - 1)],
+        [("m", 0), ("b", planes - 1)],
+        [("m", 1)],
+        [("m", 2), ("e", 0)],
+        [("m", step) for step in range(3, planes)],
     ] + [[("e", step)] for step in range(1, planes)]
+    give(1)
     next(small_run)
-    for part in acts:
+    for turn, part in enumerate(acts):
         carry.run(part)
+        if turn == 0:
+            for copy in last:
+                copy.wait()
+            for place in (2, 3):
+                give(place)
         next(small_run, None)
     own_ref[0] = carry.total()
     give(0)
@@ -1318,6 +1356,10 @@
             pltpu.VMEM((stages, SMALL // 2, D), f32),
             pltpu.VMEM((count, 8, 128), f32),
             pltpu.VMEM((GROUPS, 8, 128), f32),
+            pltpu.VMEM((2, rows, D), bf16),
+            pltpu.VMEM((2, rows, D), bf16),
+            dma((2,)),
+            dma((2,)),
             dma((stages + 2,)),
             dma((stages + 2,)),
             dma((4,)),
@@ -1958,11 +2000,10 @@
     carried_done = []
     for depth in reversed(range(LAYERS)):
         entering, held, saved = kept[depth]
-        dafter, grad_up, grad_down, feed_vec, done = feed_back(
+        dafter, grad_up, grad_down, feed_vec, sums = feed_back(
             depth, grad_hidden, saved[7], up_copy, down_copy, layer_vectors, count, dp_count, carried
         )
-        carried_done.append(done)
-        grad_hidden, grad_attn, attn_vec, grad_in, feed_done[depth] = attend_back(
+        grad_hidden, grad_attn, attn_vec, grad_in, feed_done[depth], done = attend_back(
             depth,
             bias,
             dafter,
@@ -1974,9 +2015,11 @@
             frames_t,
             grad_up,
             grad_down,
+            sums,
             count,
             dp_count,
         )
+        carried_done.append(done)
         carried = grad_attn.reshape(4 * D, D)
         vector_grads = [attn_vec, feed_vec] + vector_grads
     out_done, attn_done = carried_done

time: 375 us -> 354 us (0.944)
  Pallas kernels: 346 us -> 324 us
    pallas_call x2, Pallas kernels: 93.6 us -> 81.4 us  [attend_back(): pl.pallas_call(functools.partial(attend_back_kernel, streams, depth), gri...]
    pallas_call x2, Pallas kernels: 59.1 us -> 49.7 us  [feed_back(): pl.pallas_call(functools.partial(feed_back_kernel, streams), grid=(stream...]
  transfers between devices with their start and end apart: 4 -> 4, of which waited for: 0 -> 0; matrix products, arithmetic and copies ran while one was open for 0% -> 0% of each run, Pallas kernels for 76% -> 64%
where the time goes in v8:
time: 354 us; the launch traced here: 347 us
  Pallas kernels  324 us (92%)
  between operations  14.7 us (4%)
  starting transfers between devices  6 us (2%)
    pallas_call x2, Pallas kernels, attend_back(): pl.pallas_call(functools.partial(attend_back_kernel, streams, depth), gri...  81.4 us
    pallas_call x4, Pallas kernels, forward_layer(): pl.pallas_call(functools.partial(forward_kernel, depth, stream), grid=(1,...  68.2 us
    pallas_call x2, Pallas kernels, feed_back(): pl.pallas_call(functools.partial(feed_back_kernel, streams), grid=(stream...  49.7 us
    pallas_call x1, Pallas kernels, muon(): pl.pallas_call(functools.partial(muon_kernel, count), out_shape=[blocks,...  45.3 us
    pallas_call x1, Pallas kernels, reduce_grads(): pl.pallas_call(functools.partial(reduce_kernel, count), out_shape=[jax.Sh...  43.2 us
    pallas_call x1, Pallas kernels, finish(): pl.pallas_call(finish_kernel, grid=(steps,), out_shape=[like(attn), like(...  13 us
    pallas_call x1, Pallas kernels, embed(): pl.pallas_call(functools.partial(embed_kernel, count), out_shape=[jax.Sha...  12.2 us
    pallas_call x1, Pallas kernels, head(): pl.pallas_call(functools.partial(head_kernel, scale), grid=(streams,), ou...  10.6 us
  transfers between devices with their start and end apart: 4, of which 0 were waited for; matrix products, arithmetic and copies ran while one was open for 0% of the time, Pallas kernels for 64%

profile of v8, /device:TPU:0, one launch (start us, length us, event | category | flops | bytes accessed | tf_op | source)
XLA Modules:
  0.0 346.6 jit_solution(13030023184470247911)
XLA Ops:
  7.2 0.0 copy-start
  7.2 0.0 all-gather.6.cloned.1.call-start
  7.3 12.2 %embed.1 = (f32[2,512,512]{2,1,0:T(8,128)}, bf16[2,512,512]{2,1,0:T(8,128)(2,1)}, f32[8,128]{1,0:T(8,128)}, bf16[6,64,512]{2,1,0:T(8,128)(2,1)}) custom-call(bf16[2,80,512]{2,1,0:T(8,128)(2,1)} %bitcast.40, s32[2,512]{1,0:T(2,128)} %mask_ref.3, bf16[80,512]{1,0:T(8,128)(2,1)} %in_ref.1, f32[5,512]{1,0:T(8,128)} %refs_15_.1, f32[2,4,64,512]{3,2,1,0:T(8,128)} %refs_1_.1, ...), custom_call_target="tpu_custom_call" | custom-call | flops 200000000 | bytes 4000000 | tf_op jit(solution)/shard_map/embed/pallas_call | solution.py:1702
  19.5 0.0 all-gather.6.cloned.1.call-update
  19.5 0.0 all-gather.4.cloned.1.call-start
  19.6 0.0 copy-done
  19.6 0.6 copy.78.vec_ref
  20.2 17.0 %layer_forward.4 = (f32[2,512,512]{2,1,0:T(8,128)}, bf16[512,512]{1,0:T(8,128)(2,1)}, bf16[2,1024,512]{2,1,0:T(8,128)(2,1)}, bf16[2,512,512]{2,1,0:T(8,128)(2,1)...) custom-call(f32[1]{0:T(128)} %bitcast.bias_ref, ...), custom_call_target="tpu_custom_call" | custom-call | flops 10000000000 | bytes 20000000 | tf_op jit(solution)/shard_map/layer_forward/pallas_call | solution.py:246
  37.2 2.2 collective-permute-start.1
  39.4 17.0 %layer_forward.5 = (f32[2,512,512]{2,1,0:T(8,128)}, bf16[512,512]{1,0:T(8,128)(2,1)}, bf16[2,1024,512]{2,1,0:T(8,128)(2,1)}, bf16[2,512,512]{2,1,0:T(8,128)(2,1)...) custom-call(f32[1]{0:T(128)} %bitcast.bias_ref, ...), custom_call_target="tpu_custom_call", output_to_operand_aliasing={{0}: (7, {}), {2}: (8, {}), {3}: (9, {}), {4}: (10, {}), {5... | custom-call | flops 10000000000 | bytes 20000000 | tf_op jit(solution)/shard_map/layer_forward/pallas_call | solution.py:246
  56.5 3.7 %collective-permute-start = (bf16[512,512]{1,0:T(8,128)(2,1)}, bf16[512,512]{1,0:T(8,128)(2,1)S(1)}, u32[]{:S(2)}, u32[]{:S(2)}) collective-permute-start(bf16[512,512]{1,0:T(8,128)(2,1)} %get-tuple-element.134), channel_id=1, source_target_pairs={{0,4},{4,8},{8,12},{12,16},{16,20},{20,24},{24,28},{1,5},{5,9},{9,... | collective-permute-start | bytes 1572872 | tf_op jit(solution)/shard_map/ppermute | solution.py:695
  60.2 0.0 collective-permute-done.1.mem_ref
  60.2 0.0 copy-start.1
  60.2 0.8 copy-done.1
  61.0 17.2 %layer_forward.6 = (f32[2,512,512]{2,1,0:T(8,128)}, bf16[512,512]{1,0:T(8,128)(2,1)}, bf16[2,1024,512]{2,1,0:T(8,128)(2,1)}, bf16[2,512,512]{2,1,0:T(8,128)(2,1)...) custom-call(f32[1]{0:T(128)} %bitcast.bias_ref, ...), custom_call_target="tpu_custom_call" | custom-call | flops 10000000000 | bytes 20000000 | tf_op jit(solution)/shard_map/layer_forward/pallas_call | solution.py:246
  78.2 0.0 collective-permute-done.mem_ref
  78.2 0.0 copy-start.2
  78.2 0.8 copy-done.2
  79.0 17.0 %layer_forward.7 = (f32[2,512,512]{2,1,0:T(8,128)}, bf16[512,512]{1,0:T(8,128)(2,1)}, bf16[2,1024,512]{2,1,0:T(8,128)(2,1)}, bf16[2,512,512]{2,1,0:T(8,128)(2,1)...) custom-call(f32[1]{0:T(128)} %bitcast.bias_ref, ...), custom_call_target="tpu_custom_call", output_to_operand_aliasing={{0}: (7, {}), {2}: (8, {}), {3}: (9, {}), {4}: (10, {}), {5... | custom-call | flops 10000000000 | bytes 20000000 | tf_op jit(solution)/shard_map/layer_forward/pallas_call | solution.py:246
  96.0 0.0 all-gather.6.cloned.1.call-done
  96.0 10.6 %head.1 = (f32[2,512,512]{2,1,0:T(8,128)}, f32[2,2,256,512]{3,2,1,0:T(8,128)}, f32[8,512]{1,0:T(8,128)}) custom-call(f32[2,512,512]{2,1,0:T(8,128)} %get-tuple-element.145.x_ref, s32[2,512]{1,0:T(2,128)} %target_ref.1, s32[2,512]{1,0:T(2,128)} %mask_ref.3, f32[8,128]{1,0:T(8,128)} %get-tuple-element.146.total_ref, bf16[512,1024]{1,0:T(8,128)(2,1)} %out_ref.1, ...), custom_call_target="tpu_custom_call" | custom-call | flops 3300000000 | bytes 10000000 | tf_op jit(solution)/shard_map/head/pallas_call | solution.py:320
  106.6 25.4 %feed_back.2 = (f32[2,512,512]{2,1,0:T(8,128)}, bf16[4,512,512]{2,1,0:T(8,128)(2,1)}, bf16[2048,512]{1,0:T(8,128)(2,1)}, f32[8,512]{1,0:T(8,128)}, f32[4,32,512]{2,1,0:T(8,128)}) custom-call(f32[2,512,512]{2,1,0:T(8,128)} %get-tuple-element.148.g_ref, f32[2,512,512]{2,1,0:T(8,128)} %get-tuple-element.149.after_ref, bf16[2,512,2048]{2,1,0:T(8,128)(2,1)} %up_ref.11, ...), custom_call_target="tpu_custom_call" | custom-call | flops 11000000512 | bytes 20000000 | tf_op jit(solution)/shard_map/feed_back/pallas_call | solution.py:455
  132.0 40.3 %attend_back.2 = (f32[2,512,512]{2,1,0:T(8,128)}, bf16[4,512,512]{2,1,0:T(8,128)(2,1)}, f32[8,512]{1,0:T(8,128)}, f32[80,512]{1,0:T(8,128)}, bf16[2,64,512]{2,1,0:T(8,128)(2,1)}, /*index=5*/bf16[32,512]{1,0:T(8,128)(2,1)}) custom-call(f32[1]{0:T(128)} %bitcast.bias_ref, f32[2,512,512]{2,1,0:T(8,128)} %get-tuple-element.151.dafter_ref, ...), custom_call_target="tpu_custom_call" | custom-call | flops 30000001024 | bytes 20000000 | tf_op jit(solution)/shard_map/attend_back/pallas_call | solution.py:636
  172.3 0.0 all-gather.4.cloned.1.call-update
  172.3 24.3 %feed_back.3 = (f32[2,512,512]{2,1,0:T(8,128)}, bf16[4,512,512]{2,1,0:T(8,128)(2,1)}, bf16[2048,512]{1,0:T(8,128)(2,1)}, f32[8,512]{1,0:T(8,128)}, bf16[4,64,512]{2,1,0:T(8,128)(2,1)}) custom-call(f32[2,512,512]{2,1,0:T(8,128)} %get-tuple-element.162.g_ref, f32[2,512,512]{2,1,0:T(8,128)} %get-tuple-element.163.after_ref, bf16[2,512,2048]{2,1,0:T(8,128)(2,1)} %up_ref.11, ...), custom_call_target="tpu_custom_call" | custom-call | flops 11000000512 | bytes 20000000 | tf_op jit(solution)/shard_map/feed_back/pallas_call | solution.py:455
  196.6 41.1 %attend_back.3 = (f32[2,512,512]{2,1,0:T(8,128)}, bf16[4,512,512]{2,1,0:T(8,128)(2,1)}, f32[8,512]{1,0:T(8,128)}, f32[80,512]{1,0:T(8,128)}, bf16[2,64,512]{2,1,0:T(8,128)(2,1)}, /*index=5*/bf16[64,512]{1,0:T(8,128)(2,1)}) custom-call(f32[1]{0:T(128)} %bitcast.bias_ref, f32[2,512,512]{2,1,0:T(8,128)} %get-tuple-element.165.dafter_ref, ...), custom_call_target="tpu_custom_call" | custom-call | flops 30000001024 | bytes 20000000 | tf_op jit(solution)/shard_map/attend_back/pallas_call | solution.py:636
  237.7 43.2 %reduce_grads.1 = (bf16[8,4,64,512]{3,2,1,0:T(8,128)(2,1)}, bf16[6,64,512]{2,1,0:T(8,128)(2,1)}, f32[128,512]{1,0:T(8,128)}, f32[8,128]{1,0:T(8,128)}) custom-call(bf16[2,2,8,64,512]{4,3,2,1,0:T(8,128)(2,1)} %bitcast.36, bf16[64,512]{1,0:T(8,128)(2,1)} %get-tuple-element.177.attn_done_ref, bf16[2,64,512]{2,1,0:T(8,128)(2,1)} %get-tuple-element.178.feed_low_ref, ...), custom_call_target="tpu_custom_call" | custom-call | flops 100000000 | bytes 100000000 | tf_op jit(solution)/shard_map/reduce_grads/pallas_call | solution.py:1342
  280.9 45.3 %muon.1 = (bf16[4,6,64,512]{3,2,1,0:T(8,128)(2,1)}, bf16[4,6,64,512]{3,2,1,0:T(8,128)(2,1)}, f32[8,128]{1,0:T(8,128)}) custom-call(f32[8,128]{1,0:T(8,128)} %get-tuple-element.187.square_ref, bf16[8,4,64,512]{3,2,1,0:T(8,128)(2,1)} %get-tuple-element.188.whole_ref, bf16[8,6,64,512]{3,2,1,0:T(8,128)(2,1)} %bitcast.46, ...), custom_call_target="tpu_custom_call" | custom-call | flops 20000000000 | bytes 40000000 | tf_op jit(solution)/shard_map/muon/pallas_call | solution.py:1608
  326.3 0.0 all-gather.4.cloned.1.call-done
  326.3 13.0 %finish.1 = (f32[2,4,64,512]{3,2,1,0:T(8,128)}, f32[2,4,64,512]{3,2,1,0:T(8,128)}, bf16[2,4,64,512]{3,2,1,0:T(8,128)(2,1)}, f32[2,64,2048]{2,1,0:T(8,128)}, f32[...) custom-call(f32[8,128]{1,0:T(8,128)} %get-tuple-element.190.norm_ref, ...), custom_call_target="tpu_custom_call" | custom-call | flops 100000000 | bytes 40000000 | tf_op jit(solution)/shard_map/finish/pallas_call | solution.py:1898
Async XLA Ops:
  7.2 12.4 %copy-start = (f32[2,12,512]{2,0,1:T(2,128)S(1)}, f32[2,12,512]{2,0,1:T(2,128)}, u32[]{:S(2)}) copy-start(f32[2,12,512]{2,0,1:T(2,128)} %param.35) | copy-start | bytes 147460
  7.2 88.8 %all-gather.6.cloned.1.call-start = ((), (), s32[]{:S(2)}) async-start(), calls=%async_computation.1 | async-start | bytes 3538944 | tf_op jit(solution)/shard_map/all_gather | solution.py:1971
  19.5 306.8 %all-gather.4.cloned.1.call-start = ((), (), s32[]{:S(2)}) async-start(), calls=%async_computation | async-start | bytes 1081344 | tf_op jit(solution)/shard_map/all_gather | solution.py:2026
  37.2 23.0 %collective-permute-start.1 = (bf16[512,512]{1,0:T(8,128)(2,1)}, bf16[512,512]{1,0:T(8,128)(2,1)S(1)}, u32[]{:S(2)}, u32[]{:S(2)}) collective-permute-start(bf16[512,512]{1,0:T(8,128)(2,1)} %get-tuple-element.135), channel_id=1, source_target_pairs={{0,4},{4,8},{8,12},{12,16},{16,20},{20,24},{24,28},{1,5},{5,9},{9,... | collective-permute-start | bytes 1572872 | tf_op jit(solution)/shard_map/ppermute | solution.py:695
  56.5 21.7 %collective-permute-start = (bf16[512,512]{1,0:T(8,128)(2,1)}, bf16[512,512]{1,0:T(8,128)(2,1)S(1)}, u32[]{:S(2)}, u32[]{:S(2)}) collective-permute-start(bf16[512,512]{1,0:T(8,128)(2,1)} %get-tuple-element.134), channel_id=1, source_target_pairs={{0,4},{4,8},{8,12},{12,16},{16,20},{20,24},{24,28},{1,5},{5,9},{9,... | collective-permute-start | bytes 1572872 | tf_op jit(solution)/shard_map/ppermute | solution.py:695
  60.2 0.8 copy-start.1
  78.2 0.8 copy-start.2
Sparse Core Ops, SparseCore 0:
  19.6 39.9 all-gather.5
  172.5 54.9 all-gather.3

commit v9 on v8

--- a/solution.py
+++ b/solution.py
@@ -765,12 +765,14 @@
 
 
 def owners(count):
-    attn, feed = count // 4 - 1, count // 4
+    low, high = count // 4 - 1, count // 4
     return (
-        (0, 1, 2 * attn, 0),
-        (1, 1, 2 * attn + 1, 0),
-        (2, 2, 2 * feed, 0),
-        (4, 2, 2 * feed + 1, 2),
+        (0, 1, 0, 0),
+        (1, 1, count - 2, 0),
+        (2, 2, 2 * low, 0),
+        (4, 2, 2 * low + 1, 2),
+        (2, 2, 2 * high, 0),
+        (4, 2, 2 * high + 1, 2),
     )
 
 
@@ -1125,7 +1127,56 @@
 Z_SEMS = 4
 
 
-def reduce_kernel(
+def halves(value):
+    high = value.astype(bf16)
+    return high, (value - high.astype(f32)).astype(bf16)
+
+
+def times(left, right):
+    (left_high, left_low), (right_high, right_low) = left, right
+    return dot_nn(
+        jnp.concatenate([left_high, left_high, left_low], 1),
+        jnp.concatenate([right_high, right_low, right_high], 0),
+    )
+
+
+def mirrored(first, second, third):
+    return jnp.concatenate(
+        [
+            jnp.concatenate([first, second], 1),
+            jnp.concatenate([jnp.transpose(second), third], 1),
+        ],
+        0,
+    )
+
+
+def times_even(left, right):
+    (left_high, left_low), (right_high, right_low) = left, right
+    wide = jnp.concatenate([left_high, left_high, left_low], 1)
+    tall = jnp.concatenate([right_high, right_low, right_high], 0)
+    return mirrored(
+        dot_nn(wide[:HALF], tall[:, :HALF]),
+        dot_nn(wide[:HALF], tall[:, HALF:]),
+        dot_nn(wide[HALF:], tall[:, HALF:]),
+    )
+
+
+def gram_of(both):
+    high, low = both
+    wide = jnp.concatenate([high, high, low], 1)
+    tall = jnp.concatenate([high, low, high], 1)
+    return mirrored(
+        dot_nt(wide[:HALF], tall[:HALF]),
+        dot_nt(wide[:HALF], tall[HALF:]),
+        dot_nt(wide[HALF:], tall[HALF:]),
+    )
+
+
+def clip_of(norm):
+    return jnp.minimum(1.0, 0.25 / (norm + 1e-06))
+
+
+def tail_kernel(
     count,
     attn_grad_ref,
     attn_done_ref,
@@ -1138,22 +1189,37 @@
     vec2_ref,
     vec3_ref,
     outer_ref,
+    mom_ref,
+    update_ref,
+    every_ref,
+    small_out,
+    norm_ref,
     whole_ref,
     own_ref,
-    small_out,
-    square_out,
+    mom_s,
     small_ref,
-    small_core,
     small_s,
-    small_got,
+    got_core,
+    got_x,
+    got_y,
+    got_z,
     sq_seg,
     sq_dp,
     keep_s,
     give_s,
+    made_ref,
+    x_s,
+    q_s,
+    gram_s,
+    high_s,
+    low_s,
+    mom_sem,
     last_send,
     last_recv,
     small_send,
     small_recv,
+    join_send,
+    join_recv,
     whole_send,
     whole_recv,
     half_sem,
@@ -1161,6 +1227,12 @@
     sq_recv,
     sqd_send,
     sqd_recv,
+    send,
+    recv,
+    on_send,
+    on_recv,
+    own_send,
+    own_recv,
     *refs,
 ):
     carry = AttnCarry(attn_grad_ref, refs[:CARRY_REFS], refs[CARRY_REFS:])
@@ -1169,9 +1241,12 @@
     planes = count // 2
     plane = seg // 2
     group = 2 * y + x
+    rows = own_ref.shape[1]
     targets = [{"seg": other} for other in others(seg, count)] + list(near) + list(far)
     hail(targets)
     carry.load_all()
+    mom_copy = pltpu.make_async_copy(mom_ref, mom_s, mom_sem.at[0])
+    mom_copy.start()
     own_ref[1] = attn_done_ref[...]
 
     @pl.when(x == y)
@@ -1190,43 +1265,55 @@
         remote(give_s.at[0], own_ref.at[2 + y], last_send.at[0], last_recv.at[0], across_y),
         remote(give_s.at[1], own_ref.at[4 + x], last_send.at[1], last_recv.at[1], across_x),
     )
-
     inputs = din_ref.shape[0]
     small_ref[0:inputs, :] = din_ref[...]
     for place, ref in enumerate((vec0_ref, vec1_ref, vec2_ref, vec3_ref, outer_ref)):
         small_ref[inputs + 8 * place : inputs + 8 * place + 8, :] = ref[...]
     small_ref[inputs + 40 :, :] = jnp.zeros((SMALL - inputs - 40, D), f32)
     meet(targets)
+
+    def span(first, size):
+        return pl.ds(pl.multiple_of(first, 8), size)
+
+    by_core, by_x, by_y = SMALL // 2, SMALL // 4, SMALL // 8
+    core_at = core * by_core
+    x_at = core_at + x * by_x
+    y_at = x_at + y * by_y
+
     def small_steps():
-        copy = remote(small_ref, small_core, small_send.at[0], small_recv.at[0], across_core)
+        kept = span(core_at, by_core)
+        copy = remote(
+            small_ref.at[span(by_core - core_at, by_core)], got_core, small_send.at[0], small_recv.at[0], across_core
+        )
         copy.start()
         yield
         copy.wait()
-        small_s[...] = small_ref[...] + small_core[...]
-        half = pl.ds(pl.multiple_of(core * (SMALL // 2), 8), SMALL // 2)
-        targets = [across_x, across_y] + far
-        step = 1
+        small_s[kept, :] = small_ref[kept, :] + got_core[...]
+        sent = span(core_at + by_x - x * by_x, by_x)
+        copy = remote(small_s.at[sent], got_x, small_send.at[1], small_recv.at[1], across_x)
+        copy.start()
+        yield
+        copy.wait()
+        small_s[span(x_at, by_x), :] += got_x[...]
+        sent = span(x_at + by_y - y * by_y, by_y)
+        copy = remote(small_s.at[sent], got_y, small_send.at[2], small_recv.at[2], across_y)
+        copy.start()
+        yield
+        copy.wait()
+        kept = span(y_at, by_y)
+        small_s[kept, :] += got_y[...]
+        partners, step = list(far), 1
         while step < planes:
-            targets.append({"seg": seg + 2 * step - 4 * step * ((plane // step) % 2)})
+            partners.append({"seg": 2 * carry.toggled(step) + core})
             step *= 2
-        for place, target in enumerate(targets):
+        for place, partner in enumerate(partners):
             copy = remote(
-                small_s.at[half],
-                small_got.at[place],
-                small_send.at[place + 1],
-                small_recv.at[place + 1],
-                target,
+                small_s.at[kept], got_z.at[place], small_send.at[3 + place], small_recv.at[3 + place], partner
             )
             copy.start()
             yield
             copy.wait()
-            small_s[half, :] += small_got[place]
-        small_out[half, :] = small_s[half, :]
-        last = len(targets) + 1
-        copy = remote(small_out.at[half], small_out.at[half], small_send.at[last], small_recv.at[last], across_core)
-        copy.start()
-        yield
-        copy.wait()
+            small_s[kept, :] += got_z[place]
 
     small_run = small_steps()
     next(small_run)
@@ -1270,25 +1357,39 @@
         if turn == 0:
             for copy in last:
                 copy.wait()
-            for place in (2, 3):
+            for place in range(2, 6):
                 give(place)
         next(small_run, None)
     own_ref[0] = carry.total()
     give(0)
     for _ in small_run:
         pass
+
+    mine = span(y_at, by_y)
+    small_out[mine, :] = small_s[mine, :]
+
+    def join(place):
+        first, size, partner = ((y_at, by_y, across_y), (x_at, by_x, across_x), (core_at, by_core, across_core))[place]
+        block = small_out.at[span(first, size)]
+        return remote(block, block, join_send.at[place], join_recv.at[place], partner)
+
+    join(0).start()
     shard = dout_ref[...].astype(f32)
     square = jnp.sum(jnp.sum(shard * shard, 0, keepdims=True), 1, keepdims=True)
     for unit in range(UNITS):
         value = own_ref[unit].astype(f32)
         square = square + jnp.sum(jnp.sum(value * value, 0, keepdims=True), 1, keepdims=True)
+    sums = small_s[mine, :]
+    is_loss = lax.broadcasted_iota(jnp.int32, (by_y, D), 0) + y_at == inputs + 37
+    sums = jnp.where(is_loss, 0.0, sums)
+    square = square + jnp.sum(jnp.sum(sums * sums, 0, keepdims=True), 1, keepdims=True) * (1.0 / planes)
     sq_seg[seg] = jnp.broadcast_to(square, (8, 128))
     for step, other in enumerate(others(seg, count)):
         remote(sq_seg.at[seg], sq_seg.at[seg], sq_send.at[step], sq_recv.at[seg], {"seg": other}).start()
 
     def halves_copy(spot):
-        span = slice(spot, spot + 2)
-        return remote(whole_ref.at[:, span], whole_ref.at[:, span], half_sem.at[0], half_sem.at[1], across_core)
+        part = slice(spot, spot + 2)
+        return remote(whole_ref.at[:, part], whole_ref.at[:, part], half_sem.at[0], half_sem.at[1], across_core)
 
     for place, (first, width, owner, spot) in enumerate(roles):
         if width == 2:
@@ -1304,13 +1405,21 @@
     sq_dp[group] = jnp.sum(sq_seg[...], 0)
     for place, target in enumerate(near):
         remote(sq_dp.at[group], sq_dp.at[group], sqd_send.at[place], sqd_recv.at[place], target).start()
-    sums = small_out[...]
-    is_loss = lax.broadcasted_iota(jnp.int32, (SMALL, D), 0) == inputs + 37
-    sums = jnp.where(is_loss, 0.0, sums)
-    small_square = jnp.sum(jnp.sum(sums * sums, 0, keepdims=True), 1, keepdims=True)
+    join(0).wait()
+    join(1).start()
     for place, target in enumerate(near):
         remote(sq_dp.at[group], sq_dp.at[group], sqd_send.at[place], sqd_recv.at[place], target).wait()
-    square_out[...] = jnp.sum(sq_dp[...], 0) + jnp.broadcast_to(small_square, (8, 128))
+    norm = jnp.sqrt(jnp.sum(sq_dp[...], 0)[0:1, 0:1])
+    norm_ref[...] = jnp.broadcast_to(norm, norm_ref.shape)
+    clip = clip_of(norm)
+
+    def own_rows(side):
+        return remote(own_ref, every_ref.at[group], own_send.at[side], own_recv.at[side], near[side])
+
+    for side in range(3):
+        own_rows(side).start()
+    every_ref[group] = own_ref[...]
+    mom_copy.wait()
 
     for place, (first, width, owner, spot) in enumerate(roles):
 
@@ -1322,6 +1431,136 @@
                 for other in others(seg, count):
                     wait_bytes(whole_ref.at[other, spot : spot + width], whole_recv.at[other])
 
+    is_down = group >= 2
+    eye = (
+        lax.broadcasted_iota(jnp.int32, (D, D), 0) == lax.broadcasted_iota(jnp.int32, (D, D), 1)
+    ).astype(f32)
+    low = count // 4 - 1
+    half = plane // (planes // 2)
+    base = half * planes
+    neighbours = [base + lax.rem(seg - base + step, planes) for step in range(1, planes)]
+    feed_maker = 2 * (low + half)
+    makers = [0, count - 2, feed_maker, feed_maker, feed_maker + 1, feed_maker + 1]
+
+    def receivers(unit):
+        return others(seg, count) if unit < 2 else neighbours
+
+    def present(unit, slot, other):
+        return remote(
+            made_ref.at[other, slot],
+            update_ref.at[group, unit],
+            send.at[slot, other],
+            recv.at[unit],
+            {"seg": other},
+        )
+
+    def hand_out(unit, slot):
+        for other in receivers(unit):
+            present(unit, slot, other).start()
+        update_ref[group, unit] = made_ref[seg, slot]
+
+    def onward(unit, side):
+        block = update_ref.at[group, unit]
+        return remote(block, block, on_send.at[side, unit], on_recv.at[side, unit], near[side])
+
+    @pl.when((seg == 0) | (seg == count - 2))
+    def _():
+        start = (0.5 * mom_s[:, plane // (planes - 1)].astype(f32)).reshape(D, D)
+        start = start + clip * whole_ref[:, 0].astype(f32).reshape(D, D)
+        size = jnp.sum(jnp.sum(start * start, 0, keepdims=True), 1, keepdims=True)
+        x_s[...] = start / (jnp.sqrt(size) + 1e-07)
+
+        def sweep(_, state):
+            value = x_s[...]
+            both = halves(value)
+            gram = gram_of(both)
+            gram_both = halves(gram)
+            poly = -4.775 * gram + 2.0315 * times_even(gram_both, gram_both)
+            x_s[...] = 3.4445 * value + times(halves(poly), both)
+            return state
+
+        lax.fori_loop(0, 5, sweep, 0)
+        made_ref[:, 0] = x_s[...].astype(bf16).reshape(count, rows, D)
+        for unit in range(2):
+
+            @pl.when(seg == makers[unit])
+            def _():
+                hand_out(unit, 0)
+
+    @pl.when((plane == low) | (plane == low + 1))
+    def _():
+        gram_s[...] = jnp.zeros_like(gram_s)
+
+        def gather(tile, size):
+            value = (0.5 * mom_s[:, 2 + tile].astype(f32)).reshape(D, D)
+            value = value + clip * whole_ref[:, tile].astype(f32).reshape(D, D)
+            high, rest = halves(value)
+            high_s[tile] = high
+            low_s[tile] = rest
+
+            @pl.when(is_down)
+            def _():
+                high_s[tile] = jnp.transpose(high_s[tile])
+                low_s[tile] = jnp.transpose(low_s[tile])
+
+            gram_s[...] += gram_of((high_s[tile], low_s[tile]))
+            return size + jnp.sum(jnp.sum(value * value, 0, keepdims=True), 1, keepdims=True)
+
+        size = lax.fori_loop(0, 4, gather, jnp.zeros((1, 1), f32))
+        scale = 1.0 / (jnp.sqrt(size) + 1e-07)
+        gram_s[...] = gram_s[...] * (scale * scale)
+
+        def poly_of(gram, gram_both):
+            return 3.4445 * eye - 4.775 * gram + 2.0315 * times_even(gram_both, gram_both)
+
+        def advance(gram_both, poly_both):
+            gram_s[...] = times_even(halves(times_even(gram_both, poly_both)), poly_both)
+
+        gram = gram_s[...]
+        gram_both = halves(gram)
+        poly = poly_of(gram, gram_both)
+        q_s[...] = poly
+        advance(gram_both, halves(poly))
+
+        def sweep(_, state):
+            gram = gram_s[...]
+            gram_both = halves(gram)
+            poly_both = halves(poly_of(gram, gram_both))
+            q_s[...] = times_even(halves(q_s[...]), poly_both)
+            advance(gram_both, poly_both)
+            return state
+
+        lax.fori_loop(0, 3, sweep, 0)
+        gram = gram_s[...]
+        last_both = halves(times_even(halves(q_s[...]), halves(poly_of(gram, halves(gram)))) * scale)
+        for slot in range(2):
+            tile = 2 * core + slot
+            x_s[...] = times(last_both, (high_s[tile], low_s[tile]))
+
+            @pl.when(is_down)
+            def _():
+                x_s[...] = jnp.transpose(x_s[...])
+
+            made_ref[:, slot] = x_s[...].astype(bf16).reshape(count, rows, D)
+            for side in range(2):
+
+                @pl.when(core == side)
+                def _():
+                    hand_out(2 + 2 * side + slot, slot)
+
+    join(1).wait()
+    join(2).start()
+    for unit in (0, 1, 2, 4, 3, 5):
+
+        @pl.when(seg != makers[unit])
+        def _():
+            wait_bytes(update_ref.at[group, unit], recv.at[unit])
+
+        for side in range(3):
+            onward(unit, side).start()
+    join(2).wait()
+    for side in range(3):
+        own_rows(side).wait()
     carry.drain()
     for place, (first, width, owner, spot) in enumerate(roles):
 
@@ -1331,42 +1570,72 @@
 
     for step in range(count - 1):
         wait_bytes(sq_seg.at[0], sq_send.at[step])
-
-
-def reduce_grads(count, dp_count, attn, done, feed_low, feed_high, dout, pieces):
+    for unit in range(UNITS):
+        for side in range(3):
+            onward(unit, side).wait()
+
+        @pl.when(seg == makers[unit])
+        def _():
+            slot = 0 if unit < 2 else unit % 2
+            for other in receivers(unit):
+                present(unit, slot, other).wait_send()
+
+
+def tail(count, dp_count, attn, done, feed_low, feed_high, dout, pieces, momenta):
     rows = D // count
     planes = count // 2
-    stages = 2 + planes.bit_length() + max(0, dp_count.bit_length() - 3)
+    stages = planes.bit_length() + max(0, dp_count.bit_length() - 3)
     dma = pltpu.SemaphoreType.DMA
-    vmem = pl.BlockSpec(memory_space=pltpu.VMEM)
+    vmem, anywhere = pl.BlockSpec(memory_space=pltpu.VMEM), pl.BlockSpec(memory_space=pl.ANY)
+    blocks = jax.ShapeDtypeStruct((GROUPS, UNITS, rows, D), bf16)
     return pl.pallas_call(
-        functools.partial(reduce_kernel, count),
+        functools.partial(tail_kernel, count),
         out_shape=[
-            jax.ShapeDtypeStruct((count, 4, rows, D), bf16),
-            jax.ShapeDtypeStruct((UNITS, rows, D), bf16),
+            blocks,
+            blocks,
             jax.ShapeDtypeStruct((SMALL, D), f32),
             jax.ShapeDtypeStruct((8, 128), f32),
         ],
-        in_specs=[pl.BlockSpec(memory_space=pl.ANY)] + [vmem] * 10,
+        in_specs=[anywhere] + [vmem] * 10 + [anywhere],
         out_specs=[vmem] * 4,
         scratch_shapes=[
+            pltpu.VMEM((count, 4, rows, D), bf16),
+            pltpu.VMEM((UNITS, rows, D), bf16),
+            pltpu.VMEM(momenta.shape, bf16),
             pltpu.VMEM((SMALL, D), f32),
             pltpu.VMEM((SMALL, D), f32),
-            pltpu.VMEM((SMALL, D), f32),
-            pltpu.VMEM((stages, SMALL // 2, D), f32),
+            pltpu.VMEM((SMALL // 2, D), f32),
+            pltpu.VMEM((SMALL // 4, D), f32),
+            pltpu.VMEM((SMALL // 8, D), f32),
+            pltpu.VMEM((stages, SMALL // 8, D), f32),
             pltpu.VMEM((count, 8, 128), f32),
             pltpu.VMEM((GROUPS, 8, 128), f32),
             pltpu.VMEM((2, rows, D), bf16),
             pltpu.VMEM((2, rows, D), bf16),
+            pltpu.VMEM((count, 2, rows, D), bf16),
+            pltpu.VMEM((D, D), f32),
+            pltpu.VMEM((D, D), f32),
+            pltpu.VMEM((D, D), f32),
+            pltpu.VMEM((4, D, D), bf16),
+            pltpu.VMEM((4, D, D), bf16),
+            dma((1,)),
             dma((2,)),
             dma((2,)),
-            dma((stages + 2,)),
-            dma((stages + 2,)),
-            dma((4,)),
+            dma((stages + 3,)),
+            dma((stages + 3,)),
+            dma((3,)),
+            dma((3,)),
+            dma((6,)),
             dma((count,)),
             dma((2,)),
             dma((count,)),
             dma((count,)),
+            dma((3,)),
+            dma((3,)),
+            dma((2, count)),
+            dma((UNITS,)),
+            dma((3, UNITS)),
+            dma((3, UNITS)),
             dma((3,)),
             dma((3,)),
         ]
@@ -1374,262 +1643,9 @@
         compiler_params=pltpu.CompilerParams(
             collective_id=1, has_side_effects=True, vmem_limit_bytes=VMEM_LIMIT
         ),
-        cost_estimate=pl.CostEstimate(flops=10**8, bytes_accessed=10**8, transcendentals=0),
-        name="reduce_grads",
-    )(attn.reshape(2, 2, count, rows, D), done, feed_low, feed_high, dout, *pieces)
-
-
-def halves(value):
-    high = value.astype(bf16)
-    return high, (value - high.astype(f32)).astype(bf16)
-
-
-def times(left, right):
-    (left_high, left_low), (right_high, right_low) = left, right
-    return dot_nn(
-        jnp.concatenate([left_high, left_high, left_low], 1),
-        jnp.concatenate([right_high, right_low, right_high], 0),
-    )
-
-
-def mirrored(first, second, third):
-    return jnp.concatenate(
-        [
-            jnp.concatenate([first, second], 1),
-            jnp.concatenate([jnp.transpose(second), third], 1),
-        ],
-        0,
-    )
-
-
-def times_even(left, right):
-    (left_high, left_low), (right_high, right_low) = left, right
-    wide = jnp.concatenate([left_high, left_high, left_low], 1)
-    tall = jnp.concatenate([right_high, right_low, right_high], 0)
-    return mirrored(
-        dot_nn(wide[:HALF], tall[:, :HALF]),
-        dot_nn(wide[:HALF], tall[:, HALF:]),
-        dot_nn(wide[HALF:], tall[:, HALF:]),
-    )
-
-
-def gram_of(both):
-    high, low = both
-    wide = jnp.concatenate([high, high, low], 1)
-    tall = jnp.concatenate([high, low, high], 1)
-    return mirrored(
-        dot_nt(wide[:HALF], tall[:HALF]),
-        dot_nt(wide[:HALF], tall[HALF:]),
-        dot_nt(wide[HALF:], tall[HALF:]),
-    )
-
-
-def clip_of(norm):
-    return jnp.minimum(1.0, 0.25 / (norm + 1e-06))
-
-
-def muon_kernel(
-    count,
-    square_ref,
-    whole_ref,
-    mom_ref,
-    own_ref,
-    update_ref,
-    every_ref,
-    norm_ref,
-    made_ref,
-    x_s,
-    q_s,
-    gram_s,
-    high_s,
-    low_s,
-    send,
-    recv,
-    on_send,
-    on_recv,
-    own_send,
-    own_recv,
-):
-    seg, dp, core, x, y, across_core, near, far = peers()
-    group = 2 * y + x
-    plane = seg // 2
-    targets = [{"seg": other} for other in others(seg, count)] + list(near)
-    hail(targets)
-    is_down = group >= 2
-    norm = jnp.sqrt(square_ref[0:1, 0:1])
-    norm_ref[...] = jnp.broadcast_to(norm, norm_ref.shape)
-    clip = clip_of(norm)
-    eye = (
-        lax.broadcasted_iota(jnp.int32, (D, D), 0) == lax.broadcasted_iota(jnp.int32, (D, D), 1)
-    ).astype(f32)
-    rows = whole_ref.shape[2]
-    makers = [attn for _, _, attn, _ in owners(count)]
-    units = [makers[0], makers[1], makers[2], makers[2], makers[3], makers[3]]
-
-    def own_rows(side):
-        return remote(own_ref, every_ref.at[group], own_send.at[side], own_recv.at[side], near[side])
-
-    def gift(unit, slot, other):
-        return remote(
-            made_ref.at[other, slot],
-            update_ref.at[group, unit],
-            send.at[slot, other],
-            recv.at[unit],
-            {"seg": other},
-        )
-
-    def give(unit, slot):
-        for other in others(seg, count):
-            gift(unit, slot, other).start()
-        update_ref[group, unit] = made_ref[seg, slot]
-
-    def onward(unit, side):
-        block = update_ref.at[group, unit]
-        return remote(block, block, on_send.at[side, unit], on_recv.at[side, unit], near[side])
-
-    meet(targets)
-    for side in range(3):
-        own_rows(side).start()
-    every_ref[group] = own_ref[...]
-
-    @pl.when(plane == count // 4 - 1)
-    def _():
-        start = (0.5 * mom_ref[:, core].astype(f32)).reshape(D, D)
-        start = start + clip * whole_ref[:, 0].astype(f32).reshape(D, D)
-        size = jnp.sum(jnp.sum(start * start, 0, keepdims=True), 1, keepdims=True)
-        x_s[...] = start / (jnp.sqrt(size) + 1e-07)
-
-        def sweep(_, carry):
-            value = x_s[...]
-            both = halves(value)
-            gram = gram_of(both)
-            gram_both = halves(gram)
-            poly = -4.775 * gram + 2.0315 * times_even(gram_both, gram_both)
-            x_s[...] = 3.4445 * value + times(halves(poly), both)
-            return carry
-
-        lax.fori_loop(0, 5, sweep, 0)
-        made_ref[:, 0] = x_s[...].astype(bf16).reshape(count, rows, D)
-        for unit in range(2):
-
-            @pl.when(core == unit)
-            def _():
-                give(unit, 0)
-
-    @pl.when(plane == count // 4)
-    def _():
-        gram_s[...] = jnp.zeros_like(gram_s)
-
-        def gather(tile, size):
-            value = (0.5 * mom_ref[:, 2 + tile].astype(f32)).reshape(D, D)
-            value = value + clip * whole_ref[:, tile].astype(f32).reshape(D, D)
-            high, low = halves(value)
-            high_s[tile] = high
-            low_s[tile] = low
-
-            @pl.when(is_down)
-            def _():
-                high_s[tile] = jnp.transpose(high_s[tile])
-                low_s[tile] = jnp.transpose(low_s[tile])
-
-            both = high_s[tile], low_s[tile]
-            gram_s[...] += gram_of(both)
-            return size + jnp.sum(jnp.sum(value * value, 0, keepdims=True), 1, keepdims=True)
-
-        size = lax.fori_loop(0, 4, gather, jnp.zeros((1, 1), f32))
-        scale = 1.0 / (jnp.sqrt(size) + 1e-07)
-        gram_s[...] = gram_s[...] * (scale * scale)
-
-        def poly_of(gram, gram_both):
-            return 3.4445 * eye - 4.775 * gram + 2.0315 * times_even(gram_both, gram_both)
-
-        def advance(gram_both, poly_both):
-            gram_s[...] = times_even(halves(times_even(gram_both, poly_both)), poly_both)
-
-        gram = gram_s[...]
-        gram_both = halves(gram)
-        poly = poly_of(gram, gram_both)
-        q_s[...] = poly
-        advance(gram_both, halves(poly))
-
-        def sweep(_, carry):
-            gram = gram_s[...]
-            gram_both = halves(gram)
-            poly_both = halves(poly_of(gram, gram_both))
-            q_s[...] = times_even(halves(q_s[...]), poly_both)
-            advance(gram_both, poly_both)
-            return carry
-
-        lax.fori_loop(0, 3, sweep, 0)
-        gram = gram_s[...]
-        last = times_even(halves(q_s[...]), halves(poly_of(gram, halves(gram)))) * scale
-        last_both = halves(last)
-        for slot in range(2):
-            tile = 2 * core + slot
-            x_s[...] = times(last_both, (high_s[tile], low_s[tile]))
-
-            @pl.when(is_down)
-            def _():
-                x_s[...] = jnp.transpose(x_s[...])
-
-            made_ref[:, slot] = x_s[...].astype(bf16).reshape(count, rows, D)
-            for half in range(2):
-
-                @pl.when(core == half)
-                def _():
-                    give(2 + 2 * half + slot, slot)
-
-    for unit in (0, 1, 2, 4, 3, 5):
-
-        @pl.when(seg != units[unit])
-        def _():
-            wait_bytes(update_ref.at[group, unit], recv.at[unit])
-
-        for side in range(3):
-            onward(unit, side).start()
-    for side in range(3):
-        own_rows(side).wait()
-    for unit in range(UNITS):
-        for side in range(3):
-            onward(unit, side).wait()
-
-        @pl.when(seg == units[unit])
-        def _():
-            slot = 0 if unit < 2 else unit % 2
-            for other in others(seg, count):
-                gift(unit, slot, other).wait_send()
-
-
-def muon(count, squares, whole, momenta, own):
-    rows = whole.shape[2]
-    dma = pltpu.SemaphoreType.DMA
-    vmem = pl.BlockSpec(memory_space=pltpu.VMEM)
-    blocks = jax.ShapeDtypeStruct((GROUPS, UNITS, rows, D), bf16)
-    return pl.pallas_call(
-        functools.partial(muon_kernel, count),
-        out_shape=[blocks, blocks, jax.ShapeDtypeStruct((8, 128), f32)],
-        in_specs=[vmem] * 4,
-        out_specs=[vmem] * 3,
-        scratch_shapes=[
-            pltpu.VMEM((count, 2, rows, D), bf16),
-            pltpu.VMEM((D, D), f32),
-            pltpu.VMEM((D, D), f32),
-            pltpu.VMEM((D, D), f32),
-            pltpu.VMEM((4, D, D), bf16),
-            pltpu.VMEM((4, D, D), bf16),
-            dma((2, count)),
-            dma((UNITS,)),
-            dma((3, UNITS)),
-            dma((3, UNITS)),
-            dma((3,)),
-            dma((3,)),
-        ],
-        compiler_params=pltpu.CompilerParams(
-            collective_id=2, has_side_effects=True, vmem_limit_bytes=VMEM_LIMIT
-        ),
-        cost_estimate=pl.CostEstimate(flops=2 * 10**10, bytes_accessed=4 * 10**7, transcendentals=0),
-        name="muon",
-    )(squares, whole, momenta, own)
+        cost_estimate=pl.CostEstimate(flops=2 * 10**10, bytes_accessed=10**8, transcendentals=0),
+        name="tail",
+    )(attn.reshape(2, 2, count, rows, D), done, feed_low, feed_high, dout, *pieces, momenta)
 
 
 def embed_kernel(
@@ -2025,7 +2041,7 @@
     out_done, attn_done = carried_done
     every_out = lax.all_gather(out_done, ("dp", "seg"), axis=0, tiled=True)[: GROUPS * D // 2]
     every_out = every_out.reshape(GROUPS, D // 2, D)
-    whole, own, small, squares = reduce_grads(
+    updates, every, small, norm = tail(
         count,
         dp_count,
         grad_attn,
@@ -2034,8 +2050,8 @@
         feed_done[1],
         out_done,
         [grad_in] + vector_grads + [head_outer],
+        momenta,
     )
-    updates, every, norm = muon(count, squares, whole, momenta, own)
     split = (LAYERS, 4, rows, D)
     halved = (2, D // 2, out_proj.shape[1])
     (

time: 354 us -> 343 us (0.969)
  Pallas kernels: 324 us -> 314 us
    pallas_call x2 -> x1, Pallas kernels: 88.5 us -> 78.3 us  [tail(): pl.pallas_call(functools.partial(tail_kernel, count), out_shape=[blocks,...]
  transfers between devices with their start and end apart: 4 -> 4, of which waited for: 0 -> 0; matrix products, arithmetic and copies ran while one was open for 0% -> 0% of each run, Pallas kernels for 64% -> 63%
where the time goes in v9:
time: 343 us; the launch traced here: 337 us
  Pallas kernels  314 us (92%)
  between operations  14.7 us (4%)
  starting transfers between devices  6.01 us (2%)
    pallas_call x2, Pallas kernels, attend_back(): pl.pallas_call(functools.partial(attend_back_kernel, streams, depth), gri...  81.6 us
    pallas_call x1, Pallas kernels, tail(): pl.pallas_call(functools.partial(tail_kernel, count), out_shape=[blocks,...  78.3 us
    pallas_call x4, Pallas kernels, forward_layer(): pl.pallas_call(functools.partial(forward_kernel, depth, stream), grid=(1,...  68.2 us
    pallas_call x2, Pallas kernels, feed_back(): pl.pallas_call(functools.partial(feed_back_kernel, streams), grid=(stream...  49.7 us
    pallas_call x1, Pallas kernels, finish(): pl.pallas_call(finish_kernel, grid=(steps,), out_shape=[like(attn), like(...  13 us
    pallas_call x1, Pallas kernels, embed(): pl.pallas_call(functools.partial(embed_kernel, count), out_shape=[jax.Sha...  12.2 us
    pallas_call x1, Pallas kernels, head(): pl.pallas_call(functools.partial(head_kernel, scale), grid=(streams,), ou...  10.6 us
  transfers between devices with their start and end apart: 4, of which 0 were waited for; matrix products, arithmetic and copies ran while one was open for 0% of the time, Pallas kernels for 63%

profile of v9, /device:TPU:0, one launch (start us, length us, event | category | flops | bytes accessed | tf_op | source)
XLA Modules:
  0.0 336.6 jit_solution(4644398928812006830)
XLA Ops:
  7.2 0.0 copy-start
  7.2 0.0 all-gather.6.cloned.1.call-start
  7.3 12.2 %embed.1 = (f32[2,512,512]{2,1,0:T(8,128)}, bf16[2,512,512]{2,1,0:T(8,128)(2,1)}, f32[8,128]{1,0:T(8,128)}, bf16[6,64,512]{2,1,0:T(8,128)(2,1)}) custom-call(bf16[2,80,512]{2,1,0:T(8,128)(2,1)} %bitcast.39, s32[2,512]{1,0:T(2,128)} %mask_ref.3, bf16[80,512]{1,0:T(8,128)(2,1)} %in_ref.1, f32[5,512]{1,0:T(8,128)} %refs_15_.1, f32[2,4,64,512]{3,2,1,0:T(8,128)} %refs_1_.1, ...), custom_call_target="tpu_custom_call" | custom-call | flops 200000000 | bytes 4000000 | tf_op jit(solution)/shard_map/embed/pallas_call | solution.py:1718
  19.5 0.0 all-gather.6.cloned.1.call-update
  19.5 0.0 all-gather.4.cloned.1.call-start
  19.6 0.0 copy-done
  19.6 0.6 copy.78.vec_ref
  20.2 17.0 %layer_forward.4 = (f32[2,512,512]{2,1,0:T(8,128)}, bf16[512,512]{1,0:T(8,128)(2,1)}, bf16[2,1024,512]{2,1,0:T(8,128)(2,1)}, bf16[2,512,512]{2,1,0:T(8,128)(2,1)...) custom-call(f32[1]{0:T(128)} %bitcast.bias_ref, ...), custom_call_target="tpu_custom_call" | custom-call | flops 10000000000 | bytes 20000000 | tf_op jit(solution)/shard_map/layer_forward/pallas_call | solution.py:246
  37.2 2.2 collective-permute-start.1
  39.4 17.0 %layer_forward.5 = (f32[2,512,512]{2,1,0:T(8,128)}, bf16[512,512]{1,0:T(8,128)(2,1)}, bf16[2,1024,512]{2,1,0:T(8,128)(2,1)}, bf16[2,512,512]{2,1,0:T(8,128)(2,1)...) custom-call(f32[1]{0:T(128)} %bitcast.bias_ref, ...), custom_call_target="tpu_custom_call", output_to_operand_aliasing={{0}: (7, {}), {2}: (8, {}), {3}: (9, {}), {4}: (10, {}), {5... | custom-call | flops 10000000000 | bytes 20000000 | tf_op jit(solution)/shard_map/layer_forward/pallas_call | solution.py:246
  56.5 3.7 %collective-permute-start = (bf16[512,512]{1,0:T(8,128)(2,1)}, bf16[512,512]{1,0:T(8,128)(2,1)S(1)}, u32[]{:S(2)}, u32[]{:S(2)}) collective-permute-start(bf16[512,512]{1,0:T(8,128)(2,1)} %get-tuple-element.131), channel_id=1, source_target_pairs={{0,4},{4,8},{8,12},{12,16},{16,20},{20,24},{24,28},{1,5},{5,9},{9,... | collective-permute-start | bytes 1572872 | tf_op jit(solution)/shard_map/ppermute | solution.py:695
  60.2 0.0 collective-permute-done.1.mem_ref
  60.2 0.0 copy-start.1
  60.2 0.8 copy-done.1
  61.0 17.2 %layer_forward.6 = (f32[2,512,512]{2,1,0:T(8,128)}, bf16[512,512]{1,0:T(8,128)(2,1)}, bf16[2,1024,512]{2,1,0:T(8,128)(2,1)}, bf16[2,512,512]{2,1,0:T(8,128)(2,1)...) custom-call(f32[1]{0:T(128)} %bitcast.bias_ref, ...), custom_call_target="tpu_custom_call" | custom-call | flops 10000000000 | bytes 20000000 | tf_op jit(solution)/shard_map/layer_forward/pallas_call | solution.py:246
  78.2 0.0 collective-permute-done.mem_ref
  78.2 0.0 copy-start.2
  78.2 0.8 copy-done.2
  79.0 17.0 %layer_forward.7 = (f32[2,512,512]{2,1,0:T(8,128)}, bf16[512,512]{1,0:T(8,128)(2,1)}, bf16[2,1024,512]{2,1,0:T(8,128)(2,1)}, bf16[2,512,512]{2,1,0:T(8,128)(2,1)...) custom-call(f32[1]{0:T(128)} %bitcast.bias_ref, ...), custom_call_target="tpu_custom_call", output_to_operand_aliasing={{0}: (7, {}), {2}: (8, {}), {3}: (9, {}), {4}: (10, {}), {5... | custom-call | flops 10000000000 | bytes 20000000 | tf_op jit(solution)/shard_map/layer_forward/pallas_call | solution.py:246
  96.0 0.0 all-gather.6.cloned.1.call-done
  96.0 10.6 %head.1 = (f32[2,512,512]{2,1,0:T(8,128)}, f32[2,2,256,512]{3,2,1,0:T(8,128)}, f32[8,512]{1,0:T(8,128)}) custom-call(f32[2,512,512]{2,1,0:T(8,128)} %get-tuple-element.142.x_ref, s32[2,512]{1,0:T(2,128)} %target_ref.1, s32[2,512]{1,0:T(2,128)} %mask_ref.3, f32[8,128]{1,0:T(8,128)} %get-tuple-element.143.total_ref, bf16[512,1024]{1,0:T(8,128)(2,1)} %out_ref.1, ...), custom_call_target="tpu_custom_call" | custom-call | flops 3300000000 | bytes 10000000 | tf_op jit(solution)/shard_map/head/pallas_call | solution.py:320
  106.6 25.4 %feed_back.2 = (f32[2,512,512]{2,1,0:T(8,128)}, bf16[4,512,512]{2,1,0:T(8,128)(2,1)}, bf16[2048,512]{1,0:T(8,128)(2,1)}, f32[8,512]{1,0:T(8,128)}, f32[4,32,512]{2,1,0:T(8,128)}) custom-call(f32[2,512,512]{2,1,0:T(8,128)} %get-tuple-element.145.g_ref, f32[2,512,512]{2,1,0:T(8,128)} %get-tuple-element.146.after_ref, bf16[2,512,2048]{2,1,0:T(8,128)(2,1)} %up_ref.11, ...), custom_call_target="tpu_custom_call" | custom-call | flops 11000000512 | bytes 20000000 | tf_op jit(solution)/shard_map/feed_back/pallas_call | solution.py:455
  132.0 40.3 %attend_back.2 = (f32[2,512,512]{2,1,0:T(8,128)}, bf16[4,512,512]{2,1,0:T(8,128)(2,1)}, f32[8,512]{1,0:T(8,128)}, f32[80,512]{1,0:T(8,128)}, bf16[2,64,512]{2,1,0:T(8,128)(2,1)}, /*index=5*/bf16[32,512]{1,0:T(8,128)(2,1)}) custom-call(f32[1]{0:T(128)} %bitcast.bias_ref, f32[2,512,512]{2,1,0:T(8,128)} %get-tuple-element.148.dafter_ref, ...), custom_call_target="tpu_custom_call" | custom-call | flops 30000001024 | bytes 20000000 | tf_op jit(solution)/shard_map/attend_back/pallas_call | solution.py:636
  172.3 0.0 all-gather.4.cloned.1.call-update
  172.4 24.3 %feed_back.3 = (f32[2,512,512]{2,1,0:T(8,128)}, bf16[4,512,512]{2,1,0:T(8,128)(2,1)}, bf16[2048,512]{1,0:T(8,128)(2,1)}, f32[8,512]{1,0:T(8,128)}, bf16[4,64,512]{2,1,0:T(8,128)(2,1)}) custom-call(f32[2,512,512]{2,1,0:T(8,128)} %get-tuple-element.159.g_ref, f32[2,512,512]{2,1,0:T(8,128)} %get-tuple-element.160.after_ref, bf16[2,512,2048]{2,1,0:T(8,128)(2,1)} %up_ref.11, ...), custom_call_target="tpu_custom_call" | custom-call | flops 11000000512 | bytes 20000000 | tf_op jit(solution)/shard_map/feed_back/pallas_call | solution.py:455
  196.6 41.2 %attend_back.3 = (f32[2,512,512]{2,1,0:T(8,128)}, bf16[4,512,512]{2,1,0:T(8,128)(2,1)}, f32[8,512]{1,0:T(8,128)}, f32[80,512]{1,0:T(8,128)}, bf16[2,64,512]{2,1,0:T(8,128)(2,1)}, /*index=5*/bf16[64,512]{1,0:T(8,128)(2,1)}) custom-call(f32[1]{0:T(128)} %bitcast.bias_ref, f32[2,512,512]{2,1,0:T(8,128)} %get-tuple-element.162.dafter_ref, ...), custom_call_target="tpu_custom_call" | custom-call | flops 30000001024 | bytes 20000000 | tf_op jit(solution)/shard_map/attend_back/pallas_call | solution.py:636
  237.9 78.3 %tail.1 = (bf16[4,6,64,512]{3,2,1,0:T(8,128)(2,1)}, bf16[4,6,64,512]{3,2,1,0:T(8,128)(2,1)}, f32[128,512]{1,0:T(8,128)}, f32[8,128]{1,0:T(8,128)}) custom-call(bf16[2,2,8,64,512]{4,3,2,1,0:T(8,128)(2,1)} %bitcast.56, bf16[64,512]{1,0:T(8,128)(2,1)} %get-tuple-element.174.attn_done_ref, bf16[2,64,512]{2,1,0:T(8,128)(2,1)} %get-tuple-element.175.feed_low_ref, ...), custom_call_target="tpu_custom_call" | custom-call | flops 20000000000 | bytes 100000000 | tf_op jit(solution)/shard_map/tail/pallas_call | solution.py:1591
  316.2 0.0 all-gather.4.cloned.1.call-done
  316.2 13.0 %finish.1 = (f32[2,4,64,512]{3,2,1,0:T(8,128)}, f32[2,4,64,512]{3,2,1,0:T(8,128)}, bf16[2,4,64,512]{3,2,1,0:T(8,128)(2,1)}, f32[2,64,2048]{2,1,0:T(8,128)}, f32[...) custom-call(f32[8,128]{1,0:T(8,128)} %get-tuple-element.184.norm_ref, ...), custom_call_target="tpu_custom_call" | custom-call | flops 100000000 | bytes 40000000 | tf_op jit(solution)/shard_map/finish/pallas_call | solution.py:1914
Async XLA Ops:
  7.2 12.4 %copy-start = (f32[2,12,512]{2,0,1:T(2,128)S(1)}, f32[2,12,512]{2,0,1:T(2,128)}, u32[]{:S(2)}) copy-start(f32[2,12,512]{2,0,1:T(2,128)} %param.35) | copy-start | bytes 147460
  7.2 88.8 %all-gather.6.cloned.1.call-start = ((), (), s32[]{:S(2)}) async-start(), calls=%async_computation.1 | async-start | bytes 3538944 | tf_op jit(solution)/shard_map/all_gather | solution.py:1987
  19.5 296.7 %all-gather.4.cloned.1.call-start = ((), (), s32[]{:S(2)}) async-start(), calls=%async_computation | async-start | bytes 1081344 | tf_op jit(solution)/shard_map/all_gather | solution.py:2042
  37.2 23.0 %collective-permute-start.1 = (bf16[512,512]{1,0:T(8,128)(2,1)}, bf16[512,512]{1,0:T(8,128)(2,1)S(1)}, u32[]{:S(2)}, u32[]{:S(2)}) collective-permute-start(bf16[512,512]{1,0:T(8,128)(2,1)} %get-tuple-element.132), channel_id=1, source_target_pairs={{0,4},{4,8},{8,12},{12,16},{16,20},{20,24},{24,28},{1,5},{5,9},{9,... | collective-permute-start | bytes 1572872 | tf_op jit(solution)/shard_map/ppermute | solution.py:695
  56.5 21.7 %collective-permute-start = (bf16[512,512]{1,0:T(8,128)(2,1)}, bf16[512,512]{1,0:T(8,128)(2,1)S(1)}, u32[]{:S(2)}, u32[]{:S(2)}) collective-permute-start(bf16[512,512]{1,0:T(8,128)(2,1)} %get-tuple-element.131), channel_id=1, source_target_pairs={{0,4},{4,8},{8,12},{12,16},{16,20},{20,24},{24,28},{1,5},{5,9},{9,... | collective-permute-start | bytes 1572872 | tf_op jit(solution)/shard_map/ppermute | solution.py:695
  60.2 0.8 copy-start.1
  78.2 0.8 copy-start.2
Sparse Core Ops, SparseCore 0:
  19.6 39.9 all-gather.5
  172.5 54.9 all-gather.3

commit v10 on v9

--- a/solution.py
+++ b/solution.py
@@ -19,6 +19,7 @@
 PAIR = 2 * HEAD_DIM
 TILE = 512
 VMEM_LIMIT = 56 * 1024 * 1024
+TAIL_LIMIT = 32 * 1024 * 1024
 GELU_SCALE = math.sqrt(2.0 / math.pi)
 
 f32 = jnp.float32
@@ -135,20 +136,20 @@
 
     def pair_body(pair, carry):
         lanes = pair_lanes(pair)
+        blocks = []
         for block in range(2):
             rows = slice(block * HALF, (block + 1) * HALF)
             q_pair = q_ref[rows, lanes]
             q_both = jnp.concatenate([q_pair * first, q_pair * second], 0)
-            spans = [(0, SEG, 0)]
+            spans = [(0, SEG)]
             if block:
-                spans.append((SEG, SEG + HALF, 1))
-            spans.append((SEG + block * HALF, SEG + (block + 1) * HALF, 2))
-            scores = []
-            for low, high, kind in spans:
-                part = dot_nt(q_both, k_ref[low:high, lanes])
-                if kind == 2:
-                    part = jnp.where(diagonal, part, -1e30)
-                scores.append(part)
+                spans.append((SEG, SEG + HALF))
+            spans.append((SEG + block * HALF, SEG + (block + 1) * HALF))
+            scores = [dot_nt(q_both, k_ref[low:high, lanes]) for low, high in spans]
+            scores[-1] = jnp.where(diagonal, scores[-1], -1e30)
+            blocks.append((rows, spans, scores))
+        results = []
+        for rows, spans, scores in blocks:
             peaks = [jnp.max(part, -1, keepdims=True) for part in scores]
             peaks[0] = peaks[0] + memory_bias
             most = functools.reduce(jnp.maximum, peaks)
@@ -160,12 +161,12 @@
                 jnp.add,
                 [
                     dot_nn(part.astype(bf16), v_ref[low:high, lanes])
-                    for part, (low, high, kind) in zip(weights, spans)
+                    for part, (low, high) in zip(weights, spans)
                 ],
             )
-            mixed = mixed / total
+            results.append((rows, mixed / total, most + jnp.log(total)))
+        for rows, mixed, lse in results:
             mixed_ref[rows, lanes] = jnp.where(lane < HEAD_DIM, mixed[:HALF], mixed[HALF:]).astype(bf16)
-            lse = most + jnp.log(total)
             kept = jnp.where(lane == 2 * pair, lse[:HALF], lse_s[rows, :])
             lse_s[rows, :] = jnp.where(lane == 2 * pair + 1, lse[HALF:], kept)
         return carry
@@ -560,10 +561,20 @@
             return jnp.concatenate([one[:, :HALF], two[:, :HALF], one[:, HALF:], two[:, HALF:]], 1)
 
         lse_all, delta_all = rows_of(lse_ref), rows_of(delta_s)
+        starts = (0, 0, 0, 2 * HALF)
+
+        def products(block):
+            keys = slice(block * HALF, (block + 1) * HALF)
+            scores = dot_nt(k_ref[keys, lanes], q_all[starts[block] :])
+            return scores, dot_nt(v_ref[keys, lanes], do_all[starts[block] :])
+
+        ahead = products(0)
         for block in range(4):
+            scores, dweights = ahead
+            if block < 3:
+                ahead = products(block + 1)
             keys = slice(block * HALF, (block + 1) * HALF)
-            start = 2 * HALF if block == 3 else 0
-            scores = dot_nt(k_ref[keys, lanes], q_all[start:])
+            start = starts[block]
             shift = lse_all - memory_bias if block < 2 else lse_all[:, start:]
             weights = jnp.exp(scores - shift)
             if block == 2:
@@ -572,7 +583,6 @@
                 )
             if block == 3:
                 weights = jnp.where(diagonal, weights, 0.0)
-            dweights = dot_nt(v_ref[keys, lanes], do_all[start:])
             dscores = (weights * (dweights - delta_all[:, start:])).astype(bf16)
             dv_s[keys, lanes] = dot_nn(weights.astype(bf16), do_all[start:]).astype(bf16)
             dk_s[keys, lanes] = dot_nn(dscores, q_all[start:]).astype(bf16)
@@ -1641,7 +1651,7 @@
         ]
         + carry_scratch("attn", rows, count, dp_count),
         compiler_params=pltpu.CompilerParams(
-            collective_id=1, has_side_effects=True, vmem_limit_bytes=VMEM_LIMIT
+            collective_id=1, has_side_effects=True, vmem_limit_bytes=TAIL_LIMIT
         ),
         cost_estimate=pl.CostEstimate(flops=2 * 10**10, bytes_accessed=10**8, transcendentals=0),
         name="tail",
@@ -1940,7 +1950,7 @@
         + [vec_spec] * 3
         + [outer_spec] * 3
         + [whole_spec((1, 1))] * 2,
-        compiler_params=pltpu.CompilerParams(vmem_limit_bytes=VMEM_LIMIT),
+        compiler_params=pltpu.CompilerParams(vmem_limit_bytes=(8 + 48 // steps) * 1024 * 1024),
         cost_estimate=pl.CostEstimate(flops=10**8, bytes_accessed=4 * 10**7, transcendentals=0),
         name="finish",
     )(norm, every, updates, dout, small, *arrays)

time: 343 us -> 359 us (1.047)
  local copies, waits for them, and re-layouts: 2.22 us -> 28.3 us
  Pallas kernels: 314 us -> 303 us
    unnamed x7 -> x81, local copies, waits for them, and re-layouts: 2.22 us -> 28.3 us
    pallas_call x4, Pallas kernels: 68.2 us -> 62.3 us  [forward_layer(): pl.pallas_call(functools.partial(forward_kernel, depth, stream), grid=(1,...]
    pallas_call x1, Pallas kernels: 13 us -> 8.29 us  [finish(): pl.pallas_call(finish_kernel, grid=(steps,), out_shape=[like(attn), like(...]
  transfers between devices with their start and end apart: 4 -> 4, of which waited for: 0 -> 0; matrix products, arithmetic and copies ran while one was open for 0% -> 0% of each run, Pallas kernels for 63% -> 58%
where the time goes in v10:
time: 359 us; the launch traced here: 352 us
  Pallas kernels  303 us (84%)
  local copies, waits for them, and re-layouts  28.3 us (8%)
  between operations  14.9 us (4%)
  starting transfers between devices  6.06 us (2%)
    pallas_call x2, Pallas kernels, attend_back(): pl.pallas_call(functools.partial(attend_back_kernel, streams, depth), gri...  81.5 us
    pallas_call x1, Pallas kernels, tail(): pl.pallas_call(functools.partial(tail_kernel, count), out_shape=[blocks,...  75.4 us
    pallas_call x4, Pallas kernels, forward_layer(): pl.pallas_call(functools.partial(forward_kernel, depth, stream), grid=(1,...  62.3 us
    pallas_call x2, Pallas kernels, feed_back(): pl.pallas_call(functools.partial(feed_back_kernel, streams), grid=(stream...  52.4 us
    unnamed x81, local copies, waits for them, and re-layouts  28.3 us
    pallas_call x1, Pallas kernels, embed(): pl.pallas_call(functools.partial(embed_kernel, count), out_shape=[jax.Sha...  12.2 us
    pallas_call x1, Pallas kernels, head(): pl.pallas_call(functools.partial(head_kernel, scale), grid=(streams,), ou...  10.6 us
    pallas_call x1, Pallas kernels, finish(): pl.pallas_call(finish_kernel, grid=(steps,), out_shape=[like(attn), like(...  8.29 us
  transfers between devices with their start and end apart: 4, of which 0 were waited for; matrix products, arithmetic and copies ran while one was open for 0% of the time, Pallas kernels for 58%

profile of v10, /device:TPU:0, one launch (start us, length us, event | category | flops | bytes accessed | tf_op | source)
XLA Modules:
  0.0 352.0 jit_solution(9535808340484211087)
XLA Ops:
  7.2 0.0 copy-start.14
  7.2 0.0 all-gather.6.cloned.1.call-start
  7.3 12.2 %embed.1 = (f32[2,512,512]{2,1,0:T(8,128)}, bf16[2,512,512]{2,1,0:T(8,128)(2,1)}, f32[8,128]{1,0:T(8,128)}, bf16[6,64,512]{2,1,0:T(8,128)(2,1)}) custom-call(bf16[2,80,512]{2,1,0:T(8,128)(2,1)} %bitcast.44, s32[2,512]{1,0:T(2,128)} %mask_ref.3, bf16[80,512]{1,0:T(8,128)(2,1)} %in_ref.1, f32[5,512]{1,0:T(8,128)} %refs_15_.1, f32[2,4,64,512]{3,2,1,0:T(8,128)} %refs_1_.1, ...), custom_call_target="tpu_custom_call" | custom-call | flops 200000000 | bytes 4000000 | tf_op jit(solution)/shard_map/embed/pallas_call | solution.py:1728
  19.5 0.0 all-gather.6.cloned.1.call-update
  19.5 0.0 all-gather.4.cloned.1.call-start
  19.6 0.6 copy.78.vec_ref
  20.2 15.5 %layer_forward.4 = (f32[2,512,512]{2,1,0:T(8,128)}, bf16[512,512]{1,0:T(8,128)(2,1)}, bf16[2,1024,512]{2,1,0:T(8,128)(2,1)}, bf16[2,512,512]{2,1,0:T(8,128)(2,1)...) custom-call(f32[1]{0:T(128)} %bitcast.bias_ref, ...), custom_call_target="tpu_custom_call" | custom-call | flops 10000000000 | bytes 20000000 | tf_op jit(solution)/shard_map/layer_forward/pallas_call | solution.py:247
  35.8 2.2 collective-permute-start.1
  38.0 15.6 %layer_forward.5 = (f32[2,512,512]{2,1,0:T(8,128)}, bf16[512,512]{1,0:T(8,128)(2,1)}, bf16[2,1024,512]{2,1,0:T(8,128)(2,1)}, bf16[2,512,512]{2,1,0:T(8,128)(2,1)...) custom-call(f32[1]{0:T(128)} %bitcast.bias_ref, ...), custom_call_target="tpu_custom_call", output_to_operand_aliasing={{0}: (7, {}), {2}: (8, {}), {3}: (9, {}), {4}: (10, {}), {5... | custom-call | flops 10000000000 | bytes 20000000 | tf_op jit(solution)/shard_map/layer_forward/pallas_call | solution.py:247
  53.6 3.8 %collective-permute-start = (bf16[512,512]{1,0:T(8,128)(2,1)}, bf16[512,512]{1,0:T(8,128)(2,1)S(1)}, u32[]{:S(2)}, u32[]{:S(2)}) collective-permute-start(bf16[512,512]{1,0:T(8,128)(2,1)} %get-tuple-element.131), channel_id=1, source_target_pairs={{0,4},{4,8},{8,12},{12,16},{16,20},{20,24},{24,28},{1,5},{5,9},{9,... | collective-permute-start | bytes 1572872 | tf_op jit(solution)/shard_map/ppermute | solution.py:705
  57.3 0.0 copy-start.38
  57.4 0.8 copy-done.38
  58.1 15.7 %layer_forward.6 = (f32[2,512,512]{2,1,0:T(8,128)}, bf16[512,512]{1,0:T(8,128)(2,1)}, bf16[2,1024,512]{2,1,0:T(8,128)(2,1)}, bf16[2,512,512]{2,1,0:T(8,128)(2,1)...) custom-call(f32[1]{0:T(128)} %bitcast.bias_ref, ...), custom_call_target="tpu_custom_call" | custom-call | flops 10000000000 | bytes 20000000 | tf_op jit(solution)/shard_map/layer_forward/pallas_call | solution.py:247
  73.9 0.8 copy-done.39
  74.7 15.5 %layer_forward.7 = (f32[2,512,512]{2,1,0:T(8,128)}, bf16[512,512]{1,0:T(8,128)(2,1)}, bf16[2,1024,512]{2,1,0:T(8,128)(2,1)}, bf16[2,512,512]{2,1,0:T(8,128)(2,1)...) custom-call(f32[1]{0:T(128)} %bitcast.bias_ref, ...), custom_call_target="tpu_custom_call", output_to_operand_aliasing={{0}: (7, {}), {2}: (8, {}), {3}: (9, {}), {4}: (10, {}), {5... | custom-call | flops 10000000000 | bytes 20000000 | tf_op jit(solution)/shard_map/layer_forward/pallas_call | solution.py:247
  90.2 0.0 all-gather.6.cloned.1.call-done
  90.2 10.6 %head.1 = (f32[2,512,512]{2,1,0:T(8,128)}, f32[2,2,256,512]{3,2,1,0:T(8,128)}, f32[8,512]{1,0:T(8,128)}) custom-call(f32[2,512,512]{2,1,0:T(8,128)} %get-tuple-element.142.x_ref, s32[2,512]{1,0:T(2,128)} %target_ref.1, s32[2,512]{1,0:T(2,128)} %mask_ref.3, f32[8,128]{1,0:T(8,128)} %get-tuple-element.143.total_ref, bf16[512,1024]{1,0:T(8,128)(2,1)} %out_ref.1, ...), custom_call_target="tpu_custom_call" | custom-call | flops 3300000000 | bytes 10000000 | tf_op jit(solution)/shard_map/head/pallas_call | solution.py:321
  100.8 28.3 %feed_back.2 = (f32[2,512,512]{2,1,0:T(8,128)}, bf16[4,512,512]{2,1,0:T(8,128)(2,1)}, bf16[2048,512]{1,0:T(8,128)(2,1)}, f32[8,512]{1,0:T(8,128)}, f32[4,32,512]{2,1,0:T(8,128)}) custom-call(f32[2,512,512]{2,1,0:T(8,128)} %get-tuple-element.145.g_ref, f32[2,512,512]{2,1,0:T(8,128)} %get-tuple-element.146.after_ref, bf16[2,512,2048]{2,1,0:T(8,128)(2,1)} %up_ref.11, ...), custom_call_target="tpu_custom_call" | custom-call | flops 11000000512 | bytes 20000000 | tf_op jit(solution)/shard_map/feed_back/pallas_call | solution.py:456
  129.1 40.3 %attend_back.2 = (f32[2,512,512]{2,1,0:T(8,128)}, bf16[4,512,512]{2,1,0:T(8,128)(2,1)}, f32[8,512]{1,0:T(8,128)}, f32[80,512]{1,0:T(8,128)}, bf16[2,64,512]{2,1,0:T(8,128)(2,1)}, /*index=5*/bf16[32,512]{1,0:T(8,128)(2,1)}) custom-call(f32[1]{0:T(128)} %bitcast.bias_ref, f32[2,512,512]{2,1,0:T(8,128)} %get-tuple-element.148.dafter_ref, ...), custom_call_target="tpu_custom_call" | custom-call | flops 30000001024 | bytes 20000000 | tf_op jit(solution)/shard_map/attend_back/pallas_call | solution.py:646
  169.4 0.0 all-gather.4.cloned.1.call-update
  169.4 24.1 %feed_back.3 = (f32[2,512,512]{2,1,0:T(8,128)}, bf16[4,512,512]{2,1,0:T(8,128)(2,1)}, bf16[2048,512]{1,0:T(8,128)(2,1)}, f32[8,512]{1,0:T(8,128)}, bf16[4,64,512]{2,1,0:T(8,128)(2,1)}) custom-call(f32[2,512,512]{2,1,0:T(8,128)} %get-tuple-element.159.g_ref, f32[2,512,512]{2,1,0:T(8,128)} %get-tuple-element.160.after_ref, bf16[2,512,2048]{2,1,0:T(8,128)(2,1)} %up_ref.11, ...), custom_call_target="tpu_custom_call" | custom-call | flops 11000000512 | bytes 20000000 | tf_op jit(solution)/shard_map/feed_back/pallas_call | solution.py:456
  193.6 41.2 %attend_back.3 = (f32[2,512,512]{2,1,0:T(8,128)}, bf16[4,512,512]{2,1,0:T(8,128)(2,1)}, f32[8,512]{1,0:T(8,128)}, f32[80,512]{1,0:T(8,128)}, bf16[2,64,512]{2,1,0:T(8,128)(2,1)}, /*index=5*/bf16[64,512]{1,0:T(8,128)(2,1)}) custom-call(f32[1]{0:T(128)} %bitcast.bias_ref, f32[2,512,512]{2,1,0:T(8,128)} %get-tuple-element.162.dafter_ref, ...), custom_call_target="tpu_custom_call" | custom-call | flops 30000001024 | bytes 20000000 | tf_op jit(solution)/shard_map/attend_back/pallas_call | solution.py:646
  234.9 1.6 copy-done.28
  236.5 0.9 copy-done.30
  237.4 0.9 copy-done.32
  238.3 0.8 copy-done.35
  239.2 0.7 copy-done.37
  239.9 75.4 %tail.1 = (bf16[4,6,64,512]{3,2,1,0:T(8,128)(2,1)S(1)}, bf16[4,6,64,512]{3,2,1,0:T(8,128)(2,1)S(1)}, f32[128,512]{1,0:T(8,128)S(1)}, f32[8,128]{1,0:T(8,128)S(1)}) custom-call(bf16[2,2,8,64,512]{4,3,2,1,0:T(8,128)(2,1)S(1)} %bitcast.43, bf16[64,512]{1,0:T(8,128)(2,1)S(1)} %copy-done.35, bf16[2,64,512]{2,1,0:T(8,128)(2,1)S(1)} %copy-done.32, ...), custom_call_target="tpu_custom_call" | custom-call | flops 20000000000 | bytes 100000000 | tf_op jit(solution)/shard_map/tail/pallas_call | solution.py:1601
  315.4 1.1 copy-done.6
  316.5 1.1 copy-done.8
  317.7 0.6 copy-done.25
  318.3 1.6 copy-done.3
  319.9 1.6 copy-done.4
  321.5 1.6 copy-done.5
  323.1 1.4 copy-done.7
  324.5 1.4 copy-done.9
  325.9 1.2 copy-done.10
  327.1 1.2 copy-done.11
  328.3 1.2 copy-done.12
  329.6 1.2 copy-done.13
  330.8 0.9 copy-done.16
  331.7 0.9 copy-done.17
  332.6 0.9 copy-done.18
  333.5 0.8 copy-done.21
  334.3 0.7 copy-done.23
  335.0 0.7 copy-done.24
  335.8 0.7 copy-done.26
  336.5 8.3 %finish.1 = (f32[2,4,64,512]{3,2,1,0:T(8,128)}, f32[2,4,64,512]{3,2,1,0:T(8,128)}, bf16[2,4,64,512]{3,2,1,0:T(8,128)(2,1)}, f32[2,64,2048]{2,1,0:T(8,128)}, f32[...) custom-call(f32[8,128]{1,0:T(8,128)S(1)} %copy-done.26, ...), custom_call_target="tpu_custom_call" | custom-call | flops 100000000 | bytes 40000000 | tf_op jit(solution)/shard_map/finish/pallas_call | solution.py:1924
  (55 shorter events, 0.1 us)
Async XLA Ops:
  7.2 12.4 %copy-start.14 = (f32[2,12,512]{2,0,1:T(2,128)S(1)}, f32[2,12,512]{2,0,1:T(2,128)}, u32[]{:S(2)}) copy-start(f32[2,12,512]{2,0,1:T(2,128)} %param.35) | copy-start | bytes 147460
  7.2 83.0 %all-gather.6.cloned.1.call-start = ((), (), s32[]{:S(2)}) async-start(), calls=%async_computation.1 | async-start | bytes 3538944 | tf_op jit(solution)/shard_map/all_gather | solution.py:1997
  19.5 298.7 %all-gather.4.cloned.1.call-start = ((), (), s32[]{:S(2)}) async-start(), calls=%async_computation | async-start | bytes 1081344 | tf_op jit(solution)/shard_map/all_gather | solution.py:2052
  35.8 21.6 %collective-permute-start.1 = (bf16[512,512]{1,0:T(8,128)(2,1)}, bf16[512,512]{1,0:T(8,128)(2,1)S(1)}, u32[]{:S(2)}, u32[]{:S(2)}) collective-permute-start(bf16[512,512]{1,0:T(8,128)(2,1)} %get-tuple-element.132), channel_id=1, source_target_pairs={{0,4},{4,8},{8,12},{12,16},{16,20},{20,24},{24,28},{1,5},{5,9},{9,... | collective-permute-start | bytes 1572872 | tf_op jit(solution)/shard_map/ppermute | solution.py:705
  53.6 20.3 %collective-permute-start = (bf16[512,512]{1,0:T(8,128)(2,1)}, bf16[512,512]{1,0:T(8,128)(2,1)S(1)}, u32[]{:S(2)}, u32[]{:S(2)}) collective-permute-start(bf16[512,512]{1,0:T(8,128)(2,1)} %get-tuple-element.131), channel_id=1, source_target_pairs={{0,4},{4,8},{8,12},{12,16},{16,20},{20,24},{24,28},{1,5},{5,9},{9,... | collective-permute-start | bytes 1572872 | tf_op jit(solution)/shard_map/ppermute | solution.py:705
  57.3 0.8 copy-start.38
  73.9 0.8 copy-start.39
  193.5 41.3 %copy-start.22 = (bf16[32,512]{1,0:T(8,128)(2,1)S(1)}, bf16[32,512]{1,0:T(8,128)(2,1)}, u32[]{:S(2)}) copy-start(bf16[32,512]{1,0:T(8,128)(2,1)} %get-tuple-element.177.dout_ref) | copy-start | bytes 98308
  193.5 41.3 %copy-start.27 = (bf16[48,64,512]{2,1,0:T(8,128)(2,1)S(1)}, bf16[48,64,512]{2,1,0:T(8,128)(2,1)}, u32[]{:S(2)}) copy-start(bf16[48,64,512]{2,1,0:T(8,128)(2,1)} %all-gather.6.cloned.1.call-done) | copy-start | bytes 9437188
  193.5 41.3 %copy-start.29 = (f32[8,512]{1,0:T(8,128)S(1)}, f32[8,512]{1,0:T(8,128)}, u32[]{:S(2)}) copy-start(f32[8,512]{1,0:T(8,128)} %get-tuple-element.183.outer_ref) | copy-start | bytes 49156
  193.6 41.3 %copy-start.31 = (bf16[2,64,512]{2,1,0:T(8,128)(2,1)S(1)}, bf16[2,64,512]{2,1,0:T(8,128)(2,1)}, u32[]{:S(2)}) copy-start(bf16[2,64,512]{2,1,0:T(8,128)(2,1)} %get-tuple-element.176.feed_high_ref) | copy-start | bytes 393220
  193.6 41.3 %copy-start.33 = (f32[8,512]{1,0:T(8,128)S(1)}, f32[8,512]{1,0:T(8,128)}, u32[]{:S(2)}) copy-start(f32[8,512]{1,0:T(8,128)} %get-tuple-element.182.vec3_ref) | copy-start | bytes 49156
  193.6 41.3 %copy-start.34 = (f32[8,512]{1,0:T(8,128)S(1)}, f32[8,512]{1,0:T(8,128)}, u32[]{:S(2)}) copy-start(f32[8,512]{1,0:T(8,128)} %get-tuple-element.180.vec1_ref) | copy-start | bytes 49156
  193.6 41.3 %copy-start.36 = (f32[8,512]{1,0:T(8,128)S(1)}, f32[8,512]{1,0:T(8,128)}, u32[]{:S(2)}) copy-start(f32[8,512]{1,0:T(8,128)} %get-tuple-element.181.vec2_ref) | copy-start | bytes 49156
  234.9 1.6 copy-start.28
  236.5 0.9 copy-start.30
  237.4 0.9 copy-start.32
  238.3 0.8 copy-start.35
  239.2 0.7 copy-start.37
  239.9 78.4 %copy-start = (f32[2,4,64,512]{3,2,1,0:T(8,128)S(1)}, f32[2,4,64,512]{3,2,1,0:T(8,128)}, u32[]{:S(2)}) copy-start(f32[2,4,64,512]{3,2,1,0:T(8,128)} %refs_1_.1) | copy-start | bytes 3145732
  239.9 78.4 %copy-start.1 = (f32[2,64,2048]{2,1,0:T(8,128)S(1)}, f32[2,64,2048]{2,1,0:T(8,128)}, u32[]{:S(2)}) copy-start(f32[2,64,2048]{2,1,0:T(8,128)} %refs_3_.1) | copy-start | bytes 3145732
  239.9 78.4 %copy-start.2 = (f32[2,256,512]{2,1,0:T(8,128)S(1)}, f32[2,256,512]{2,1,0:T(8,128)}, u32[]{:S(2)}) copy-start(f32[2,256,512]{2,1,0:T(8,128)} %param.46) | copy-start | bytes 3145732
  239.9 78.4 %copy-start.15 = (f32[2,12,512]{2,0,1:T(2,128)S(1)}, f32[2,12,512]{2,0,1:T(2,128)}, u32[]{:S(2)}) copy-start(f32[2,12,512]{2,0,1:T(2,128)} %param.35) | copy-start | bytes 147460
  239.9 78.4 %copy-start.19 = (f32[5,512]{1,0:T(8,128)S(1)}, f32[5,512]{1,0:T(8,128)}, u32[]{:S(2)}) copy-start(f32[5,512]{1,0:T(8,128)} %refs_15_.1) | copy-start | bytes 30724
  239.9 78.4 %copy-start.20 = (f32[2,12,512]{2,0,1:T(2,128)S(1)}, f32[2,12,512]{2,0,1:T(2,128)}, u32[]{:S(2)}) copy-start(f32[2,12,512]{2,0,1:T(2,128)} %param.36) | copy-start | bytes 147460
  315.4 1.1 copy-start.6
  316.5 1.1 copy-start.8
  317.6 0.6 copy-start.25
  318.3 1.6 copy-start.3
  319.9 1.6 copy-start.4
  321.5 1.6 copy-start.5
  323.1 1.4 copy-start.7
  324.5 1.4 copy-start.9
  325.9 1.2 copy-start.10
  327.1 1.2 copy-start.11
  328.3 1.2 copy-start.12
  329.6 1.2 copy-start.13
  330.8 0.9 copy-start.16
  331.7 0.9 copy-start.17
  332.6 0.9 copy-start.18
  333.5 0.8 copy-start.21
  334.3 0.7 copy-start.23
  335.0 0.7 copy-start.24
  335.8 0.7 copy-start.26
Sparse Core Ops, SparseCore 0:
  19.6 40.6 all-gather.5
  169.5 54.8 all-gather.3

commit v11 on v10

--- a/solution.py
+++ b/solution.py
@@ -19,7 +19,6 @@
 PAIR = 2 * HEAD_DIM
 TILE = 512
 VMEM_LIMIT = 56 * 1024 * 1024
-TAIL_LIMIT = 32 * 1024 * 1024
 GELU_SCALE = math.sqrt(2.0 / math.pi)
 
 f32 = jnp.float32
@@ -179,9 +178,17 @@
     normed_two = (unit * vec_ref[2:3, :] + vec_ref[3:4, :]).astype(bf16)
     for copy in weights_in:
         copy.wait()
+
+    def inner_of(tile):
+        columns = slice(tile * TILE, (tile + 1) * TILE)
+        return dot_nn(normed_two, up_s[:, columns]) + vec_ref[8 + tile : 9 + tile, :]
+
+    ahead = inner_of(0)
     for tile in range(FF // TILE):
         columns = slice(tile * TILE, (tile + 1) * TILE)
-        inner = dot_nn(normed_two, up_s[:, columns]) + vec_ref[8 + tile : 9 + tile, :]
+        inner = ahead
+        if tile + 1 < FF // TILE:
+            ahead = inner_of(tile + 1)
         act_s[:, columns] = (
             0.5 * inner * (1.0 + jnp.tanh(GELU_SCALE * (inner + 0.044715 * inner * inner * inner)))
         ).astype(bf16)
@@ -378,10 +385,17 @@
         meet(carry.targets)
         carry.send_all()
 
+    def products(tile):
+        columns = slice(tile * TILE, (tile + 1) * TILE)
+        inner = dot_nn(normed, up_ref[:, columns]) + vec_ref[8 + tile : 9 + tile, :]
+        return inner, dot_nt(branch, down_ref[columns, :])
+
+    ahead = products(0)
     for tile in range(FF // TILE):
         columns = slice(tile * TILE, (tile + 1) * TILE)
-        inner = dot_nn(normed, up_ref[:, columns]) + vec_ref[8 + tile : 9 + tile, :]
-        dact = dot_nt(branch, down_ref[columns, :])
+        inner, dact = ahead
+        if tile + 1 < FF // TILE:
+            ahead = products(tile + 1)
         square = inner * inner
         bent = jnp.tanh(inner * (GELU_SCALE + (GELU_SCALE * 0.044715) * square))
         half = 0.5 * (1.0 + bent)
@@ -1331,27 +1345,35 @@
     for copy in last:
         copy.start()
     roles = owners(count)
-
-    def gift(place):
-        first, width, owner, spot = roles[place]
+    parts = []
+    for place, (first, width, owner, spot) in enumerate(roles):
+        if width == 1:
+            parts.append((place, first, spot))
+        elif spot == 0:
+            parts += [(place, 2 + y, y), (place, 3 - y, 1 - y)]
+        else:
+            parts += [(place, 4 + x, 2 + x), (place, 5 - x, 3 - x)]
+
+    def gift(part):
+        place, unit, spot = parts[part]
         return remote(
-            own_ref.at[first : first + width],
-            whole_ref.at[seg, spot : spot + width],
-            whole_send.at[place],
+            own_ref.at[unit],
+            whole_ref.at[seg, spot],
+            whole_send.at[part],
             whole_recv.at[seg],
-            {"seg": owner},
+            {"seg": roles[place][2]},
         )
 
-    def give(place):
-        first, width, owner, spot = roles[place]
-
-        @pl.when(seg != owner)
+    def give(part):
+        place, unit, spot = parts[part]
+
+        @pl.when(seg != roles[place][2])
         def _():
-            gift(place).start()
-
-        @pl.when(seg == owner)
+            gift(part).start()
+
+        @pl.when(seg == roles[place][2])
         def _():
-            whole_ref[seg, spot : spot + width] = own_ref[first : first + width]
+            whole_ref[seg, spot] = own_ref[unit]
 
     acts = [
         [("b", step) for step in range(planes - 1)],
@@ -1360,15 +1382,16 @@
         [("m", 2), ("e", 0)],
         [("m", step) for step in range(3, planes)],
     ] + [[("e", step)] for step in range(1, planes)]
-    give(1)
+    for part in (2, 4, 6, 8, 1):
+        give(part)
     next(small_run)
     for turn, part in enumerate(acts):
         carry.run(part)
         if turn == 0:
             for copy in last:
                 copy.wait()
-            for place in range(2, 6):
-                give(place)
+            for later in (3, 5, 7, 9):
+                give(later)
         next(small_run, None)
     own_ref[0] = carry.total()
     give(0)
@@ -1572,11 +1595,11 @@
     for side in range(3):
         own_rows(side).wait()
     carry.drain()
-    for place, (first, width, owner, spot) in enumerate(roles):
-
-        @pl.when(seg != owner)
+    for part, (place, unit, spot) in enumerate(parts):
+
+        @pl.when(seg != roles[place][2])
         def _():
-            gift(place).wait_send()
+            gift(part).wait_send()
 
     for step in range(count - 1):
         wait_bytes(sq_seg.at[0], sq_send.at[step])
@@ -1635,7 +1658,7 @@
             dma((stages + 3,)),
             dma((3,)),
             dma((3,)),
-            dma((6,)),
+            dma((10,)),
             dma((count,)),
             dma((2,)),
             dma((count,)),
@@ -1651,7 +1674,7 @@
         ]
         + carry_scratch("attn", rows, count, dp_count),
         compiler_params=pltpu.CompilerParams(
-            collective_id=1, has_side_effects=True, vmem_limit_bytes=TAIL_LIMIT
+            collective_id=1, has_side_effects=True, vmem_limit_bytes=VMEM_LIMIT
         ),
         cost_estimate=pl.CostEstimate(flops=2 * 10**10, bytes_accessed=10**8, transcendentals=0),
         name="tail",
@@ -1950,7 +1973,7 @@
         + [vec_spec] * 3
         + [outer_spec] * 3
         + [whole_spec((1, 1))] * 2,
-        compiler_params=pltpu.CompilerParams(vmem_limit_bytes=(8 + 48 // steps) * 1024 * 1024),
+        compiler_params=pltpu.CompilerParams(vmem_limit_bytes=VMEM_LIMIT),
         cost_estimate=pl.CostEstimate(flops=10**8, bytes_accessed=4 * 10**7, transcendentals=0),
         name="finish",
     )(norm, every, updates, dout, small, *arrays)

time: 359 us -> 337 us (0.939)
  local copies, waits for them, and re-layouts: 28.3 us -> 2.22 us
  Pallas kernels: 303 us -> 308 us
    unnamed x81 -> x7, local copies, waits for them, and re-layouts: 28.3 us -> 2.22 us
    pallas_call x1, Pallas kernels: 8.29 us -> 13 us  [finish(): pl.pallas_call(finish_kernel, grid=(steps,), out_shape=[like(attn), like(...]
  transfers between devices with their start and end apart: 4 -> 4, of which waited for: 0 -> 0; matrix products, arithmetic and copies ran while one was open for 0% -> 0% of each run, Pallas kernels for 58% -> 61%
where the time goes in v11:
time: 337 us; the launch traced here: 331 us
  Pallas kernels  308 us (91%)
  between operations  14.7 us (4%)
  starting transfers between devices  6.06 us (2%)
    pallas_call x2, Pallas kernels, attend_back(): pl.pallas_call(functools.partial(attend_back_kernel, streams, depth), gri...  81.3 us
    pallas_call x1, Pallas kernels, tail(): pl.pallas_call(functools.partial(tail_kernel, count), out_shape=[blocks,...  76 us
    pallas_call x4, Pallas kernels, forward_layer(): pl.pallas_call(functools.partial(forward_kernel, depth, stream), grid=(1,...  62.3 us
    pallas_call x2, Pallas kernels, feed_back(): pl.pallas_call(functools.partial(feed_back_kernel, streams), grid=(stream...  52.6 us
    pallas_call x1, Pallas kernels, finish(): pl.pallas_call(finish_kernel, grid=(steps,), out_shape=[like(attn), like(...  13 us
    pallas_call x1, Pallas kernels, embed(): pl.pallas_call(functools.partial(embed_kernel, count), out_shape=[jax.Sha...  12.2 us
    pallas_call x1, Pallas kernels, head(): pl.pallas_call(functools.partial(head_kernel, scale), grid=(streams,), ou...  10.6 us
  transfers between devices with their start and end apart: 4, of which 0 were waited for; matrix products, arithmetic and copies ran while one was open for 0% of the time, Pallas kernels for 61%

profile of v11, /device:TPU:0, one launch (start us, length us, event | category | flops | bytes accessed | tf_op | source)
XLA Modules:
  0.0 331.2 jit_solution(11232862060380097714)
XLA Ops:
  7.2 0.0 copy-start
  7.2 0.0 all-gather.6.cloned.1.call-start
  7.3 12.2 %embed.1 = (f32[2,512,512]{2,1,0:T(8,128)}, bf16[2,512,512]{2,1,0:T(8,128)(2,1)}, f32[8,128]{1,0:T(8,128)}, bf16[6,64,512]{2,1,0:T(8,128)(2,1)}) custom-call(bf16[2,80,512]{2,1,0:T(8,128)(2,1)} %bitcast.39, s32[2,512]{1,0:T(2,128)} %mask_ref.3, bf16[80,512]{1,0:T(8,128)(2,1)} %in_ref.1, f32[5,512]{1,0:T(8,128)} %refs_15_.1, f32[2,4,64,512]{3,2,1,0:T(8,128)} %refs_1_.1, ...), custom_call_target="tpu_custom_call" | custom-call | flops 200000000 | bytes 4000000 | tf_op jit(solution)/shard_map/embed/pallas_call | solution.py:1751
  19.5 0.0 all-gather.6.cloned.1.call-update
  19.5 0.0 all-gather.4.cloned.1.call-start
  19.6 0.0 copy-done
  19.6 0.6 copy.78.vec_ref
  20.2 15.5 %layer_forward.4 = (f32[2,512,512]{2,1,0:T(8,128)}, bf16[512,512]{1,0:T(8,128)(2,1)}, bf16[2,1024,512]{2,1,0:T(8,128)(2,1)}, bf16[2,512,512]{2,1,0:T(8,128)(2,1)...) custom-call(f32[1]{0:T(128)} %bitcast.bias_ref, ...), custom_call_target="tpu_custom_call" | custom-call | flops 10000000000 | bytes 20000000 | tf_op jit(solution)/shard_map/layer_forward/pallas_call | solution.py:254
  35.8 2.2 collective-permute-start.1
  38.0 15.6 %layer_forward.5 = (f32[2,512,512]{2,1,0:T(8,128)}, bf16[512,512]{1,0:T(8,128)(2,1)}, bf16[2,1024,512]{2,1,0:T(8,128)(2,1)}, bf16[2,512,512]{2,1,0:T(8,128)(2,1)...) custom-call(f32[1]{0:T(128)} %bitcast.bias_ref, ...), custom_call_target="tpu_custom_call", output_to_operand_aliasing={{0}: (7, {}), {2}: (8, {}), {3}: (9, {}), {4}: (10, {}), {5... | custom-call | flops 10000000000 | bytes 20000000 | tf_op jit(solution)/shard_map/layer_forward/pallas_call | solution.py:254
  53.6 3.8 %collective-permute-start = (bf16[512,512]{1,0:T(8,128)(2,1)}, bf16[512,512]{1,0:T(8,128)(2,1)S(1)}, u32[]{:S(2)}, u32[]{:S(2)}) collective-permute-start(bf16[512,512]{1,0:T(8,128)(2,1)} %get-tuple-element.131), channel_id=1, source_target_pairs={{0,4},{4,8},{8,12},{12,16},{16,20},{20,24},{24,28},{1,5},{5,9},{9,... | collective-permute-start | bytes 1572872 | tf_op jit(solution)/shard_map/ppermute | solution.py:719
  57.3 0.0 collective-permute-done.1.mem_ref
  57.3 0.0 copy-start.1
  57.4 0.8 copy-done.1
  58.1 15.7 %layer_forward.6 = (f32[2,512,512]{2,1,0:T(8,128)}, bf16[512,512]{1,0:T(8,128)(2,1)}, bf16[2,1024,512]{2,1,0:T(8,128)(2,1)}, bf16[2,512,512]{2,1,0:T(8,128)(2,1)...) custom-call(f32[1]{0:T(128)} %bitcast.bias_ref, ...), custom_call_target="tpu_custom_call" | custom-call | flops 10000000000 | bytes 20000000 | tf_op jit(solution)/shard_map/layer_forward/pallas_call | solution.py:254
  73.9 0.0 collective-permute-done.mem_ref
  73.9 0.0 copy-start.2
  73.9 0.8 copy-done.2
  74.7 15.5 %layer_forward.7 = (f32[2,512,512]{2,1,0:T(8,128)}, bf16[512,512]{1,0:T(8,128)(2,1)}, bf16[2,1024,512]{2,1,0:T(8,128)(2,1)}, bf16[2,512,512]{2,1,0:T(8,128)(2,1)...) custom-call(f32[1]{0:T(128)} %bitcast.bias_ref, ...), custom_call_target="tpu_custom_call", output_to_operand_aliasing={{0}: (7, {}), {2}: (8, {}), {3}: (9, {}), {4}: (10, {}), {5... | custom-call | flops 10000000000 | bytes 20000000 | tf_op jit(solution)/shard_map/layer_forward/pallas_call | solution.py:254
  90.2 0.0 all-gather.6.cloned.1.call-done
  90.2 10.6 %head.1 = (f32[2,512,512]{2,1,0:T(8,128)}, f32[2,2,256,512]{3,2,1,0:T(8,128)}, f32[8,512]{1,0:T(8,128)}) custom-call(f32[2,512,512]{2,1,0:T(8,128)} %get-tuple-element.142.x_ref, s32[2,512]{1,0:T(2,128)} %target_ref.1, s32[2,512]{1,0:T(2,128)} %mask_ref.3, f32[8,128]{1,0:T(8,128)} %get-tuple-element.143.total_ref, bf16[512,1024]{1,0:T(8,128)(2,1)} %out_ref.1, ...), custom_call_target="tpu_custom_call" | custom-call | flops 3300000000 | bytes 10000000 | tf_op jit(solution)/shard_map/head/pallas_call | solution.py:328
  100.8 28.4 %feed_back.2 = (f32[2,512,512]{2,1,0:T(8,128)}, bf16[4,512,512]{2,1,0:T(8,128)(2,1)}, bf16[2048,512]{1,0:T(8,128)(2,1)}, f32[8,512]{1,0:T(8,128)}, f32[4,32,512]{2,1,0:T(8,128)}) custom-call(f32[2,512,512]{2,1,0:T(8,128)} %get-tuple-element.145.g_ref, f32[2,512,512]{2,1,0:T(8,128)} %get-tuple-element.146.after_ref, bf16[2,512,2048]{2,1,0:T(8,128)(2,1)} %up_ref.11, ...), custom_call_target="tpu_custom_call" | custom-call | flops 11000000512 | bytes 20000000 | tf_op jit(solution)/shard_map/feed_back/pallas_call | solution.py:470
  129.2 40.3 %attend_back.2 = (f32[2,512,512]{2,1,0:T(8,128)}, bf16[4,512,512]{2,1,0:T(8,128)(2,1)}, f32[8,512]{1,0:T(8,128)}, f32[80,512]{1,0:T(8,128)}, bf16[2,64,512]{2,1,0:T(8,128)(2,1)}, /*index=5*/bf16[32,512]{1,0:T(8,128)(2,1)}) custom-call(f32[1]{0:T(128)} %bitcast.bias_ref, f32[2,512,512]{2,1,0:T(8,128)} %get-tuple-element.148.dafter_ref, ...), custom_call_target="tpu_custom_call" | custom-call | flops 30000001024 | bytes 20000000 | tf_op jit(solution)/shard_map/attend_back/pallas_call | solution.py:660
  169.5 0.0 all-gather.4.cloned.1.call-update
  169.5 24.3 %feed_back.3 = (f32[2,512,512]{2,1,0:T(8,128)}, bf16[4,512,512]{2,1,0:T(8,128)(2,1)}, bf16[2048,512]{1,0:T(8,128)(2,1)}, f32[8,512]{1,0:T(8,128)}, bf16[4,64,512]{2,1,0:T(8,128)(2,1)}) custom-call(f32[2,512,512]{2,1,0:T(8,128)} %get-tuple-element.159.g_ref, f32[2,512,512]{2,1,0:T(8,128)} %get-tuple-element.160.after_ref, bf16[2,512,2048]{2,1,0:T(8,128)(2,1)} %up_ref.11, ...), custom_call_target="tpu_custom_call" | custom-call | flops 11000000512 | bytes 20000000 | tf_op jit(solution)/shard_map/feed_back/pallas_call | solution.py:470
  193.8 41.0 %attend_back.3 = (f32[2,512,512]{2,1,0:T(8,128)}, bf16[4,512,512]{2,1,0:T(8,128)(2,1)}, f32[8,512]{1,0:T(8,128)}, f32[80,512]{1,0:T(8,128)}, bf16[2,64,512]{2,1,0:T(8,128)(2,1)}, /*index=5*/bf16[64,512]{1,0:T(8,128)(2,1)}) custom-call(f32[1]{0:T(128)} %bitcast.bias_ref, f32[2,512,512]{2,1,0:T(8,128)} %get-tuple-element.162.dafter_ref, ...), custom_call_target="tpu_custom_call" | custom-call | flops 30000001024 | bytes 20000000 | tf_op jit(solution)/shard_map/attend_back/pallas_call | solution.py:660
  234.8 76.0 %tail.1 = (bf16[4,6,64,512]{3,2,1,0:T(8,128)(2,1)}, bf16[4,6,64,512]{3,2,1,0:T(8,128)(2,1)}, f32[128,512]{1,0:T(8,128)}, f32[8,128]{1,0:T(8,128)}) custom-call(bf16[2,2,8,64,512]{4,3,2,1,0:T(8,128)(2,1)} %bitcast.56, bf16[64,512]{1,0:T(8,128)(2,1)} %get-tuple-element.174.attn_done_ref, bf16[2,64,512]{2,1,0:T(8,128)(2,1)} %get-tuple-element.175.feed_low_ref, ...), custom_call_target="tpu_custom_call" | custom-call | flops 20000000000 | bytes 100000000 | tf_op jit(solution)/shard_map/tail/pallas_call | solution.py:1624
  310.8 0.0 all-gather.4.cloned.1.call-done
  310.8 13.0 %finish.1 = (f32[2,4,64,512]{3,2,1,0:T(8,128)}, f32[2,4,64,512]{3,2,1,0:T(8,128)}, bf16[2,4,64,512]{3,2,1,0:T(8,128)(2,1)}, f32[2,64,2048]{2,1,0:T(8,128)}, f32[...) custom-call(f32[8,128]{1,0:T(8,128)} %get-tuple-element.184.norm_ref, ...), custom_call_target="tpu_custom_call" | custom-call | flops 100000000 | bytes 40000000 | tf_op jit(solution)/shard_map/finish/pallas_call | solution.py:1947
Async XLA Ops:
  7.2 12.4 %copy-start = (f32[2,12,512]{2,0,1:T(2,128)S(1)}, f32[2,12,512]{2,0,1:T(2,128)}, u32[]{:S(2)}) copy-start(f32[2,12,512]{2,0,1:T(2,128)} %param.35) | copy-start | bytes 147460
  7.2 83.0 %all-gather.6.cloned.1.call-start = ((), (), s32[]{:S(2)}) async-start(), calls=%async_computation.1 | async-start | bytes 3538944 | tf_op jit(solution)/shard_map/all_gather | solution.py:2020
  19.5 291.3 %all-gather.4.cloned.1.call-start = ((), (), s32[]{:S(2)}) async-start(), calls=%async_computation | async-start | bytes 1081344 | tf_op jit(solution)/shard_map/all_gather | solution.py:2075
  35.8 21.6 %collective-permute-start.1 = (bf16[512,512]{1,0:T(8,128)(2,1)}, bf16[512,512]{1,0:T(8,128)(2,1)S(1)}, u32[]{:S(2)}, u32[]{:S(2)}) collective-permute-start(bf16[512,512]{1,0:T(8,128)(2,1)} %get-tuple-element.132), channel_id=1, source_target_pairs={{0,4},{4,8},{8,12},{12,16},{16,20},{20,24},{24,28},{1,5},{5,9},{9,... | collective-permute-start | bytes 1572872 | tf_op jit(solution)/shard_map/ppermute | solution.py:719
  53.6 20.3 %collective-permute-start = (bf16[512,512]{1,0:T(8,128)(2,1)}, bf16[512,512]{1,0:T(8,128)(2,1)S(1)}, u32[]{:S(2)}, u32[]{:S(2)}) collective-permute-start(bf16[512,512]{1,0:T(8,128)(2,1)} %get-tuple-element.131), channel_id=1, source_target_pairs={{0,4},{4,8},{8,12},{12,16},{16,20},{20,24},{24,28},{1,5},{5,9},{9,... | collective-permute-start | bytes 1572872 | tf_op jit(solution)/shard_map/ppermute | solution.py:719
  57.3 0.8 copy-start.1
  73.9 0.8 copy-start.2
Sparse Core Ops, SparseCore 0:
  19.6 40.6 all-gather.5
  169.6 54.8 all-gather.3

commit v12 on v11

--- a/solution.py
+++ b/solution.py
@@ -366,7 +366,7 @@
 
     @pl.when(step == 0)
     def _():
-        hail(carry.targets)
+        hail(carry.targets[:3])
         carry.load_all()
         dvec_ref[...] = jnp.zeros_like(dvec_ref)
 
@@ -382,7 +382,7 @@
 
     @pl.when(step == 0)
     def _():
-        meet(carry.targets)
+        meet(carry.targets[:3])
         carry.send_all()
 
     def products(tile):

time: 337 us -> 336 us (level)
    pallas_call x2, Pallas kernels: 52.6 us -> 47.5 us  [feed_back(): pl.pallas_call(functools.partial(feed_back_kernel, streams), grid=(stream...]
    pallas_call x2, Pallas kernels: 81.3 us -> 86.1 us  [attend_back(): pl.pallas_call(functools.partial(attend_back_kernel, streams, depth), gri...]
where the time goes in v12:
time: 336 us; the launch traced here: 330 us
  Pallas kernels  307 us (91%)
  between operations  14.7 us (4%)
  starting transfers between devices  6.06 us (2%)
    pallas_call x2, Pallas kernels, attend_back(): pl.pallas_call(functools.partial(attend_back_kernel, streams, depth), gri...  86.1 us
    pallas_call x1, Pallas kernels, tail(): pl.pallas_call(functools.partial(tail_kernel, count), out_shape=[blocks,...  75.3 us
    pallas_call x4, Pallas kernels, forward_layer(): pl.pallas_call(functools.partial(forward_kernel, depth, stream), grid=(1,...  62.3 us
    pallas_call x2, Pallas kernels, feed_back(): pl.pallas_call(functools.partial(feed_back_kernel, streams), grid=(stream...  47.5 us
    pallas_call x1, Pallas kernels, finish(): pl.pallas_call(finish_kernel, grid=(steps,), out_shape=[like(attn), like(...  13 us
    pallas_call x1, Pallas kernels, embed(): pl.pallas_call(functools.partial(embed_kernel, count), out_shape=[jax.Sha...  12.2 us
    pallas_call x1, Pallas kernels, head(): pl.pallas_call(functools.partial(head_kernel, scale), grid=(streams,), ou...  10.6 us
  transfers between devices with their start and end apart: 4, of which 0 were waited for; matrix products, arithmetic and copies ran while one was open for 0% of the time, Pallas kernels for 61%

profile of v12, /device:TPU:0, one launch (start us, length us, event | category | flops | bytes accessed | tf_op | source)
XLA Modules:
  0.0 330.1 jit_solution(4677180076229477977)
XLA Ops:
  7.2 0.0 copy-start
  7.2 0.0 all-gather.6.cloned.1.call-start
  7.3 12.2 %embed.1 = (f32[2,512,512]{2,1,0:T(8,128)}, bf16[2,512,512]{2,1,0:T(8,128)(2,1)}, f32[8,128]{1,0:T(8,128)}, bf16[6,64,512]{2,1,0:T(8,128)(2,1)}) custom-call(bf16[2,80,512]{2,1,0:T(8,128)(2,1)} %bitcast.39, s32[2,512]{1,0:T(2,128)} %mask_ref.3, bf16[80,512]{1,0:T(8,128)(2,1)} %in_ref.1, f32[5,512]{1,0:T(8,128)} %refs_15_.1, f32[2,4,64,512]{3,2,1,0:T(8,128)} %refs_1_.1, ...), custom_call_target="tpu_custom_call" | custom-call | flops 200000000 | bytes 4000000 | tf_op jit(solution)/shard_map/embed/pallas_call | solution.py:1751
  19.5 0.0 all-gather.6.cloned.1.call-update
  19.5 0.0 all-gather.4.cloned.1.call-start
  19.6 0.0 copy-done
  19.6 0.6 copy.78.vec_ref
  20.2 15.5 %layer_forward.4 = (f32[2,512,512]{2,1,0:T(8,128)}, bf16[512,512]{1,0:T(8,128)(2,1)}, bf16[2,1024,512]{2,1,0:T(8,128)(2,1)}, bf16[2,512,512]{2,1,0:T(8,128)(2,1)...) custom-call(f32[1]{0:T(128)} %bitcast.bias_ref, ...), custom_call_target="tpu_custom_call" | custom-call | flops 10000000000 | bytes 20000000 | tf_op jit(solution)/shard_map/layer_forward/pallas_call | solution.py:254
  35.8 2.2 collective-permute-start.1
  38.0 15.6 %layer_forward.5 = (f32[2,512,512]{2,1,0:T(8,128)}, bf16[512,512]{1,0:T(8,128)(2,1)}, bf16[2,1024,512]{2,1,0:T(8,128)(2,1)}, bf16[2,512,512]{2,1,0:T(8,128)(2,1)...) custom-call(f32[1]{0:T(128)} %bitcast.bias_ref, ...), custom_call_target="tpu_custom_call", output_to_operand_aliasing={{0}: (7, {}), {2}: (8, {}), {3}: (9, {}), {4}: (10, {}), {5... | custom-call | flops 10000000000 | bytes 20000000 | tf_op jit(solution)/shard_map/layer_forward/pallas_call | solution.py:254
  53.6 3.8 %collective-permute-start = (bf16[512,512]{1,0:T(8,128)(2,1)}, bf16[512,512]{1,0:T(8,128)(2,1)S(1)}, u32[]{:S(2)}, u32[]{:S(2)}) collective-permute-start(bf16[512,512]{1,0:T(8,128)(2,1)} %get-tuple-element.131), channel_id=1, source_target_pairs={{0,4},{4,8},{8,12},{12,16},{16,20},{20,24},{24,28},{1,5},{5,9},{9,... | collective-permute-start | bytes 1572872 | tf_op jit(solution)/shard_map/ppermute | solution.py:719
  57.3 0.0 collective-permute-done.1.mem_ref
  57.3 0.0 copy-start.1
  57.4 0.8 copy-done.1
  58.1 15.7 %layer_forward.6 = (f32[2,512,512]{2,1,0:T(8,128)}, bf16[512,512]{1,0:T(8,128)(2,1)}, bf16[2,1024,512]{2,1,0:T(8,128)(2,1)}, bf16[2,512,512]{2,1,0:T(8,128)(2,1)...) custom-call(f32[1]{0:T(128)} %bitcast.bias_ref, ...), custom_call_target="tpu_custom_call" | custom-call | flops 10000000000 | bytes 20000000 | tf_op jit(solution)/shard_map/layer_forward/pallas_call | solution.py:254
  73.9 0.0 collective-permute-done.mem_ref
  73.9 0.0 copy-start.2
  73.9 0.8 copy-done.2
  74.7 15.5 %layer_forward.7 = (f32[2,512,512]{2,1,0:T(8,128)}, bf16[512,512]{1,0:T(8,128)(2,1)}, bf16[2,1024,512]{2,1,0:T(8,128)(2,1)}, bf16[2,512,512]{2,1,0:T(8,128)(2,1)...) custom-call(f32[1]{0:T(128)} %bitcast.bias_ref, ...), custom_call_target="tpu_custom_call", output_to_operand_aliasing={{0}: (7, {}), {2}: (8, {}), {3}: (9, {}), {4}: (10, {}), {5... | custom-call | flops 10000000000 | bytes 20000000 | tf_op jit(solution)/shard_map/layer_forward/pallas_call | solution.py:254
  90.2 0.0 all-gather.6.cloned.1.call-done
  90.2 10.6 %head.1 = (f32[2,512,512]{2,1,0:T(8,128)}, f32[2,2,256,512]{3,2,1,0:T(8,128)}, f32[8,512]{1,0:T(8,128)}) custom-call(f32[2,512,512]{2,1,0:T(8,128)} %get-tuple-element.142.x_ref, s32[2,512]{1,0:T(2,128)} %target_ref.1, s32[2,512]{1,0:T(2,128)} %mask_ref.3, f32[8,128]{1,0:T(8,128)} %get-tuple-element.143.total_ref, bf16[512,1024]{1,0:T(8,128)(2,1)} %out_ref.1, ...), custom_call_target="tpu_custom_call" | custom-call | flops 3300000000 | bytes 10000000 | tf_op jit(solution)/shard_map/head/pallas_call | solution.py:328
  100.8 23.8 %feed_back.2 = (f32[2,512,512]{2,1,0:T(8,128)}, bf16[4,512,512]{2,1,0:T(8,128)(2,1)}, bf16[2048,512]{1,0:T(8,128)(2,1)}, f32[8,512]{1,0:T(8,128)}, f32[4,32,512]{2,1,0:T(8,128)}) custom-call(f32[2,512,512]{2,1,0:T(8,128)} %get-tuple-element.145.g_ref, f32[2,512,512]{2,1,0:T(8,128)} %get-tuple-element.146.after_ref, bf16[2,512,2048]{2,1,0:T(8,128)(2,1)} %up_ref.11, ...), custom_call_target="tpu_custom_call" | custom-call | flops 11000000512 | bytes 20000000 | tf_op jit(solution)/shard_map/feed_back/pallas_call | solution.py:470
  124.6 44.9 %attend_back.2 = (f32[2,512,512]{2,1,0:T(8,128)}, bf16[4,512,512]{2,1,0:T(8,128)(2,1)}, f32[8,512]{1,0:T(8,128)}, f32[80,512]{1,0:T(8,128)}, bf16[2,64,512]{2,1,0:T(8,128)(2,1)}, /*index=5*/bf16[32,512]{1,0:T(8,128)(2,1)}) custom-call(f32[1]{0:T(128)} %bitcast.bias_ref, f32[2,512,512]{2,1,0:T(8,128)} %get-tuple-element.148.dafter_ref, ...), custom_call_target="tpu_custom_call" | custom-call | flops 30000001024 | bytes 20000000 | tf_op jit(solution)/shard_map/attend_back/pallas_call | solution.py:660
  169.6 0.0 all-gather.4.cloned.1.call-update
  169.6 23.7 %feed_back.3 = (f32[2,512,512]{2,1,0:T(8,128)}, bf16[4,512,512]{2,1,0:T(8,128)(2,1)}, bf16[2048,512]{1,0:T(8,128)(2,1)}, f32[8,512]{1,0:T(8,128)}, bf16[4,64,512]{2,1,0:T(8,128)(2,1)}) custom-call(f32[2,512,512]{2,1,0:T(8,128)} %get-tuple-element.159.g_ref, f32[2,512,512]{2,1,0:T(8,128)} %get-tuple-element.160.after_ref, bf16[2,512,2048]{2,1,0:T(8,128)(2,1)} %up_ref.11, ...), custom_call_target="tpu_custom_call" | custom-call | flops 11000000512 | bytes 20000000 | tf_op jit(solution)/shard_map/feed_back/pallas_call | solution.py:470
  193.3 41.2 %attend_back.3 = (f32[2,512,512]{2,1,0:T(8,128)}, bf16[4,512,512]{2,1,0:T(8,128)(2,1)}, f32[8,512]{1,0:T(8,128)}, f32[80,512]{1,0:T(8,128)}, bf16[2,64,512]{2,1,0:T(8,128)(2,1)}, /*index=5*/bf16[64,512]{1,0:T(8,128)(2,1)}) custom-call(f32[1]{0:T(128)} %bitcast.bias_ref, f32[2,512,512]{2,1,0:T(8,128)} %get-tuple-element.162.dafter_ref, ...), custom_call_target="tpu_custom_call" | custom-call | flops 30000001024 | bytes 20000000 | tf_op jit(solution)/shard_map/attend_back/pallas_call | solution.py:660
  234.5 75.3 %tail.1 = (bf16[4,6,64,512]{3,2,1,0:T(8,128)(2,1)}, bf16[4,6,64,512]{3,2,1,0:T(8,128)(2,1)}, f32[128,512]{1,0:T(8,128)}, f32[8,128]{1,0:T(8,128)}) custom-call(bf16[2,2,8,64,512]{4,3,2,1,0:T(8,128)(2,1)} %bitcast.56, bf16[64,512]{1,0:T(8,128)(2,1)} %get-tuple-element.174.attn_done_ref, bf16[2,64,512]{2,1,0:T(8,128)(2,1)} %get-tuple-element.175.feed_low_ref, ...), custom_call_target="tpu_custom_call" | custom-call | flops 20000000000 | bytes 100000000 | tf_op jit(solution)/shard_map/tail/pallas_call | solution.py:1624
  309.8 0.0 all-gather.4.cloned.1.call-done
  309.8 13.0 %finish.1 = (f32[2,4,64,512]{3,2,1,0:T(8,128)}, f32[2,4,64,512]{3,2,1,0:T(8,128)}, bf16[2,4,64,512]{3,2,1,0:T(8,128)(2,1)}, f32[2,64,2048]{2,1,0:T(8,128)}, f32[...) custom-call(f32[8,128]{1,0:T(8,128)} %get-tuple-element.184.norm_ref, ...), custom_call_target="tpu_custom_call" | custom-call | flops 100000000 | bytes 40000000 | tf_op jit(solution)/shard_map/finish/pallas_call | solution.py:1947
Async XLA Ops:
  7.2 12.4 %copy-start = (f32[2,12,512]{2,0,1:T(2,128)S(1)}, f32[2,12,512]{2,0,1:T(2,128)}, u32[]{:S(2)}) copy-start(f32[2,12,512]{2,0,1:T(2,128)} %param.35) | copy-start | bytes 147460
  7.2 83.0 %all-gather.6.cloned.1.call-start = ((), (), s32[]{:S(2)}) async-start(), calls=%async_computation.1 | async-start | bytes 3538944 | tf_op jit(solution)/shard_map/all_gather | solution.py:2020
  19.5 290.3 %all-gather.4.cloned.1.call-start = ((), (), s32[]{:S(2)}) async-start(), calls=%async_computation | async-start | bytes 1081344 | tf_op jit(solution)/shard_map/all_gather | solution.py:2075
  35.8 21.6 %collective-permute-start.1 = (bf16[512,512]{1,0:T(8,128)(2,1)}, bf16[512,512]{1,0:T(8,128)(2,1)S(1)}, u32[]{:S(2)}, u32[]{:S(2)}) collective-permute-start(bf16[512,512]{1,0:T(8,128)(2,1)} %get-tuple-element.132), channel_id=1, source_target_pairs={{0,4},{4,8},{8,12},{12,16},{16,20},{20,24},{24,28},{1,5},{5,9},{9,... | collective-permute-start | bytes 1572872 | tf_op jit(solution)/shard_map/ppermute | solution.py:719
  53.6 20.3 %collective-permute-start = (bf16[512,512]{1,0:T(8,128)(2,1)}, bf16[512,512]{1,0:T(8,128)(2,1)S(1)}, u32[]{:S(2)}, u32[]{:S(2)}) collective-permute-start(bf16[512,512]{1,0:T(8,128)(2,1)} %get-tuple-element.131), channel_id=1, source_target_pairs={{0,4},{4,8},{8,12},{12,16},{16,20},{20,24},{24,28},{1,5},{5,9},{9,... | collective-permute-start | bytes 1572872 | tf_op jit(solution)/shard_map/ppermute | solution.py:719
  57.3 0.8 copy-start.1
  73.9 0.8 copy-start.2
Sparse Core Ops, SparseCore 0:
  19.6 40.6 all-gather.5
  169.7 54.4 all-gather.3
